TPU v7x, 32 devices: a whole 2x2x4 slice. The times are simulated.
32 devices in a mesh: ctx: 8 (over z, x), tp: 4 (over y, core).
Axes of the slice: x: 2, y: 2, z: 4, core: 2. Of those that a mesh axis runs over, the one named last changes fastest.
Arguments:
- residual: bfloat16 [2048, 8192], P('ctx', 'tp'), may hold values from -40 to 40
- query_in: bfloat16 [2048, 8192], P('ctx', 'tp'), may hold values from -6 to 6
- key_in: bfloat16 [2048, 8192], P('ctx', 'tp'), may hold values from -6 to 6
- value_in: bfloat16 [2048, 8192], P('ctx', 'tp'), may hold values from -6 to 6
- short_filter: float32 [3, 7, 8192], P(None, None, 'tp'), may hold values from -2 to 2
- residues: float32 [16, 8192], P(None, 'tp'), may hold values from -0.32 to 0.32
- decay_rate: float32 [16, 8192], P(None, 'tp'), may hold values from 9.765625e-05 to 0.05
- skip_gain: float32 [8192], P('tp'), may hold values from 0.5 to 1.5
- norm_gain: float32 [8192], P('tp'), may hold values from 0.5 to 1.5
- cotangent: bfloat16 [2048, 8192], P('ctx', 'tp'), may hold values from -6 to 6
Outputs:
- normed: bfloat16 [2048, 8192], P('ctx', 'tp')
- grad_residual: bfloat16 [2048, 8192], P('ctx', 'tp')
- grad_query: bfloat16 [2048, 8192], P('ctx', 'tp')
- grad_key: bfloat16 [2048, 8192], P('ctx', 'tp')
- grad_value: bfloat16 [2048, 8192], P('ctx', 'tp')
- grad_short: float32 [3, 7, 8192], P(None, None, 'tp')
- grad_residues: float32 [16, 8192], P(None, 'tp')
- grad_rate: float32 [16, 8192], P(None, 'tp')
- grad_skip: float32 [8192], P('tp')
- grad_norm_gain: float32 [8192], P('tp')
All inputs are finite; a program needn't handle non-finite values.
Results may differ from a plain program's by a relative error of at most 0.002.
Values may be sent and summed in bfloat16 or wider, within the bound.
No kernel may reach another device: no remote copies, remote signals or barrier semaphores. Data moves between devices by JAX's collectives and lax.ppermute only.
A program may use at most 128 MiB of HBM per device.

v0:
```python
import jax
import jax.numpy as jnp
from jax import lax
from jax.sharding import PartitionSpec as P

D = 8192


exact_mode = lax.Precision.HIGHEST


def prefix(value, axis, join, neutral, backward):
    count, mine = (lax.axis_size(axis), lax.axis_index(axis))
    pieces = jax.tree.map(lambda part: lax.all_gather(part, axis), value)
    if backward:
        pieces = jax.tree.map(lambda part: part[::-1], pieces)
        mine = count - 1 - mine
    so_far = jax.tree.map(
        lambda part, zero: jnp.full_like(part, 0) + jnp.asarray(zero, part.dtype), value, neutral
    )

    def lap(position, so_far):
        longer = join(so_far, jax.tree.map(lambda part: part[position], pieces))
        return jax.tree.map(lambda new, old: jnp.where(position < mine, new, old), longer, so_far)

    return lax.fori_loop(0, count - 1, lap, so_far)


def shifted(block, axis, distance):
    devices = range(lax.axis_size(axis))
    route = [(i - distance, i) for i in devices if i - distance in devices]
    return lax.ppermute(block, axis, route)


def as_sent(value):

    def short(part):
        return part.astype(jnp.bfloat16) if part.dtype == jnp.float32 else part

    return jax.tree.map(short, value)


def make_tables(decay_rate, residues, block_len):
    lag_values = jnp.arange(block_len).astype(jnp.float32)
    powers = jnp.exp(-decay_rate[None, :, :] * lag_values[:, None, None])
    kernel = jnp.einsum("kmc,mc->kc", powers, residues, precision=exact_mode)
    offsets = jnp.arange(block_len)
    shifter = (offsets[:, None, None] - offsets[None, :, None] == offsets[None, None, :]).astype(
        jnp.float32
    )
    toeplitz = jnp.einsum("tsk,kc->tsc", shifter, kernel, precision=exact_mode)
    return (lag_values, powers, shifter, toeplitz)


def short_conv(extended, taps, row_count):
    tap_count = taps.shape[0]
    result = taps[0] * extended[tap_count - 1 : tap_count - 1 + row_count]
    for offset in range(1, tap_count):
        result = (
            result
            + taps[offset] * extended[tap_count - 1 - offset : tap_count - 1 - offset + row_count]
        )
    return result


def conv_back(extended_grad, taps, row_count):
    tap_count = taps.shape[0]
    result = taps[0] * extended_grad[0:row_count]
    for offset in range(1, tap_count):
        result = result + taps[offset] * extended_grad[offset : offset + row_count]
    return result


def filter_grad(grad_feat, padded, tap_count, row_count):
    margin = tap_count - 1
    columns = [
        jnp.sum(grad_feat * padded[margin - offset : margin - offset + row_count], axis=0)
        for offset in range(tap_count)
    ]
    return jnp.stack(columns)


def summary_pass(u_blocks, decay_rate, tables):
    lag_values, powers, shifter, toeplitz = tables
    block_len = powers.shape[0]
    behind = powers[::-1]
    behind_lag = behind * lag_values[::-1][:, None, None]
    fading = jnp.exp(-decay_rate * block_len)

    def summary_advance(running, u_block):
        state_x, state_p = running
        gathered = jnp.einsum("smc,sc->mc", behind, u_block, precision=exact_mode)
        weighted = jnp.einsum("smc,sc->mc", behind_lag, u_block, precision=exact_mode)
        state_p = fading * state_p - block_len * fading * state_x - weighted
        state_x = fading * state_x + gathered
        return ((state_x, state_p), None)

    zero_state = jnp.zeros_like(decay_rate)
    (state_x, state_p), _ = lax.scan(summary_advance, (zero_state, zero_state), u_blocks)
    return (state_x, state_p)


def output_pass(u_blocks, state_x, state_p, decay_rate, residues, skip_gain, tables):
    lag_values, powers, shifter, toeplitz = tables
    block_len = powers.shape[0]
    ahead_pow = powers * jnp.exp(-decay_rate)[None]
    behind = powers[::-1]
    fading = jnp.exp(-decay_rate * block_len)

    def output_advance(running, u_block):
        state_x, state_p = running
        inside = jnp.einsum("tsc,sc->tc", toeplitz, u_block, precision=exact_mode)
        carried = jnp.einsum("tmc,mc->tc", ahead_pow, residues * state_x, precision=exact_mode)
        result = inside + carried + skip_gain * u_block
        gathered = jnp.einsum("smc,sc->mc", behind, u_block, precision=exact_mode)
        state_x = fading * state_x + gathered
        return ((state_x, state_p), result)

    (state_x, state_p), results = lax.scan(output_advance, (state_x, state_p), u_blocks)
    return (results, state_x, state_p)


def gradient_pass(u_blocks, dz_blocks, state_x, state_p, decay_rate, tables):
    lag_values, powers, shifter, toeplitz = tables
    block_len = powers.shape[0]
    ahead_pow = powers * jnp.exp(-decay_rate)[None]
    ahead_lag = ahead_pow * (lag_values + 1.0)[:, None, None]
    powers_lag = powers * lag_values[:, None, None]
    behind = powers[::-1]
    behind_lag = behind * lag_values[::-1][:, None, None]
    fading = jnp.exp(-decay_rate * block_len)

    def gradient_advance(running, pair):
        state_x, state_p, sum_res, sum_rate = running
        u_block, dz_block = pair
        products = dz_block[:, None, :] * u_block[None, :, :]
        lagged = jnp.einsum("tsk,tsc->kc", shifter, products, precision=exact_mode)
        nearby = jnp.einsum("tmc,tc->mc", ahead_pow, dz_block, precision=exact_mode)
        nearby_lag = jnp.einsum("tmc,tc->mc", ahead_lag, dz_block, precision=exact_mode)
        sum_res = (
            sum_res
            + jnp.einsum("kc,kmc->mc", lagged, powers, precision=exact_mode)
            + nearby * state_x
        )
        sum_rate = (
            sum_rate
            - jnp.einsum("kc,kmc->mc", lagged, powers_lag, precision=exact_mode)
            - nearby_lag * state_x
            + nearby * state_p
        )
        gathered = jnp.einsum("smc,sc->mc", behind, u_block, precision=exact_mode)
        weighted = jnp.einsum("smc,sc->mc", behind_lag, u_block, precision=exact_mode)
        state_p = fading * state_p - block_len * fading * state_x - weighted
        state_x = fading * state_x + gathered
        return ((state_x, state_p, sum_res, sum_rate), None)

    zero_sum = jnp.zeros_like(state_x)
    (state_x, state_p, sum_res, sum_rate), _ = lax.scan(
        gradient_advance, (state_x, state_p, zero_sum, zero_sum), (u_blocks, dz_blocks)
    )
    return (sum_res, sum_rate)


def adjoint_pass(dz_blocks, adjoint, decay_rate, residues, tables):
    lag_values, powers, shifter, toeplitz = tables
    block_len = powers.shape[0]
    behind_next = powers[::-1] * jnp.exp(-decay_rate)[None]
    fading = jnp.exp(-decay_rate * block_len)

    def adjoint_advance(adjoint, dz_block):
        inside = jnp.einsum("tsc,tc->sc", toeplitz, dz_block, precision=exact_mode)
        carried = jnp.einsum("smc,mc->sc", behind_next, residues * adjoint, precision=exact_mode)
        adjoint = (
            jnp.einsum("tmc,tc->mc", powers, dz_block, precision=exact_mode) + fading * adjoint
        )
        return (adjoint, inside + carried)

    adjoint, results = lax.scan(adjoint_advance, adjoint, dz_blocks, reverse=True)
    return (results, adjoint)


def exit_term(adjoint, decay_rate, residues, lag_values, row_count, block_len):
    starts = jnp.arange(row_count // block_len).astype(jnp.float32) * block_len
    weighted_res = residues * adjoint

    def block_term(start):
        behind_pow = jnp.exp(-decay_rate[None] * (row_count - start - lag_values)[:, None, None])
        return jnp.einsum("smc,mc->sc", behind_pow, weighted_res, precision=exact_mode)

    return lax.map(block_term, starts).reshape(row_count, -1)


def carry_forward(summary, slope_sum, decay_rate, row_count):

    def join_states(earlier, later):
        fading = jnp.exp(-decay_rate * (row_count * later[0]))
        return (
            earlier[0] + later[0],
            fading * earlier[1] + later[1],
            fading * earlier[2] - row_count * later[0] * fading * earlier[1] + later[2],
        )

    neutral = (jnp.zeros((), jnp.float32), jnp.zeros_like(summary), jnp.zeros_like(summary))
    _, state_x, state_p = prefix(
        (jnp.ones((), jnp.float32), summary, slope_sum), "ctx", join_states, neutral, False
    )
    return (state_x, state_p)


def carry_backward(entry_sum, decay_rate, row_count):

    def join_adjoint(earlier, later):
        fading = jnp.exp(-decay_rate * (row_count * later[0]))
        return (earlier[0] + later[0], later[1] + fading * earlier[1])

    neutral = (jnp.zeros((), jnp.float32), jnp.zeros_like(entry_sum))
    _, adjoint = prefix((jnp.ones((), jnp.float32), entry_sum), "ctx", join_adjoint, neutral, True)
    return adjoint


def shards(
    residual,
    query_in,
    key_in,
    value_in,
    short_filter,
    residues,
    decay_rate,
    skip_gain,
    norm_gain,
    cotangent,
):
    row_count = residual.shape[0]
    channels = residual.shape[1]
    tap_count = short_filter.shape[1]
    margin = tap_count - 1
    block_len = min(32, row_count)
    streams = (query_in, key_in, value_in)
    trailing = jnp.stack([stream[row_count - margin :] for stream in streams])
    incoming = shifted(trailing, "ctx", 1)
    padded = [
        jnp.concatenate([incoming[stream_id], streams[stream_id]], axis=0).astype(jnp.float32)
        for stream_id in range(3)
    ]
    featured = [
        short_conv(padded[stream_id], short_filter[stream_id], row_count) for stream_id in range(3)
    ]
    mixed_uv = featured[1] * featured[2]
    tables = make_tables(decay_rate, residues, block_len)
    lag_values = tables[0]
    zero_state = jnp.zeros_like(decay_rate)
    u_blocks = mixed_uv.reshape(row_count // block_len, block_len, channels)
    summary, slope_sum = summary_pass(u_blocks, decay_rate, tables)
    state_x, state_p = carry_forward(summary, slope_sum, decay_rate, row_count)
    modal_blocks, _, _ = output_pass(
        u_blocks, state_x, zero_state, decay_rate, residues, skip_gain, tables
    )
    modal = modal_blocks.reshape(row_count, channels)
    summed = residual.astype(jnp.float32) + featured[0] * modal
    cot_values = cotangent.astype(jnp.float32)
    gain_term = cot_values * norm_gain
    squares, inner_sum = lax.psum(
        (jnp.sum(summed * summed, axis=1), jnp.sum(gain_term * summed, axis=1)), "tp"
    )
    inv_rms = lax.rsqrt(squares / D + 1e-05)
    normed = (summed * inv_rms[:, None] * norm_gain).astype(jnp.bfloat16)
    grad_sum = inv_rms[:, None] * gain_term - summed * (inv_rms**3 * inner_sum / D)[:, None]
    grad_modal = grad_sum * featured[0]
    grad_front = grad_sum * modal
    dz_blocks = grad_modal.reshape(row_count // block_len, block_len, channels)
    sum_res, sum_rate = gradient_pass(u_blocks, dz_blocks, state_x, state_p, decay_rate, tables)
    mixed_blocks, entry_sum = adjoint_pass(dz_blocks, zero_state, decay_rate, residues, tables)
    adjoint = carry_backward(entry_sum, decay_rate, row_count)
    grad_mixed = (
        mixed_blocks.reshape(row_count, channels)
        + exit_term(adjoint, decay_rate, residues, lag_values, row_count, block_len)
        + skip_gain * grad_modal
    )
    grad_feats = (grad_front, grad_mixed * featured[2], grad_mixed * featured[1])
    leading = jnp.stack([grad_feat[:margin] for grad_feat in grad_feats])
    overflow = shifted(as_sent(leading), "ctx", -1).astype(leading.dtype)
    grad_streams = [
        conv_back(
            jnp.concatenate([grad_feats[stream_id], overflow[stream_id]], axis=0),
            short_filter[stream_id],
            row_count,
        ).astype(jnp.bfloat16)
        for stream_id in range(3)
    ]
    local_short = jnp.stack(
        [
            filter_grad(grad_feats[stream_id], padded[stream_id], tap_count, row_count)
            for stream_id in range(3)
        ]
    )
    local_skip = jnp.sum(grad_modal * mixed_uv, axis=0)
    local_gain = jnp.sum(cot_values * summed * inv_rms[:, None], axis=0)
    grad_short, grad_residues, grad_rate, grad_skip, grad_gain = lax.psum(
        (local_short, sum_res, residues * sum_rate, local_skip, local_gain), "ctx"
    )
    return (
        normed,
        grad_sum.astype(jnp.bfloat16),
        grad_streams[0],
        grad_streams[1],
        grad_streams[2],
        grad_short,
        grad_residues,
        grad_rate,
        grad_skip,
        grad_gain,
    )


def solution(mesh):
    placed = (
        P("ctx", "tp"),
        P("ctx", "tp"),
        P("ctx", "tp"),
        P("ctx", "tp"),
        P(None, None, "tp"),
        P(None, "tp"),
        P(None, "tp"),
        P("tp"),
        P("tp"),
        P("ctx", "tp"),
    )
    return jax.shard_map(
        shards,
        mesh=mesh,
        in_specs=placed,
        out_specs=(
            P("ctx", "tp"),
            P("ctx", "tp"),
            P("ctx", "tp"),
            P("ctx", "tp"),
            P("ctx", "tp"),
            P(None, None, "tp"),
            P(None, "tp"),
            P(None, "tp"),
            P("tp"),
            P("tp"),
        ),
        check_vma=False,
    )
```

profile of v0, /device:TPU:0, one launch (start us, length us, event | category | flops | bytes accessed | tf_op | source)
XLA Modules:
  0.0 705.5 jit_solution(7220383609164106365)
XLA Ops:
  8.8 4.8 collective-permute-start
  31.6 4.9 fusion.110
  36.5 44.9 %while.111 = (s32[]{:T(128)}, f32[16,2048]{1,0:T(8,128)S(1)}, f32[16,2048]{1,0:T(8,128)S(1)}, f32[16,2048]{1,0:T(8,128)S(1)}, f32[8,32,2048]{2,1,0:T(8,128)}, /*...) while((s32[]{:T(128)}, f32[16,2048]{1,0:T(8,128)S(1)}, ...), condition=%wide.region_1.2_spmd.clone, body=%wide.region_0.1_spmd.clone.sunk | while | flops 4423683 | bytes 10354795 | solution.py:99
  84.2 20.0 %all-reduce = f32[8]{0:T(128)S(1)} all-reduce(f32[8]{0:T(128)S(1)} %dynamic-update-slice), channel_id=1, replica_groups=mesh['ctx'=8,'tp'=4] {'ctx'}, use_global_device_ids=true, to_apply=%add | all-reduce | flops 8 | bytes 64
  106.2 5.7 fusion.96
  113.6 9.2 %all-gather.7.cloned.1.call-done = f32[128,2048]{1,0:T(8,128)} async-done(((f32[16,2048]{1,0:T(8,128)}), f32[128,2048]{1,0:T(8,128)}) %all-gather.7.cloned.1.call-update) | async-done | bytes 1048592 | tf_op jit(solution)/shard_map/all_gather | solution.py:14
  122.8 41.6 %all-gather.9.cloned.1.call-done = f32[128,2048]{1,0:T(8,128)} async-done(((f32[16,2048]{1,0:T(8,128)}), f32[128,2048]{1,0:T(8,128)}) %all-gather.9.cloned.1.call-update) | async-done | bytes 1048592 | tf_op jit(solution)/shard_map/all_gather | solution.py:14
  164.4 16.2 %while.112 = (s32[]{:T(128)}, f32[16,2048]{1,0:T(8,128)S(1)}, f32[16,2048]{1,0:T(8,128)S(1)}, s32[]{:T(128)}, f32[8]{0:T(128)S(1)}, /*index=5*/f32[16,2048]{1,0:...) while((s32[]{:T(128)}, f32[16,2048]{1,0:T(8,128)S(1)}, ...), condition=%wide.region_3.4_spmd.clone, body=%wide.region_2.3_spmd.clone.sunk | while | flops 393221 | bytes 917665 | solution.py:26
  182.9 104.5 %while.109 = (s32[]{:T(128)}, f32[16,2048]{1,0:T(8,128)}, f32[8,32,2048]{2,1,0:T(8,128)}, f32[16,2048]{1,0:T(8,128)S(1)}, f32[8,32,2048]{2,1,0:T(8,128)}, /*inde...) while((s32[]{:T(128)}, f32[16,2048]{1,0:T(8,128)}, ...), condition=%wide.region_5.6_spmd.clone, body=%wide.region_4.5_spmd.clone.sunk | while | flops 10616834 | bytes 17048348 | solution.py:119
  189.4 4.8 multiply_reduce_fusion.50
  215.5 4.8 multiply_reduce_fusion.50
  241.7 4.8 multiply_reduce_fusion.50
  287.4 10.8 %multiply_reduce_fusion.38 = (f32[256]{0:T(256)S(1)}, f32[256,2048]{1,0:T(8,128)}, f32[256,2048]{1,0:T(8,128)}) fusion(f32[8,32,2048]{2,1,0:T(8,128)} %get-tuple-element.774, bf16[256,2048]{1,0:T(8,128)(2,1)} %param.24, f32[262,2048]{1,0:T(8,128)} %maximum_convert_fusion, f32[2048]{0:T(1024)S(1)} %bitcast.320, f32[2048]{0:T(1024)S(1)} %bitcast.322, ...), kind=kLoop, calls=%fused_computation.189 | loop fusion | flops 9436928 | bytes 22078464 | tf_op jit(solution)/shard_map/reduce_sum | solution.py:263
  298.1 5.6 psum.49
  306.3 6.8 psum.50
  313.1 14.0 %multiply_reduce_fusion.31 = (f32[2048]{0:T(1024)S(1)}, f32[2048]{0:T(1024)S(1)}, f32[2048]{0:T(1024)S(1)}, f32[2048]{0:T(1024)S(1)}, f32[2048]{0:T(1024)S(1)}, ...) fusion(f32[262,2048]{1,0:T(8,128)} %maximum_convert_fusion, ...), kind=kLoop, calls=%fused_computation.181 | loop fusion | flops 14139392 | bytes 30484480 | tf_op jit(solution)/shard_map/reduce_sum | solution.py:77
  328.7 98.9 %while.113 = (s32[]{:T(128)}, f32[16,2048]{1,0:T(8,128)}, f32[8,32,2048]{2,1,0:T(8,128)}, f32[8,32,2048]{2,1,0:T(8,128)}, f32[16,2048]{1,0:T(8,128)S(1)}, /*inde...) while((s32[]{:T(128)}, f32[16,2048]{1,0:T(8,128)}, ...), condition=%wide.region_11.12_spmd.clone, body=%wide.region_10.11_spmd.clone.sunk | while | flops 9469956 | bytes 16122139 | solution.py:178
  427.9 96.1 %while.115 = (s32[]{:T(128)}, f32[16,2048]{1,0:T(8,128)S(1)}, f32[16,2048]{1,0:T(8,128)S(1)}, f32[16,2048]{1,0:T(8,128)S(1)}, f32[16,2048]{1,0:T(8,128)S(1)}, /*...) while((s32[]{:T(128)}, f32[16,2048]{1,0:T(8,128)S(1)}, ...), condition=%wide.region_39.40_spmd.clone.clone.clone, body=%wide.region_38.39_spmd.clone.clone.clone.sunk | while | flops 824606720 | bytes 48632316 | solution.py:158
  429.1 5.6 fusion.124
  441.1 5.6 fusion.124
  453.1 5.6 fusion.124
  465.2 5.6 fusion.124
  477.2 5.6 fusion.124
  489.2 5.6 fusion.124
  501.2 5.6 fusion.124
  513.2 5.6 fusion.124
  524.1 35.9 %all-reduce.1 = (f32[2048]{0:T(1024)}, f32[2048]{0:T(1024)}) all-reduce(f32[2048]{0:T(1024)S(1)} %get-tuple-element.1303, f32[2048]{0:T(1024)S(1)} %get-tuple-element.1130), channel_id=1, replica_groups=mesh['ctx'=8,'tp'=4] {'ctx'}, use_global_device_ids=true, to_apply=%region_43.44 | all-reduce | flops 4096 | bytes 32768 | tf_op jit(solution)/shard_map/psum | solution.py:298
  563.8 15.6 %while.114 = (s32[]{:T(128)}, f32[16,2048]{1,0:T(8,128)S(1)}, s32[]{:T(128)}, f32[8,16,2048]{2,1,0:T(8,128)}, f32[8]{0:T(128)S(1)}, /*index=5*/f32[16,2048]{1,0:T(8,128)S(1)}, s32[]{:T(128)}, f32[1]{0:T(128)}, s32[]{:T(128)}) while((s32[]{:T(128)}, f32[16,2048]{1,0:T(8,128)S(1)}, s32[]{:T(128)}, f32[8,16,2048]{2,1,0:T(8,128)}, ...), condition=%wide.region_13.14_spmd.clone, body=%wide.region_12.13_spmd.clone.sunk | while | flops 163845 | bytes 524433 | solution.py:26
  581.6 25.4 %while.110 = (s32[]{:T(128)}, f32[8,32,2048]{2,1,0:T(8,128)}, f32[1,16,2048]{2,1,0:T(8,128)S(1)}, f32[8]{0:T(128)S(1)}, f32[16,2048]{1,0:T(8,128)S(1)}, /*index=5*/s32[]{:T(128)}, f32[1]{0:T(128)}) while((s32[]{:T(128)}, f32[8,32,2048]{2,1,0:T(8,128)}, f32[1,16,2048]{2,1,0:T(8,128)S(1)}, f32[8]{0:T(128)S(1)}, ...), condition=%wide.region_15.16_spmd.clone, body=%wide.region_14.15_spmd.clone.sunk | while | flops 3080259 | bytes 1049449 | solution.py:190
  610.6 6.2 multiply_reduce_fusion.24
  625.4 8.2 %fusion.43 = bf16[256,2048]{1,0:T(8,128)(2,1)} fusion(f32[6,2048]{1,0:T(8,128)S(1)} %get-tuple-element.1306, f32[256,2048]{1,0:T(8,128)} %copy-done.10, f32[2048]{0:T(1024)S(1)} %bitcast.359, f32[2048]{0:T(1024)S(1)} %bitcast.357, f32[2048]{0:T(1024)S(1)} %bitcast.347, f32[2048]{0:T(1024)S(1)} %bitcast.349, f32[2048]{0:T(1024)S(1)} %bitcast.351, ...), kind=kLoop, calls=%fused_computation.100 | loop fusion | flops 10485760 | bytes 3252224 | tf_op jit(solution)/shard_map/convert_element_type | solution.py:287
  639.8 54.1 %all-reduce.5.cloned.1.call-done = (f32[3,7,2048]{2,1,0:T(8,128)}, f32[16,2048]{1,0:T(8,128)}, f32[16,2048]{1,0:T(8,128)}) async-done(((f32[3,7,2048]{2,1,0:T(8,128)}, f32[16,2048]{1,0:T(8,128)}, f32[16,2048]{1,0:T(8,128)}), (f32[3,7,2048]{2,1,0:T(8,128)}, f32[16,2048]{1,0:T(8,128)}, f32[16,2048]{1,0:T(8,128)})) %all-reduce.5.cloned.1.call-update) | async-done | bytes 434192 | tf_op jit(solution)/shard_map/psum | solution.py:298
  (456 shorter events, 387.7 us)
Async XLA Ops:
  7.2 115.6 %all-gather.7.cloned.1.call-start = ((), (), s32[]{:S(2)}) async-start(), calls=%async_computation | async-start | bytes 1179648 | tf_op jit(solution)/shard_map/all_gather | solution.py:14
  8.8 19.5 %collective-permute-start = (bf16[3,6,2048]{2,1,0:T(8,128)(2,1)S(1)}, bf16[3,6,2048]{2,1,0:T(8,128)(2,1)S(1)}, u32[]{:S(2)}, u32[]{:S(2)}) collective-permute-start(bf16[3,6,2048]{2,1,0:T(8,128)(2,1)S(1)} %pad_maximum_fusion.4), channel_id=1, source_target_pairs={{0,4},{4,8},{8,12},{12,16},{16,20},{20,24},{24,28},{1,5},{5,9},{9,... | collective-permute-start | bytes 221192 | tf_op jit(solution)/shard_map/ppermute | solution.py:32
  15.4 16.0 %copy-start.30 = (f32[1,1,2048]{2,1,0:T(1,128)}, f32[1,1,2048]{2,1,0:T(1,128)S(1)}, u32[]{:S(2)}) copy-start(f32[1,1,2048]{2,1,0:T(1,128)S(1)} %get-tuple-element.1315) | copy-start | bytes 24580
  15.4 16.0 %copy-start.32 = (f32[1,1,2048]{2,1,0:T(1,128)}, f32[1,1,2048]{2,1,0:T(1,128)S(1)}, u32[]{:S(2)}) copy-start(f32[1,1,2048]{2,1,0:T(1,128)S(1)} %get-tuple-element.1316) | copy-start | bytes 24580
  15.4 16.0 %copy-start.34 = (f32[1,1,2048]{2,1,0:T(1,128)}, f32[1,1,2048]{2,1,0:T(1,128)S(1)}, u32[]{:S(2)}) copy-start(f32[1,1,2048]{2,1,0:T(1,128)S(1)} %get-tuple-element.1317) | copy-start | bytes 24580
  15.4 16.0 %copy-start.36 = (f32[1,1,2048]{2,1,0:T(1,128)}, f32[1,1,2048]{2,1,0:T(1,128)S(1)}, u32[]{:S(2)}) copy-start(f32[1,1,2048]{2,1,0:T(1,128)S(1)} %get-tuple-element.1318) | copy-start | bytes 24580
  15.4 16.0 %copy-start.38 = (f32[1,1,2048]{2,1,0:T(1,128)}, f32[1,1,2048]{2,1,0:T(1,128)S(1)}, u32[]{:S(2)}) copy-start(f32[1,1,2048]{2,1,0:T(1,128)S(1)} %get-tuple-element.1319) | copy-start | bytes 24580
  15.4 16.0 %copy-start.40 = (f32[1,1,2048]{2,1,0:T(1,128)}, f32[1,1,2048]{2,1,0:T(1,128)S(1)}, u32[]{:S(2)}) copy-start(f32[1,1,2048]{2,1,0:T(1,128)S(1)} %get-tuple-element.1320) | copy-start | bytes 24580
  15.5 16.0 %copy-start.42 = (f32[1,1,2048]{2,1,0:T(1,128)}, f32[1,1,2048]{2,1,0:T(1,128)S(1)}, u32[]{:S(2)}) copy-start(f32[1,1,2048]{2,1,0:T(1,128)S(1)} %get-tuple-element.1321) | copy-start | bytes 24580
  15.5 16.0 %copy-start.44 = (f32[1,1,2048]{2,1,0:T(1,128)}, f32[1,1,2048]{2,1,0:T(1,128)S(1)}, u32[]{:S(2)}) copy-start(f32[1,1,2048]{2,1,0:T(1,128)S(1)} %get-tuple-element.1310) | copy-start | bytes 24580
  15.5 16.0 %copy-start.46 = (f32[1,1,2048]{2,1,0:T(1,128)}, f32[1,1,2048]{2,1,0:T(1,128)S(1)}, u32[]{:S(2)}) copy-start(f32[1,1,2048]{2,1,0:T(1,128)S(1)} %get-tuple-element.1311) | copy-start | bytes 24580
  15.5 16.0 %copy-start.48 = (f32[1,1,2048]{2,1,0:T(1,128)}, f32[1,1,2048]{2,1,0:T(1,128)S(1)}, u32[]{:S(2)}) copy-start(f32[1,1,2048]{2,1,0:T(1,128)S(1)} %get-tuple-element.1312) | copy-start | bytes 24580
  15.5 16.0 %copy-start.50 = (f32[1,1,2048]{2,1,0:T(1,128)}, f32[1,1,2048]{2,1,0:T(1,128)S(1)}, u32[]{:S(2)}) copy-start(f32[1,1,2048]{2,1,0:T(1,128)S(1)} %get-tuple-element.1313) | copy-start | bytes 24580
  15.5 16.0 %copy-start.52 = (f32[1,1,2048]{2,1,0:T(1,128)}, f32[1,1,2048]{2,1,0:T(1,128)S(1)}, u32[]{:S(2)}) copy-start(f32[1,1,2048]{2,1,0:T(1,128)S(1)} %get-tuple-element.1314) | copy-start | bytes 24580
  15.5 271.8 %copy-start.22 = (f32[1,1,2048]{2,1,0:T(1,128)}, f32[1,1,2048]{2,1,0:T(1,128)S(1)}, u32[]{:S(2)}) copy-start(f32[1,1,2048]{2,1,0:T(1,128)S(1)} %get-tuple-element.1324) | copy-start | bytes 24580
  15.5 271.8 %copy-start.24 = (f32[1,1,2048]{2,1,0:T(1,128)}, f32[1,1,2048]{2,1,0:T(1,128)S(1)}, u32[]{:S(2)}) copy-start(f32[1,1,2048]{2,1,0:T(1,128)S(1)} %get-tuple-element.1325) | copy-start | bytes 24580
  15.5 271.8 %copy-start.26 = (f32[1,1,2048]{2,1,0:T(1,128)}, f32[1,1,2048]{2,1,0:T(1,128)S(1)}, u32[]{:S(2)}) copy-start(f32[1,1,2048]{2,1,0:T(1,128)S(1)} %get-tuple-element.1326) | copy-start | bytes 24580
  15.5 271.8 %copy-start.28 = (f32[1,1,2048]{2,1,0:T(1,128)}, f32[1,1,2048]{2,1,0:T(1,128)S(1)}, u32[]{:S(2)}) copy-start(f32[1,1,2048]{2,1,0:T(1,128)S(1)} %get-tuple-element.1327) | copy-start | bytes 24580
  36.5 46.4 %copy-start.60 = (u32[32]{0:T(128)S(1)}, u32[32]{0:T(128)}, u32[]{:S(2)}) copy-start(u32[32]{0:T(128)} %constant.186) | copy-start | bytes 388
  36.5 68.6 %copy-start.6 = (f32[16,2048]{1,0:T(8,128)S(1)}, f32[16,2048]{1,0:T(8,128)}, u32[]{:S(2)}) copy-start(f32[16,2048]{1,0:T(8,128)} %param.29) | copy-start | bytes 393220
  82.0 82.4 %all-gather.9.cloned.1.call-start = ((), (), s32[]{:S(2)}) async-start(), calls=%async_computation.1 | async-start | bytes 1179648 | tf_op jit(solution)/shard_map/all_gather | solution.py:14
  82.8 478.7 %all-gather.11.cloned.1.call-start = ((), (), s32[]{:S(2)}) async-start(), calls=%async_computation.2 | async-start | bytes 1179648 | tf_op jit(solution)/shard_map/all_gather | solution.py:14
  287.3 16.4 %copy-start.58 = (f32[2048]{0:T(1024)S(1)}, f32[2048]{0:T(1024)}, u32[]{:S(2)}) copy-start(f32[2048]{0:T(1024)} %param.32) | copy-start | bytes 24580
  427.7 266.3 %all-reduce.5.cloned.1.call-start = ((), (), s32[]{:S(2)}) async-start(), calls=%async_computation.3 | async-start | bytes 917504 | tf_op jit(solution)/shard_map/psum | solution.py:298
  524.0 39.8 %copy-start.11 = (f32[16,2048]{1,0:T(8,128)}, f32[16,2048]{1,0:T(8,128)S(1)}, u32[]{:S(2)}) copy-start(f32[16,2048]{1,0:T(8,128)S(1)} %get-tuple-element.780) | copy-start | bytes 393220
  524.0 39.7 %copy-start.14 = (f32[16,2048]{1,0:T(8,128)S(1)}, f32[16,2048]{1,0:T(8,128)}, u32[]{:S(2)}) copy-start(f32[16,2048]{1,0:T(8,128)} %custom-call.5) | copy-start | bytes 393220
  563.8 17.9 %copy-start.20 = (f32[1,16,2048]{2,1,0:T(8,128)S(1)}, f32[1,16,2048]{2,1,0:T(8,128)}, u32[]{:S(2)}) copy-start(f32[1,16,2048]{2,1,0:T(8,128)} %get-tuple-element.1992) | copy-start | bytes 393220
  563.8 17.9 %copy-start.59 = (f32[8]{0:T(128)S(1)}, f32[8]{0:T(128)}, u32[]{:S(2)}) copy-start(f32[8]{0:T(128)} %convert_multiply_fusion.2) | copy-start | bytes 100
  618.8 6.5 collective-permute-start.1
  622.5 11.2 %copy-start.37 = (f32[1,1,2048]{2,1,0:T(1,128)S(1)}, f32[1,1,2048]{2,1,0:T(1,128)}, u32[]{:S(2)}) copy-start(f32[1,1,2048]{2,1,0:T(1,128)} %copy-done.36) | copy-start | bytes 24580
  622.5 11.2 %copy-start.39 = (f32[1,1,2048]{2,1,0:T(1,128)S(1)}, f32[1,1,2048]{2,1,0:T(1,128)}, u32[]{:S(2)}) copy-start(f32[1,1,2048]{2,1,0:T(1,128)} %copy-done.38) | copy-start | bytes 24580
  622.6 11.2 %copy-start.41 = (f32[1,1,2048]{2,1,0:T(1,128)S(1)}, f32[1,1,2048]{2,1,0:T(1,128)}, u32[]{:S(2)}) copy-start(f32[1,1,2048]{2,1,0:T(1,128)} %copy-done.40) | copy-start | bytes 24580
  (63 other events, 409.6 us)
Sparse Core Ops, SparseCore 0:
  82.1 40.5 all-gather.6
  125.5 38.8 all-gather.8
  427.8 38.3 all-gather.10
  622.7 71.1 all-reduce.4
where the time goes:
time: 714 us; the launch traced here: 705 us
  other arithmetic  360 us (50%)
  waiting for transfers between devices  108 us (15%)
  local copies, waits for them, and re-layouts  81.2 us (11%)
  blocking collectives  68.3 us (10%)
  matrix products  50.2 us (7%)
  loops' own time  16 us (2%)
  between operations  14.9 us (2%)
    psum x1, waiting for transfers between devices, shards(): lax.psum((local_short, sum_res, residues * sum_rate, local_skip, local_ga...  54.1 us
    all_gather x3, waiting for transfers between devices, prefix(): pieces = jax.tree.map(lambda part: lax.all_gather(part, axis), value)  50.8 us
    dot_general x8, matrix products, gradient_advance(): lagged = jnp.einsum('tsk,tsc->kc', shifter, products, precision=exact_mode)  44.6 us
    dot_general x8, other arithmetic, output_advance(): inside = jnp.einsum('tsc,sc->tc', toeplitz, u_block, precision=exact_mode)  38.3 us
    dot_general x8, other arithmetic, adjoint_advance(): inside = jnp.einsum('tsc,tc->sc', toeplitz, dz_block, precision=exact_mode)  36.2 us
    dot_general x8, other arithmetic, summary_advance(): jnp.einsum('smc,sc->mc', behind_lag, u_block, precision=exact_mode)  36 us
    psum x1, blocking collectives, shards(): lax.psum((local_short, sum_res, residues * sum_rate, local_skip, local_ga...  35.9 us
    while x96, local copies, waits for them, and re-layouts  32.7 us
  transfers between devices with their start and end apart: 6, of which 4 were waited for; matrix products, arithmetic and copies ran while one was open for 20% of the time, Pallas kernels for 0%

commit v1 on v0

v1 whole, which is shorter than its diff:
```python
import functools

import jax
import jax.numpy as jnp
from jax import lax
from jax.experimental import pallas as pl
from jax.experimental.pallas import tpu as pltpu
from jax.sharding import PartitionSpec as P

LANES = 128
SUB = 8
WIDE = SUB * LANES
F32 = jnp.float32
BF16 = jnp.bfloat16
VMEM_LIMIT = 48 * 1024 * 1024


def row(ref, t):
    return ref[pl.ds(pl.multiple_of(t * SUB, SUB), SUB), :]


def put(ref, t, value):
    ref[pl.ds(pl.multiple_of(t * SUB, SUB), SUB), :] = value


def spread(src, dst, first, count):
    def some(i, carry):
        start = pl.multiple_of(i * 16, 16)
        for g in range(SUB):
            piece = src[pl.ds(start, 16), g * LANES : (g + 1) * LANES].astype(F32)
            dst[pl.ds((start + first) * SUB + g, 16, stride=SUB), :] = piece
        return carry

    lax.fori_loop(0, count // 16, some, 0)


def gather_rows(src, dst, count):
    def some(i, carry):
        start = pl.multiple_of(i * 16, 16)
        for g in range(SUB):
            piece = src[pl.ds(start * SUB + g, 16, stride=SUB), :]
            dst[pl.ds(start, 16), g * LANES : (g + 1) * LANES] = piece.astype(dst.dtype)
        return carry

    lax.fori_loop(0, count // 16, some, 0)


def total(values):
    values = list(values)
    while len(values) > 1:
        values = [
            values[i] + values[i + 1] if i + 1 < len(values) else values[i]
            for i in range(0, len(values), 2)
        ]
    return values[0]


def taps_of(filt, stream, taps):
    return [row(filt, stream * taps + j) for j in range(taps)]


def conv_at(window, taps, i):
    margin = len(taps) - 1
    return total([taps[j] * window[margin + i - j] for j in range(margin + 1)])


def features_kernel(
    modes, taps, steps, key, value, filt3, decay, resid, k_ext, v_ext, f1, f2, u, lam, res, filt, x_out
):
    margin = taps - 1
    for g in range(SUB):
        lanes = slice(g * LANES, (g + 1) * LANES)
        lam[pl.ds(g, modes, stride=SUB), :] = decay[:, lanes]
        res[pl.ds(g, modes, stride=SUB), :] = resid[:, lanes]
        for i in range(3):
            filt[pl.ds(i * taps * SUB + g, taps, stride=SUB), :] = filt3[i, :, lanes]
    spread(key, k_ext, SUB, steps)
    spread(value, v_ext, SUB, steps)
    taps1, taps2 = taps_of(filt, 1, taps), taps_of(filt, 2, taps)

    def conv(c, carry):
        t0 = c * SUB
        kw = [row(k_ext, t0 + SUB - margin + i) for i in range(SUB + margin)]
        for i in range(SUB):
            put(f1, t0 + i, conv_at(kw, taps1, i))
        vw = [row(v_ext, t0 + SUB - margin + i) for i in range(SUB + margin)]
        for i in range(SUB):
            second = conv_at(vw, taps2, i)
            put(f2, t0 + i, second)
            put(u, t0 + i, second * row(f1, t0 + i))
        return carry

    lax.fori_loop(1, steps // SUB, conv, 0)
    fade = [jnp.exp(-row(lam, m)) for m in range(modes)]

    def advance(c, x):
        for i in range(SUB):
            now = row(u, c * SUB + i)
            x = tuple(fade[m] * x[m] + now for m in range(modes))
        return x

    x = lax.fori_loop(
        1, steps // SUB, advance, tuple(jnp.zeros((SUB, LANES), F32) for _ in range(modes))
    )
    for m in range(modes):
        put(x_out, m, x[m])


def head_kernel(
    modes, taps, steps, halo, k_head, v_head, filt, lam, x_part, k_in, v_in, f1_in, f2_in, u_in,
    k_ext, v_ext, f1, f2, u, x_out,
):
    del k_in, v_in, f1_in, f2_in, u_in
    margin = taps - 1
    for g in range(SUB):
        lanes = slice(g * LANES, (g + 1) * LANES)
        k_ext[pl.ds(g, SUB, stride=SUB), :] = halo[1, :, lanes].astype(F32)
        v_ext[pl.ds(g, SUB, stride=SUB), :] = halo[2, :, lanes].astype(F32)
    taps1, taps2 = taps_of(filt, 1, taps), taps_of(filt, 2, taps)
    kw = [row(k_ext, SUB - margin + i) for i in range(margin)] + [row(k_head, i) for i in range(SUB)]
    vw = [row(v_ext, SUB - margin + i) for i in range(margin)] + [row(v_head, i) for i in range(SUB)]
    mixed = []
    for i in range(SUB):
        first, second = conv_at(kw, taps1, i), conv_at(vw, taps2, i)
        put(f1, i, first)
        put(f2, i, second)
        put(u, i, first * second)
        mixed.append(first * second)
    for m in range(modes):
        rate = row(lam, m)
        fade = jnp.exp(-rate)
        x = mixed[0]
        for i in range(1, SUB):
            x = fade * x + mixed[i]
        put(x_out, m, row(x_part, m) + jnp.exp(-rate * float(steps - SUB)) * x)


def query_kernel(taps, steps, query, residual, cot, halo, filt, q_ext, f0, res_pos, cot_pos):
    margin = taps - 1
    for g in range(SUB):
        lanes = slice(g * LANES, (g + 1) * LANES)
        q_ext[pl.ds(g, SUB, stride=SUB), :] = halo[0, :, lanes].astype(F32)
    spread(query, q_ext, SUB, steps)
    spread(residual, res_pos, 0, steps)
    spread(cot, cot_pos, 0, steps)
    taps0 = taps_of(filt, 0, taps)

    def conv(c, carry):
        t0 = c * SUB
        qw = [row(q_ext, t0 + SUB - margin + i) for i in range(SUB + margin)]
        for i in range(SUB):
            put(f0, t0 + i, conv_at(qw, taps0, i))
        return carry

    lax.fori_loop(0, steps // SUB, conv, 0)


def own_modal_kernel(modes, steps, u, lam, res, skip, y, p_out):
    gain = skip[...]
    half = modes // 2
    for part in range(2):
        ms = range(part * half, (part + 1) * half)
        fade = [jnp.exp(-row(lam, m)) for m in ms]
        weight = [row(res, m) for m in ms]

        def advance(c, state, part=part, fade=fade, weight=weight):
            x, p = state
            for i in range(SUB):
                t = c * SUB + i
                now = row(u, t)
                x = tuple(f * v + now for f, v in zip(fade, x))
                p = tuple(f * w + v for f, w, v in zip(fade, p, x))
                own = total([w * v for w, v in zip(weight, x)])
                put(y, t, own + (gain * now if part == 0 else row(y, t)))
            return x, p

        zeros = tuple(jnp.zeros((SUB, LANES), F32) for _ in ms)
        _, p = lax.fori_loop(0, steps // SUB, advance, (zeros, zeros))
        for m, v in zip(ms, p):
            put(p_out, m, v)


def summed_kernel(modes, steps, blocks, y, f0, res_pos, cot_pos, x_in, lam, res, gain, modal, summed, sums, squares, inner):
    block = pl.program_id(0)

    @pl.when(block == 0)
    def _():
        squares[...] = jnp.zeros_like(squares)
        inner[...] = jnp.zeros_like(inner)

    fade = [jnp.exp(-row(lam, m)) for m in range(modes)]
    factor = gain[...]

    def advance(c, w):
        for i in range(SUB):
            t = c * SUB + i
            w = tuple(f * v for f, v in zip(fade, w))
            long = row(y, t) + total(w)
            put(modal, t, long)
            now = row(res_pos, t) + row(f0, t) * long
            put(summed, t, now)
            put(squares, t, row(squares, t) + now * now)
            put(inner, t, row(inner, t) + factor * row(cot_pos, t) * now)
        return w

    lax.fori_loop(
        0, steps // SUB, advance, tuple(row(res, m) * row(x_in, m) for m in range(modes))
    )

    @pl.when(block == blocks - 1)
    def _():
        for which, scratch in enumerate((squares, inner)):
            for b in range(steps // LANES):
                part = total(
                    [
                        scratch[pl.ds(b * LANES * SUB + g, LANES, stride=SUB), :]
                        for g in range(SUB)
                    ]
                )
                sums[which : which + 1, b * LANES : (b + 1) * LANES] = jnp.sum(
                    part.T, axis=0, keepdims=True
                )


def grad_modal_kernel(modes, steps, width, sums, summed, cot_pos, f0, modal, lam, gain, scale, gm, a_out, gf0_head):
    @pl.when(pl.program_id(0) == 0)
    def _():
        inv = lax.rsqrt(sums[0:1, :] / width + 1e-05)
        coef = inv * inv * inv * sums[1:2, :] / width
        for which, value in enumerate((inv, coef)):
            for b in range(steps // LANES):
                piece = value[:, b * LANES : (b + 1) * LANES]
                scale[pl.ds(which * steps + b * LANES, LANES), :] = jnp.broadcast_to(
                    piece, (LANES, LANES)
                ).T

    fade = [jnp.exp(-row(lam, m)) for m in range(modes)]
    factor = gain[...]

    def advance(c, a):
        t0 = steps - SUB - c * SUB
        for i in reversed(range(SUB)):
            t = t0 + i
            inv = scale[pl.ds(t, 1), :]
            coef = scale[pl.ds(steps + t, 1), :]
            grad = inv * (factor * row(cot_pos, t)) - coef * row(summed, t)
            now = grad * row(f0, t)
            put(gm, t, now)
            a = tuple(f * v + now for f, v in zip(fade, a))
        return a

    a = lax.fori_loop(
        0, steps // SUB, advance, tuple(jnp.zeros((SUB, LANES), F32) for _ in range(modes))
    )
    for m in range(modes):
        put(a_out, m, fade[m] * a[m])
    for t in range(SUB):
        inv = scale[pl.ds(t, 1), :]
        coef = scale[pl.ds(steps + t, 1), :]
        grad = inv * (factor * row(cot_pos, t)) - coef * row(summed, t)
        put(gf0_head, t, grad * row(modal, t))


def own_adjoint_kernel(modes, steps, gm, u, lam, res, skip, gmx, res_sum, rate_sum, lag_out, skip_out):
    gain = skip[...]
    half = modes // 2
    zero = jnp.zeros((SUB, LANES), F32)
    for part in range(2):
        ms = range(part * half, (part + 1) * half)
        fade = [jnp.exp(-row(lam, m)) for m in ms]
        weight = [row(res, m) for m in ms]

        def advance(c, state, part=part, fade=fade, weight=weight):
            adj, lag, by_res, by_rate, by_skip = state
            t0 = steps - SUB - c * SUB
            for i in reversed(range(SUB)):
                t = t0 + i
                now, mixed = row(gm, t), row(u, t)
                older = tuple(f * v for f, v in zip(fade, adj))
                lag = tuple(f * v + o for f, v, o in zip(fade, lag, older))
                adj = tuple(o + now for o in older)
                by_res = tuple(s + mixed * v for s, v in zip(by_res, adj))
                by_rate = tuple(s + mixed * v for s, v in zip(by_rate, lag))
                own = total([w * v for w, v in zip(weight, adj)])
                if part == 0:
                    put(gmx, t, own + gain * now)
                    by_skip = by_skip + now * mixed
                else:
                    put(gmx, t, own + row(gmx, t))
            return adj, lag, by_res, by_rate, by_skip

        zeros = tuple(zero for _ in ms)
        _, lag, by_res, by_rate, by_skip = lax.fori_loop(
            0, steps // SUB, advance, (zeros, zeros, zeros, zeros, zero)
        )
        for i, m in enumerate(ms):
            put(res_sum, m, by_res[i])
            put(rate_sum, m, by_rate[i])
            put(lag_out, m, fade[i] * lag[i])
        if part == 0:
            skip_out[...] = by_skip


def outputs_kernel(taps, steps, scale, summed, cot_pos, modal, q_ext, gf0_next, filt, gain, normed, grad_res, grad_query, short0, gain_out, work, gf0):
    margin = taps - 1
    factor = gain[...]
    gf0[pl.ds(steps * SUB, SUB * SUB), :] = gf0_next[...]
    taps0 = taps_of(filt, 0, taps)

    def norm(c, acc):
        for i in range(SUB):
            t = c * SUB + i
            inv = scale[pl.ds(t, 1), :]
            here = row(summed, t) * inv
            put(work, t, here * factor)
            acc = acc + row(cot_pos, t) * here
        return acc

    gain_out[...] = lax.fori_loop(0, steps // SUB, norm, jnp.zeros((SUB, LANES), F32))
    gather_rows(work, normed, steps)

    def grads(c, carry):
        for i in range(SUB):
            t = c * SUB + i
            inv = scale[pl.ds(t, 1), :]
            coef = scale[pl.ds(steps + t, 1), :]
            grad = inv * (factor * row(cot_pos, t)) - coef * row(summed, t)
            put(work, t, grad)
            put(gf0, t, grad * row(modal, t))
        return carry

    lax.fori_loop(0, steps // SUB, grads, 0)
    gather_rows(work, grad_res, steps)
    sums = filter_pass(taps, steps, gf0, q_ext)
    for j in range(taps):
        put(short0, j, sums[j])
    back_pass(taps, steps, gf0, taps0, work)
    gather_rows(work, grad_query, steps)


def filter_pass(taps, steps, grad, ext):
    margin = taps - 1

    def some(c, acc):
        t0 = c * SUB
        window = [row(ext, t0 + SUB - margin + i) for i in range(SUB + margin)]
        for i in range(SUB):
            now = row(grad, t0 + i)
            acc = tuple(acc[j] + now * window[margin + i - j] for j in range(taps))
        return acc

    zero = jnp.zeros((SUB, LANES), F32)
    return lax.fori_loop(0, steps // SUB, some, tuple(zero for _ in range(taps)))


def back_pass(taps, steps, grad, weights, out):
    margin = taps - 1

    def some(c, carry):
        t0 = c * SUB
        window = [row(grad, t0 + i) for i in range(SUB + margin)]
        for i in range(SUB):
            put(out, t0 + i, total([weights[j] * window[i + j] for j in range(taps)]))
        return carry

    lax.fori_loop(0, steps // SUB, some, 0)


def mixed_kernel(modes, taps, steps, gmx, f1, f2, k_ext, v_ext, lam, res, alpha, x_in, p_own, lag_own, rate_own, gf1, gf2, sums):
    rates = [row(lam, m) for m in range(modes)]
    fade = [jnp.exp(-r) for r in rates]

    def advance(c, w):
        t0 = steps - SUB - c * SUB
        for i in reversed(range(SUB)):
            t = t0 + i
            grad = row(gmx, t) + total(w)
            put(gf1, t, grad * row(f2, t))
            put(gf2, t, grad * row(f1, t))
            w = tuple(f * v for f, v in zip(fade, w))
        return w

    lax.fori_loop(
        0, steps // SUB, advance, tuple(row(res, m) * row(alpha, m) for m in range(modes))
    )
    for which, (grad, ext) in enumerate(((gf1, k_ext), (gf2, v_ext))):
        parts = filter_pass(taps, steps, grad, ext)
        for j in range(taps):
            put(sums, which * taps + j, parts[j])
    for m in range(modes):
        before, after = row(x_in, m), row(alpha, m)
        across = float(steps) * jnp.exp(-rates[m] * float(steps)) * before * after
        lagged = row(rate_own, m) + before * row(lag_own, m) + after * row(p_own, m) + across
        put(sums, 2 * taps + m, -row(res, m) * lagged)


def back_kernel(taps, steps, gf1, gf2, next_head, filt, grad_key, grad_value, work, ext):
    for which, (grad, out) in enumerate(((gf1, grad_key), (gf2, grad_value))):
        ext[pl.ds(0, steps * SUB), :] = grad[...]
        ext[pl.ds(steps * SUB, SUB * SUB), :] = next_head[which, 0]
        back_pass(taps, steps, ext, taps_of(filt, which + 1, taps), work)
        gather_rows(work, out, steps)


def finish_kernel(modes, taps, late, late_other, early, early_other, short, res, rate, skip, gain, work, work2):
    work[...] = late[...] + late_other[...]
    work2[...] = early[...] + early_other[...]
    for g in range(SUB):
        lanes = slice(g * LANES, (g + 1) * LANES)
        short[0, :, lanes] = work2[pl.ds(g, taps, stride=SUB), :]
        short[1, :, lanes] = work[pl.ds(g, taps, stride=SUB), :]
        short[2, :, lanes] = work[pl.ds(taps * SUB + g, taps, stride=SUB), :]
        rate[:, lanes] = work[pl.ds(2 * taps * SUB + g, modes, stride=SUB), :]
        res[:, lanes] = work2[pl.ds(taps * SUB + g, modes, stride=SUB), :]
    skip[...] = row(work2, taps + modes)
    gain[...] = row(work2, taps + modes + 1)


def shift(value, axis, distance):
    devices = range(lax.axis_size(axis))
    route = [(i - distance, i) for i in devices if i - distance in devices]
    return lax.ppermute(value, axis, route)


def carried_in(own, lam, span, axis, sign):
    count = lax.axis_size(axis)
    reach = min(2, count - 1)
    parts = [shift(own, axis, sign * k) for k in range(1, reach + 1)]
    state = parts[0]
    for k in range(1, reach):
        state = state + jnp.exp(-lam * float(span * k)) * parts[k]
    while reach < count - 1:
        state = state + jnp.exp(-lam * float(span * reach)) * shift(state, axis, sign * reach)
        reach *= 2
    return state


def sum_but_last(value, axis):
    count, step = lax.axis_size(axis), 1
    while True:
        other = lax.ppermute(value, axis, [(i, i ^ step) for i in range(count)])
        step *= 2
        if step >= count:
            return value, other
        value = value + other


def shards(
    residual, query_in, key_in, value_in, short_filter, residues, decay_rate, skip_gain, norm_gain, cotangent
):
    steps, channels = residual.shape
    modes, taps = residues.shape[0], short_filter.shape[1]
    blocks = channels // WIDE
    width = channels * lax.axis_size("tp")
    skip, gain = (v.reshape(blocks * SUB, LANES) for v in (skip_gain, norm_gain))

    def pos(count):
        return jax.ShapeDtypeStruct((blocks * count * SUB, LANES), F32)

    def pos_spec(count):
        return pl.BlockSpec((count * SUB, LANES), lambda h: (h, 0))

    def head_spec(total_steps, start):
        return pl.BlockSpec((SUB * SUB, LANES), lambda h: (h * (total_steps // SUB) + start, 0))

    wide_spec = pl.BlockSpec((steps, WIDE), lambda h: (0, h))
    wide = jax.ShapeDtypeStruct((steps, channels), BF16)
    mode_spec, one_spec, filt_spec = pos_spec(modes), pos_spec(1), pos_spec(3 * taps)
    seq_spec, ext_spec = pos_spec(steps), pos_spec(steps + SUB)
    seq, ext, mode, one = pos(steps), pos(steps + SUB), pos(modes), pos(1)
    halo_spec = pl.BlockSpec((3, SUB, WIDE), lambda h: (0, 0, h))
    param_spec = pl.BlockSpec((modes, WIDE), lambda h: (0, h))
    short_spec = pl.BlockSpec((3, taps, WIDE), lambda h: (0, 0, h))

    def call(body, ins, in_specs, outs, out_specs, ops, name, scratch=(), aliases=None):
        elements = steps * channels
        return pl.pallas_call(
            body,
            grid=(blocks,),
            in_specs=in_specs,
            out_specs=out_specs,
            out_shape=outs,
            scratch_shapes=list(scratch),
            input_output_aliases=aliases or {},
            compiler_params=pltpu.CompilerParams(
                dimension_semantics=("arbitrary",), vmem_limit_bytes=VMEM_LIMIT
            ),
            cost_estimate=pl.CostEstimate(
                flops=ops * elements, bytes_accessed=4 * elements, transcendentals=0
            ),
            name=name,
        )(*ins)

    trailing = jnp.stack([s[steps - SUB :] for s in (query_in, key_in, value_in)])
    halo = shift(trailing, "ctx", 1)

    k_ext, v_ext, f1, f2, u, lam, res, filt, x_part = call(
        functools.partial(features_kernel, modes, taps, steps),
        (key_in, value_in, short_filter, decay_rate, residues),
        [wide_spec, wide_spec, short_spec, param_spec, param_spec],
        [ext, ext, seq, seq, seq, mode, mode, pos(3 * taps), mode],
        [ext_spec, ext_spec, seq_spec, seq_spec, seq_spec, mode_spec, mode_spec, filt_spec, mode_spec],
        64,
        "features",
    )
    any_spec = pl.BlockSpec(memory_space=pl.ANY)
    k_ext, v_ext, f1, f2, u, x_own = call(
        functools.partial(head_kernel, modes, taps, steps),
        (halo, k_ext, v_ext, filt, lam, x_part, k_ext, v_ext, f1, f2, u),
        [halo_spec, head_spec(steps + SUB, 1), head_spec(steps + SUB, 1), filt_spec, mode_spec, mode_spec]
        + [any_spec] * 5,
        [ext, ext, seq, seq, seq, mode],
        [head_spec(steps + SUB, 0)] * 2 + [head_spec(steps, 0)] * 3 + [mode_spec],
        2,
        "head",
        aliases={6: 0, 7: 1, 8: 2, 9: 3, 10: 4},
    )
    x_in = carried_in(x_own, lam, steps, "ctx", 1)
    q_ext, f0, res_pos, cot_pos = call(
        functools.partial(query_kernel, taps, steps),
        (query_in, residual, cotangent, halo, filt),
        [wide_spec, wide_spec, wide_spec, halo_spec, filt_spec],
        [ext, seq, seq, seq],
        [ext_spec, seq_spec, seq_spec, seq_spec],
        30,
        "query",
    )
    y, p_own = call(
        functools.partial(own_modal_kernel, modes, steps),
        (u, lam, res, skip),
        [seq_spec, mode_spec, mode_spec, one_spec],
        [seq, mode],
        [seq_spec, mode_spec],
        96,
        "own_modal",
    )
    modal, summed, sums = call(
        functools.partial(summed_kernel, modes, steps, blocks),
        (y, f0, res_pos, cot_pos, x_in, lam, res, gain),
        [seq_spec] * 4 + [mode_spec] * 3 + [one_spec],
        [seq, seq, jax.ShapeDtypeStruct((2, steps), F32)],
        [seq_spec, seq_spec, pl.BlockSpec((2, steps), lambda h: (0, 0))],
        40,
        "summed",
        scratch=[pltpu.VMEM((steps * SUB, LANES), F32)] * 2,
    )
    sums = lax.psum(sums, "tp")
    scale, gm, a_own, gf0_head = call(
        functools.partial(grad_modal_kernel, modes, steps, width),
        (sums, summed, cot_pos, f0, modal, lam, gain),
        [pl.BlockSpec((2, steps), lambda h: (0, 0)), seq_spec, seq_spec, seq_spec, head_spec(steps, 0), mode_spec, one_spec],
        [jax.ShapeDtypeStruct((2 * steps, LANES), F32), seq, mode, pos(SUB)],
        [pl.BlockSpec((2 * steps, LANES), lambda h: (0, 0)), seq_spec, mode_spec, pos_spec(SUB)],
        40,
        "grad_modal",
    )
    alpha = carried_in(a_own, lam, steps, "ctx", -1)
    gf0_next = shift(gf0_head, "ctx", -1)
    gmx, res_sum, rate_own, lag_own, skip_sum = call(
        functools.partial(own_adjoint_kernel, modes, steps),
        (gm, u, lam, res, skip),
        [seq_spec, seq_spec, mode_spec, mode_spec, one_spec],
        [seq, mode, mode, mode, one],
        [seq_spec, mode_spec, mode_spec, mode_spec, one_spec],
        160,
        "own_adjoint",
    )
    scale_spec = pl.BlockSpec((2 * steps, LANES), lambda h: (0, 0))
    normed, grad_residual, grad_query, short0, gain_sum = call(
        functools.partial(outputs_kernel, taps, steps),
        (scale, summed, cot_pos, modal, q_ext, gf0_next, filt, gain),
        [scale_spec, seq_spec, seq_spec, seq_spec, ext_spec, pos_spec(SUB), filt_spec, one_spec],
        [wide, wide, wide, pos(taps), one],
        [wide_spec, wide_spec, wide_spec, pos_spec(taps), one_spec],
        50,
        "outputs",
        scratch=[
            pltpu.VMEM((steps * SUB, LANES), F32),
            pltpu.VMEM(((steps + SUB) * SUB, LANES), F32),
        ],
    )
    early_rows = taps + modes + 2
    early = jnp.concatenate(
        [
            v.reshape(blocks, -1, LANES)
            for v in (short0, res_sum + x_in * a_own, skip_sum, gain_sum)
        ],
        axis=1,
    ).reshape(-1, LANES)
    early, early_other = sum_but_last(early, "ctx")
    late_rows = 2 * taps + modes
    gf1, gf2, late = call(
        functools.partial(mixed_kernel, modes, taps, steps),
        (gmx, f1, f2, k_ext, v_ext, lam, res, alpha, x_in, p_own, lag_own, rate_own),
        [seq_spec] * 3 + [ext_spec] * 2 + [mode_spec] * 7,
        [seq, seq, pos(late_rows)],
        [seq_spec, seq_spec, pos_spec(late_rows)],
        64,
        "mixed",
    )
    late, late_other = sum_but_last(late, "ctx")
    heads = jnp.stack([v.reshape(blocks, steps * SUB, LANES)[:, : SUB * SUB] for v in (gf1, gf2)])
    next_head = shift(heads, "ctx", -1)
    grad_key, grad_value = call(
        functools.partial(back_kernel, taps, steps),
        (gf1, gf2, next_head, filt),
        [seq_spec, seq_spec, pl.BlockSpec((2, 1, SUB * SUB, LANES), lambda h: (0, h, 0, 0)), filt_spec],
        [wide, wide],
        [wide_spec, wide_spec],
        28,
        "back",
        scratch=[
            pltpu.VMEM((steps * SUB, LANES), F32),
            pltpu.VMEM(((steps + SUB) * SUB, LANES), F32),
        ],
    )
    late_spec, early_spec = pos_spec(late_rows), pos_spec(early_rows)
    grad_short, grad_residues, grad_rate, grad_skip, grad_gain = call(
        functools.partial(finish_kernel, modes, taps),
        (late, late_other, early, early_other),
        [late_spec, late_spec, early_spec, early_spec],
        [
            jax.ShapeDtypeStruct(short_filter.shape, F32),
            jax.ShapeDtypeStruct(residues.shape, F32),
            jax.ShapeDtypeStruct(residues.shape, F32),
            one,
            one,
        ],
        [short_spec, param_spec, param_spec, one_spec, one_spec],
        1,
        "finish",
        scratch=[
            pltpu.VMEM((late_rows * SUB, LANES), F32),
            pltpu.VMEM((early_rows * SUB, LANES), F32),
        ],
    )
    return (
        normed,
        grad_residual,
        grad_query,
        grad_key,
        grad_value,
        grad_short,
        grad_residues,
        grad_rate,
        grad_skip.reshape(channels),
        grad_gain.reshape(channels),
    )


def solution(mesh):
    both, modes, vector = P("ctx", "tp"), P(None, "tp"), P("tp")
    return jax.shard_map(
        shards,
        mesh=mesh,
        in_specs=(both, both, both, both, P(None, None, "tp"), modes, modes, vector, vector, both),
        out_specs=(both,) * 5 + (P(None, None, "tp"), modes, modes, vector, vector),
        check_vma=False,
    )
```

time: 714 us -> 170 us (0.24)
  the two profiles are of different devices: /device:TPU:0 before, /device:TPU:14 now
where the time goes in v1:
time: 170 us
  Pallas kernels  68.8 us (40%)
  starting transfers between devices  44.8 us (26%)
  waiting for transfers between devices  29.6 us (17%)
  local copies, waits for them, and re-layouts  19.1 us (11%)
  blocking collectives  5.84 us (3%)
    pallas_call x11, Pallas kernels, call(): pl.pallas_call(body, grid=(blocks,), in_specs=in_specs, out_specs=out_spe...  68.8 us
    ppermute x11, starting transfers between devices, shift(): return lax.ppermute(value, axis, route)  33.6 us
    ppermute x11, waiting for transfers between devices, shift(): return lax.ppermute(value, axis, route)  21.8 us
    unnamed x42, local copies, waits for them, and re-layouts  17.5 us
    ppermute x6, starting transfers between devices, sum_but_last(): other = lax.ppermute(value, axis, [(i, i ^ step) for i in range(count)])  11.2 us
    ppermute x6, waiting for transfers between devices, sum_but_last(): other = lax.ppermute(value, axis, [(i, i ^ step) for i in range(count)])  7.84 us
    psum x1, blocking collectives, shards(): sums = lax.psum(sums, 'tp')  5.84 us
  transfers between devices with their start and end apart: 17, of which 7 were waited for; matrix products, arithmetic and copies ran while one was open for 3% of the time, Pallas kernels for 33%

profile of v1, /device:TPU:14, one launch (start us, length us, event | category | flops | bytes accessed | tf_op | source)
XLA Modules:
  0.0 169.5 jit_solution(11195265028698713549)
XLA Ops:
  2.2 3.5 %collective-permute-start = (bf16[3,8,2048]{2,1,0:T(8,128)(2,1)S(1)}, bf16[3,8,2048]{2,1,0:T(8,128)(2,1)S(1)}, u32[]{:S(2)}, u32[]{:S(2)}) collective-permute-start(bf16[3,8,2048]{2,1,0:T(8,128)(2,1)S(1)} %pad_maximum_fusion.2), channel_id=1, source_target_pairs={{0,4},{4,8},{8,12},{12,16},{16,20},{20,24},{24,28},{1,5},{5,9},{9,... | collective-permute-start | bytes 294920 | tf_op jit(solution)/shard_map/ppermute | solution.py:422
  10.9 7.8 %features.1 = (f32[4224,128]{1,0:T(8,128)}, f32[4224,128]{1,0:T(8,128)}, f32[4096,128]{1,0:T(8,128)S(1)}, f32[4096,128]{1,0:T(8,128)}, f32[4096,128]{1,0:T(8,128...) custom-call(bf16[256,2048]{1,0:T(8,128)(2,1)S(1)} %copy-done.10, ...), custom_call_target="tpu_custom_call" | custom-call | flops 33554432 | bytes 2097152 | tf_op jit(solution)/shard_map/features/pallas_call | solution.py:477
  18.7 3.3 %copy.25.k_in = f32[4224,128]{1,0:T(8,128)} copy(f32[4224,128]{1,0:T(8,128)} %get-tuple-element.58.k_head) | data formatting | bytes 4325376
  22.0 1.4 copy.26.v_in
  24.3 1.8 %head.1 = (f32[4224,128]{1,0:T(8,128)}, f32[4224,128]{1,0:T(8,128)}, f32[4096,128]{1,0:T(8,128)S(1)}, f32[4096,128]{1,0:T(8,128)S(1)}, f32[4096,128]{1,0:T(8,128)}, /*index=5*/f32[256,128]{1,0:T(8,128)S(1)}) custom-call(bf16[3,8,2048]{2,1,0:T(8,128)(2,1)S(1)} %collective-permute-done.h, ...), custom_call_target="tpu_custom_call", output_to_operand_aliasing={{0}: (6, {}), {1}: (7, {}), {2}: (8, {}), {3}: (9, {}), {4}... | custom-call | flops 1048576 | bytes 2097152 | tf_op jit(solution)/shard_map/head/pallas_call | solution.py:477
  26.1 1.4 copy-done.4
  28.8 3.5 %collective-permute-start.2 = (f32[256,128]{1,0:T(8,128)S(1)}, f32[256,128]{1,0:T(8,128)S(1)}, u32[]{:S(2)}, u32[]{:S(2)}) collective-permute-start(f32[256,128]{1,0:T(8,128)S(1)} %get-tuple-element.72), channel_id=1, source_target_pairs={{0,8},{4,12},{8,16},{12,20},{16,24},{20,28},{1,9},{5,13},{9,17},{1... | collective-permute-start | bytes 393224 | tf_op jit(solution)/shard_map/ppermute | solution.py:422
  32.3 3.4 %collective-permute-start.1 = (f32[256,128]{1,0:T(8,128)S(1)}, f32[256,128]{1,0:T(8,128)S(1)}, u32[]{:S(2)}, u32[]{:S(2)}) collective-permute-start(f32[256,128]{1,0:T(8,128)S(1)} %get-tuple-element.72), channel_id=1, source_target_pairs={{0,4},{4,8},{8,12},{12,16},{16,20},{20,24},{24,28},{1,5},{5,9},{9,... | collective-permute-start | bytes 393224 | tf_op jit(solution)/shard_map/ppermute | solution.py:422
  35.7 3.4 %collective-permute-done.1 = f32[256,128]{1,0:T(8,128)S(1)} collective-permute-done((f32[256,128]{1,0:T(8,128)S(1)}, f32[256,128]{1,0:T(8,128)S(1)}, u32[]{:S(2)}, u32[]{:S(2)}) %collective-permute-start.1) | collective-permute-done | bytes 131104 | tf_op jit(solution)/shard_map/ppermute | solution.py:422
  39.2 2.1 %collective-permute-start.3 = (f32[256,128]{1,0:T(8,128)S(1)}, f32[256,128]{1,0:T(8,128)S(1)}, u32[]{:S(2)}, u32[]{:S(2)}) collective-permute-start(f32[256,128]{1,0:T(8,128)S(1)} %multiply_add_fusion.6), channel_id=1, source_target_pairs={{0,8},{4,12},{8,16},{12,20},{16,24},{20,28},{1,9},{5,13},{9,17},{1... | collective-permute-start | bytes 393224 | tf_op jit(solution)/shard_map/ppermute | solution.py:422
  41.3 4.9 %collective-permute-done.3 = f32[256,128]{1,0:T(8,128)S(1)} collective-permute-done((f32[256,128]{1,0:T(8,128)S(1)}, f32[256,128]{1,0:T(8,128)S(1)}, u32[]{:S(2)}, u32[]{:S(2)}) %collective-permute-start.3) | collective-permute-done | bytes 131104 | tf_op jit(solution)/shard_map/ppermute | solution.py:422
  46.2 1.4 collective-permute-start.4
  47.7 4.9 %query.2 = (f32[4224,128]{1,0:T(8,128)}, f32[4096,128]{1,0:T(8,128)S(1)}, f32[4096,128]{1,0:T(8,128)}, f32[4096,128]{1,0:T(8,128)}) custom-call(bf16[256,2048]{1,0:T(8,128)(2,1)S(1)} %copy-done.11, bf16[256,2048]{1,0:T(8,128)(2,1)S(1)} %copy-done.12, bf16[256,2048]{1,0:T(8,128)(2,1)S(1)} %copy-done.13, bf16[3,8,2048]{2,1,0:T(8,128)(2,1)S(1)} %collective-permute-done.halo, ...), custom_call_target="tpu_custom_call" | custom-call | flops 15728640 | bytes 2097152 | tf_op jit(solution)/shard_map/query/pallas_call | solution.py:477
  53.9 7.2 %own_modal.1 = (f32[4096,128]{1,0:T(8,128)S(1)}, f32[256,128]{1,0:T(8,128)S(1)}) custom-call(f32[4096,128]{1,0:T(8,128)S(1)} %copy-done.1, f32[256,128]{1,0:T(8,128)S(1)} %get-tuple-element.61.lam, f32[256,128]{1,0:T(8,128)S(1)} %get-tuple-element.67.res, f32[16,128]{1,0:T(8,128)S(1)} %bitcast.28), custom_call_target="tpu_custom_call" | custom-call | flops 50331648 | bytes 2097152 | tf_op jit(solution)/shard_map/own_modal/pallas_call | solution.py:477
  62.5 5.9 %summed.1 = (f32[4096,128]{1,0:T(8,128)S(1)}, f32[4096,128]{1,0:T(8,128)S(1)}, f32[2,256]{1,0:T(2,128)S(1)}) custom-call(f32[4096,128]{1,0:T(8,128)} %copy-done.7, f32[4096,128]{1,0:T(8,128)} %copy-done.3, f32[4096,128]{1,0:T(8,128)} %get-tuple-element.70.res_pos, f32[4096,128]{1,0:T(8,128)} %get-tuple-element.71.cot_pos, ...), custom_call_target="tpu_custom_call" | custom-call | flops 20971520 | bytes 2097152 | tf_op jit(solution)/shard_map/summed/pallas_call | solution.py:477
  69.7 5.8 %psum.7.sums = f32[2,256]{1,0:T(2,128)S(1)} all-reduce(f32[2,256]{1,0:T(2,128)S(1)} %get-tuple-element.73), channel_id=1, replica_groups=mesh['ctx'=8,'tp'=4] {'tp'}, use_global_device_ids=true, to_apply=%region_0.0 | all-reduce | flops 512 | bytes 4096 | tf_op jit(solution)/shard_map/psum | solution.py:547
  75.5 4.8 %grad_modal.1 = (f32[512,128]{1,0:T(8,128)S(1)}, f32[4096,128]{1,0:T(8,128)S(1)}, f32[256,128]{1,0:T(8,128)S(1)}, f32[128,128]{1,0:T(8,128)S(1)}) custom-call(f32[2,256]{1,0:T(2,128)S(1)} %psum.7.sums, f32[4096,128]{1,0:T(8,128)S(1)} %get-tuple-element.74.summed, f32[4096,128]{1,0:T(8,128)} %get-tuple-element.71.cot_pos, f32[4096,128]{1,0:T(8,128)} %copy-done.3, ...), custom_call_target="tpu_custom_call" | custom-call | flops 20971520 | bytes 2097152 | tf_op jit(solution)/shard_map/grad_modal/pallas_call | solution.py:477
  80.3 3.9 %collective-permute-start.7 = (f32[256,128]{1,0:T(8,128)S(1)}, f32[256,128]{1,0:T(8,128)S(1)}, u32[]{:S(2)}, u32[]{:S(2)}) collective-permute-start(f32[256,128]{1,0:T(8,128)S(1)} %get-tuple-element.88), channel_id=1, source_target_pairs={{8,0},{12,4},{16,8},{20,12},{24,16},{28,20},{9,1},{13,5},{17,9},{2... | collective-permute-start | bytes 393224 | tf_op jit(solution)/shard_map/ppermute | solution.py:422
  84.2 4.8 %collective-permute-start.6 = (f32[256,128]{1,0:T(8,128)S(1)}, f32[256,128]{1,0:T(8,128)S(1)}, u32[]{:S(2)}, u32[]{:S(2)}) collective-permute-start(f32[256,128]{1,0:T(8,128)S(1)} %get-tuple-element.88), channel_id=1, source_target_pairs={{4,0},{8,4},{12,8},{16,12},{20,16},{24,20},{28,24},{5,1},{9,5},{13... | collective-permute-start | bytes 393224 | tf_op jit(solution)/shard_map/ppermute | solution.py:422
  89.1 3.3 %collective-permute-done.6 = f32[256,128]{1,0:T(8,128)S(1)} collective-permute-done((f32[256,128]{1,0:T(8,128)S(1)}, f32[256,128]{1,0:T(8,128)S(1)}, u32[]{:S(2)}, u32[]{:S(2)}) %collective-permute-start.6) | collective-permute-done | bytes 131104 | tf_op jit(solution)/shard_map/ppermute | solution.py:422
  92.5 3.9 %collective-permute-start.8 = (f32[256,128]{1,0:T(8,128)S(1)}, f32[256,128]{1,0:T(8,128)S(1)}, u32[]{:S(2)}, u32[]{:S(2)}) collective-permute-start(f32[256,128]{1,0:T(8,128)S(1)} %multiply_add_fusion.3), channel_id=1, source_target_pairs={{8,0},{12,4},{16,8},{20,12},{24,16},{28,20},{9,1},{13,5},{17,9},{2... | collective-permute-start | bytes 393224 | tf_op jit(solution)/shard_map/ppermute | solution.py:422
  96.4 1.9 %collective-permute-start.5 = (f32[128,128]{1,0:T(8,128)S(1)}, f32[128,128]{1,0:T(8,128)S(1)}, u32[]{:S(2)}, u32[]{:S(2)}) collective-permute-start(f32[128,128]{1,0:T(8,128)S(1)} %get-tuple-element.78), channel_id=1, source_target_pairs={{4,0},{8,4},{12,8},{16,12},{20,16},{24,20},{28,24},{5,1},{9,5},{13... | collective-permute-start | bytes 196616 | tf_op jit(solution)/shard_map/ppermute | solution.py:422
  98.3 13.9 %own_adjoint.1 = (f32[4096,128]{1,0:T(8,128)S(1)}, f32[256,128]{1,0:T(8,128)S(1)}, f32[256,128]{1,0:T(8,128)S(1)}, f32[256,128]{1,0:T(8,128)S(1)}, f32[16,128]{1,0:T(8,128)S(1)}) custom-call(f32[4096,128]{1,0:T(8,128)S(1)} %get-tuple-element.82.gm, f32[4096,128]{1,0:T(8,128)} %get-tuple-element.66.u, f32[256,128]{1,0:T(8,128)S(1)} %get-tuple-element.61.lam, ...), custom_call_target="tpu_custom_call" | custom-call | flops 83886080 | bytes 2097152 | tf_op jit(solution)/shard_map/own_adjoint/pallas_call | solution.py:477
  113.6 8.5 %outputs.1 = (bf16[256,2048]{1,0:T(8,128)(2,1)}, bf16[256,2048]{1,0:T(8,128)(2,1)}, bf16[256,2048]{1,0:T(8,128)(2,1)}, f32[112,128]{1,0:T(8,128)S(1)}, f32[16,128]{1,0:T(8,128)S(1)}) custom-call(f32[512,128]{1,0:T(8,128)S(1)} %get-tuple-element.76.scale, f32[4096,128]{1,0:T(8,128)S(1)} %get-tuple-element.74.summed, f32[4096,128]{1,0:T(8,128)S(1)} %copy-done, ...), custom_call_target="tpu_custom_call" | custom-call | flops 26214400 | bytes 2097152 | tf_op jit(solution)/shard_map/outputs/pallas_call | solution.py:477
  123.1 8.3 %mixed.1 = (f32[4096,128]{1,0:T(8,128)S(1)}, f32[4096,128]{1,0:T(8,128)S(1)}, f32[480,128]{1,0:T(8,128)S(1)}) custom-call(f32[4096,128]{1,0:T(8,128)} %copy-done.8, f32[4096,128]{1,0:T(8,128)} %copy-done.4, f32[4096,128]{1,0:T(8,128)} %copy-done.6, f32[4224,128]{1,0:T(8,128)} %get-tuple-element.86.k_ext, f32[4224,128]{1,0:T(8,128)} %get-tuple-element.87.v_ext, ...), custom_call_target="tpu_custom_call" | custom-call | flops 33554432 | bytes 2097152 | tf_op jit(solution)/shard_map/mixed/pallas_call | solution.py:477
  132.8 5.2 %collective-permute-done.11 = f32[480,128]{1,0:T(8,128)S(1)} collective-permute-done((f32[480,128]{1,0:T(8,128)S(1)}, f32[480,128]{1,0:T(8,128)S(1)}, u32[]{:S(2)}, u32[]{:S(2)}) %collective-permute-start.11) | collective-permute-done | bytes 245792 | tf_op jit(solution)/shard_map/ppermute | solution.py:441
  138.6 5.2 %collective-permute-start.16 = (f32[400,128]{1,0:T(8,128)S(1)}, f32[400,128]{1,0:T(8,128)S(1)}, u32[]{:S(2)}, u32[]{:S(2)}) collective-permute-start(f32[400,128]{1,0:T(8,128)S(1)} %add.45.early), channel_id=1, source_target_pairs={{0,16},{4,20},{8,24},{12,28},{16,0},{20,4},{24,8},{28,12},{1,17},{... | collective-permute-start | bytes 614408 | tf_op jit(solution)/shard_map/ppermute | solution.py:441
  143.8 2.1 %collective-permute-done.12 = f32[480,128]{1,0:T(8,128)S(1)} collective-permute-done((f32[480,128]{1,0:T(8,128)S(1)}, f32[480,128]{1,0:T(8,128)S(1)}, u32[]{:S(2)}, u32[]{:S(2)}) %collective-permute-start.12) | collective-permute-done | bytes 245792 | tf_op jit(solution)/shard_map/ppermute | solution.py:441
  146.0 3.7 %collective-permute-start.13 = (f32[480,128]{1,0:T(8,128)S(1)}, f32[480,128]{1,0:T(8,128)S(1)}, u32[]{:S(2)}, u32[]{:S(2)}) collective-permute-start(f32[480,128]{1,0:T(8,128)S(1)} %add.42.late), channel_id=1, source_target_pairs={{0,16},{4,20},{8,24},{12,28},{16,0},{20,4},{24,8},{28,12},{1,17},{... | collective-permute-start | bytes 737288 | tf_op jit(solution)/shard_map/ppermute | solution.py:441
  149.7 3.9 %collective-permute-start.10 = (f32[2,2,64,128]{3,2,1,0:T(8,128)S(1)}, f32[2,2,64,128]{3,2,1,0:T(8,128)S(1)}, u32[]{:S(2)}, u32[]{:S(2)}) collective-permute-start(f32[2,2,64,128]{3,2,1,0:T(8,128)S(1)} %pad_maximum_fusion.1), channel_id=1, source_target_pairs={{4,0},{8,4},{12,8},{16,12},{20,16},{24,20},{28,24},{5,1},{9,5},{13... | collective-permute-start | bytes 393224 | tf_op jit(solution)/shard_map/ppermute | solution.py:422
  153.7 10.1 %collective-permute-done.10.next_head = f32[2,2,64,128]{3,2,1,0:T(8,128)S(1)} collective-permute-done((f32[2,2,64,128]{3,2,1,0:T(8,128)S(1)}, f32[2,2,64,128]{3,2,1,0:T(8,128)S(1)}, u32[]{:S(2)}, u32[]{:S(2)}) %collective-permute-start.10) | collective-permute-done | bytes 131104 | tf_op jit(solution)/shard_map/ppermute | solution.py:422
  163.7 4.9 %back.1 = (bf16[256,2048]{1,0:T(8,128)(2,1)}, bf16[256,2048]{1,0:T(8,128)(2,1)}) custom-call(f32[4096,128]{1,0:T(8,128)S(1)} %get-tuple-element.92.gf1, f32[4096,128]{1,0:T(8,128)S(1)} %get-tuple-element.93.gf2, f32[2,2,64,128]{3,2,1,0:T(8,128)S(1)} %collective-permute-done.10.next_head, f32[336,128]{1,0:T(8,128)S(1)} %get-tuple-element.60.filt), custom_call_target="tpu_custom_call" | custom-call | flops 14680064 | bytes 2097152 | tf_op jit(solution)/shard_map/back/pallas_call | solution.py:477
  (74 shorter events, 18.5 us)
Async XLA Ops:
  2.2 21.1 %collective-permute-start = (bf16[3,8,2048]{2,1,0:T(8,128)(2,1)S(1)}, bf16[3,8,2048]{2,1,0:T(8,128)(2,1)S(1)}, u32[]{:S(2)}, u32[]{:S(2)}) collective-permute-start(bf16[3,8,2048]{2,1,0:T(8,128)(2,1)S(1)} %pad_maximum_fusion.2), channel_id=1, source_target_pairs={{0,4},{4,8},{8,12},{12,16},{16,20},{20,24},{24,28},{1,5},{5,9},{9,... | collective-permute-start | bytes 294920 | tf_op jit(solution)/shard_map/ppermute | solution.py:422
  18.7 3.3 %copy-start.19 = (f32[4224,128]{1,0:T(8,128)S(1)}, f32[4224,128]{1,0:T(8,128)}, u32[]{:S(2)}) copy-start(f32[4224,128]{1,0:T(8,128)} %get-tuple-element.59.v_head) | copy-start | bytes 6488068
  22.0 2.4 %copy-start.5 = (f32[4096,128]{1,0:T(8,128)S(1)}, f32[4096,128]{1,0:T(8,128)}, u32[]{:S(2)}) copy-start(f32[4096,128]{1,0:T(8,128)} %get-tuple-element.64.f2_in) | copy-start | bytes 6291460
  24.3 23.3 %copy-start.11 = (bf16[256,2048]{1,0:T(8,128)(2,1)S(1)}, bf16[256,2048]{1,0:T(8,128)(2,1)}, u32[]{:S(2)}) copy-start(bf16[256,2048]{1,0:T(8,128)(2,1)} %query.3) | copy-start | bytes 3145732
  24.3 23.3 %copy-start.12 = (bf16[256,2048]{1,0:T(8,128)(2,1)S(1)}, bf16[256,2048]{1,0:T(8,128)(2,1)}, u32[]{:S(2)}) copy-start(bf16[256,2048]{1,0:T(8,128)(2,1)} %residual.1) | copy-start | bytes 3145732
  24.3 23.3 %copy-start.13 = (bf16[256,2048]{1,0:T(8,128)(2,1)S(1)}, bf16[256,2048]{1,0:T(8,128)(2,1)}, u32[]{:S(2)}) copy-start(bf16[256,2048]{1,0:T(8,128)(2,1)} %cot.1) | copy-start | bytes 3145732
  26.1 1.4 copy-start.4
  27.5 1.3 copy-start.6
  28.8 6.9 %collective-permute-start.2 = (f32[256,128]{1,0:T(8,128)S(1)}, f32[256,128]{1,0:T(8,128)S(1)}, u32[]{:S(2)}, u32[]{:S(2)}) collective-permute-start(f32[256,128]{1,0:T(8,128)S(1)} %get-tuple-element.72), channel_id=1, source_target_pairs={{0,8},{4,12},{8,16},{12,20},{16,24},{20,28},{1,9},{5,13},{9,17},{1... | collective-permute-start | bytes 393224 | tf_op jit(solution)/shard_map/ppermute | solution.py:422
  32.3 6.9 %collective-permute-start.1 = (f32[256,128]{1,0:T(8,128)S(1)}, f32[256,128]{1,0:T(8,128)S(1)}, u32[]{:S(2)}, u32[]{:S(2)}) collective-permute-start(f32[256,128]{1,0:T(8,128)S(1)} %get-tuple-element.72), channel_id=1, source_target_pairs={{0,4},{4,8},{8,12},{12,16},{16,20},{20,24},{24,28},{1,5},{5,9},{9,... | collective-permute-start | bytes 393224 | tf_op jit(solution)/shard_map/ppermute | solution.py:422
  39.2 14.7 %copy-start.1 = (f32[4096,128]{1,0:T(8,128)S(1)}, f32[4096,128]{1,0:T(8,128)}, u32[]{:S(2)}) copy-start(f32[4096,128]{1,0:T(8,128)} %get-tuple-element.66.u) | copy-start | bytes 6291460
  39.2 14.7 %copy-start.18 = (f32[2048]{0:T(1024)S(1)}, f32[2048]{0:T(1024)}, u32[]{:S(2)}) copy-start(f32[2048]{0:T(1024)} %param.17) | copy-start | bytes 24580
  39.2 7.0 %collective-permute-start.3 = (f32[256,128]{1,0:T(8,128)S(1)}, f32[256,128]{1,0:T(8,128)S(1)}, u32[]{:S(2)}, u32[]{:S(2)}) collective-permute-start(f32[256,128]{1,0:T(8,128)S(1)} %multiply_add_fusion.6), channel_id=1, source_target_pairs={{0,8},{4,12},{8,16},{12,20},{16,24},{20,28},{1,9},{5,13},{9,17},{1... | collective-permute-start | bytes 393224 | tf_op jit(solution)/shard_map/ppermute | solution.py:422
  46.2 16.2 %collective-permute-start.4 = (f32[256,128]{1,0:T(8,128)S(1)}, f32[256,128]{1,0:T(8,128)S(1)}, u32[]{:S(2)}, u32[]{:S(2)}) collective-permute-start(f32[256,128]{1,0:T(8,128)S(1)} %multiply_add_fusion.5), channel_id=1, source_target_pairs={{0,16},{4,20},{8,24},{12,28},{1,17},{5,21},{9,25},{13,29},{2,18},{... | collective-permute-start | bytes 393224 | tf_op jit(solution)/shard_map/ppermute | solution.py:422
  52.5 1.3 copy-start.3
  53.9 8.6 %copy-start.17 = (f32[2048]{0:T(1024)S(1)}, f32[2048]{0:T(1024)}, u32[]{:S(2)}) copy-start(f32[2048]{0:T(1024)} %param.18) | copy-start | bytes 24580
  61.1 1.4 copy-start.7
  68.4 1.3 copy-start.2
  80.3 8.8 %collective-permute-start.7 = (f32[256,128]{1,0:T(8,128)S(1)}, f32[256,128]{1,0:T(8,128)S(1)}, u32[]{:S(2)}, u32[]{:S(2)}) collective-permute-start(f32[256,128]{1,0:T(8,128)S(1)} %get-tuple-element.88), channel_id=1, source_target_pairs={{8,0},{12,4},{16,8},{20,12},{24,16},{28,20},{9,1},{13,5},{17,9},{2... | collective-permute-start | bytes 393224 | tf_op jit(solution)/shard_map/ppermute | solution.py:422
  84.2 8.2 %collective-permute-start.6 = (f32[256,128]{1,0:T(8,128)S(1)}, f32[256,128]{1,0:T(8,128)S(1)}, u32[]{:S(2)}, u32[]{:S(2)}) collective-permute-start(f32[256,128]{1,0:T(8,128)S(1)} %get-tuple-element.88), channel_id=1, source_target_pairs={{4,0},{8,4},{12,8},{16,12},{20,16},{24,20},{28,24},{5,1},{9,5},{13... | collective-permute-start | bytes 393224 | tf_op jit(solution)/shard_map/ppermute | solution.py:422
  92.5 19.8 %collective-permute-start.8 = (f32[256,128]{1,0:T(8,128)S(1)}, f32[256,128]{1,0:T(8,128)S(1)}, u32[]{:S(2)}, u32[]{:S(2)}) collective-permute-start(f32[256,128]{1,0:T(8,128)S(1)} %multiply_add_fusion.3), channel_id=1, source_target_pairs={{8,0},{12,4},{16,8},{20,12},{24,16},{28,20},{9,1},{13,5},{17,9},{2... | collective-permute-start | bytes 393224 | tf_op jit(solution)/shard_map/ppermute | solution.py:422
  96.4 17.2 %collective-permute-start.5 = (f32[128,128]{1,0:T(8,128)S(1)}, f32[128,128]{1,0:T(8,128)S(1)}, u32[]{:S(2)}, u32[]{:S(2)}) collective-permute-start(f32[128,128]{1,0:T(8,128)S(1)} %get-tuple-element.78), channel_id=1, source_target_pairs={{4,0},{8,4},{12,8},{16,12},{20,16},{24,20},{28,24},{5,1},{9,5},{13... | collective-permute-start | bytes 196616 | tf_op jit(solution)/shard_map/ppermute | solution.py:422
  98.3 15.3 %copy-start = (f32[4096,128]{1,0:T(8,128)S(1)}, f32[4096,128]{1,0:T(8,128)}, u32[]{:S(2)}) copy-start(f32[4096,128]{1,0:T(8,128)} %get-tuple-element.71.cot_pos) | copy-start | bytes 6291460
  112.2 9.9 %copy-start.8 = (f32[4096,128]{1,0:T(8,128)}, f32[4096,128]{1,0:T(8,128)S(1)}, u32[]{:S(2)}) copy-start(f32[4096,128]{1,0:T(8,128)S(1)} %get-tuple-element.83.gmx) | copy-start | bytes 6291460
  112.3 10.8 %collective-permute-start.9 = (f32[256,128]{1,0:T(8,128)S(1)}, f32[256,128]{1,0:T(8,128)S(1)}, u32[]{:S(2)}, u32[]{:S(2)}) collective-permute-start(f32[256,128]{1,0:T(8,128)S(1)} %multiply_add_fusion.2), channel_id=1, source_target_pairs={{16,0},{20,4},{24,8},{28,12},{17,1},{21,5},{25,9},{29,13},{18,2},{... | collective-permute-start | bytes 393224 | tf_op jit(solution)/shard_map/ppermute | solution.py:422
  122.2 10.5 %collective-permute-start.14 = (f32[400,128]{1,0:T(8,128)S(1)}, f32[400,128]{1,0:T(8,128)S(1)}, u32[]{:S(2)}, u32[]{:S(2)}) collective-permute-start(f32[400,128]{1,0:T(8,128)S(1)} %bitcast.32), channel_id=1, source_target_pairs={{0,4},{4,0},{8,12},{12,8},{16,20},{20,16},{24,28},{28,24},{1,5},{5... | collective-permute-start | bytes 614408 | tf_op jit(solution)/shard_map/ppermute | solution.py:441
  131.4 6.5 %collective-permute-start.11 = (f32[480,128]{1,0:T(8,128)S(1)}, f32[480,128]{1,0:T(8,128)S(1)}, u32[]{:S(2)}, u32[]{:S(2)}) collective-permute-start(f32[480,128]{1,0:T(8,128)S(1)} %get-tuple-element.96), channel_id=1, source_target_pairs={{0,4},{4,0},{8,12},{12,8},{16,20},{20,16},{24,28},{28,24},{1,5},{5... | collective-permute-start | bytes 737288 | tf_op jit(solution)/shard_map/ppermute | solution.py:441
  132.7 5.9 %collective-permute-start.15 = (f32[400,128]{1,0:T(8,128)S(1)}, f32[400,128]{1,0:T(8,128)S(1)}, u32[]{:S(2)}, u32[]{:S(2)}) collective-permute-start(f32[400,128]{1,0:T(8,128)S(1)} %bitcast_add_fusion), channel_id=1, source_target_pairs={{0,8},{4,12},{8,0},{12,4},{16,24},{20,28},{24,16},{28,20},{1,9},{5... | collective-permute-start | bytes 614408 | tf_op jit(solution)/shard_map/ppermute | solution.py:441
  138.0 8.0 %collective-permute-start.12 = (f32[480,128]{1,0:T(8,128)S(1)}, f32[480,128]{1,0:T(8,128)S(1)}, u32[]{:S(2)}, u32[]{:S(2)}) collective-permute-start(f32[480,128]{1,0:T(8,128)S(1)} %add.41), channel_id=1, source_target_pairs={{0,8},{4,12},{8,0},{12,4},{16,24},{20,28},{24,16},{28,20},{1,9},{5... | collective-permute-start | bytes 737288 | tf_op jit(solution)/shard_map/ppermute | solution.py:441
  138.6 30.0 %collective-permute-start.16 = (f32[400,128]{1,0:T(8,128)S(1)}, f32[400,128]{1,0:T(8,128)S(1)}, u32[]{:S(2)}, u32[]{:S(2)}) collective-permute-start(f32[400,128]{1,0:T(8,128)S(1)} %add.45.early), channel_id=1, source_target_pairs={{0,16},{4,20},{8,24},{12,28},{16,0},{20,4},{24,8},{28,12},{1,17},{... | collective-permute-start | bytes 614408 | tf_op jit(solution)/shard_map/ppermute | solution.py:441
  146.0 22.7 %collective-permute-start.13 = (f32[480,128]{1,0:T(8,128)S(1)}, f32[480,128]{1,0:T(8,128)S(1)}, u32[]{:S(2)}, u32[]{:S(2)}) collective-permute-start(f32[480,128]{1,0:T(8,128)S(1)} %add.42.late), channel_id=1, source_target_pairs={{0,16},{4,20},{8,24},{12,28},{16,0},{20,4},{24,8},{28,12},{1,17},{... | collective-permute-start | bytes 737288 | tf_op jit(solution)/shard_map/ppermute | solution.py:441
  149.7 14.0 %collective-permute-start.10 = (f32[2,2,64,128]{3,2,1,0:T(8,128)S(1)}, f32[2,2,64,128]{3,2,1,0:T(8,128)S(1)}, u32[]{:S(2)}, u32[]{:S(2)}) collective-permute-start(f32[2,2,64,128]{3,2,1,0:T(8,128)S(1)} %pad_maximum_fusion.1), channel_id=1, source_target_pairs={{4,0},{8,4},{12,8},{16,12},{20,16},{24,20},{28,24},{5,1},{9,5},{13... | collective-permute-start | bytes 393224 | tf_op jit(solution)/shard_map/ppermute | solution.py:422
  (5 other events, 5.2 us)

commit v2 on v1

--- a/solution.py
+++ b/solution.py
@@ -12,7 +12,7 @@
 WIDE = SUB * LANES
 F32 = jnp.float32
 BF16 = jnp.bfloat16
-VMEM_LIMIT = 48 * 1024 * 1024
+VMEM_LIMIT = 10 * 1024 * 1024
 
 
 def row(ref, t):
@@ -107,10 +107,10 @@
 
 
 def head_kernel(
-    modes, taps, steps, halo, k_head, v_head, filt, lam, x_part, k_in, v_in, f1_in, f2_in, u_in,
+    modes, taps, steps, halo, k_head, v_head, filt, lam, x_part, f1_in, f2_in, u_in,
     k_ext, v_ext, f1, f2, u, x_out,
 ):
-    del k_in, v_in, f1_in, f2_in, u_in
+    del f1_in, f2_in, u_in
     margin = taps - 1
     for g in range(SUB):
         lanes = slice(g * LANES, (g + 1) * LANES)
@@ -366,7 +366,7 @@
     lax.fori_loop(0, steps // SUB, some, 0)
 
 
-def mixed_kernel(modes, taps, steps, gmx, f1, f2, k_ext, v_ext, lam, res, alpha, x_in, p_own, lag_own, rate_own, gf1, gf2, sums):
+def mixed_kernel(modes, taps, steps, gmx, f1, f2, k_ext, v_ext, lam, res, alpha, x_in, p_own, lag_own, rate_own, gf1, gf2, heads, sums):
     rates = [row(lam, m) for m in range(modes)]
     fade = [jnp.exp(-r) for r in rates]
 
@@ -383,6 +383,8 @@
     lax.fori_loop(
         0, steps // SUB, advance, tuple(row(res, m) * row(alpha, m) for m in range(modes))
     )
+    heads[0, 0] = gf1[: SUB * SUB, :]
+    heads[1, 0] = gf2[: SUB * SUB, :]
     for which, (grad, ext) in enumerate(((gf1, k_ext), (gf2, v_ext))):
         parts = filter_pass(taps, steps, grad, ext)
         for j in range(taps):
@@ -422,27 +424,34 @@
     return lax.ppermute(value, axis, route)
 
 
-def carried_in(own, lam, span, axis, sign):
+def join(state, others, lam, span, under):
+    for k, other in enumerate(others):
+        state = state + jnp.exp(lam * -float(span * (k + 1))) * other
+    return state if under is None else state + under[0, 0]
+
+
+def carried_in(own, lam, span, axis, sign, under):
     count = lax.axis_size(axis)
     reach = min(2, count - 1)
-    parts = [shift(own, axis, sign * k) for k in range(1, reach + 1)]
-    state = parts[0]
-    for k in range(1, reach):
-        state = state + jnp.exp(-lam * float(span * k)) * parts[k]
+    under = list(under) + [None] * count
+    first, *rest = [shift(own, axis, sign * k) for k in range(1, reach + 1)]
+    state = join(first, rest, lam, span, under.pop(0))
     while reach < count - 1:
-        state = state + jnp.exp(-lam * float(span * reach)) * shift(state, axis, sign * reach)
+        other = shift(state, axis, sign * reach)
+        state = join(state, [other], lam, span * reach, under.pop(0))
         reach *= 2
     return state
 
 
-def sum_but_last(value, axis):
+def sum_but_last(value, axis, under=None):
     count, step = lax.axis_size(axis), 1
     while True:
         other = lax.ppermute(value, axis, [(i, i ^ step) for i in range(count)])
         step *= 2
         if step >= count:
             return value, other
-        value = value + other
+        value = value + other if under is None else value + other + under[0, 0]
+        under = None
 
 
 def shards(
@@ -457,6 +466,9 @@
     def pos(count):
         return jax.ShapeDtypeStruct((blocks * count * SUB, LANES), F32)
 
+    def kept(count):
+        return pltpu.VMEM((blocks * count * SUB, LANES), F32)
+
     def pos_spec(count):
         return pl.BlockSpec((count * SUB, LANES), lambda h: (h, 0))
 
@@ -467,15 +479,28 @@
     wide = jax.ShapeDtypeStruct((steps, channels), BF16)
     mode_spec, one_spec, filt_spec = pos_spec(modes), pos_spec(1), pos_spec(3 * taps)
     seq_spec, ext_spec = pos_spec(steps), pos_spec(steps + SUB)
-    seq, ext, mode, one = pos(steps), pos(steps + SUB), pos(modes), pos(1)
+    seq, ext, mode, one = kept(steps), kept(steps + SUB), pos(modes), pos(1)
     halo_spec = pl.BlockSpec((3, SUB, WIDE), lambda h: (0, 0, h))
     param_spec = pl.BlockSpec((modes, WIDE), lambda h: (0, h))
     short_spec = pl.BlockSpec((3, taps, WIDE), lambda h: (0, 0, h))
 
     def call(body, ins, in_specs, outs, out_specs, ops, name, scratch=(), aliases=None):
-        elements = steps * channels
+        elements, n_refs = steps * channels, len(ins) + len(outs)
+
+        def with_done(*refs):
+            done = refs[n_refs]
+            done[...] = jnp.zeros_like(done)
+            body(*refs[:n_refs], *refs[n_refs + 1 :])
+
+        near = blocks * steps * SUB
+        ins = [
+            pltpu.with_memory_space_constraint(v, pltpu.VMEM) if v.shape[0] >= near else v
+            for v in ins
+        ]
+        outs = [*outs, jax.ShapeDtypeStruct((SUB, LANES), F32)]
+        out_specs = [*out_specs, pl.BlockSpec((SUB, LANES), lambda h: (0, 0))]
         return pl.pallas_call(
-            body,
+            with_done,
             grid=(blocks,),
             in_specs=in_specs,
             out_specs=out_specs,
@@ -491,12 +516,16 @@
             name=name,
         )(*ins)
 
+    far = [
+        pltpu.with_memory_space_constraint(v, pltpu.HBM)
+        for v in (residual, query_in, key_in, value_in, cotangent, short_filter, decay_rate, residues)
+    ]
     trailing = jnp.stack([s[steps - SUB :] for s in (query_in, key_in, value_in)])
     halo = shift(trailing, "ctx", 1)
 
-    k_ext, v_ext, f1, f2, u, lam, res, filt, x_part = call(
+    k_ext, v_ext, f1, f2, u, lam, res, filt, x_part, _ = call(
         functools.partial(features_kernel, modes, taps, steps),
-        (key_in, value_in, short_filter, decay_rate, residues),
+        (far[2], far[3], *far[5:]),
         [wide_spec, wide_spec, short_spec, param_spec, param_spec],
         [ext, ext, seq, seq, seq, mode, mode, pos(3 * taps), mode],
         [ext_spec, ext_spec, seq_spec, seq_spec, seq_spec, mode_spec, mode_spec, filt_spec, mode_spec],
@@ -504,28 +533,27 @@
         "features",
     )
     any_spec = pl.BlockSpec(memory_space=pl.ANY)
-    k_ext, v_ext, f1, f2, u, x_own = call(
+    k_ext, v_ext, f1, f2, u, x_own, _ = call(
         functools.partial(head_kernel, modes, taps, steps),
-        (halo, k_ext, v_ext, filt, lam, x_part, k_ext, v_ext, f1, f2, u),
+        (halo, k_ext, v_ext, filt, lam, x_part, f1, f2, u),
         [halo_spec, head_spec(steps + SUB, 1), head_spec(steps + SUB, 1), filt_spec, mode_spec, mode_spec]
-        + [any_spec] * 5,
+        + [any_spec] * 3,
         [ext, ext, seq, seq, seq, mode],
         [head_spec(steps + SUB, 0)] * 2 + [head_spec(steps, 0)] * 3 + [mode_spec],
         2,
         "head",
-        aliases={6: 0, 7: 1, 8: 2, 9: 3, 10: 4},
-    )
-    x_in = carried_in(x_own, lam, steps, "ctx", 1)
-    q_ext, f0, res_pos, cot_pos = call(
+        aliases={1: 0, 2: 1, 6: 2, 7: 3, 8: 4},
+    )
+    q_ext, f0, res_pos, cot_pos, query_done = call(
         functools.partial(query_kernel, taps, steps),
-        (query_in, residual, cotangent, halo, filt),
+        (far[1], far[0], far[4], halo, filt),
         [wide_spec, wide_spec, wide_spec, halo_spec, filt_spec],
         [ext, seq, seq, seq],
         [ext_spec, seq_spec, seq_spec, seq_spec],
         30,
         "query",
     )
-    y, p_own = call(
+    y, p_own, modal_done = call(
         functools.partial(own_modal_kernel, modes, steps),
         (u, lam, res, skip),
         [seq_spec, mode_spec, mode_spec, one_spec],
@@ -534,7 +562,8 @@
         96,
         "own_modal",
     )
-    modal, summed, sums = call(
+    x_in = carried_in(x_own, lam, steps, "ctx", 1, [query_done, modal_done])
+    modal, summed, sums, _ = call(
         functools.partial(summed_kernel, modes, steps, blocks),
         (y, f0, res_pos, cot_pos, x_in, lam, res, gain),
         [seq_spec] * 4 + [mode_spec] * 3 + [one_spec],
@@ -545,7 +574,7 @@
         scratch=[pltpu.VMEM((steps * SUB, LANES), F32)] * 2,
     )
     sums = lax.psum(sums, "tp")
-    scale, gm, a_own, gf0_head = call(
+    scale, gm, a_own, gf0_head, _ = call(
         functools.partial(grad_modal_kernel, modes, steps, width),
         (sums, summed, cot_pos, f0, modal, lam, gain),
         [pl.BlockSpec((2, steps), lambda h: (0, 0)), seq_spec, seq_spec, seq_spec, head_spec(steps, 0), mode_spec, one_spec],
@@ -554,9 +583,8 @@
         40,
         "grad_modal",
     )
-    alpha = carried_in(a_own, lam, steps, "ctx", -1)
     gf0_next = shift(gf0_head, "ctx", -1)
-    gmx, res_sum, rate_own, lag_own, skip_sum = call(
+    gmx, res_sum, rate_own, lag_own, skip_sum, adjoint_done = call(
         functools.partial(own_adjoint_kernel, modes, steps),
         (gm, u, lam, res, skip),
         [seq_spec, seq_spec, mode_spec, mode_spec, one_spec],
@@ -566,7 +594,7 @@
         "own_adjoint",
     )
     scale_spec = pl.BlockSpec((2 * steps, LANES), lambda h: (0, 0))
-    normed, grad_residual, grad_query, short0, gain_sum = call(
+    normed, grad_residual, grad_query, short0, gain_sum, outputs_done = call(
         functools.partial(outputs_kernel, taps, steps),
         (scale, summed, cot_pos, modal, q_ext, gf0_next, filt, gain),
         [scale_spec, seq_spec, seq_spec, seq_spec, ext_spec, pos_spec(SUB), filt_spec, one_spec],
@@ -579,6 +607,7 @@
             pltpu.VMEM(((steps + SUB) * SUB, LANES), F32),
         ],
     )
+    alpha = carried_in(a_own, lam, steps, "ctx", -1, [adjoint_done, outputs_done])
     early_rows = taps + modes + 2
     early = jnp.concatenate(
         [
@@ -589,22 +618,21 @@
     ).reshape(-1, LANES)
     early, early_other = sum_but_last(early, "ctx")
     late_rows = 2 * taps + modes
-    gf1, gf2, late = call(
+    next_spec = pl.BlockSpec((2, 1, SUB * SUB, LANES), lambda h: (0, h, 0, 0))
+    gf1, gf2, heads, late, _ = call(
         functools.partial(mixed_kernel, modes, taps, steps),
         (gmx, f1, f2, k_ext, v_ext, lam, res, alpha, x_in, p_own, lag_own, rate_own),
         [seq_spec] * 3 + [ext_spec] * 2 + [mode_spec] * 7,
-        [seq, seq, pos(late_rows)],
-        [seq_spec, seq_spec, pos_spec(late_rows)],
+        [seq, seq, jax.ShapeDtypeStruct((2, blocks, SUB * SUB, LANES), F32), pos(late_rows)],
+        [seq_spec, seq_spec, next_spec, pos_spec(late_rows)],
         64,
         "mixed",
     )
-    late, late_other = sum_but_last(late, "ctx")
-    heads = jnp.stack([v.reshape(blocks, steps * SUB, LANES)[:, : SUB * SUB] for v in (gf1, gf2)])
     next_head = shift(heads, "ctx", -1)
-    grad_key, grad_value = call(
+    grad_key, grad_value, back_done = call(
         functools.partial(back_kernel, taps, steps),
         (gf1, gf2, next_head, filt),
-        [seq_spec, seq_spec, pl.BlockSpec((2, 1, SUB * SUB, LANES), lambda h: (0, h, 0, 0)), filt_spec],
+        [seq_spec, seq_spec, next_spec, filt_spec],
         [wide, wide],
         [wide_spec, wide_spec],
         28,
@@ -614,8 +642,9 @@
             pltpu.VMEM(((steps + SUB) * SUB, LANES), F32),
         ],
     )
+    late, late_other = sum_but_last(late, "ctx", back_done)
     late_spec, early_spec = pos_spec(late_rows), pos_spec(early_rows)
-    grad_short, grad_residues, grad_rate, grad_skip, grad_gain = call(
+    grad_short, grad_residues, grad_rate, grad_skip, grad_gain, _ = call(
         functools.partial(finish_kernel, modes, taps),
         (late, late_other, early, early_other),
         [late_spec, late_spec, early_spec, early_spec],

time: 170 us -> 162 us (0.953)
  the two profiles are of different devices: /device:TPU:14 before, /device:TPU:0 now
where the time goes in v2:
time: 162 us
  Pallas kernels  59.4 us (37%)
  waiting for transfers between devices  44.1 us (27%)
  starting transfers between devices  29.7 us (18%)
  local copies, waits for them, and re-layouts  18.3 us (11%)
  blocking collectives  5.63 us (3%)
  other arithmetic  3.68 us (2%)
    pallas_call x11, Pallas kernels, call(): pl.pallas_call(with_done, grid=(blocks,), in_specs=in_specs, out_specs=ou...  59.4 us
    ppermute x11, starting transfers between devices, shift(): return lax.ppermute(value, axis, route)  24.5 us
    ppermute x11, waiting for transfers between devices, shift(): return lax.ppermute(value, axis, route)  23.4 us
    ppermute x6, waiting for transfers between devices, sum_but_last(): other = lax.ppermute(value, axis, [(i, i ^ step) for i in range(count)])  20.7 us
    unnamed x44, local copies, waits for them, and re-layouts  14.2 us
    psum x1, blocking collectives, shards(): sums = lax.psum(sums, 'tp')  5.63 us
    ppermute x6, starting transfers between devices, sum_but_last(): other = lax.ppermute(value, axis, [(i, i ^ step) for i in range(count)])  5.23 us
  transfers between devices with their start and end apart: 17, of which 7 were waited for; matrix products, arithmetic and copies ran while one was open for 2% of the time, Pallas kernels for 27%

profile of v2, /device:TPU:0, one launch (start us, length us, event | category | flops | bytes accessed | tf_op | source)
XLA Modules:
  0.0 161.7 jit_solution(15375025470976485971)
XLA Ops:
  2.2 4.8 %collective-permute-start = (bf16[3,8,2048]{2,1,0:T(8,128)(2,1)S(1)}, bf16[3,8,2048]{2,1,0:T(8,128)(2,1)S(1)}, u32[]{:S(2)}, u32[]{:S(2)}) collective-permute-start(bf16[3,8,2048]{2,1,0:T(8,128)(2,1)S(1)} %pad_maximum_fusion.1), channel_id=1, source_target_pairs={{0,4},{4,8},{8,12},{12,16},{16,20},{20,24},{24,28},{1,5},{5,9},{9,... | collective-permute-start | bytes 294920 | tf_op jit(solution)/shard_map/ppermute | solution.py:424
  7.1 7.4 %features.1 = (f32[4224,128]{1,0:T(8,128)S(1)}, f32[4224,128]{1,0:T(8,128)S(1)}, f32[4096,128]{1,0:T(8,128)S(1)}, f32[4096,128]{1,0:T(8,128)S(1)}, f32[4096,128]...) custom-call(bf16[256,2048]{1,0:T(8,128)(2,1)} %refs_0_.2, ...), custom_call_target="tpu_custom_call" | custom-call | flops 33554432 | bytes 2097152 | tf_op jit(solution)/shard_map/features/pallas_call | solution.py:502
  15.2 1.4 copy-done.2
  16.6 1.4 copy-done.4
  18.0 1.4 copy-done.14
  19.3 1.3 copy-done.16
  20.6 3.6 %collective-permute-start.2 = (f32[256,128]{1,0:T(8,128)S(1)}, f32[256,128]{1,0:T(8,128)S(1)}, u32[]{:S(2)}, u32[]{:S(2)}) collective-permute-start(f32[256,128]{1,0:T(8,128)S(1)} %get-tuple-element.78), channel_id=1, source_target_pairs={{0,8},{4,12},{8,16},{12,20},{16,24},{20,28},{1,9},{5,13},{9,17},{1... | collective-permute-start | bytes 393224 | tf_op jit(solution)/shard_map/ppermute | solution.py:424
  24.2 3.5 %collective-permute-start.1 = (f32[256,128]{1,0:T(8,128)S(1)}, f32[256,128]{1,0:T(8,128)S(1)}, u32[]{:S(2)}, u32[]{:S(2)}) collective-permute-start(f32[256,128]{1,0:T(8,128)S(1)} %get-tuple-element.78), channel_id=1, source_target_pairs={{0,4},{4,8},{8,12},{12,16},{16,20},{20,24},{24,28},{1,5},{5,9},{9,... | collective-permute-start | bytes 393224 | tf_op jit(solution)/shard_map/ppermute | solution.py:424
  27.7 4.2 %query.1 = (f32[4224,128]{1,0:T(8,128)S(1)}, f32[4096,128]{1,0:T(8,128)S(1)}, f32[4096,128]{1,0:T(8,128)S(1)}, f32[4096,128]{1,0:T(8,128)S(1)}, f32[8,128]{1,0:T(8,128)S(1)}) custom-call(bf16[256,2048]{1,0:T(8,128)(2,1)} %refs_0_.3, bf16[256,2048]{1,0:T(8,128)(2,1)} %refs_1_.3, bf16[256,2048]{1,0:T(8,128)(2,1)} %refs_2_.3, ...), custom_call_target="tpu_custom_call" | custom-call | flops 15728640 | bytes 2097152 | tf_op jit(solution)/shard_map/query/pallas_call | solution.py:502
  31.9 1.4 copy-done.18
  34.5 3.5 %collective-permute-start.3 = (f32[256,128]{1,0:T(8,128)S(1)}, f32[256,128]{1,0:T(8,128)S(1)}, u32[]{:S(2)}, u32[]{:S(2)}) collective-permute-start(f32[256,128]{1,0:T(8,128)S(1)} %add_add_fusion.4), channel_id=1, source_target_pairs={{0,8},{4,12},{8,16},{12,20},{16,24},{20,28},{1,9},{5,13},{9,17},{1... | collective-permute-start | bytes 393224 | tf_op jit(solution)/shard_map/ppermute | solution.py:424
  38.0 7.2 %own_modal.1 = (f32[4096,128]{1,0:T(8,128)S(1)}, f32[256,128]{1,0:T(8,128)S(1)}, f32[8,128]{1,0:T(8,128)S(1)}) custom-call(f32[4096,128]{1,0:T(8,128)S(1)} %get-tuple-element.72.refs_0_.refs_1_, f32[256,128]{1,0:T(8,128)S(1)} %get-tuple-element.67.refs_4_.refs_1_.refs_5_.refs_2_, f32[256,128]{1,0:T(8,128)S(1)} %get-tuple-element.73.refs_2_.refs_6_.refs_3_, ...), custom_call_target="tpu_custom_call" | custom-call | flops 50331648 | bytes 2097152 | tf_op jit(solution)/shard_map/own_modal/pallas_call | solution.py:502
  46.5 1.4 collective-permute-start.4
  47.9 2.5 %collective-permute-done.4 = f32[256,128]{1,0:T(8,128)S(1)} collective-permute-done((f32[256,128]{1,0:T(8,128)S(1)}, f32[256,128]{1,0:T(8,128)S(1)}, u32[]{:S(2)}, u32[]{:S(2)}) %collective-permute-start.4) | collective-permute-done | bytes 131104 | tf_op jit(solution)/shard_map/ppermute | solution.py:424
  50.4 4.3 %summed.1 = (f32[4096,128]{1,0:T(8,128)S(1)}, f32[4096,128]{1,0:T(8,128)S(1)}, f32[2,256]{1,0:T(2,128)S(1)}, f32[8,128]{1,0:T(8,128)}) custom-call(f32[4096,128]{1,0:T(8,128)S(1)} %get-tuple-element.74.refs_0_, f32[4096,128]{1,0:T(8,128)S(1)} %get-tuple-element.75.refs_1_.refs_3_, f32[4096,128]{1,0:T(8,128)S(1)} %get-tuple-element.76.refs_2_, ...), custom_call_target="tpu_custom_call" | custom-call | flops 20971520 | bytes 2097152 | tf_op jit(solution)/shard_map/summed/pallas_call | solution.py:502
  57.3 5.6 %psum.7.refs_0_ = f32[2,256]{1,0:T(2,128)S(1)} all-reduce(f32[2,256]{1,0:T(2,128)S(1)} %get-tuple-element.81), channel_id=1, replica_groups=mesh['ctx'=8,'tp'=4] {'tp'}, use_global_device_ids=true, to_apply=%region_0.0 | all-reduce | flops 512 | bytes 4096 | tf_op jit(solution)/shard_map/psum | solution.py:576
  62.9 1.6 copy-done.7
  64.5 1.6 copy-done.10
  66.1 1.6 copy-done.13
  67.7 3.7 %grad_modal.1 = (f32[512,128]{1,0:T(8,128)S(1)}, f32[4096,128]{1,0:T(8,128)S(1)}, f32[256,128]{1,0:T(8,128)S(1)}, f32[128,128]{1,0:T(8,128)S(1)}, f32[8,128]{1,0:T(8,128)}) custom-call(f32[2,256]{1,0:T(2,128)S(1)} %psum.7.refs_0_, f32[4096,128]{1,0:T(8,128)S(1)} %copy-done.10, f32[4096,128]{1,0:T(8,128)S(1)} %get-tuple-element.77.refs_3_.refs_2_, ...), custom_call_target="tpu_custom_call" | custom-call | flops 20971520 | bytes 2097152 | tf_op jit(solution)/shard_map/grad_modal/pallas_call | solution.py:502
  74.0 12.6 %own_adjoint.1 = (f32[4096,128]{1,0:T(8,128)S(1)}, f32[256,128]{1,0:T(8,128)S(1)}, f32[256,128]{1,0:T(8,128)S(1)}, f32[256,128]{1,0:T(8,128)S(1)}, f32[16,128]{1,0:T(8,128)S(1)}, /*index=5*/f32[8,128]{1,0:T(8,128)S(1)}) custom-call(f32[4096,128]{1,0:T(8,128)S(1)} %get-tuple-element.90.refs_0_, f32[4096,128]{1,0:T(8,128)S(1)} %copy-done.1, ...), custom_call_target="tpu_custom_call" | custom-call | flops 83886080 | bytes 2097152 | tf_op jit(solution)/shard_map/own_adjoint/pallas_call | solution.py:502
  90.5 5.5 %collective-permute-done.5.refs_5_ = f32[128,128]{1,0:T(8,128)S(1)} collective-permute-done((f32[128,128]{1,0:T(8,128)S(1)}, f32[128,128]{1,0:T(8,128)S(1)}, u32[]{:S(2)}, u32[]{:S(2)}) %collective-permute-start.5) | collective-permute-done | bytes 65568 | tf_op jit(solution)/shard_map/ppermute | solution.py:424
  96.0 7.0 %outputs.1 = (bf16[256,2048]{1,0:T(8,128)(2,1)}, bf16[256,2048]{1,0:T(8,128)(2,1)}, bf16[256,2048]{1,0:T(8,128)(2,1)}, f32[112,128]{1,0:T(8,128)S(1)}, f32[16,128]{1,0:T(8,128)S(1)}, /*index=5*/f32[8,128]{1,0:T(8,128)S(1)}) custom-call(f32[512,128]{1,0:T(8,128)S(1)} %get-tuple-element.84.refs_0_, f32[4096,128]{1,0:T(8,128)S(1)} %copy-done.11, ...), custom_call_target="tpu_custom_call" | custom-call | flops 26214400 | bytes 2097152 | tf_op jit(solution)/shard_map/outputs/pallas_call | solution.py:502
  105.5 11.2 %collective-permute-done.9 = f32[256,128]{1,0:T(8,128)S(1)} collective-permute-done((f32[256,128]{1,0:T(8,128)S(1)}, f32[256,128]{1,0:T(8,128)S(1)}, u32[]{:S(2)}, u32[]{:S(2)}) %collective-permute-start.9) | collective-permute-done | bytes 131104 | tf_op jit(solution)/shard_map/ppermute | solution.py:424
  116.8 6.4 %mixed.1 = (f32[4096,128]{1,0:T(8,128)S(1)}, f32[4096,128]{1,0:T(8,128)S(1)}, f32[2,2,64,128]{3,2,1,0:T(8,128)S(1)}, f32[480,128]{1,0:T(8,128)S(1)}, f32[8,128]{1,0:T(8,128)}) custom-call(f32[4096,128]{1,0:T(8,128)S(1)} %get-tuple-element.91.refs_0_, f32[4096,128]{1,0:T(8,128)S(1)} %copy-done.15, f32[4096,128]{1,0:T(8,128)S(1)} %copy-done.17, ...), custom_call_target="tpu_custom_call" | custom-call | flops 33554432 | bytes 2097152 | tf_op jit(solution)/shard_map/mixed/pallas_call | solution.py:502
  124.5 2.9 %collective-permute-start.11 = (f32[480,128]{1,0:T(8,128)S(1)}, f32[480,128]{1,0:T(8,128)S(1)}, u32[]{:S(2)}, u32[]{:S(2)}) collective-permute-start(f32[480,128]{1,0:T(8,128)S(1)} %get-tuple-element.107), channel_id=1, source_target_pairs={{0,4},{4,0},{8,12},{12,8},{16,20},{20,16},{24,28},{28,24},{1,5},{5... | collective-permute-start | bytes 737288 | tf_op jit(solution)/shard_map/ppermute | solution.py:449
  127.5 4.2 %collective-permute-done.10.refs_2_ = f32[2,2,64,128]{3,2,1,0:T(8,128)S(1)} collective-permute-done((f32[2,2,64,128]{3,2,1,0:T(8,128)S(1)}, f32[2,2,64,128]{3,2,1,0:T(8,128)S(1)}, u32[]{:S(2)}, u32[]{:S(2)}) %collective-permute-start.10) | collective-permute-done | bytes 131104 | tf_op jit(solution)/shard_map/ppermute | solution.py:424
  131.7 4.9 %back.1 = (bf16[256,2048]{1,0:T(8,128)(2,1)}, bf16[256,2048]{1,0:T(8,128)(2,1)}, f32[8,128]{1,0:T(8,128)S(1)}) custom-call(f32[4096,128]{1,0:T(8,128)S(1)} %get-tuple-element.102.refs_0_, f32[4096,128]{1,0:T(8,128)S(1)} %get-tuple-element.103.refs_1_, f32[2,2,64,128]{3,2,1,0:T(8,128)S(1)} %collective-permute-done.10.refs_2_, ...), custom_call_target="tpu_custom_call" | custom-call | flops 14680064 | bytes 2097152 | tf_op jit(solution)/shard_map/back/pallas_call | solution.py:502
  137.9 2.1 %collective-permute-start.15 = (f32[400,128]{1,0:T(8,128)S(1)}, f32[400,128]{1,0:T(8,128)S(1)}, u32[]{:S(2)}, u32[]{:S(2)}) collective-permute-start(f32[400,128]{1,0:T(8,128)S(1)} %bitcast_add_fusion), channel_id=1, source_target_pairs={{0,8},{4,12},{8,0},{12,4},{16,24},{20,28},{24,16},{28,20},{1,9},{5... | collective-permute-start | bytes 614408 | tf_op jit(solution)/shard_map/ppermute | solution.py:449
  140.0 7.4 %collective-permute-done.12 = f32[480,128]{1,0:T(8,128)S(1)} collective-permute-done((f32[480,128]{1,0:T(8,128)S(1)}, f32[480,128]{1,0:T(8,128)S(1)}, u32[]{:S(2)}, u32[]{:S(2)}) %collective-permute-start.12) | collective-permute-done | bytes 245792 | tf_op jit(solution)/shard_map/ppermute | solution.py:449
  147.5 3.6 %collective-permute-done.15 = f32[400,128]{1,0:T(8,128)S(1)} collective-permute-done((f32[400,128]{1,0:T(8,128)S(1)}, f32[400,128]{1,0:T(8,128)S(1)}, u32[]{:S(2)}, u32[]{:S(2)}) %collective-permute-start.15) | collective-permute-done | bytes 204832 | tf_op jit(solution)/shard_map/ppermute | solution.py:449
  151.2 9.7 %collective-permute-done.16.refs_3_ = f32[400,128]{1,0:T(8,128)S(1)} collective-permute-done((f32[400,128]{1,0:T(8,128)S(1)}, f32[400,128]{1,0:T(8,128)S(1)}, u32[]{:S(2)}, u32[]{:S(2)}) %collective-permute-start.16) | collective-permute-done | bytes 204832 | tf_op jit(solution)/shard_map/ppermute | solution.py:449
  (78 shorter events, 20.1 us)
Async XLA Ops:
  2.2 12.3 %collective-permute-start = (bf16[3,8,2048]{2,1,0:T(8,128)(2,1)S(1)}, bf16[3,8,2048]{2,1,0:T(8,128)(2,1)S(1)}, u32[]{:S(2)}, u32[]{:S(2)}) collective-permute-start(bf16[3,8,2048]{2,1,0:T(8,128)(2,1)S(1)} %pad_maximum_fusion.1), channel_id=1, source_target_pairs={{0,4},{4,8},{8,12},{12,16},{16,20},{20,24},{24,28},{1,5},{5,9},{9,... | collective-permute-start | bytes 294920 | tf_op jit(solution)/shard_map/ppermute | solution.py:424
  20.6 24.6 %copy-start = (f32[4096,128]{1,0:T(8,128)}, f32[4096,128]{1,0:T(8,128)S(1)}, u32[]{:S(2)}) copy-start(f32[4096,128]{1,0:T(8,128)S(1)} %get-tuple-element.72.refs_0_.refs_1_) | copy-start | bytes 6291460
  20.6 17.4 %copy-start.21 = (f32[2048]{0:T(1024)S(1)}, f32[2048]{0:T(1024)}, u32[]{:S(2)}) copy-start(f32[2048]{0:T(1024)} %param.17) | copy-start | bytes 24580
  20.6 13.2 %collective-permute-start.2 = (f32[256,128]{1,0:T(8,128)S(1)}, f32[256,128]{1,0:T(8,128)S(1)}, u32[]{:S(2)}, u32[]{:S(2)}) collective-permute-start(f32[256,128]{1,0:T(8,128)S(1)} %get-tuple-element.78), channel_id=1, source_target_pairs={{0,8},{4,12},{8,16},{12,20},{16,24},{20,28},{1,9},{5,13},{9,17},{1... | collective-permute-start | bytes 393224 | tf_op jit(solution)/shard_map/ppermute | solution.py:424
  24.2 9.6 %collective-permute-start.1 = (f32[256,128]{1,0:T(8,128)S(1)}, f32[256,128]{1,0:T(8,128)S(1)}, u32[]{:S(2)}, u32[]{:S(2)}) collective-permute-start(f32[256,128]{1,0:T(8,128)S(1)} %get-tuple-element.78), channel_id=1, source_target_pairs={{0,4},{4,8},{8,12},{12,16},{16,20},{20,24},{24,28},{1,5},{5,9},{9,... | collective-permute-start | bytes 393224 | tf_op jit(solution)/shard_map/ppermute | solution.py:424
  33.3 21.4 %copy-start.12 = (f32[4096,128]{1,0:T(8,128)}, f32[4096,128]{1,0:T(8,128)S(1)}, u32[]{:S(2)}) copy-start(f32[4096,128]{1,0:T(8,128)S(1)} %get-tuple-element.75.refs_1_.refs_3_) | copy-start | bytes 6291460
  33.3 17.1 %copy-start.20 = (f32[2048]{0:T(1024)S(1)}, f32[2048]{0:T(1024)}, u32[]{:S(2)}) copy-start(f32[2048]{0:T(1024)} %param.18) | copy-start | bytes 24580
  34.5 11.2 %collective-permute-start.3 = (f32[256,128]{1,0:T(8,128)S(1)}, f32[256,128]{1,0:T(8,128)S(1)}, u32[]{:S(2)}, u32[]{:S(2)}) collective-permute-start(f32[256,128]{1,0:T(8,128)S(1)} %add_add_fusion.4), channel_id=1, source_target_pairs={{0,8},{4,12},{8,16},{12,20},{16,24},{20,28},{1,9},{5,13},{9,17},{1... | collective-permute-start | bytes 393224 | tf_op jit(solution)/shard_map/ppermute | solution.py:424
  46.5 3.9 %collective-permute-start.4 = (f32[256,128]{1,0:T(8,128)S(1)}, f32[256,128]{1,0:T(8,128)S(1)}, u32[]{:S(2)}, u32[]{:S(2)}) collective-permute-start(f32[256,128]{1,0:T(8,128)S(1)} %add_add_fusion.3), channel_id=1, source_target_pairs={{0,16},{4,20},{8,24},{12,28},{1,17},{5,21},{9,25},{13,29},{2,18},{... | collective-permute-start | bytes 393224 | tf_op jit(solution)/shard_map/ppermute | solution.py:424
  62.9 1.6 copy-start.7
  64.5 1.6 copy-start.10
  66.1 1.6 copy-start.13
  67.7 6.3 %copy-start.1 = (f32[4096,128]{1,0:T(8,128)S(1)}, f32[4096,128]{1,0:T(8,128)}, u32[]{:S(2)}) copy-start(f32[4096,128]{1,0:T(8,128)} %copy-done) | copy-start | bytes 6291460
  67.7 28.3 %copy-start.19 = (f32[4224,128]{1,0:T(8,128)S(1)}, f32[4224,128]{1,0:T(8,128)}, u32[]{:S(2)}) copy-start(f32[4224,128]{1,0:T(8,128)} %copy-done.18) | copy-start | bytes 6488068
  71.4 15.7 %collective-permute-start.7 = (f32[256,128]{1,0:T(8,128)S(1)}, f32[256,128]{1,0:T(8,128)S(1)}, u32[]{:S(2)}, u32[]{:S(2)}) collective-permute-start(f32[256,128]{1,0:T(8,128)S(1)} %get-tuple-element.96), channel_id=1, source_target_pairs={{8,0},{12,4},{16,8},{20,12},{24,16},{28,20},{9,1},{13,5},{17,9},{2... | collective-permute-start | bytes 393224 | tf_op jit(solution)/shard_map/ppermute | solution.py:424
  72.7 14.5 %collective-permute-start.6 = (f32[256,128]{1,0:T(8,128)S(1)}, f32[256,128]{1,0:T(8,128)S(1)}, u32[]{:S(2)}, u32[]{:S(2)}) collective-permute-start(f32[256,128]{1,0:T(8,128)S(1)} %get-tuple-element.96), channel_id=1, source_target_pairs={{4,0},{8,4},{12,8},{16,12},{20,16},{24,20},{28,24},{5,1},{9,5},{13... | collective-permute-start | bytes 393224 | tf_op jit(solution)/shard_map/ppermute | solution.py:424
  74.0 21.9 %copy-start.8 = (f32[4096,128]{1,0:T(8,128)S(1)}, f32[4096,128]{1,0:T(8,128)}, u32[]{:S(2)}) copy-start(f32[4096,128]{1,0:T(8,128)} %copy-done.6) | copy-start | bytes 6291460
  74.0 21.9 %copy-start.11 = (f32[4096,128]{1,0:T(8,128)S(1)}, f32[4096,128]{1,0:T(8,128)}, u32[]{:S(2)}) copy-start(f32[4096,128]{1,0:T(8,128)} %copy-done.9) | copy-start | bytes 6291460
  87.9 15.7 %collective-permute-start.8 = (f32[256,128]{1,0:T(8,128)S(1)}, f32[256,128]{1,0:T(8,128)S(1)}, u32[]{:S(2)}, u32[]{:S(2)}) collective-permute-start(f32[256,128]{1,0:T(8,128)S(1)} %add_add_fusion.2), channel_id=1, source_target_pairs={{8,0},{12,4},{16,8},{20,12},{24,16},{28,20},{9,1},{13,5},{17,9},{2... | collective-permute-start | bytes 393224 | tf_op jit(solution)/shard_map/ppermute | solution.py:424
  89.2 6.8 %collective-permute-start.5 = (f32[128,128]{1,0:T(8,128)S(1)}, f32[128,128]{1,0:T(8,128)S(1)}, u32[]{:S(2)}, u32[]{:S(2)}) collective-permute-start(f32[128,128]{1,0:T(8,128)S(1)} %get-tuple-element.86), channel_id=1, source_target_pairs={{4,0},{8,4},{12,8},{16,12},{20,16},{24,20},{28,24},{5,1},{9,5},{13... | collective-permute-start | bytes 196616 | tf_op jit(solution)/shard_map/ppermute | solution.py:424
  96.0 20.8 %copy-start.3 = (f32[4224,128]{1,0:T(8,128)S(1)}, f32[4224,128]{1,0:T(8,128)}, u32[]{:S(2)}) copy-start(f32[4224,128]{1,0:T(8,128)} %copy-done.2) | copy-start | bytes 6488068
  96.0 20.8 %copy-start.5 = (f32[4224,128]{1,0:T(8,128)S(1)}, f32[4224,128]{1,0:T(8,128)}, u32[]{:S(2)}) copy-start(f32[4224,128]{1,0:T(8,128)} %copy-done.4) | copy-start | bytes 6488068
  96.0 20.8 %copy-start.15 = (f32[4096,128]{1,0:T(8,128)S(1)}, f32[4096,128]{1,0:T(8,128)}, u32[]{:S(2)}) copy-start(f32[4096,128]{1,0:T(8,128)} %copy-done.14) | copy-start | bytes 6291460
  96.0 20.8 %copy-start.17 = (f32[4096,128]{1,0:T(8,128)S(1)}, f32[4096,128]{1,0:T(8,128)}, u32[]{:S(2)}) copy-start(f32[4096,128]{1,0:T(8,128)} %copy-done.16) | copy-start | bytes 6291460
  104.2 12.5 %collective-permute-start.9 = (f32[256,128]{1,0:T(8,128)S(1)}, f32[256,128]{1,0:T(8,128)S(1)}, u32[]{:S(2)}, u32[]{:S(2)}) collective-permute-start(f32[256,128]{1,0:T(8,128)S(1)} %add_add_fusion.1), channel_id=1, source_target_pairs={{16,0},{20,4},{24,8},{28,12},{17,1},{21,5},{25,9},{29,13},{18,2},{... | collective-permute-start | bytes 393224 | tf_op jit(solution)/shard_map/ppermute | solution.py:424
  123.2 8.5 %collective-permute-start.10 = (f32[2,2,64,128]{3,2,1,0:T(8,128)S(1)}, f32[2,2,64,128]{3,2,1,0:T(8,128)S(1)}, u32[]{:S(2)}, u32[]{:S(2)}) collective-permute-start(f32[2,2,64,128]{3,2,1,0:T(8,128)S(1)} %get-tuple-element.104), channel_id=1, source_target_pairs={{4,0},{8,4},{12,8},{16,12},{20,16},{24,20},{28,24},{5,1},{9,5},{13... | collective-permute-start | bytes 393224 | tf_op jit(solution)/shard_map/ppermute | solution.py:424
  124.5 12.6 %collective-permute-start.11 = (f32[480,128]{1,0:T(8,128)S(1)}, f32[480,128]{1,0:T(8,128)S(1)}, u32[]{:S(2)}, u32[]{:S(2)}) collective-permute-start(f32[480,128]{1,0:T(8,128)S(1)} %get-tuple-element.107), channel_id=1, source_target_pairs={{0,4},{4,0},{8,12},{12,8},{16,20},{20,16},{24,28},{28,24},{1,5},{5... | collective-permute-start | bytes 737288 | tf_op jit(solution)/shard_map/ppermute | solution.py:449
  127.4 10.5 %collective-permute-start.14 = (f32[400,128]{1,0:T(8,128)S(1)}, f32[400,128]{1,0:T(8,128)S(1)}, u32[]{:S(2)}, u32[]{:S(2)}) collective-permute-start(f32[400,128]{1,0:T(8,128)S(1)} %bitcast.29), channel_id=1, source_target_pairs={{0,4},{4,0},{8,12},{12,8},{16,20},{20,16},{24,28},{28,24},{1,5},{5... | collective-permute-start | bytes 614408 | tf_op jit(solution)/shard_map/ppermute | solution.py:449
  137.8 9.6 %collective-permute-start.12 = (f32[480,128]{1,0:T(8,128)S(1)}, f32[480,128]{1,0:T(8,128)S(1)}, u32[]{:S(2)}, u32[]{:S(2)}) collective-permute-start(f32[480,128]{1,0:T(8,128)S(1)} %add_add_fusion), channel_id=1, source_target_pairs={{0,8},{4,12},{8,0},{12,4},{16,24},{20,28},{24,16},{28,20},{1,9},{5... | collective-permute-start | bytes 737288 | tf_op jit(solution)/shard_map/ppermute | solution.py:449
  137.9 13.2 %collective-permute-start.15 = (f32[400,128]{1,0:T(8,128)S(1)}, f32[400,128]{1,0:T(8,128)S(1)}, u32[]{:S(2)}, u32[]{:S(2)}) collective-permute-start(f32[400,128]{1,0:T(8,128)S(1)} %bitcast_add_fusion), channel_id=1, source_target_pairs={{0,8},{4,12},{8,0},{12,4},{16,24},{20,28},{24,16},{28,20},{1,9},{5... | collective-permute-start | bytes 614408 | tf_op jit(solution)/shard_map/ppermute | solution.py:449
  147.5 13.4 %collective-permute-start.13 = (f32[480,128]{1,0:T(8,128)S(1)}, f32[480,128]{1,0:T(8,128)S(1)}, u32[]{:S(2)}, u32[]{:S(2)}) collective-permute-start(f32[480,128]{1,0:T(8,128)S(1)} %add.82.refs_0_), channel_id=1, source_target_pairs={{0,16},{4,20},{8,24},{12,28},{16,0},{20,4},{24,8},{28,12},{1,17},{... | collective-permute-start | bytes 737288 | tf_op jit(solution)/shard_map/ppermute | solution.py:449
  151.1 9.8 %collective-permute-start.16 = (f32[400,128]{1,0:T(8,128)S(1)}, f32[400,128]{1,0:T(8,128)S(1)}, u32[]{:S(2)}, u32[]{:S(2)}) collective-permute-start(f32[400,128]{1,0:T(8,128)S(1)} %add.85.refs_2_), channel_id=1, source_target_pairs={{0,16},{4,20},{8,24},{12,28},{16,0},{20,4},{24,8},{28,12},{1,17},{... | collective-permute-start | bytes 614408 | tf_op jit(solution)/shard_map/ppermute | solution.py:449
  (7 other events, 9.4 us)

commit v3 on v2

v3 whole, which is shorter than its diff:
```python
import functools

import jax
import jax.numpy as jnp
from jax import lax
from jax.experimental import pallas as pl
from jax.experimental.pallas import tpu as pltpu
from jax.sharding import PartitionSpec as P

LANES = 128
SUB = 8
WIDE = SUB * LANES
F32 = jnp.float32
BF16 = jnp.bfloat16
VMEM_LIMIT = 10 * 1024 * 1024


def row(ref, t):
    return ref[pl.ds(pl.multiple_of(t * SUB, SUB), SUB), :]


def put(ref, t, value):
    ref[pl.ds(pl.multiple_of(t * SUB, SUB), SUB), :] = value


def spread(src, dst, first, count):
    def some(i, carry):
        start = pl.multiple_of(i * 16, 16)
        for g in range(SUB):
            piece = src[pl.ds(start, 16), g * LANES : (g + 1) * LANES].astype(F32)
            dst[pl.ds((start + first) * SUB + g, 16, stride=SUB), :] = piece
        return carry

    lax.fori_loop(0, count // 16, some, 0)


def gather_rows(src, dst, count):
    def some(i, carry):
        start = pl.multiple_of(i * 16, 16)
        for g in range(SUB):
            piece = src[pl.ds(start * SUB + g, 16, stride=SUB), :]
            dst[pl.ds(start, 16), g * LANES : (g + 1) * LANES] = piece.astype(dst.dtype)
        return carry

    lax.fori_loop(0, count // 16, some, 0)


def total(values):
    values = list(values)
    while len(values) > 1:
        values = [
            values[i] + values[i + 1] if i + 1 < len(values) else values[i]
            for i in range(0, len(values), 2)
        ]
    return values[0]


def taps_of(filt, stream, taps):
    return [row(filt, stream * taps + j) for j in range(taps)]


def conv_at(window, taps, i):
    margin = len(taps) - 1
    return total([taps[j] * window[margin + i - j] for j in range(margin + 1)])


def trailing_kernel(query, key, value, out):
    for i, ref in enumerate((query, key, value)):
        out[i] = ref[...].astype(F32)[SUB:, :].astype(BF16)


def features_kernel(
    modes, taps, steps, key, value, filt3, decay, resid, k_ext, v_ext, f1, f2, u, g, lam, res, filt, x_out
):
    margin = taps - 1
    for s in range(SUB):
        lanes = slice(s * LANES, (s + 1) * LANES)
        lam[pl.ds(s, modes, stride=SUB), :] = decay[:, lanes]
        res[pl.ds(s, modes, stride=SUB), :] = resid[:, lanes]
        for i in range(3):
            filt[pl.ds(i * taps * SUB + s, taps, stride=SUB), :] = filt3[i, :, lanes]
    spread(key, k_ext, SUB, steps)
    spread(value, v_ext, SUB, steps)
    taps1, taps2 = taps_of(filt, 1, taps), taps_of(filt, 2, taps)

    def conv(c, carry):
        t0 = c * SUB
        kw = [row(k_ext, t0 + SUB - margin + i) for i in range(SUB + margin)]
        for i in range(SUB):
            put(f1, t0 + i, conv_at(kw, taps1, i))
        vw = [row(v_ext, t0 + SUB - margin + i) for i in range(SUB + margin)]
        for i in range(SUB):
            second = conv_at(vw, taps2, i)
            put(f2, t0 + i, second)
            put(u, t0 + i, second * row(f1, t0 + i))
        return carry

    lax.fori_loop(1, steps // SUB, conv, 0)
    fade, skip = fades(lam, modes, 1), fades(lam, modes, SUB)

    def advance(c, x):
        now = [row(u, c * SUB + i) for i in range(SUB)]
        new = []
        for m in range(modes):
            own = horner(fade[m], now)
            put(g, c * modes + m, own)
            new.append(own + skip[m] * x[m])
        return tuple(new)

    x = lax.fori_loop(1, steps // SUB, advance, zeros(modes))
    for m in range(modes):
        put(x_out, m, x[m])


def zeros(count):
    return tuple(jnp.zeros((SUB, LANES), F32) for _ in range(count))


def fades(lam, modes, span):
    return [jnp.exp(row(lam, m) * -float(span)) for m in range(modes)]


def horner(fade, values):
    result = values[0]
    for value in values[1:]:
        result = fade * result + value
    return result


def head_kernel(
    modes, taps, steps, halo, k_head, v_head, filt, lam, x_part, f1_in, f2_in, u_in, g_in,
    k_ext, v_ext, f1, f2, u, g, x_out,
):
    del f1_in, f2_in, u_in, g_in
    margin = taps - 1
    for s in range(SUB):
        lanes = slice(s * LANES, (s + 1) * LANES)
        k_ext[pl.ds(s, SUB, stride=SUB), :] = halo[1, :, lanes].astype(F32)
        v_ext[pl.ds(s, SUB, stride=SUB), :] = halo[2, :, lanes].astype(F32)
    taps1, taps2 = taps_of(filt, 1, taps), taps_of(filt, 2, taps)
    kw = [row(k_ext, SUB - margin + i) for i in range(margin)] + [row(k_head, i) for i in range(SUB)]
    vw = [row(v_ext, SUB - margin + i) for i in range(margin)] + [row(v_head, i) for i in range(SUB)]
    mixed = []
    for i in range(SUB):
        first, second = conv_at(kw, taps1, i), conv_at(vw, taps2, i)
        put(f1, i, first)
        put(f2, i, second)
        put(u, i, first * second)
        mixed.append(first * second)
    fade, rest = fades(lam, modes, 1), fades(lam, modes, steps - SUB)
    for m in range(modes):
        own = horner(fade[m], mixed)
        put(g, m, own)
        put(x_out, m, row(x_part, m) + rest[m] * own)


def query_kernel(taps, steps, query, halo, filt, q_ext, f0):
    margin = taps - 1
    for s in range(SUB):
        lanes = slice(s * LANES, (s + 1) * LANES)
        q_ext[pl.ds(s, SUB, stride=SUB), :] = halo[0, :, lanes].astype(F32)
    spread(query, q_ext, SUB, steps)
    taps0 = taps_of(filt, 0, taps)

    def conv(c, carry):
        t0 = c * SUB
        qw = [row(q_ext, t0 + SUB - margin + i) for i in range(SUB + margin)]
        for i in range(SUB):
            put(f0, t0 + i, conv_at(qw, taps0, i))
        return carry

    lax.fori_loop(0, steps // SUB, conv, 0)


def inputs_kernel(steps, residual, cot, res_pos, cot_pos):
    spread(residual, res_pos, 0, steps)
    spread(cot, cot_pos, 0, steps)


def near_taps(lam, res, skip, modes):
    fade, weight = fades(lam, modes, 1), [row(res, m) for m in range(modes)]
    result = []
    for k in range(SUB):
        result.append(total(weight) if k else total(weight) + skip[...])
        weight = [f * w for f, w in zip(fade, weight)]
    return result


def near_kernel(modes, steps, u, lam, res, skip, y):
    near = near_taps(lam, res, skip, modes)

    def some(c, carry):
        now = [row(u, c * SUB + i) for i in range(SUB)]
        for i in range(SUB):
            put(y, c * SUB + i, total([near[k] * now[i - k] for k in range(i + 1)]))
        return carry

    lax.fori_loop(0, steps // SUB, some, 0)


def lags_kernel(modes, steps, u, x_at, lam, lag, lag_sum):
    fade, skip = fades(lam, modes, 1), fades(lam, modes, SUB)

    def some(c, sums):
        now = [row(u, c * SUB + i) * float(SUB - i) for i in range(SUB)]
        new = []
        for m in range(modes):
            border = horner(fade[m], now) + float(SUB) * skip[m] * row(x_at, c * modes + m)
            put(lag, c * modes + m, border)
            new.append(skip[m] * sums[m] + border)
        return tuple(new)

    sums = lax.fori_loop(0, steps // SUB, some, zeros(modes))
    for m in range(modes):
        put(lag_sum, m, sums[m])


def summed_kernel(modes, steps, blocks, y, f0, res_pos, cot_pos, g, x_in, lam, res, gain, modal, summed, x_at, sums, squares, inner):
    block = pl.program_id(0)

    @pl.when(block == 0)
    def _():
        squares[...] = jnp.zeros_like(squares)
        inner[...] = jnp.zeros_like(inner)

    fade, skip = fades(lam, modes, 1), fades(lam, modes, SUB)
    factor = gain[...]

    def advance(c, x):
        w = [row(res, m) * x[m] for m in range(modes)]
        for m in range(modes):
            put(x_at, c * modes + m, x[m])
        for i in range(SUB):
            t = c * SUB + i
            w = [f * v for f, v in zip(fade, w)]
            long = row(y, t) + total(w)
            put(modal, t, long)
            now = row(res_pos, t) + row(f0, t) * long
            put(summed, t, now)
            put(squares, t, row(squares, t) + now * now)
            put(inner, t, row(inner, t) + factor * row(cot_pos, t) * now)
        return tuple(row(g, c * modes + m) + skip[m] * x[m] for m in range(modes))

    lax.fori_loop(0, steps // SUB, advance, tuple(row(x_in, m) for m in range(modes)))

    @pl.when(block == blocks - 1)
    def _():
        for which, scratch in enumerate((squares, inner)):
            for b in range(steps // LANES):
                part = total(
                    [
                        scratch[pl.ds(b * LANES * SUB + s, LANES, stride=SUB), :]
                        for s in range(SUB)
                    ]
                )
                sums[which : which + 1, b * LANES : (b + 1) * LANES] = jnp.sum(
                    part.T, axis=0, keepdims=True
                )


def grad_modal_kernel(modes, steps, width, shares, *refs):
    own_sums, (summed, cot_pos, f0, modal, lam, gain, ready) = refs[:shares], refs[shares : shares + 7]
    scale, gm, adj, a_out, border = refs[shares + 7 :]
    del ready

    @pl.when(pl.program_id(0) == 0)
    def _():
        sums = total([ref[...] for ref in own_sums])
        inv = lax.rsqrt(sums[0:1, :] / width + 1e-05)
        coef = inv * inv * inv * sums[1:2, :] / width
        for which, value in enumerate((inv, coef)):
            for b in range(steps // LANES):
                piece = value[:, b * LANES : (b + 1) * LANES]
                scale[pl.ds(which * steps + b * LANES, LANES), :] = jnp.broadcast_to(
                    piece, (LANES, LANES)
                ).T

    fade, skip = fades(lam, modes, 1), fades(lam, modes, SUB)
    factor = gain[...]

    def advance(c, a):
        block = steps // SUB - 1 - c
        now = [None] * SUB
        for i in reversed(range(SUB)):
            t = block * SUB + i
            inv = scale[pl.ds(t, 1), :]
            coef = scale[pl.ds(steps + t, 1), :]
            grad = inv * (factor * row(cot_pos, t)) - coef * row(summed, t)
            now[i] = grad * row(f0, t)
            put(gm, t, now[i])
        new = []
        for m in range(modes):
            own = fade[m] * horner(fade[m], now[::-1])
            put(adj, block * modes + m, own)
            new.append(own + skip[m] * a[m])
        return tuple(new)

    a = lax.fori_loop(0, steps // SUB, advance, zeros(modes))
    for m in range(modes):
        put(a_out, m, a[m])
        put(border, m, a[m])
    for t in range(SUB):
        inv = scale[pl.ds(t, 1), :]
        coef = scale[pl.ds(steps + t, 1), :]
        grad = inv * (factor * row(cot_pos, t)) - coef * row(summed, t)
        put(border, modes + t, grad * row(modal, t))


def own_adjoint_kernel(modes, steps, gm, u, adj, x_at, lag, lam, res, skip, gmy, res_sum, rate_sum, skip_sum):
    near = near_taps(lam, res, skip, modes)
    fade, far = fades(lam, modes, 1), fades(lam, modes, SUB)
    last = steps // SUB - 1

    def pairs(c, lags):
        now = [row(gm, c * SUB + i) for i in range(SUB)]
        for i in range(SUB):
            put(gmy, c * SUB + i, total([near[k] * now[i + k] for k in range(SUB - i)]))
        before = [row(u, c * SUB + i) for i in range(SUB)]
        return tuple(
            lags[k] + total([now[i] * before[i - k] for i in range(k, SUB)]) for k in range(SUB)
        )

    lags = lax.fori_loop(0, steps // SUB, pairs, zeros(SUB))
    skip_sum[...] = lags[0]
    half = modes // 2
    for part in range(2):
        ms = range(part * half, (part + 1) * half)

        def across(c, state, ms=ms):
            after, by_res, by_rate = (list(v) for v in state)
            block = last - c
            now = [row(gm, block * SUB + i) * float(i) for i in range(1, SUB)]
            for i, m in enumerate(ms):
                x, own = row(x_at, block * modes + m), row(adj, block * modes + m)
                tail = fade[m] * fade[m] * horner(fade[m], now[::-1])
                by_res[i] = by_res[i] + x * own
                by_rate[i] = by_rate[i] + (x * tail + after[i] * row(lag, block * modes + m))
                after[i] = own + far[m] * after[i]
            return tuple(after), tuple(by_res), tuple(by_rate)

        none = zeros(half)
        _, by_res, by_rate = lax.fori_loop(0, steps // SUB, across, (none, none, none))
        for i, m in enumerate(ms):
            put(res_sum, m, by_res[i] + horner(fade[m], lags[::-1]))
            weighted = [lags[k] * float(k) for k in range(1, SUB)]
            put(rate_sum, m, by_rate[i] + fade[m] * horner(fade[m], weighted[::-1]))


def norm_kernel(steps, scale, summed, cot_pos, gain, normed, grad_res, gain_out, work):
    factor = gain[...]

    def norm(c, acc):
        for i in range(SUB):
            t = c * SUB + i
            here = row(summed, t) * scale[pl.ds(t, 1), :]
            put(work, t, here * factor)
            acc = acc + row(cot_pos, t) * here
        return acc

    gain_out[...] = lax.fori_loop(0, steps // SUB, norm, zeros(1)[0])
    gather_rows(work, normed, steps)

    def grads(c, carry):
        for i in range(SUB):
            t = c * SUB + i
            inv = scale[pl.ds(t, 1), :]
            coef = scale[pl.ds(steps + t, 1), :]
            put(work, t, inv * (factor * row(cot_pos, t)) - coef * row(summed, t))
        return carry

    lax.fori_loop(0, steps // SUB, grads, 0)
    gather_rows(work, grad_res, steps)


def grad_query_kernel(modes, taps, steps, scale, summed, cot_pos, modal, q_ext, gf0_next, filt, gain, res_sum, skip_sum, gain_sum, grad_query, early, work, gf0):
    factor = gain[...]
    gf0[pl.ds(steps * SUB, SUB * SUB), :] = gf0_next[...]
    taps0 = taps_of(filt, 0, taps)

    def grads(c, carry):
        for i in range(SUB):
            t = c * SUB + i
            inv = scale[pl.ds(t, 1), :]
            coef = scale[pl.ds(steps + t, 1), :]
            grad = inv * (factor * row(cot_pos, t)) - coef * row(summed, t)
            put(gf0, t, grad * row(modal, t))
        return carry

    lax.fori_loop(0, steps // SUB, grads, 0)
    sums = filter_pass(taps, steps, gf0, q_ext)
    for j in range(taps):
        put(early, j, sums[j])
    early[pl.ds(taps * SUB, modes * SUB), :] = res_sum[...]
    put(early, taps + modes, skip_sum[...])
    put(early, taps + modes + 1, gain_sum[...])
    back_pass(taps, steps, gf0, taps0, work)
    gather_rows(work, grad_query, steps)


def filter_pass(taps, steps, grad, ext):
    margin = taps - 1

    def some(c, acc):
        t0 = c * SUB
        window = [row(ext, t0 + SUB - margin + i) for i in range(SUB + margin)]
        for i in range(SUB):
            now = row(grad, t0 + i)
            acc = tuple(acc[j] + now * window[margin + i - j] for j in range(taps))
        return acc

    zero = jnp.zeros((SUB, LANES), F32)
    return lax.fori_loop(0, steps // SUB, some, tuple(zero for _ in range(taps)))


def back_pass(taps, steps, grad, weights, out):
    margin = taps - 1

    def some(c, carry):
        t0 = c * SUB
        window = [row(grad, t0 + i) for i in range(SUB + margin)]
        for i in range(SUB):
            put(out, t0 + i, total([weights[j] * window[i + j] for j in range(taps)]))
        return carry

    lax.fori_loop(0, steps // SUB, some, 0)


def mixed_kernel(modes, taps, steps, gmy, f1, f2, k_ext, v_ext, adj, lam, res, alpha, gf1, gf2, heads, sums):
    fade, skip = fades(lam, modes, 1), fades(lam, modes, SUB)

    def advance(c, after):
        block = steps // SUB - 1 - c
        w = [row(res, m) * after[m] for m in range(modes)]
        for i in reversed(range(SUB)):
            t = block * SUB + i
            grad = row(gmy, t) + total(w)
            put(gf1, t, grad * row(f2, t))
            put(gf2, t, grad * row(f1, t))
            w = [f * v for f, v in zip(fade, w)]
        return tuple(row(adj, block * modes + m) + skip[m] * after[m] for m in range(modes))

    lax.fori_loop(0, steps // SUB, advance, tuple(row(alpha, m) for m in range(modes)))
    heads[0, 0] = gf1[: SUB * SUB, :]
    heads[1, 0] = gf2[: SUB * SUB, :]
    for which, (grad, ext) in enumerate(((gf1, k_ext), (gf2, v_ext))):
        parts = filter_pass(taps, steps, grad, ext)
        for j in range(taps):
            put(sums, which * taps + j, parts[j])


def back_kernel(taps, steps, gf1, gf2, next_head, filt, grad_key, grad_value, work, ext):
    for which, (grad, out) in enumerate(((gf1, grad_key), (gf2, grad_value))):
        ext[pl.ds(0, steps * SUB), :] = grad[...]
        ext[pl.ds(steps * SUB, SUB * SUB), :] = next_head[which, 0]
        back_pass(taps, steps, ext, taps_of(filt, which + 1, taps), work)
        gather_rows(work, out, steps)


def pack_kernel(modes, first_rows, half, early, res, rate_sum, lag_sum, alpha, kept, sent):
    odd = lax.axis_index("ctx") % 2
    rows = (first_rows + modes) * SUB
    for out, start in ((kept, odd * half), (sent, (1 - odd) * half)):
        for b in range(half):
            source = pl.multiple_of((start + b) * (first_rows * SUB), SUB)
            out[pl.ds(b * rows, first_rows * SUB), :] = early[pl.ds(source, first_rows * SUB), :]
            source = pl.multiple_of((start + b) * (modes * SUB), SUB)
            mine = pl.ds(source, modes * SUB)
            lagged = rate_sum[mine, :] + alpha[mine, :] * lag_sum[mine, :]
            out[pl.ds(b * rows + first_rows * SUB, modes * SUB), :] = -res[mine, :] * lagged


def finish_kernel(modes, taps, half, late, late_other, early, early_other, short, res, rate, skip, gain, work, work2):
    odd = lax.axis_index("ctx") % 2
    mine = jnp.where(odd == pl.program_id(0) // half, 1.0, 0.0)
    work[...] = late[...] + late_other[...]
    work2[...] = mine * early[...] + (1.0 - mine) * early_other[...]
    for s in range(SUB):
        lanes = slice(s * LANES, (s + 1) * LANES)
        short[0, :, lanes] = work2[pl.ds(s, taps, stride=SUB), :]
        short[1, :, lanes] = work[pl.ds(s, taps, stride=SUB), :]
        short[2, :, lanes] = work[pl.ds(taps * SUB + s, taps, stride=SUB), :]
        res[:, lanes] = work2[pl.ds(taps * SUB + s, modes, stride=SUB), :]
        rate[:, lanes] = work2[pl.ds((taps + modes + 2) * SUB + s, modes, stride=SUB), :]
    skip[...] = row(work2, taps + modes)
    gain[...] = row(work2, taps + modes + 1)


def shift(value, axis, distance):
    devices = range(lax.axis_size(axis))
    route = [(i - distance, i) for i in devices if i - distance in devices]
    return lax.ppermute(value, axis, route)


def carried_in(own, first, lam, span, axis, sign, under):
    count, reach = lax.axis_size(axis), 1
    under = list(under) + [None] * count
    before, upto = None, own
    while reach < count:
        other = first if reach == 1 else shift(upto, axis, sign * reach)
        wait = under.pop(0)
        if wait is not None:
            other = other + wait
        before = other if before is None else before + jnp.exp(lam * -float(span * (reach - 1))) * other
        upto = upto + jnp.exp(lam * -float(span * reach)) * other
        reach *= 2
    return before


def others_of(value, axis):
    count = lax.axis_size(axis)
    return [
        lax.ppermute(value, axis, [(i, (i + k) % count) for i in range(count)])
        for k in range(1, count)
    ]


def swap(value, axis, step):
    return lax.ppermute(value, axis, [(i, i ^ step) for i in range(lax.axis_size(axis))])


def sum_but_last(value, axis, first, under=None):
    count, step = lax.axis_size(axis), first
    while True:
        other = swap(value, axis, step)
        step *= 2
        if step >= count:
            return value, other
        value = value + other if under is None else value + other + under
        under = None


def shards(
    residual, query_in, key_in, value_in, short_filter, residues, decay_rate, skip_gain, norm_gain, cotangent
):
    steps, channels = residual.shape
    modes, taps = residues.shape[0], short_filter.shape[1]
    blocks = channels // WIDE
    width = channels * lax.axis_size("tp")
    skip, gain = (v.reshape(blocks * SUB, LANES) for v in (skip_gain, norm_gain))

    def pos(count):
        return jax.ShapeDtypeStruct((blocks * count * SUB, LANES), F32)

    def kept(count):
        return pltpu.VMEM((blocks * count * SUB, LANES), F32)

    def pos_spec(count):
        return pl.BlockSpec((count * SUB, LANES), lambda h: (h, 0))

    def head_spec(total_steps, start):
        return pl.BlockSpec((SUB * SUB, LANES), lambda h: (h * (total_steps // SUB) + start, 0))

    wide_spec = pl.BlockSpec((steps, WIDE), lambda h: (0, h))
    wide = jax.ShapeDtypeStruct((steps, channels), BF16)
    mode_spec, one_spec, filt_spec = pos_spec(modes), pos_spec(1), pos_spec(3 * taps)
    seq_spec, ext_spec = pos_spec(steps), pos_spec(steps + SUB)
    seq, ext, mode, one = kept(steps), kept(steps + SUB), pos(modes), pos(1)
    eights, eights_spec = kept(steps // SUB * modes), pos_spec(steps // SUB * modes)
    halo_spec = pl.BlockSpec((3, SUB, WIDE), lambda h: (0, 0, h))
    param_spec = pl.BlockSpec((modes, WIDE), lambda h: (0, h))
    short_spec = pl.BlockSpec((3, taps, WIDE), lambda h: (0, 0, h))

    def call(body, ins, in_specs, outs, out_specs, ops, name, scratch=(), aliases=None, done_rows=None):
        elements, n_refs = steps * channels, len(ins) + len(outs)

        def with_done(*refs):
            done = refs[n_refs]
            done[...] = jnp.zeros_like(done)
            body(*refs[:n_refs], *refs[n_refs + 1 :])

        near = blocks * steps * SUB
        ins = [
            pltpu.with_memory_space_constraint(v, pltpu.VMEM) if v.shape[0] >= near and v.dtype == F32 else v
            for v in ins
        ]
        done_shape = (blocks * (done_rows or modes) * SUB, LANES)
        outs = [*outs, jax.ShapeDtypeStruct(done_shape, F32)]
        out_specs = [*out_specs, pl.BlockSpec(done_shape, lambda h: (0, 0))]
        return pl.pallas_call(
            with_done,
            grid=(blocks,),
            in_specs=in_specs,
            out_specs=out_specs,
            out_shape=outs,
            scratch_shapes=list(scratch),
            input_output_aliases=aliases or {},
            compiler_params=pltpu.CompilerParams(
                dimension_semantics=("arbitrary",), vmem_limit_bytes=VMEM_LIMIT
            ),
            cost_estimate=pl.CostEstimate(
                flops=ops * elements, bytes_accessed=4 * elements, transcendentals=0
            ),
            name=name,
        )(*ins)

    far = [
        pltpu.with_memory_space_constraint(v, pltpu.HBM)
        for v in (residual, query_in, key_in, value_in, cotangent, short_filter, decay_rate, residues)
    ]
    last_spec = pl.BlockSpec((2 * SUB, channels), lambda h: (steps // (2 * SUB) - 1, 0))
    trailing = pl.pallas_call(
        trailing_kernel,
        grid=(1,),
        in_specs=[last_spec] * 3,
        out_specs=pl.BlockSpec((3, SUB, channels), lambda h: (0, 0, 0)),
        out_shape=jax.ShapeDtypeStruct((3, SUB, channels), BF16),
        compiler_params=pltpu.CompilerParams(vmem_limit_bytes=VMEM_LIMIT),
        cost_estimate=pl.CostEstimate(flops=channels, bytes_accessed=channels, transcendentals=0),
        name="trailing",
    )(*far[1:4])
    halo = shift(trailing, "ctx", 1)

    k_ext, v_ext, f1, f2, u, g, lam, res, filt, x_part, _ = call(
        functools.partial(features_kernel, modes, taps, steps),
        (far[2], far[3], *far[5:]),
        [wide_spec, wide_spec, short_spec, param_spec, param_spec],
        [ext, ext, seq, seq, seq, eights, mode, mode, pos(3 * taps), mode],
        [ext_spec, ext_spec, seq_spec, seq_spec, seq_spec, eights_spec, mode_spec, mode_spec, filt_spec, mode_spec],
        64,
        "features",
    )
    any_spec = pl.BlockSpec(memory_space=pl.ANY)
    k_ext, v_ext, f1, f2, u, g, x_own, _ = call(
        functools.partial(head_kernel, modes, taps, steps),
        (halo, k_ext, v_ext, filt, lam, x_part, f1, f2, u, g),
        [halo_spec, head_spec(steps + SUB, 1), head_spec(steps + SUB, 1), filt_spec, mode_spec, mode_spec]
        + [any_spec] * 4,
        [ext, ext, seq, seq, seq, eights, mode],
        [head_spec(steps + SUB, 0)] * 2
        + [head_spec(steps, 0)] * 3
        + [pl.BlockSpec((modes * SUB, LANES), lambda h: (h * (steps // SUB), 0)), mode_spec],
        2,
        "head",
        aliases={1: 0, 2: 1, 6: 2, 7: 3, 8: 4, 9: 5},
    )
    q_ext, f0, query_done = call(
        functools.partial(query_kernel, taps, steps),
        (far[1], halo, filt),
        [wide_spec, halo_spec, filt_spec],
        [ext, seq],
        [ext_spec, seq_spec],
        20,
        "query",
    )
    res_pos, cot_pos, inputs_done = call(
        functools.partial(inputs_kernel, steps),
        (far[0], far[4]),
        [wide_spec] * 2,
        [seq, seq],
        [seq_spec] * 2,
        10,
        "inputs",
    )
    y, near_done = call(
        functools.partial(near_kernel, modes, steps),
        (u, lam, res, skip),
        [seq_spec, mode_spec, mode_spec, one_spec],
        [seq],
        [seq_spec],
        10,
        "near",
    )
    x_in = carried_in(x_own, shift(x_own, "ctx", 1), lam, steps, "ctx", 1, [query_done, inputs_done, near_done])
    modal, summed, x_at, sums, _ = call(
        functools.partial(summed_kernel, modes, steps, blocks),
        (y, f0, res_pos, cot_pos, g, x_in, lam, res, gain),
        [seq_spec] * 4 + [eights_spec] + [mode_spec] * 3 + [one_spec],
        [seq, seq, eights, jax.ShapeDtypeStruct((2, steps), F32)],
        [seq_spec, seq_spec, eights_spec, pl.BlockSpec((2, steps), lambda h: (0, 0))],
        50,
        "summed",
        scratch=[pltpu.VMEM((steps * SUB, LANES), F32)] * 2,
    )
    all_sums = [sums, *others_of(sums, "tp")]
    lag, lag_sum, lags_done = call(
        functools.partial(lags_kernel, modes, steps),
        (u, x_at, lam),
        [seq_spec, eights_spec, mode_spec],
        [eights, mode],
        [eights_spec, mode_spec],
        32,
        "lags",
    )
    scale_spec = pl.BlockSpec((2 * steps, LANES), lambda h: (0, 0))
    scale, gm, adj, a_own, border, _ = call(
        functools.partial(grad_modal_kernel, modes, steps, width, len(all_sums)),
        (*all_sums, summed, cot_pos, f0, modal, lam, gain, lags_done),
        [pl.BlockSpec((2, steps), lambda h: (0, 0))] * len(all_sums)
        + [seq_spec, seq_spec, seq_spec, head_spec(steps, 0), mode_spec, one_spec, any_spec],
        [pltpu.VMEM((2 * steps, LANES), F32), seq, eights, mode, pos(modes + SUB)],
        [scale_spec, seq_spec, eights_spec, mode_spec, pos_spec(modes + SUB)],
        45,
        "grad_modal",
    )
    border = shift(border, "ctx", -1)
    normed, grad_residual, gain_sum, norm_done = call(
        functools.partial(norm_kernel, steps),
        (scale, summed, cot_pos, gain),
        [scale_spec, seq_spec, seq_spec, one_spec],
        [wide, wide, one],
        [wide_spec, wide_spec, one_spec],
        25,
        "norm",
        scratch=[pltpu.VMEM((steps * SUB, LANES), F32)],
    )
    gmy, res_sum, rate_sum, skip_sum, adjoint_done = call(
        functools.partial(own_adjoint_kernel, modes, steps),
        (gm, u, adj, x_at, lag, lam, res, skip),
        [seq_spec, seq_spec, eights_spec, eights_spec, eights_spec, mode_spec, mode_spec, one_spec],
        [seq, mode, mode, one],
        [seq_spec, mode_spec, mode_spec, one_spec],
        75,
        "own_adjoint",
    )
    early_rows = taps + modes + 2
    grad_query, early, query_back_done = call(
        functools.partial(grad_query_kernel, modes, taps, steps),
        (scale, summed, cot_pos, modal, q_ext, border, filt, gain, res_sum, skip_sum, gain_sum),
        [scale_spec, seq_spec, seq_spec, seq_spec, ext_spec, head_spec(modes + SUB, modes // SUB), filt_spec, one_spec, mode_spec, one_spec, one_spec],
        [wide, pos(early_rows)],
        [wide_spec, pos_spec(early_rows)],
        45,
        "grad_query",
        scratch=[
            pltpu.VMEM((steps * SUB, LANES), F32),
            pltpu.VMEM(((steps + SUB) * SUB, LANES), F32),
        ],
    )
    border_rows = modes + SUB
    alpha_first = border.reshape(blocks, border_rows * SUB, LANES)[:, : modes * SUB]
    alpha = carried_in(a_own, alpha_first.reshape(a_own.shape), lam, steps, "ctx", -1, [norm_done, adjoint_done, query_back_done])

    half = blocks // 2
    whole_spec = pl.BlockSpec(memory_space=pltpu.VMEM)
    half_shape = jax.ShapeDtypeStruct((half * (early_rows + modes) * SUB, LANES), F32)
    kept_half, sent_half = pl.pallas_call(
        functools.partial(pack_kernel, modes, early_rows, half),
        in_specs=[whole_spec] * 5,
        out_specs=[whole_spec] * 2,
        out_shape=[half_shape] * 2,
        compiler_params=pltpu.CompilerParams(vmem_limit_bytes=VMEM_LIMIT),
        cost_estimate=pl.CostEstimate(flops=half_shape.size, bytes_accessed=0, transcendentals=0),
        name="pack",
    )(early, res, rate_sum, lag_sum, alpha)
    early_rows += modes
    early = kept_half + swap(sent_half, "ctx", 1)
    late_rows = 2 * taps
    next_spec = pl.BlockSpec((2, 1, SUB * SUB, LANES), lambda h: (0, h, 0, 0))
    gf1, gf2, heads, late, _ = call(
        functools.partial(mixed_kernel, modes, taps, steps),
        (gmy, f1, f2, k_ext, v_ext, adj, lam, res, alpha),
        [seq_spec] * 3 + [ext_spec] * 2 + [eights_spec] + [mode_spec] * 3,
        [seq, seq, jax.ShapeDtypeStruct((2, blocks, SUB * SUB, LANES), F32), pos(late_rows)],
        [seq_spec, seq_spec, next_spec, pos_spec(late_rows)],
        75,
        "mixed",
    )
    next_head = shift(heads, "ctx", -1)
    grad_key, grad_value, back_done = call(
        functools.partial(back_kernel, taps, steps),
        (gf1, gf2, next_head, filt),
        [seq_spec, seq_spec, next_spec, filt_spec],
        [wide, wide],
        [wide_spec, wide_spec],
        28,
        "back",
        scratch=[
            pltpu.VMEM((steps * SUB, LANES), F32),
            pltpu.VMEM(((steps + SUB) * SUB, LANES), F32),
        ],
        done_rows=late_rows,
    )
    if lax.axis_size("ctx") > 2:
        one_part, other_part = sum_but_last(early, "ctx", 2)
        early = one_part + other_part
    early_other = swap(early, "ctx", 1)
    late, late_other = sum_but_last(late, "ctx", 1, back_done)
    late_spec = pos_spec(late_rows)
    half_spec = pl.BlockSpec((early_rows * SUB, LANES), lambda h: (h % half, 0))
    grad_short, grad_residues, grad_rate, grad_skip, grad_gain, _ = call(
        functools.partial(finish_kernel, modes, taps, half),
        (late, late_other, early, early_other),
        [late_spec, late_spec, half_spec, half_spec],
        [
            jax.ShapeDtypeStruct(short_filter.shape, F32),
            jax.ShapeDtypeStruct(residues.shape, F32),
            jax.ShapeDtypeStruct(residues.shape, F32),
            one,
            one,
        ],
        [short_spec, param_spec, param_spec, one_spec, one_spec],
        1,
        "finish",
        scratch=[
            pltpu.VMEM((late_rows * SUB, LANES), F32),
            pltpu.VMEM((early_rows * SUB, LANES), F32),
        ],
    )
    return (
        normed,
        grad_residual,
        grad_query,
        grad_key,
        grad_value,
        grad_short,
        grad_residues,
        grad_rate,
        grad_skip.reshape(channels),
        grad_gain.reshape(channels),
    )


def solution(mesh):
    both, modes, vector = P("ctx", "tp"), P(None, "tp"), P("tp")
    return jax.shard_map(
        shards,
        mesh=mesh,
        in_specs=(both, both, both, both, P(None, None, "tp"), modes, modes, vector, vector, both),
        out_specs=(both,) * 5 + (P(None, None, "tp"), modes, modes, vector, vector),
        check_vma=False,
    )
```

time: 162 us -> 127 us (0.78)
  local copies, waits for them, and re-layouts: 18.3 us -> 0.02 us
  waiting for transfers between devices: 44.1 us -> 30.7 us
  starting transfers between devices: 29.7 us -> 35.8 us
  blocking collectives: 5.63 us -> 0 us
  other arithmetic: 3.68 us -> 0.4 us
    unnamed x44 -> x4, local copies, waits for them, and re-layouts: 14.2 us -> 0.01 us
    ppermute x11 -> x8, waiting for transfers between devices: 23.4 us -> 14.9 us  [shift(): return lax.ppermute(value, axis, route)]
    ppermute x6 -> x10, starting transfers between devices: 5.23 us -> 12 us  [the longest x7 10.3 us: swap(): lax.ppermute(value, axis, [(i, i ^ step) for i in range(lax.axis_size(axi...]
    psum x1 -> x0, blocking collectives: 5.63 us -> none  [shards(): sums = lax.psum(sums, 'tp')]
    ppermute x6 -> x10, waiting for transfers between devices: 20.7 us -> 15.8 us  [the longest x7 15.8 us: swap(): lax.ppermute(value, axis, [(i, i ^ step) for i in range(lax.axis_size(axi...]
    add x11, other arithmetic: 3.64 us -> 0.4 us  [the longest x4 0.16 us: carried_in(): upto = upto + jnp.exp(lam * -float(span * reach)) * other]
    slice x5 -> x1, local copies, waits for them, and re-layouts: 2.56 us -> 0.01 us  [shards(): border.reshape(blocks, border_rows * SUB, LANES)[:, :modes * SUB]]
    pallas_call x11 -> x14, Pallas kernels: 59.4 us -> 57.4 us  [call(): pl.pallas_call(with_done, grid=(blocks,), in_specs=in_specs, out_specs=ou...]
  transfers between devices with their start and end apart: 17 -> 18, of which waited for: 7 -> 8; matrix products, arithmetic and copies ran while one was open for 2% -> 0% of each run, Pallas kernels for 27% -> 36%
where the time goes in v3:
time: 127 us; the launch traced here: 126 us
  Pallas kernels  58.3 us (46%)
  starting transfers between devices  35.8 us (28%)
  waiting for transfers between devices  30.7 us (24%)
    pallas_call x14, Pallas kernels, call(): pl.pallas_call(with_done, grid=(blocks,), in_specs=in_specs, out_specs=ou...  57.4 us
    ppermute x8, starting transfers between devices, shift(): return lax.ppermute(value, axis, route)  23.7 us
    ppermute x7, waiting for transfers between devices, swap(): lax.ppermute(value, axis, [(i, i ^ step) for i in range(lax.axis_size(axi...  15.8 us
    ppermute x8, waiting for transfers between devices, shift(): return lax.ppermute(value, axis, route)  14.9 us
    ppermute x7, starting transfers between devices, swap(): lax.ppermute(value, axis, [(i, i ^ step) for i in range(lax.axis_size(axi...  10.3 us
  transfers between devices with their start and end apart: 18, of which 8 were waited for; matrix products, arithmetic and copies ran while one was open for 0% of the time, Pallas kernels for 36%

profile of v3, /device:TPU:0, one launch (start us, length us, event | category | flops | bytes accessed | tf_op | source)
XLA Modules:
  0.0 126.1 jit_solution(17652815605333007600)
XLA Ops:
  1.6 4.8 %collective-permute-start = (bf16[3,8,2048]{2,1,0:T(8,128)(2,1)S(1)}, bf16[3,8,2048]{2,1,0:T(8,128)(2,1)S(1)}, u32[]{:S(2)}, u32[]{:S(2)}) collective-permute-start(bf16[3,8,2048]{2,1,0:T(8,128)(2,1)S(1)} %trailing.1), channel_id=1, source_target_pairs={{0,4},{4,8},{8,12},{12,16},{16,20},{20,24},{24,28},{1,5},{5,9},{9,... | collective-permute-start | bytes 294920 | tf_op jit(solution)/shard_map/ppermute | solution.py:491
  6.4 8.0 %features.1 = (f32[4224,128]{1,0:T(8,128)S(1)}, f32[4224,128]{1,0:T(8,128)S(1)}, f32[4096,128]{1,0:T(8,128)S(1)}, f32[4096,128]{1,0:T(8,128)S(1)}, f32[4096,128]...) custom-call(bf16[256,2048]{1,0:T(8,128)(2,1)} %refs_0_.3, ...), custom_call_target="tpu_custom_call" | custom-call | flops 33554432 | bytes 2097152 | tf_op jit(solution)/shard_map/features/pallas_call | solution.py:579
  15.2 3.4 %collective-permute-start.1 = (f32[256,128]{1,0:T(8,128)S(1)}, f32[256,128]{1,0:T(8,128)S(1)}, u32[]{:S(2)}, u32[]{:S(2)}) collective-permute-start(f32[256,128]{1,0:T(8,128)S(1)} %get-tuple-element.89), channel_id=1, source_target_pairs={{0,4},{4,8},{8,12},{12,16},{16,20},{20,24},{24,28},{1,5},{5,9},{9,... | collective-permute-start | bytes 393224 | tf_op jit(solution)/shard_map/ppermute | solution.py:491
  18.7 2.8 %query.3 = (f32[4224,128]{1,0:T(8,128)S(1)}, f32[4096,128]{1,0:T(8,128)S(1)}, f32[256,128]{1,0:T(8,128)S(1)}) custom-call(bf16[256,2048]{1,0:T(8,128)(2,1)} %refs_0_.4, bf16[3,8,2048]{2,1,0:T(8,128)(2,1)S(1)} %collective-permute-done.refs_0_.refs_1_, f32[336,128]{1,0:T(8,128)S(1)} %get-tuple-element.75.refs_3_.refs_2_.refs_6_), custom_call_target="tpu_custom_call" | custom-call | flops 10485760 | bytes 2097152 | tf_op jit(solution)/shard_map/query/pallas_call | solution.py:579
  21.5 4.9 %collective-permute-start.2 = (f32[256,128]{1,0:T(8,128)S(1)}, f32[256,128]{1,0:T(8,128)S(1)}, u32[]{:S(2)}, u32[]{:S(2)}) collective-permute-start(f32[256,128]{1,0:T(8,128)S(1)} %get-tuple-element.136), channel_id=1, source_target_pairs={{0,8},{4,12},{8,16},{12,20},{16,24},{20,28},{1,9},{5,13},{9,17},{1... | collective-permute-start | bytes 393224 | tf_op jit(solution)/shard_map/ppermute | solution.py:491
  26.5 2.3 %inputs.1 = (f32[4096,128]{1,0:T(8,128)S(1)}, f32[4096,128]{1,0:T(8,128)S(1)}, f32[256,128]{1,0:T(8,128)S(1)}) custom-call(bf16[256,2048]{1,0:T(8,128)(2,1)} %refs_0_.5, bf16[256,2048]{1,0:T(8,128)(2,1)} %refs_1_.3), custom_call_target="tpu_custom_call" | custom-call | flops 5242880 | bytes 2097152 | tf_op jit(solution)/shard_map/inputs/pallas_call | solution.py:579
  29.0 5.4 %collective-permute-start.3 = (f32[256,128]{1,0:T(8,128)S(1)}, f32[256,128]{1,0:T(8,128)S(1)}, u32[]{:S(2)}, u32[]{:S(2)}) collective-permute-start(f32[256,128]{1,0:T(8,128)S(1)} %multiply_add_fusion.4), channel_id=1, source_target_pairs={{0,16},{4,20},{8,24},{12,28},{1,17},{5,21},{9,25},{13,29},{2,18},{... | collective-permute-start | bytes 393224 | tf_op jit(solution)/shard_map/ppermute | solution.py:491
  34.4 1.0 near.1
  35.4 1.5 %collective-permute-done.3 = f32[256,128]{1,0:T(8,128)S(1)} collective-permute-done((f32[256,128]{1,0:T(8,128)S(1)}, f32[256,128]{1,0:T(8,128)S(1)}, u32[]{:S(2)}, u32[]{:S(2)}) %collective-permute-start.3) | collective-permute-done | bytes 131104 | tf_op jit(solution)/shard_map/ppermute | solution.py:491
  37.0 5.3 %summed.1 = (f32[4096,128]{1,0:T(8,128)S(1)}, f32[4096,128]{1,0:T(8,128)S(1)}, f32[8192,128]{1,0:T(8,128)S(1)}, f32[2,256]{1,0:T(2,128)S(1)}, f32[256,128]{1,0:T(8,128)}) custom-call(f32[4096,128]{1,0:T(8,128)S(1)} %get-tuple-element.84.refs_0_, f32[4096,128]{1,0:T(8,128)S(1)} %get-tuple-element.85.refs_1_.refs_6_, ...), custom_call_target="tpu_custom_call" | custom-call | flops 26214400 | bytes 2097152 | tf_op jit(solution)/shard_map/summed/pallas_call | solution.py:579
  42.3 1.5 %collective-permute-start.5 = (f32[2,256]{1,0:T(2,128)S(1)}, f32[2,256]{1,0:T(2,128)S(1)}, u32[]{:S(2)}, u32[]{:S(2)}) collective-permute-start(f32[2,256]{1,0:T(2,128)S(1)} %get-tuple-element.93.refs_0_), channel_id=1, source_target_pairs={{0,2},{1,3},{2,0},{3,1},{4,6},{5,7},{6,4},{7,5},{8,10},{9,11},{10,... | collective-permute-start | bytes 6152 | tf_op jit(solution)/shard_map/ppermute | solution.py:512
  44.0 4.3 %lags.1 = (f32[8192,128]{1,0:T(8,128)S(1)}, f32[256,128]{1,0:T(8,128)S(1)}, f32[256,128]{1,0:T(8,128)S(1)}) custom-call(f32[4096,128]{1,0:T(8,128)S(1)} %get-tuple-element.82.refs_0_.refs_1_, f32[8192,128]{1,0:T(8,128)S(1)} %get-tuple-element.96.refs_1_.refs_3_, f32[256,128]{1,0:T(8,128)S(1)} %get-tuple-element.76.refs_4_.refs_1_.refs_6_.refs_2_.refs_8_.refs_5_), custom_call_target="tpu_custom_call" | custom-call | flops 16777216 | bytes 2097152 | tf_op jit(solution)/shard_map/lags/pallas_call | solution.py:579
  48.4 4.5 %grad_modal.1 = (f32[512,128]{1,0:T(8,128)S(1)}, f32[4096,128]{1,0:T(8,128)S(1)}, f32[8192,128]{1,0:T(8,128)S(1)}, f32[256,128]{1,0:T(8,128)S(1)}, f32[384,128]{1,0:T(8,128)S(1)}, /*index=5*/f32[256,128]{1,0:T(8,128)}) custom-call(f32[2,256]{1,0:T(2,128)S(1)} %get-tuple-element.93.refs_0_, f32[2,256]{1,0:T(2,128)S(1)} %collective-permute-done.4.refs_1_, ...), custom_call_target="tpu_custom_call" | custom-call | flops 23592960 | bytes 2097152 | tf_op jit(solution)/shard_map/grad_modal/pallas_call | solution.py:579
  52.9 1.3 %collective-permute-start.7 = (f32[384,128]{1,0:T(8,128)S(1)}, f32[384,128]{1,0:T(8,128)S(1)}, u32[]{:S(2)}, u32[]{:S(2)}) collective-permute-start(f32[384,128]{1,0:T(8,128)S(1)} %get-tuple-element.102), channel_id=1, source_target_pairs={{4,0},{8,4},{12,8},{16,12},{20,16},{24,20},{28,24},{5,1},{9,5},{13... | collective-permute-start | bytes 589832 | tf_op jit(solution)/shard_map/ppermute | solution.py:491
  54.2 3.6 %norm.1 = (bf16[256,2048]{1,0:T(8,128)(2,1)}, bf16[256,2048]{1,0:T(8,128)(2,1)}, f32[16,128]{1,0:T(8,128)S(1)}, f32[256,128]{1,0:T(8,128)S(1)}) custom-call(f32[512,128]{1,0:T(8,128)S(1)} %get-tuple-element.98.refs_0_, f32[4096,128]{1,0:T(8,128)S(1)} %get-tuple-element.94.refs_4_.refs_1_, f32[4096,128]{1,0:T(8,128)S(1)} %get-tuple-element.87.refs_3_.refs_5_.refs_2_, ...), custom_call_target="tpu_custom_call" | custom-call | flops 13107200 | bytes 2097152 | tf_op jit(solution)/shard_map/norm/pallas_call | solution.py:579
  57.7 4.2 %collective-permute-done.7.refs_5_ = f32[384,128]{1,0:T(8,128)S(1)} collective-permute-done((f32[384,128]{1,0:T(8,128)S(1)}, f32[384,128]{1,0:T(8,128)S(1)}, u32[]{:S(2)}, u32[]{:S(2)}) %collective-permute-start.7) | collective-permute-done | bytes 196640 | tf_op jit(solution)/shard_map/ppermute | solution.py:491
  62.0 1.3 %collective-permute-start.8 = (f32[256,128]{1,0:T(8,128)S(1)}, f32[256,128]{1,0:T(8,128)S(1)}, u32[]{:S(2)}, u32[]{:S(2)}) collective-permute-start(f32[256,128]{1,0:T(8,128)S(1)} %multiply_add_fusion.2), channel_id=1, source_target_pairs={{8,0},{12,4},{16,8},{20,12},{24,16},{28,20},{9,1},{13,5},{17,9},{2... | collective-permute-start | bytes 393224 | tf_op jit(solution)/shard_map/ppermute | solution.py:491
  63.3 7.5 %own_adjoint.1 = (f32[4096,128]{1,0:T(8,128)S(1)}, f32[256,128]{1,0:T(8,128)S(1)}, f32[256,128]{1,0:T(8,128)S(1)}, f32[16,128]{1,0:T(8,128)S(1)}, f32[256,128]{1,0:T(8,128)S(1)}) custom-call(f32[4096,128]{1,0:T(8,128)S(1)} %get-tuple-element.103.refs_0_, f32[4096,128]{1,0:T(8,128)S(1)} %get-tuple-element.82.refs_0_.refs_1_, ...), custom_call_target="tpu_custom_call" | custom-call | flops 39321600 | bytes 2097152 | tf_op jit(solution)/shard_map/own_adjoint/pallas_call | solution.py:579
  70.9 1.3 %collective-permute-start.9 = (f32[256,128]{1,0:T(8,128)S(1)}, f32[256,128]{1,0:T(8,128)S(1)}, u32[]{:S(2)}, u32[]{:S(2)}) collective-permute-start(f32[256,128]{1,0:T(8,128)S(1)} %multiply_add_fusion.1), channel_id=1, source_target_pairs={{16,0},{20,4},{24,8},{28,12},{17,1},{21,5},{25,9},{29,13},{18,2},{... | collective-permute-start | bytes 393224 | tf_op jit(solution)/shard_map/ppermute | solution.py:491
  72.2 4.8 %grad_query.1 = (bf16[256,2048]{1,0:T(8,128)(2,1)}, f32[400,128]{1,0:T(8,128)S(1)}, f32[256,128]{1,0:T(8,128)S(1)}) custom-call(f32[512,128]{1,0:T(8,128)S(1)} %get-tuple-element.98.refs_0_, f32[4096,128]{1,0:T(8,128)S(1)} %get-tuple-element.94.refs_4_.refs_1_, f32[4096,128]{1,0:T(8,128)S(1)} %get-tuple-element.87.refs_3_.refs_5_.refs_2_, ...), custom_call_target="tpu_custom_call" | custom-call | flops 23592960 | bytes 2097152 | tf_op jit(solution)/shard_map/grad_query/pallas_call | solution.py:579
  77.0 5.8 %collective-permute-done.9 = f32[256,128]{1,0:T(8,128)S(1)} collective-permute-done((f32[256,128]{1,0:T(8,128)S(1)}, f32[256,128]{1,0:T(8,128)S(1)}, u32[]{:S(2)}, u32[]{:S(2)}) %collective-permute-start.9) | collective-permute-done | bytes 131104 | tf_op jit(solution)/shard_map/ppermute | solution.py:491
  83.0 2.3 %collective-permute-start.14 = (f32[328,128]{1,0:T(8,128)S(1)}, f32[328,128]{1,0:T(8,128)S(1)}, u32[]{:S(2)}, u32[]{:S(2)}) collective-permute-start(f32[328,128]{1,0:T(8,128)S(1)} %get-tuple-element.130), channel_id=1, source_target_pairs={{0,4},{4,0},{8,12},{12,8},{16,20},{20,16},{24,28},{28,24},{1,5},{5... | collective-permute-start | bytes 503816 | tf_op jit(solution)/shard_map/ppermute | solution.py:518
  85.3 3.7 %collective-permute-done.14 = f32[328,128]{1,0:T(8,128)S(1)} collective-permute-done((f32[328,128]{1,0:T(8,128)S(1)}, f32[328,128]{1,0:T(8,128)S(1)}, u32[]{:S(2)}, u32[]{:S(2)}) %collective-permute-start.14) | collective-permute-done | bytes 167968 | tf_op jit(solution)/shard_map/ppermute | solution.py:518
  89.1 6.7 %mixed.1 = (f32[4096,128]{1,0:T(8,128)S(1)}, f32[4096,128]{1,0:T(8,128)S(1)}, f32[2,2,64,128]{3,2,1,0:T(8,128)S(1)}, f32[224,128]{1,0:T(8,128)S(1)}, f32[256,128]{1,0:T(8,128)}) custom-call(f32[4096,128]{1,0:T(8,128)S(1)} %get-tuple-element.110.refs_0_, f32[4096,128]{1,0:T(8,128)S(1)} %get-tuple-element.111.refs_1_, ...), custom_call_target="tpu_custom_call" | custom-call | flops 39321600 | bytes 2097152 | tf_op jit(solution)/shard_map/mixed/pallas_call | solution.py:579
  95.8 1.3 %collective-permute-start.10 = (f32[2,2,64,128]{3,2,1,0:T(8,128)S(1)}, f32[2,2,64,128]{3,2,1,0:T(8,128)S(1)}, u32[]{:S(2)}, u32[]{:S(2)}) collective-permute-start(f32[2,2,64,128]{3,2,1,0:T(8,128)S(1)} %get-tuple-element.121), channel_id=1, source_target_pairs={{4,0},{8,4},{12,8},{16,12},{20,16},{24,20},{28,24},{5,1},{9,5},{13... | collective-permute-start | bytes 393224 | tf_op jit(solution)/shard_map/ppermute | solution.py:491
  97.0 2.7 %collective-permute-start.11 = (f32[224,128]{1,0:T(8,128)S(1)}, f32[224,128]{1,0:T(8,128)S(1)}, u32[]{:S(2)}, u32[]{:S(2)}) collective-permute-start(f32[224,128]{1,0:T(8,128)S(1)} %get-tuple-element.124), channel_id=1, source_target_pairs={{0,4},{4,0},{8,12},{12,8},{16,20},{20,16},{24,28},{28,24},{1,5},{5... | collective-permute-start | bytes 344072 | tf_op jit(solution)/shard_map/ppermute | solution.py:518
  99.8 3.2 %collective-permute-done.10.refs_2_ = f32[2,2,64,128]{3,2,1,0:T(8,128)S(1)} collective-permute-done((f32[2,2,64,128]{3,2,1,0:T(8,128)S(1)}, f32[2,2,64,128]{3,2,1,0:T(8,128)S(1)}, u32[]{:S(2)}, u32[]{:S(2)}) %collective-permute-start.10) | collective-permute-done | bytes 131104 | tf_op jit(solution)/shard_map/ppermute | solution.py:491
  102.9 4.9 %back.1 = (bf16[256,2048]{1,0:T(8,128)(2,1)}, bf16[256,2048]{1,0:T(8,128)(2,1)}, f32[224,128]{1,0:T(8,128)S(1)}) custom-call(f32[4096,128]{1,0:T(8,128)S(1)} %get-tuple-element.119.refs_0_, f32[4096,128]{1,0:T(8,128)S(1)} %get-tuple-element.120.refs_1_, f32[2,2,64,128]{3,2,1,0:T(8,128)S(1)} %collective-permute-done.10.refs_2_, ...), custom_call_target="tpu_custom_call" | custom-call | flops 14680064 | bytes 2097152 | tf_op jit(solution)/shard_map/back/pallas_call | solution.py:579
  107.9 2.0 %collective-permute-start.16 = (f32[328,128]{1,0:T(8,128)S(1)}, f32[328,128]{1,0:T(8,128)S(1)}, u32[]{:S(2)}, u32[]{:S(2)}) collective-permute-start(f32[328,128]{1,0:T(8,128)S(1)} %add.78), channel_id=1, source_target_pairs={{0,16},{4,20},{8,24},{12,28},{16,0},{20,4},{24,8},{28,12},{1,17},{... | collective-permute-start | bytes 503816 | tf_op jit(solution)/shard_map/ppermute | solution.py:518
  110.0 6.0 %collective-permute-done.16 = f32[328,128]{1,0:T(8,128)S(1)} collective-permute-done((f32[328,128]{1,0:T(8,128)S(1)}, f32[328,128]{1,0:T(8,128)S(1)}, u32[]{:S(2)}, u32[]{:S(2)}) %collective-permute-start.16) | collective-permute-done | bytes 167968 | tf_op jit(solution)/shard_map/ppermute | solution.py:518
  116.0 3.1 %collective-permute-start.17 = (f32[328,128]{1,0:T(8,128)S(1)}, f32[328,128]{1,0:T(8,128)S(1)}, u32[]{:S(2)}, u32[]{:S(2)}) collective-permute-start(f32[328,128]{1,0:T(8,128)S(1)} %add.79.refs_2_), channel_id=1, source_target_pairs={{0,4},{4,0},{8,12},{12,8},{16,20},{20,16},{24,28},{28,24},{1,5},{5... | collective-permute-start | bytes 503816 | tf_op jit(solution)/shard_map/ppermute | solution.py:518
  119.2 6.0 %collective-permute-done.13.refs_1_ = f32[224,128]{1,0:T(8,128)S(1)} collective-permute-done((f32[224,128]{1,0:T(8,128)S(1)}, f32[224,128]{1,0:T(8,128)S(1)}, u32[]{:S(2)}, u32[]{:S(2)}) %collective-permute-start.13) | collective-permute-done | bytes 114720 | tf_op jit(solution)/shard_map/ppermute | solution.py:518
  (36 shorter events, 3.8 us)
Async XLA Ops:
  1.6 12.8 %collective-permute-start = (bf16[3,8,2048]{2,1,0:T(8,128)(2,1)S(1)}, bf16[3,8,2048]{2,1,0:T(8,128)(2,1)S(1)}, u32[]{:S(2)}, u32[]{:S(2)}) collective-permute-start(bf16[3,8,2048]{2,1,0:T(8,128)(2,1)S(1)} %trailing.1), channel_id=1, source_target_pairs={{0,4},{4,8},{8,12},{12,16},{16,20},{20,24},{24,28},{1,5},{5,9},{9,... | collective-permute-start | bytes 294920 | tf_op jit(solution)/shard_map/ppermute | solution.py:491
  15.2 6.3 %collective-permute-start.1 = (f32[256,128]{1,0:T(8,128)S(1)}, f32[256,128]{1,0:T(8,128)S(1)}, u32[]{:S(2)}, u32[]{:S(2)}) collective-permute-start(f32[256,128]{1,0:T(8,128)S(1)} %get-tuple-element.89), channel_id=1, source_target_pairs={{0,4},{4,8},{8,12},{12,16},{16,20},{20,24},{24,28},{1,5},{5,9},{9,... | collective-permute-start | bytes 393224 | tf_op jit(solution)/shard_map/ppermute | solution.py:491
  21.5 12.9 %copy-start.1 = (f32[2048]{0:T(1024)S(1)}, f32[2048]{0:T(1024)}, u32[]{:S(2)}) copy-start(f32[2048]{0:T(1024)} %param.17) | copy-start | bytes 24580
  21.5 7.4 %collective-permute-start.2 = (f32[256,128]{1,0:T(8,128)S(1)}, f32[256,128]{1,0:T(8,128)S(1)}, u32[]{:S(2)}, u32[]{:S(2)}) collective-permute-start(f32[256,128]{1,0:T(8,128)S(1)} %get-tuple-element.136), channel_id=1, source_target_pairs={{0,8},{4,12},{8,16},{12,20},{16,24},{20,28},{1,9},{5,13},{9,17},{1... | collective-permute-start | bytes 393224 | tf_op jit(solution)/shard_map/ppermute | solution.py:491
  28.8 8.2 %copy-start = (f32[2048]{0:T(1024)S(1)}, f32[2048]{0:T(1024)}, u32[]{:S(2)}) copy-start(f32[2048]{0:T(1024)} %param.18) | copy-start | bytes 24580
  29.0 7.9 %collective-permute-start.3 = (f32[256,128]{1,0:T(8,128)S(1)}, f32[256,128]{1,0:T(8,128)S(1)}, u32[]{:S(2)}, u32[]{:S(2)}) collective-permute-start(f32[256,128]{1,0:T(8,128)S(1)} %multiply_add_fusion.4), channel_id=1, source_target_pairs={{0,16},{4,20},{8,24},{12,28},{1,17},{5,21},{9,25},{13,29},{2,18},{... | collective-permute-start | bytes 393224 | tf_op jit(solution)/shard_map/ppermute | solution.py:491
  42.3 6.1 %collective-permute-start.6 = (f32[2,256]{1,0:T(2,128)S(1)}, f32[2,256]{1,0:T(2,128)S(1)}, u32[]{:S(2)}, u32[]{:S(2)}) collective-permute-start(f32[2,256]{1,0:T(2,128)S(1)} %get-tuple-element.93.refs_0_), channel_id=1, source_target_pairs={{0,3},{1,0},{2,1},{3,2},{4,7},{5,4},{6,5},{7,6},{8,11},{9,8},{10,9... | collective-permute-start | bytes 6152 | tf_op jit(solution)/shard_map/ppermute | solution.py:512
  42.3 6.1 %collective-permute-start.5 = (f32[2,256]{1,0:T(2,128)S(1)}, f32[2,256]{1,0:T(2,128)S(1)}, u32[]{:S(2)}, u32[]{:S(2)}) collective-permute-start(f32[2,256]{1,0:T(2,128)S(1)} %get-tuple-element.93.refs_0_), channel_id=1, source_target_pairs={{0,2},{1,3},{2,0},{3,1},{4,6},{5,7},{6,4},{7,5},{8,10},{9,11},{10,... | collective-permute-start | bytes 6152 | tf_op jit(solution)/shard_map/ppermute | solution.py:512
  43.8 4.6 %collective-permute-start.4 = (f32[2,256]{1,0:T(2,128)S(1)}, f32[2,256]{1,0:T(2,128)S(1)}, u32[]{:S(2)}, u32[]{:S(2)}) collective-permute-start(f32[2,256]{1,0:T(2,128)S(1)} %get-tuple-element.93.refs_0_), channel_id=1, source_target_pairs={{0,1},{1,2},{2,3},{3,0},{4,5},{5,6},{6,7},{7,4},{8,9},{9,10},{10,1... | collective-permute-start | bytes 6152 | tf_op jit(solution)/shard_map/ppermute | solution.py:512
  52.9 9.1 %collective-permute-start.7 = (f32[384,128]{1,0:T(8,128)S(1)}, f32[384,128]{1,0:T(8,128)S(1)}, u32[]{:S(2)}, u32[]{:S(2)}) collective-permute-start(f32[384,128]{1,0:T(8,128)S(1)} %get-tuple-element.102), channel_id=1, source_target_pairs={{4,0},{8,4},{12,8},{16,12},{20,16},{24,20},{28,24},{5,1},{9,5},{13... | collective-permute-start | bytes 589832 | tf_op jit(solution)/shard_map/ppermute | solution.py:491
  62.0 8.8 %collective-permute-start.8 = (f32[256,128]{1,0:T(8,128)S(1)}, f32[256,128]{1,0:T(8,128)S(1)}, u32[]{:S(2)}, u32[]{:S(2)}) collective-permute-start(f32[256,128]{1,0:T(8,128)S(1)} %multiply_add_fusion.2), channel_id=1, source_target_pairs={{8,0},{12,4},{16,8},{20,12},{24,16},{28,20},{9,1},{13,5},{17,9},{2... | collective-permute-start | bytes 393224 | tf_op jit(solution)/shard_map/ppermute | solution.py:491
  70.9 11.9 %collective-permute-start.9 = (f32[256,128]{1,0:T(8,128)S(1)}, f32[256,128]{1,0:T(8,128)S(1)}, u32[]{:S(2)}, u32[]{:S(2)}) collective-permute-start(f32[256,128]{1,0:T(8,128)S(1)} %multiply_add_fusion.1), channel_id=1, source_target_pairs={{16,0},{20,4},{24,8},{28,12},{17,1},{21,5},{25,9},{29,13},{18,2},{... | collective-permute-start | bytes 393224 | tf_op jit(solution)/shard_map/ppermute | solution.py:491
  83.0 6.0 %collective-permute-start.14 = (f32[328,128]{1,0:T(8,128)S(1)}, f32[328,128]{1,0:T(8,128)S(1)}, u32[]{:S(2)}, u32[]{:S(2)}) collective-permute-start(f32[328,128]{1,0:T(8,128)S(1)} %get-tuple-element.130), channel_id=1, source_target_pairs={{0,4},{4,0},{8,12},{12,8},{16,20},{20,16},{24,28},{28,24},{1,5},{5... | collective-permute-start | bytes 503816 | tf_op jit(solution)/shard_map/ppermute | solution.py:518
  89.0 18.8 %collective-permute-start.15 = (f32[328,128]{1,0:T(8,128)S(1)}, f32[328,128]{1,0:T(8,128)S(1)}, u32[]{:S(2)}, u32[]{:S(2)}) collective-permute-start(f32[328,128]{1,0:T(8,128)S(1)} %add.77), channel_id=1, source_target_pairs={{0,8},{4,12},{8,0},{12,4},{16,24},{20,28},{24,16},{28,20},{1,9},{5... | collective-permute-start | bytes 503816 | tf_op jit(solution)/shard_map/ppermute | solution.py:518
  95.8 7.1 %collective-permute-start.10 = (f32[2,2,64,128]{3,2,1,0:T(8,128)S(1)}, f32[2,2,64,128]{3,2,1,0:T(8,128)S(1)}, u32[]{:S(2)}, u32[]{:S(2)}) collective-permute-start(f32[2,2,64,128]{3,2,1,0:T(8,128)S(1)} %get-tuple-element.121), channel_id=1, source_target_pairs={{4,0},{8,4},{12,8},{16,12},{20,16},{24,20},{28,24},{5,1},{9,5},{13... | collective-permute-start | bytes 393224 | tf_op jit(solution)/shard_map/ppermute | solution.py:491
  97.0 12.8 %collective-permute-start.11 = (f32[224,128]{1,0:T(8,128)S(1)}, f32[224,128]{1,0:T(8,128)S(1)}, u32[]{:S(2)}, u32[]{:S(2)}) collective-permute-start(f32[224,128]{1,0:T(8,128)S(1)} %get-tuple-element.124), channel_id=1, source_target_pairs={{0,4},{4,0},{8,12},{12,8},{16,20},{20,16},{24,28},{28,24},{1,5},{5... | collective-permute-start | bytes 344072 | tf_op jit(solution)/shard_map/ppermute | solution.py:518
  107.9 8.1 %collective-permute-start.16 = (f32[328,128]{1,0:T(8,128)S(1)}, f32[328,128]{1,0:T(8,128)S(1)}, u32[]{:S(2)}, u32[]{:S(2)}) collective-permute-start(f32[328,128]{1,0:T(8,128)S(1)} %add.78), channel_id=1, source_target_pairs={{0,16},{4,20},{8,24},{12,28},{16,0},{20,4},{24,8},{28,12},{1,17},{... | collective-permute-start | bytes 503816 | tf_op jit(solution)/shard_map/ppermute | solution.py:518
  109.8 9.3 %collective-permute-start.12 = (f32[224,128]{1,0:T(8,128)S(1)}, f32[224,128]{1,0:T(8,128)S(1)}, u32[]{:S(2)}, u32[]{:S(2)}) collective-permute-start(f32[224,128]{1,0:T(8,128)S(1)} %add_add_fusion), channel_id=1, source_target_pairs={{0,8},{4,12},{8,0},{12,4},{16,24},{20,28},{24,16},{28,20},{1,9},{5... | collective-permute-start | bytes 344072 | tf_op jit(solution)/shard_map/ppermute | solution.py:518
  116.0 9.2 %collective-permute-start.17 = (f32[328,128]{1,0:T(8,128)S(1)}, f32[328,128]{1,0:T(8,128)S(1)}, u32[]{:S(2)}, u32[]{:S(2)}) collective-permute-start(f32[328,128]{1,0:T(8,128)S(1)} %add.79.refs_2_), channel_id=1, source_target_pairs={{0,4},{4,0},{8,12},{12,8},{16,20},{20,16},{24,28},{28,24},{1,5},{5... | collective-permute-start | bytes 503816 | tf_op jit(solution)/shard_map/ppermute | solution.py:518
  119.1 6.1 %collective-permute-start.13 = (f32[224,128]{1,0:T(8,128)S(1)}, f32[224,128]{1,0:T(8,128)S(1)}, u32[]{:S(2)}, u32[]{:S(2)}) collective-permute-start(f32[224,128]{1,0:T(8,128)S(1)} %add.76.refs_0_), channel_id=1, source_target_pairs={{0,16},{4,20},{8,24},{12,28},{16,0},{20,4},{24,8},{28,12},{1,17},{... | collective-permute-start | bytes 344072 | tf_op jit(solution)/shard_map/ppermute | solution.py:518

commit v4 on v3

--- a/solution.py
+++ b/solution.py
@@ -21,6 +21,16 @@
 
 def put(ref, t, value):
     ref[pl.ds(pl.multiple_of(t * SUB, SUB), SUB), :] = value
+
+
+def loop(start, stop, body, carry):
+    pairs = (stop - start) // 2
+
+    def two(i, carry):
+        return body(start + 2 * i + 1, body(start + 2 * i, carry))
+
+    carry = lax.fori_loop(0, pairs, two, carry)
+    return body(stop - 1, carry) if (stop - start) % 2 else carry
 
 
 def spread(src, dst, first, count):
@@ -31,7 +41,7 @@
             dst[pl.ds((start + first) * SUB + g, 16, stride=SUB), :] = piece
         return carry
 
-    lax.fori_loop(0, count // 16, some, 0)
+    loop(0, count // 16, some, 0)
 
 
 def gather_rows(src, dst, count):
@@ -42,7 +52,7 @@
             dst[pl.ds(start, 16), g * LANES : (g + 1) * LANES] = piece.astype(dst.dtype)
         return carry
 
-    lax.fori_loop(0, count // 16, some, 0)
+    loop(0, count // 16, some, 0)
 
 
 def total(values):
@@ -95,7 +105,7 @@
             put(u, t0 + i, second * row(f1, t0 + i))
         return carry
 
-    lax.fori_loop(1, steps // SUB, conv, 0)
+    loop(1, steps // SUB, conv, 0)
     fade, skip = fades(lam, modes, 1), fades(lam, modes, SUB)
 
     def advance(c, x):
@@ -107,7 +117,7 @@
             new.append(own + skip[m] * x[m])
         return tuple(new)
 
-    x = lax.fori_loop(1, steps // SUB, advance, zeros(modes))
+    x = loop(1, steps // SUB, advance, zeros(modes))
     for m in range(modes):
         put(x_out, m, x[m])
 
@@ -133,10 +143,11 @@
 ):
     del f1_in, f2_in, u_in, g_in
     margin = taps - 1
+    there = jnp.where(lax.axis_index("ctx") > 0, 1.0, 0.0)
     for s in range(SUB):
         lanes = slice(s * LANES, (s + 1) * LANES)
-        k_ext[pl.ds(s, SUB, stride=SUB), :] = halo[1, :, lanes].astype(F32)
-        v_ext[pl.ds(s, SUB, stride=SUB), :] = halo[2, :, lanes].astype(F32)
+        k_ext[pl.ds(s, SUB, stride=SUB), :] = halo[1, :, lanes].astype(F32) * there
+        v_ext[pl.ds(s, SUB, stride=SUB), :] = halo[2, :, lanes].astype(F32) * there
     taps1, taps2 = taps_of(filt, 1, taps), taps_of(filt, 2, taps)
     kw = [row(k_ext, SUB - margin + i) for i in range(margin)] + [row(k_head, i) for i in range(SUB)]
     vw = [row(v_ext, SUB - margin + i) for i in range(margin)] + [row(v_head, i) for i in range(SUB)]
@@ -156,9 +167,10 @@
 
 def query_kernel(taps, steps, query, halo, filt, q_ext, f0):
     margin = taps - 1
+    there = jnp.where(lax.axis_index("ctx") > 0, 1.0, 0.0)
     for s in range(SUB):
         lanes = slice(s * LANES, (s + 1) * LANES)
-        q_ext[pl.ds(s, SUB, stride=SUB), :] = halo[0, :, lanes].astype(F32)
+        q_ext[pl.ds(s, SUB, stride=SUB), :] = halo[0, :, lanes].astype(F32) * there
     spread(query, q_ext, SUB, steps)
     taps0 = taps_of(filt, 0, taps)
 
@@ -169,7 +181,7 @@
             put(f0, t0 + i, conv_at(qw, taps0, i))
         return carry
 
-    lax.fori_loop(0, steps // SUB, conv, 0)
+    loop(0, steps // SUB, conv, 0)
 
 
 def inputs_kernel(steps, residual, cot, res_pos, cot_pos):
@@ -195,7 +207,7 @@
             put(y, c * SUB + i, total([near[k] * now[i - k] for k in range(i + 1)]))
         return carry
 
-    lax.fori_loop(0, steps // SUB, some, 0)
+    loop(0, steps // SUB, some, 0)
 
 
 def lags_kernel(modes, steps, u, x_at, lam, lag, lag_sum):
@@ -210,12 +222,12 @@
             new.append(skip[m] * sums[m] + border)
         return tuple(new)
 
-    sums = lax.fori_loop(0, steps // SUB, some, zeros(modes))
+    sums = loop(0, steps // SUB, some, zeros(modes))
     for m in range(modes):
         put(lag_sum, m, sums[m])
 
 
-def summed_kernel(modes, steps, blocks, y, f0, res_pos, cot_pos, g, x_in, lam, res, gain, modal, summed, x_at, sums, squares, inner):
+def summed_kernel(modes, steps, blocks, group, y, f0, res_pos, cot_pos, g, before, other, lam, res, gain, modal, summed, x_at, sums, squares, inner):
     block = pl.program_id(0)
 
     @pl.when(block == 0)
@@ -225,6 +237,8 @@
 
     fade, skip = fades(lam, modes, 1), fades(lam, modes, SUB)
     factor = gain[...]
+    x_in = exclusive(before[...], other[...], lam[...], steps, group, 1)
+    x_in = tuple(x_in[m * SUB : (m + 1) * SUB, :] for m in range(modes))
 
     def advance(c, x):
         w = [row(res, m) * x[m] for m in range(modes)]
@@ -241,7 +255,7 @@
             put(inner, t, row(inner, t) + factor * row(cot_pos, t) * now)
         return tuple(row(g, c * modes + m) + skip[m] * x[m] for m in range(modes))
 
-    lax.fori_loop(0, steps // SUB, advance, tuple(row(x_in, m) for m in range(modes)))
+    loop(0, steps // SUB, advance, x_in)
 
     @pl.when(block == blocks - 1)
     def _():
@@ -259,8 +273,8 @@
 
 
 def grad_modal_kernel(modes, steps, width, shares, *refs):
-    own_sums, (summed, cot_pos, f0, modal, lam, gain, ready) = refs[:shares], refs[shares : shares + 7]
-    scale, gm, adj, a_out, border = refs[shares + 7 :]
+    own_sums, (summed, cot_pos, f0, lam, gain, ready) = refs[:shares], refs[shares : shares + 6]
+    scale, gm, adj, a_out = refs[shares + 6 :]
     del ready
 
     @pl.when(pl.program_id(0) == 0)
@@ -295,15 +309,9 @@
             new.append(own + skip[m] * a[m])
         return tuple(new)
 
-    a = lax.fori_loop(0, steps // SUB, advance, zeros(modes))
+    a = loop(0, steps // SUB, advance, zeros(modes))
     for m in range(modes):
         put(a_out, m, a[m])
-        put(border, m, a[m])
-    for t in range(SUB):
-        inv = scale[pl.ds(t, 1), :]
-        coef = scale[pl.ds(steps + t, 1), :]
-        grad = inv * (factor * row(cot_pos, t)) - coef * row(summed, t)
-        put(border, modes + t, grad * row(modal, t))
 
 
 def own_adjoint_kernel(modes, steps, gm, u, adj, x_at, lag, lam, res, skip, gmy, res_sum, rate_sum, skip_sum):
@@ -320,7 +328,7 @@
             lags[k] + total([now[i] * before[i - k] for i in range(k, SUB)]) for k in range(SUB)
         )
 
-    lags = lax.fori_loop(0, steps // SUB, pairs, zeros(SUB))
+    lags = loop(0, steps // SUB, pairs, zeros(SUB))
     skip_sum[...] = lags[0]
     half = modes // 2
     for part in range(2):
@@ -339,7 +347,7 @@
             return tuple(after), tuple(by_res), tuple(by_rate)
 
         none = zeros(half)
-        _, by_res, by_rate = lax.fori_loop(0, steps // SUB, across, (none, none, none))
+        _, by_res, by_rate = loop(0, steps // SUB, across, (none, none, none))
         for i, m in enumerate(ms):
             put(res_sum, m, by_res[i] + horner(fade[m], lags[::-1]))
             weighted = [lags[k] * float(k) for k in range(1, SUB)]
@@ -357,7 +365,7 @@
             acc = acc + row(cot_pos, t) * here
         return acc
 
-    gain_out[...] = lax.fori_loop(0, steps // SUB, norm, zeros(1)[0])
+    gain_out[...] = loop(0, steps // SUB, norm, zeros(1)[0])
     gather_rows(work, normed, steps)
 
     def grads(c, carry):
@@ -368,14 +376,12 @@
             put(work, t, inv * (factor * row(cot_pos, t)) - coef * row(summed, t))
         return carry
 
-    lax.fori_loop(0, steps // SUB, grads, 0)
+    loop(0, steps // SUB, grads, 0)
     gather_rows(work, grad_res, steps)
 
 
-def grad_query_kernel(modes, taps, steps, scale, summed, cot_pos, modal, q_ext, gf0_next, filt, gain, res_sum, skip_sum, gain_sum, grad_query, early, work, gf0):
+def query_sums_kernel(modes, taps, steps, scale, summed, cot_pos, modal, q_ext, gain, res_sum, skip_sum, gain_sum, gf0, early):
     factor = gain[...]
-    gf0[pl.ds(steps * SUB, SUB * SUB), :] = gf0_next[...]
-    taps0 = taps_of(filt, 0, taps)
 
     def grads(c, carry):
         for i in range(SUB):
@@ -386,15 +392,13 @@
             put(gf0, t, grad * row(modal, t))
         return carry
 
-    lax.fori_loop(0, steps // SUB, grads, 0)
+    loop(0, steps // SUB, grads, 0)
     sums = filter_pass(taps, steps, gf0, q_ext)
     for j in range(taps):
         put(early, j, sums[j])
     early[pl.ds(taps * SUB, modes * SUB), :] = res_sum[...]
     put(early, taps + modes, skip_sum[...])
     put(early, taps + modes + 1, gain_sum[...])
-    back_pass(taps, steps, gf0, taps0, work)
-    gather_rows(work, grad_query, steps)
 
 
 def filter_pass(taps, steps, grad, ext):
@@ -409,7 +413,7 @@
         return acc
 
     zero = jnp.zeros((SUB, LANES), F32)
-    return lax.fori_loop(0, steps // SUB, some, tuple(zero for _ in range(taps)))
+    return loop(0, steps // SUB, some, tuple(zero for _ in range(taps)))
 
 
 def back_pass(taps, steps, grad, weights, out):
@@ -422,10 +426,10 @@
             put(out, t0 + i, total([weights[j] * window[i + j] for j in range(taps)]))
         return carry
 
-    lax.fori_loop(0, steps // SUB, some, 0)
-
-
-def mixed_kernel(modes, taps, steps, gmy, f1, f2, k_ext, v_ext, adj, lam, res, alpha, gf1, gf2, heads, sums):
+    loop(0, steps // SUB, some, 0)
+
+
+def mixed_kernel(modes, taps, steps, gmy, f1, f2, gf0, adj, lam, res, alpha, gf1, gf2, heads):
     fade, skip = fades(lam, modes, 1), fades(lam, modes, SUB)
 
     def advance(c, after):
@@ -439,24 +443,65 @@
             w = [f * v for f, v in zip(fade, w)]
         return tuple(row(adj, block * modes + m) + skip[m] * after[m] for m in range(modes))
 
-    lax.fori_loop(0, steps // SUB, advance, tuple(row(alpha, m) for m in range(modes)))
-    heads[0, 0] = gf1[: SUB * SUB, :]
-    heads[1, 0] = gf2[: SUB * SUB, :]
+    loop(0, steps // SUB, advance, tuple(row(alpha, m) for m in range(modes)))
+    for which, grad in enumerate((gf0, gf1, gf2)):
+        heads[which, 0] = grad[: SUB * SUB, :]
+
+
+def filter_sums_kernel(taps, steps, gf1, gf2, k_ext, v_ext, sums):
     for which, (grad, ext) in enumerate(((gf1, k_ext), (gf2, v_ext))):
         parts = filter_pass(taps, steps, grad, ext)
         for j in range(taps):
             put(sums, which * taps + j, parts[j])
 
 
-def back_kernel(taps, steps, gf1, gf2, next_head, filt, grad_key, grad_value, work, ext):
-    for which, (grad, out) in enumerate(((gf1, grad_key), (gf2, grad_value))):
-        ext[pl.ds(0, steps * SUB), :] = grad[...]
-        ext[pl.ds(steps * SUB, SUB * SUB), :] = next_head[which, 0]
-        back_pass(taps, steps, ext, taps_of(filt, which + 1, taps), work)
-        gather_rows(work, out, steps)
-
-
-def pack_kernel(modes, first_rows, half, early, res, rate_sum, lag_sum, alpha, kept, sent):
+def back_kernel(which, taps, steps, last, grad, next_head, filt, out, work, ext):
+    there = jnp.where(lax.axis_index("ctx") < last, 1.0, 0.0)
+    ext[pl.ds(0, steps * SUB), :] = grad[...]
+    ext[pl.ds(steps * SUB, SUB * SUB), :] = next_head[which, 0] * there
+    back_pass(taps, steps, ext, taps_of(filt, which, taps), work)
+    gather_rows(work, out, steps)
+
+
+def place(group, sign):
+    at = lax.axis_index("ctx")
+    if sign < 0:
+        at = lax.axis_size("ctx") - 1 - at
+    later = (at // group) % 2
+    return (at % group).astype(F32), later.astype(F32)
+
+
+def exclusive(before, other, lam, span, group, sign):
+    at, later = place(group, sign)
+    here = later * jnp.exp(lam * (at * -float(span))) * other
+    return here if before is None else before + here
+
+
+def inclusive(own, other, lam, span, group, sign):
+    _, later = place(group, sign)
+    fall = -float(span * group)
+    return jnp.exp(lam * ((1.0 - later) * fall)) * own + jnp.exp(lam * (later * fall)) * other
+
+
+def join_kernel(span, group, sign, first, own, other, lam, *refs):
+    before, ends = (None, refs[-2:]) if first else (refs[0][...], refs[-2:])
+    ends[0][...] = exclusive(before, other[...], lam[...], span, group, sign)
+    ends[1][...] = inclusive(own[...], other[...], lam[...], span, group, sign)
+
+
+def add_kernel(one, other, after, out):
+    del after
+    out[...] = one[...] + other[...]
+
+
+def gather_kernel(early_rows, kept, other, late, after, out):
+    del after
+    out[:early_rows, :] = kept[...] + other[...]
+    out[early_rows:, :] = late[...]
+
+
+def pack_kernel(span, group, modes, first_rows, half, before, other, lam, early, res, rate_sum, lag_sum, alpha, kept, sent):
+    alpha[...] = exclusive(before[...], other[...], lam[...], span, group, -1)
     odd = lax.axis_index("ctx") % 2
     rows = (first_rows + modes) * SUB
     for out, start in ((kept, odd * half), (sent, (1 - odd) * half)):
@@ -469,64 +514,60 @@
             out[pl.ds(b * rows + first_rows * SUB, modes * SUB), :] = -res[mine, :] * lagged
 
 
-def finish_kernel(modes, taps, half, late, late_other, early, early_other, short, res, rate, skip, gain, work, work2):
-    odd = lax.axis_index("ctx") % 2
-    mine = jnp.where(odd == pl.program_id(0) // half, 1.0, 0.0)
-    work[...] = late[...] + late_other[...]
-    work2[...] = mine * early[...] + (1.0 - mine) * early_other[...]
+def finish_kernel(modes, taps, half, early_rows, late_rows, mine, other, after, short, res, rate, skip, gain, late, early):
+    del after
+    block = pl.program_id(0)
+    at = pl.multiple_of((half * early_rows + block * late_rows) * SUB, SUB)
+    late[...] = mine[pl.ds(at, late_rows * SUB), :] + other[pl.ds(at, late_rows * SUB), :]
+    own = jnp.where(lax.axis_index("ctx") % 2 == block // half, 1.0, 0.0)
+    at = pl.multiple_of((block % half) * (early_rows * SUB), SUB)
+    here = pl.ds(at, early_rows * SUB)
+    early[...] = own * mine[here, :] + (1.0 - own) * other[here, :]
     for s in range(SUB):
         lanes = slice(s * LANES, (s + 1) * LANES)
-        short[0, :, lanes] = work2[pl.ds(s, taps, stride=SUB), :]
-        short[1, :, lanes] = work[pl.ds(s, taps, stride=SUB), :]
-        short[2, :, lanes] = work[pl.ds(taps * SUB + s, taps, stride=SUB), :]
-        res[:, lanes] = work2[pl.ds(taps * SUB + s, modes, stride=SUB), :]
-        rate[:, lanes] = work2[pl.ds((taps + modes + 2) * SUB + s, modes, stride=SUB), :]
-    skip[...] = row(work2, taps + modes)
-    gain[...] = row(work2, taps + modes + 1)
-
-
-def shift(value, axis, distance):
-    devices = range(lax.axis_size(axis))
-    route = [(i - distance, i) for i in devices if i - distance in devices]
-    return lax.ppermute(value, axis, route)
-
-
-def carried_in(own, first, lam, span, axis, sign, under):
-    count, reach = lax.axis_size(axis), 1
-    under = list(under) + [None] * count
-    before, upto = None, own
-    while reach < count:
-        other = first if reach == 1 else shift(upto, axis, sign * reach)
-        wait = under.pop(0)
-        if wait is not None:
-            other = other + wait
-        before = other if before is None else before + jnp.exp(lam * -float(span * (reach - 1))) * other
-        upto = upto + jnp.exp(lam * -float(span * reach)) * other
-        reach *= 2
-    return before
-
-
-def others_of(value, axis):
+        short[0, :, lanes] = early[pl.ds(s, taps, stride=SUB), :]
+        short[1, :, lanes] = late[pl.ds(s, taps, stride=SUB), :]
+        short[2, :, lanes] = late[pl.ds(taps * SUB + s, taps, stride=SUB), :]
+        res[:, lanes] = early[pl.ds(taps * SUB + s, modes, stride=SUB), :]
+        rate[:, lanes] = early[pl.ds((taps + modes + 2) * SUB + s, modes, stride=SUB), :]
+    skip[...] = row(early, taps + modes)
+    gain[...] = row(early, taps + modes + 1)
+
+
+def ring(value, axis, distance):
     count = lax.axis_size(axis)
-    return [
-        lax.ppermute(value, axis, [(i, (i + k) % count) for i in range(count)])
-        for k in range(1, count)
-    ]
+    return lax.ppermute(value, axis, [(i, (i + distance) % count) for i in range(count)])
 
 
 def swap(value, axis, step):
     return lax.ppermute(value, axis, [(i, i ^ step) for i in range(lax.axis_size(axis))])
 
 
-def sum_but_last(value, axis, first, under=None):
-    count, step = lax.axis_size(axis), first
+def small(body, ins, after, outs, name):
+    near = pl.BlockSpec(memory_space=pltpu.VMEM)
+    return pl.pallas_call(
+        body,
+        in_specs=[near] * len(ins) + [pl.BlockSpec(memory_space=pl.ANY)] * len(after),
+        out_specs=[near] * len(outs),
+        out_shape=[jax.ShapeDtypeStruct(shape, F32) for shape in outs],
+        compiler_params=pltpu.CompilerParams(vmem_limit_bytes=VMEM_LIMIT),
+        cost_estimate=pl.CostEstimate(flops=ins[0].size, bytes_accessed=0, transcendentals=0),
+        name=name,
+    )(*ins, *after)
+
+
+def scan_but_last(own, lam, span, sign, under):
+    count, group, before = lax.axis_size("ctx"), 1, None
+    under = list(under)
     while True:
-        other = swap(value, axis, step)
-        step *= 2
-        if step >= count:
-            return value, other
-        value = value + other if under is None else value + other + under
-        under = None
+        other = swap(own, "ctx", group)
+        if 2 * group >= count:
+            return before, other, group
+        body = functools.partial(join_kernel, span, group, sign, before is None)
+        ins = [own, other, lam] + ([] if before is None else [before])
+        after = [under.pop(0)] if under else []
+        before, own = small(body, ins, after, [own.shape] * 2, "join")
+        group *= 2
 
 
 def shards(
@@ -560,7 +601,7 @@
     param_spec = pl.BlockSpec((modes, WIDE), lambda h: (0, h))
     short_spec = pl.BlockSpec((3, taps, WIDE), lambda h: (0, 0, h))
 
-    def call(body, ins, in_specs, outs, out_specs, ops, name, scratch=(), aliases=None, done_rows=None):
+    def call(body, ins, in_specs, outs, out_specs, ops, name, scratch=(), aliases=None):
         elements, n_refs = steps * channels, len(ins) + len(outs)
 
         def with_done(*refs):
@@ -573,7 +614,7 @@
             pltpu.with_memory_space_constraint(v, pltpu.VMEM) if v.shape[0] >= near and v.dtype == F32 else v
             for v in ins
         ]
-        done_shape = (blocks * (done_rows or modes) * SUB, LANES)
+        done_shape = (SUB, LANES)
         outs = [*outs, jax.ShapeDtypeStruct(done_shape, F32)]
         out_specs = [*out_specs, pl.BlockSpec(done_shape, lambda h: (0, 0))]
         return pl.pallas_call(
@@ -608,7 +649,7 @@
         cost_estimate=pl.CostEstimate(flops=channels, bytes_accessed=channels, transcendentals=0),
         name="trailing",
     )(*far[1:4])
-    halo = shift(trailing, "ctx", 1)
+    halo = ring(trailing, "ctx", 1)
 
     k_ext, v_ext, f1, f2, u, g, lam, res, filt, x_part, _ = call(
         functools.partial(features_kernel, modes, taps, steps),
@@ -651,7 +692,7 @@
         10,
         "inputs",
     )
-    y, near_done = call(
+    y, _ = call(
         functools.partial(near_kernel, modes, steps),
         (u, lam, res, skip),
         [seq_spec, mode_spec, mode_spec, one_spec],
@@ -660,18 +701,18 @@
         10,
         "near",
     )
-    x_in = carried_in(x_own, shift(x_own, "ctx", 1), lam, steps, "ctx", 1, [query_done, inputs_done, near_done])
+    before, other, group = scan_but_last(x_own, lam, steps, 1, [query_done, inputs_done])
     modal, summed, x_at, sums, _ = call(
-        functools.partial(summed_kernel, modes, steps, blocks),
-        (y, f0, res_pos, cot_pos, g, x_in, lam, res, gain),
-        [seq_spec] * 4 + [eights_spec] + [mode_spec] * 3 + [one_spec],
+        functools.partial(summed_kernel, modes, steps, blocks, group),
+        (y, f0, res_pos, cot_pos, g, before, other, lam, res, gain),
+        [seq_spec] * 4 + [eights_spec] + [mode_spec] * 4 + [one_spec],
         [seq, seq, eights, jax.ShapeDtypeStruct((2, steps), F32)],
         [seq_spec, seq_spec, eights_spec, pl.BlockSpec((2, steps), lambda h: (0, 0))],
         50,
         "summed",
         scratch=[pltpu.VMEM((steps * SUB, LANES), F32)] * 2,
     )
-    all_sums = [sums, *others_of(sums, "tp")]
+    all_sums = [sums, *(swap(sums, "tp", k) for k in range(1, lax.axis_size("tp")))]
     lag, lag_sum, lags_done = call(
         functools.partial(lags_kernel, modes, steps),
         (u, x_at, lam),
@@ -682,17 +723,16 @@
         "lags",
     )
     scale_spec = pl.BlockSpec((2 * steps, LANES), lambda h: (0, 0))
-    scale, gm, adj, a_own, border, _ = call(
+    scale, gm, adj, a_own, _ = call(
         functools.partial(grad_modal_kernel, modes, steps, width, len(all_sums)),
-        (*all_sums, summed, cot_pos, f0, modal, lam, gain, lags_done),
+        (*all_sums, summed, cot_pos, f0, lam, gain, lags_done),
         [pl.BlockSpec((2, steps), lambda h: (0, 0))] * len(all_sums)
-        + [seq_spec, seq_spec, seq_spec, head_spec(steps, 0), mode_spec, one_spec, any_spec],
-        [pltpu.VMEM((2 * steps, LANES), F32), seq, eights, mode, pos(modes + SUB)],
-        [scale_spec, seq_spec, eights_spec, mode_spec, pos_spec(modes + SUB)],
+        + [seq_spec, seq_spec, seq_spec, mode_spec, one_spec, any_spec],
+        [pltpu.VMEM((2 * steps, LANES), F32), seq, eights, mode],
+        [scale_spec, seq_spec, eights_spec, mode_spec],
         45,
         "grad_modal",
     )
-    border = shift(border, "ctx", -1)
     normed, grad_residual, gain_sum, norm_done = call(
         functools.partial(norm_kernel, steps),
         (scale, summed, cot_pos, gain),
@@ -713,74 +753,87 @@
         "own_adjoint",
     )
     early_rows = taps + modes + 2
-    grad_query, early, query_back_done = call(
-        functools.partial(grad_query_kernel, modes, taps, steps),
-        (scale, summed, cot_pos, modal, q_ext, border, filt, gain, res_sum, skip_sum, gain_sum),
-        [scale_spec, seq_spec, seq_spec, seq_spec, ext_spec, head_spec(modes + SUB, modes // SUB), filt_spec, one_spec, mode_spec, one_spec, one_spec],
-        [wide, pos(early_rows)],
-        [wide_spec, pos_spec(early_rows)],
+    gf0, early, _ = call(
+        functools.partial(query_sums_kernel, modes, taps, steps),
+        (scale, summed, cot_pos, modal, q_ext, gain, res_sum, skip_sum, gain_sum),
+        [scale_spec, seq_spec, seq_spec, seq_spec, ext_spec, one_spec, mode_spec, one_spec, one_spec],
+        [seq, pos(early_rows)],
+        [seq_spec, pos_spec(early_rows)],
+        30,
+        "query_sums",
+    )
+    before, other, group = scan_but_last(a_own, lam, steps, -1, [norm_done, adjoint_done])
+
+    half = blocks // 2
+    half_shape = (half * (early_rows + modes) * SUB, LANES)
+    alpha, kept_half, sent_half = small(
+        functools.partial(pack_kernel, steps, group, modes, early_rows, half),
+        [before, other, lam, early, res, rate_sum, lag_sum],
+        [],
+        [lam.shape, half_shape, half_shape],
+        "pack",
+    )
+    early_rows += modes
+    late_rows = 2 * taps
+    next_spec = pl.BlockSpec((3, 1, SUB * SUB, LANES), lambda h: (0, h, 0, 0))
+    other_half = swap(sent_half, "ctx", 1)
+    gf1, gf2, heads, _ = call(
+        functools.partial(mixed_kernel, modes, taps, steps),
+        (gmy, f1, f2, gf0, adj, lam, res, alpha),
+        [seq_spec] * 4 + [eights_spec] + [mode_spec] * 3,
+        [seq, seq, jax.ShapeDtypeStruct((3, blocks, SUB * SUB, LANES), F32)],
+        [seq_spec, seq_spec, next_spec],
         45,
-        "grad_query",
-        scratch=[
-            pltpu.VMEM((steps * SUB, LANES), F32),
-            pltpu.VMEM(((steps + SUB) * SUB, LANES), F32),
-        ],
-    )
-    border_rows = modes + SUB
-    alpha_first = border.reshape(blocks, border_rows * SUB, LANES)[:, : modes * SUB]
-    alpha = carried_in(a_own, alpha_first.reshape(a_own.shape), lam, steps, "ctx", -1, [norm_done, adjoint_done, query_back_done])
-
-    half = blocks // 2
+        "mixed",
+    )
+    next_head = ring(heads, "ctx", -1)
+    late, late_done = call(
+        functools.partial(filter_sums_kernel, taps, steps),
+        (gf1, gf2, k_ext, v_ext),
+        [seq_spec, seq_spec, ext_spec, ext_spec],
+        [pos(late_rows)],
+        [pos_spec(late_rows)],
+        30,
+        "filter_sums",
+    )
+
+    def back(which, grad, name):
+        return call(
+            functools.partial(back_kernel, which, taps, steps, lax.axis_size("ctx") - 1),
+            (grad, next_head, filt),
+            [seq_spec, next_spec, filt_spec],
+            [wide],
+            [wide_spec],
+            20,
+            name,
+            scratch=[
+                pltpu.VMEM((steps * SUB, LANES), F32),
+                pltpu.VMEM(((steps + SUB) * SUB, LANES), F32),
+            ],
+        )
+
+    grad_query, query_done = back(0, gf0, "back_query")
+    grad_key, key_done = back(1, gf1, "back_key")
+    grad_value, value_done = back(2, gf2, "back_value")
+    both_shape = (half_shape[0] + late.shape[0], LANES)
+    mine = small(
+        functools.partial(gather_kernel, half_shape[0]),
+        [kept_half, other_half, late],
+        [late_done],
+        [both_shape],
+        "gather",
+    )[0]
+    step, under = 2, [query_done, key_done]
+    while step < lax.axis_size("ctx"):
+        after = under.pop(0) if under else late_done
+        mine = small(add_kernel, [mine, swap(mine, "ctx", step)], [after], [both_shape], "add")[0]
+        step *= 2
+    other = swap(mine, "ctx", 1)
     whole_spec = pl.BlockSpec(memory_space=pltpu.VMEM)
-    half_shape = jax.ShapeDtypeStruct((half * (early_rows + modes) * SUB, LANES), F32)
-    kept_half, sent_half = pl.pallas_call(
-        functools.partial(pack_kernel, modes, early_rows, half),
-        in_specs=[whole_spec] * 5,
-        out_specs=[whole_spec] * 2,
-        out_shape=[half_shape] * 2,
-        compiler_params=pltpu.CompilerParams(vmem_limit_bytes=VMEM_LIMIT),
-        cost_estimate=pl.CostEstimate(flops=half_shape.size, bytes_accessed=0, transcendentals=0),
-        name="pack",
-    )(early, res, rate_sum, lag_sum, alpha)
-    early_rows += modes
-    early = kept_half + swap(sent_half, "ctx", 1)
-    late_rows = 2 * taps
-    next_spec = pl.BlockSpec((2, 1, SUB * SUB, LANES), lambda h: (0, h, 0, 0))
-    gf1, gf2, heads, late, _ = call(
-        functools.partial(mixed_kernel, modes, taps, steps),
-        (gmy, f1, f2, k_ext, v_ext, adj, lam, res, alpha),
-        [seq_spec] * 3 + [ext_spec] * 2 + [eights_spec] + [mode_spec] * 3,
-        [seq, seq, jax.ShapeDtypeStruct((2, blocks, SUB * SUB, LANES), F32), pos(late_rows)],
-        [seq_spec, seq_spec, next_spec, pos_spec(late_rows)],
-        75,
-        "mixed",
-    )
-    next_head = shift(heads, "ctx", -1)
-    grad_key, grad_value, back_done = call(
-        functools.partial(back_kernel, taps, steps),
-        (gf1, gf2, next_head, filt),
-        [seq_spec, seq_spec, next_spec, filt_spec],
-        [wide, wide],
-        [wide_spec, wide_spec],
-        28,
-        "back",
-        scratch=[
-            pltpu.VMEM((steps * SUB, LANES), F32),
-            pltpu.VMEM(((steps + SUB) * SUB, LANES), F32),
-        ],
-        done_rows=late_rows,
-    )
-    if lax.axis_size("ctx") > 2:
-        one_part, other_part = sum_but_last(early, "ctx", 2)
-        early = one_part + other_part
-    early_other = swap(early, "ctx", 1)
-    late, late_other = sum_but_last(late, "ctx", 1, back_done)
-    late_spec = pos_spec(late_rows)
-    half_spec = pl.BlockSpec((early_rows * SUB, LANES), lambda h: (h % half, 0))
     grad_short, grad_residues, grad_rate, grad_skip, grad_gain, _ = call(
-        functools.partial(finish_kernel, modes, taps, half),
-        (late, late_other, early, early_other),
-        [late_spec, late_spec, half_spec, half_spec],
+        functools.partial(finish_kernel, modes, taps, half, early_rows, late_rows),
+        (mine, other, value_done),
+        [whole_spec, whole_spec, any_spec],
         [
             jax.ShapeDtypeStruct(short_filter.shape, F32),
             jax.ShapeDtypeStruct(residues.shape, F32),

time: 127 us -> 112 us (0.88)
  starting transfers between devices: 35.8 us -> 23.8 us
  Pallas kernels: 58.3 us -> 54.3 us
  waiting for transfers between devices: 30.7 us -> 32.5 us
    ppermute x11 -> x2, starting transfers between devices: 25.5 us -> 6.49 us  [ring(): lax.ppermute(value, axis, [(i, (i + distance) % count) for i in range(cou...]
    ppermute x7 -> x13, waiting for transfers between devices: 15.8 us -> 25.8 us  [swap(): lax.ppermute(value, axis, [(i, i ^ step) for i in range(lax.axis_size(axi...]
    ppermute x11 -> x2, waiting for transfers between devices: 14.9 us -> 6.68 us  [ring(): lax.ppermute(value, axis, [(i, (i + distance) % count) for i in range(cou...]
    ppermute x7 -> x13, starting transfers between devices: 10.3 us -> 17.4 us  [swap(): lax.ppermute(value, axis, [(i, i ^ step) for i in range(lax.axis_size(axi...]
    pallas_call x14 -> x17, Pallas kernels: 57.4 us -> 52.9 us  [call(): pl.pallas_call(with_done, grid=(blocks,), in_specs=in_specs, out_specs=ou...]
  transfers between devices with their start and end apart: 18 -> 15, of which waited for: 8 -> 8; matrix products, arithmetic and copies ran while one was open for 0% -> 0% of each run, Pallas kernels for 36% -> 38%
where the time goes in v4:
time: 112 us; the launch traced here: 111 us
  Pallas kernels  54.3 us (48%)
  waiting for transfers between devices  32.5 us (29%)
  starting transfers between devices  23.8 us (21%)
    pallas_call x17, Pallas kernels, call(): pl.pallas_call(with_done, grid=(blocks,), in_specs=in_specs, out_specs=ou...  52.9 us
    ppermute x13, waiting for transfers between devices, swap(): lax.ppermute(value, axis, [(i, i ^ step) for i in range(lax.axis_size(axi...  25.8 us
    ppermute x13, starting transfers between devices, swap(): lax.ppermute(value, axis, [(i, i ^ step) for i in range(lax.axis_size(axi...  17.4 us
    ppermute x2, waiting for transfers between devices, ring(): lax.ppermute(value, axis, [(i, (i + distance) % count) for i in range(cou...  6.68 us
    ppermute x2, starting transfers between devices, ring(): lax.ppermute(value, axis, [(i, (i + distance) % count) for i in range(cou...  6.49 us
  transfers between devices with their start and end apart: 15, of which 8 were waited for; matrix products, arithmetic and copies ran while one was open for 0% of the time, Pallas kernels for 38%

profile of v4, /device:TPU:0, one launch (start us, length us, event | category | flops | bytes accessed | tf_op | source)
XLA Modules:
  0.0 111.5 jit_solution(7267834202773374083)
XLA Ops:
  0.6 0.9 trailing.1
  1.6 3.0 %collective-permute-start = (bf16[3,8,2048]{2,1,0:T(8,128)(2,1)S(1)}, bf16[3,8,2048]{2,1,0:T(8,128)(2,1)S(1)}, u32[]{:S(2)}, u32[]{:S(2)}) collective-permute-start(bf16[3,8,2048]{2,1,0:T(8,128)(2,1)S(1)} %trailing.1), channel_id=1, source_target_pairs={{0,4},{4,8},{8,12},{12,16},{16,20},{20,24},{24,28},{28,0},{1,5},{5... | collective-permute-start | bytes 294920 | tf_op jit(solution)/shard_map/ppermute | solution.py:539
  4.5 7.1 %features.1 = (f32[4224,128]{1,0:T(8,128)S(1)}, f32[4224,128]{1,0:T(8,128)S(1)}, f32[4096,128]{1,0:T(8,128)S(1)}, f32[4096,128]{1,0:T(8,128)S(1)}, f32[4096,128]...) custom-call(bf16[256,2048]{1,0:T(8,128)(2,1)} %refs_0_.3, ...), custom_call_target="tpu_custom_call" | custom-call | flops 33554432 | bytes 2097152 | tf_op jit(solution)/shard_map/features/pallas_call | solution.py:620
  12.4 1.5 %collective-permute-start.1 = (f32[256,128]{1,0:T(8,128)S(1)}, f32[256,128]{1,0:T(8,128)S(1)}, u32[]{:S(2)}, u32[]{:S(2)}) collective-permute-start(f32[256,128]{1,0:T(8,128)S(1)} %get-tuple-element.99.own), channel_id=1, source_target_pairs={{0,4},{4,0},{8,12},{12,8},{16,20},{20,16},{24,28},{28,24},{1,5},{5... | collective-permute-start | bytes 393224 | tf_op jit(solution)/shard_map/ppermute | solution.py:543
  13.9 2.5 %query.3 = (f32[4224,128]{1,0:T(8,128)S(1)}, f32[4096,128]{1,0:T(8,128)S(1)}, f32[8,128]{1,0:T(8,128)S(1)}) custom-call(bf16[256,2048]{1,0:T(8,128)(2,1)} %refs_0_.4, bf16[3,8,2048]{2,1,0:T(8,128)(2,1)S(1)} %collective-permute-done.refs_0_.refs_1_, f32[336,128]{1,0:T(8,128)S(1)} %get-tuple-element.85.refs_3_.refs_2_), custom_call_target="tpu_custom_call" | custom-call | flops 10485760 | bytes 2097152 | tf_op jit(solution)/shard_map/query/pallas_call | solution.py:620
  16.5 0.9 collective-permute-done.1.other
  17.5 1.6 %collective-permute-start.2 = (f32[256,128]{1,0:T(8,128)S(1)}, f32[256,128]{1,0:T(8,128)S(1)}, u32[]{:S(2)}, u32[]{:S(2)}) collective-permute-start(f32[256,128]{1,0:T(8,128)S(1)} %get-tuple-element.101.own), channel_id=1, source_target_pairs={{0,8},{4,12},{8,0},{12,4},{16,24},{20,28},{24,16},{28,20},{1,9},{5... | collective-permute-start | bytes 393224 | tf_op jit(solution)/shard_map/ppermute | solution.py:543
  19.1 2.0 %inputs.1 = (f32[4096,128]{1,0:T(8,128)S(1)}, f32[4096,128]{1,0:T(8,128)S(1)}, f32[8,128]{1,0:T(8,128)S(1)}) custom-call(bf16[256,2048]{1,0:T(8,128)(2,1)} %refs_0_.5, bf16[256,2048]{1,0:T(8,128)(2,1)} %refs_1_.3), custom_call_target="tpu_custom_call" | custom-call | flops 5242880 | bytes 2097152 | tf_op jit(solution)/shard_map/inputs/pallas_call | solution.py:620
  21.1 1.4 %collective-permute-done.2.other = f32[256,128]{1,0:T(8,128)S(1)} collective-permute-done((f32[256,128]{1,0:T(8,128)S(1)}, f32[256,128]{1,0:T(8,128)S(1)}, u32[]{:S(2)}, u32[]{:S(2)}) %collective-permute-start.2) | collective-permute-done | bytes 131104 | tf_op jit(solution)/shard_map/ppermute | solution.py:543
  22.6 2.7 %collective-permute-start.3 = (f32[256,128]{1,0:T(8,128)S(1)}, f32[256,128]{1,0:T(8,128)S(1)}, u32[]{:S(2)}, u32[]{:S(2)}) collective-permute-start(f32[256,128]{1,0:T(8,128)S(1)} %get-tuple-element.105), channel_id=1, source_target_pairs={{0,16},{4,20},{8,24},{12,28},{16,0},{20,4},{24,8},{28,12},{1,17},{... | collective-permute-start | bytes 393224 | tf_op jit(solution)/shard_map/ppermute | solution.py:543
  25.3 1.4 %near.1 = (f32[4096,128]{1,0:T(8,128)S(1)}, f32[8,128]{1,0:T(8,128)}) custom-call(f32[4096,128]{1,0:T(8,128)S(1)} %get-tuple-element.92.refs_0_.refs_1_, f32[256,128]{1,0:T(8,128)S(1)} %get-tuple-element.86.refs_4_.refs_1_.lam.refs_7_.refs_2_.refs_5_, f32[256,128]{1,0:T(8,128)S(1)} %get-tuple-element.93.refs_2_.refs_8_.refs_6_.res, f32[16,128]{1,0:T(8,128)S(1)} %bitcast.8), custom_call_target="tpu_custom_call" | custom-call | flops 5242880 | bytes 2097152 | tf_op jit(solution)/shard_map/near/pallas_call | solution.py:620
  26.7 3.2 %collective-permute-done.3.refs_6_ = f32[256,128]{1,0:T(8,128)S(1)} collective-permute-done((f32[256,128]{1,0:T(8,128)S(1)}, f32[256,128]{1,0:T(8,128)S(1)}, u32[]{:S(2)}, u32[]{:S(2)}) %collective-permute-start.3) | collective-permute-done | bytes 131104 | tf_op jit(solution)/shard_map/ppermute | solution.py:543
  29.9 4.8 %summed.1 = (f32[4096,128]{1,0:T(8,128)S(1)}, f32[4096,128]{1,0:T(8,128)S(1)}, f32[8192,128]{1,0:T(8,128)S(1)}, f32[2,256]{1,0:T(2,128)S(1)}, f32[8,128]{1,0:T(8,128)}) custom-call(f32[4096,128]{1,0:T(8,128)S(1)} %get-tuple-element.94.refs_0_, f32[4096,128]{1,0:T(8,128)S(1)} %get-tuple-element.95.refs_1_.refs_6_, f32[4096,128]{1,0:T(8,128)S(1)} %get-tuple-element.96.refs_2_, ...), custom_call_target="tpu_custom_call" | custom-call | flops 26214400 | bytes 2097152 | tf_op jit(solution)/shard_map/summed/pallas_call | solution.py:620
  34.7 1.6 %collective-permute-start.5 = (f32[2,256]{1,0:T(2,128)S(1)}, f32[2,256]{1,0:T(2,128)S(1)}, u32[]{:S(2)}, u32[]{:S(2)}) collective-permute-start(f32[2,256]{1,0:T(2,128)S(1)} %get-tuple-element.106.refs_0_), channel_id=1, source_target_pairs={{0,2},{1,3},{2,0},{3,1},{4,6},{5,7},{6,4},{7,5},{8,10},{9,11},{10,... | collective-permute-start | bytes 6152 | tf_op jit(solution)/shard_map/ppermute | solution.py:543
  36.5 4.0 %lags.1 = (f32[8192,128]{1,0:T(8,128)S(1)}, f32[256,128]{1,0:T(8,128)S(1)}, f32[8,128]{1,0:T(8,128)S(1)}) custom-call(f32[4096,128]{1,0:T(8,128)S(1)} %get-tuple-element.92.refs_0_.refs_1_, f32[8192,128]{1,0:T(8,128)S(1)} %get-tuple-element.108.refs_1_.refs_3_, f32[256,128]{1,0:T(8,128)S(1)} %get-tuple-element.86.refs_4_.refs_1_.lam.refs_7_.refs_2_.refs_5_), custom_call_target="tpu_custom_call" | custom-call | flops 16777216 | bytes 2097152 | tf_op jit(solution)/shard_map/lags/pallas_call | solution.py:620
  40.6 4.1 %grad_modal.1 = (f32[512,128]{1,0:T(8,128)S(1)}, f32[4096,128]{1,0:T(8,128)S(1)}, f32[8192,128]{1,0:T(8,128)S(1)}, f32[256,128]{1,0:T(8,128)S(1)}, f32[8,128]{1,0:T(8,128)}) custom-call(f32[2,256]{1,0:T(2,128)S(1)} %get-tuple-element.106.refs_0_, f32[2,256]{1,0:T(2,128)S(1)} %collective-permute-done.4.refs_1_, f32[2,256]{1,0:T(2,128)S(1)} %collective-permute-done.5.refs_2_, ...), custom_call_target="tpu_custom_call" | custom-call | flops 23592960 | bytes 2097152 | tf_op jit(solution)/shard_map/grad_modal/pallas_call | solution.py:620
  44.7 1.5 %collective-permute-start.7 = (f32[256,128]{1,0:T(8,128)S(1)}, f32[256,128]{1,0:T(8,128)S(1)}, u32[]{:S(2)}, u32[]{:S(2)}) collective-permute-start(f32[256,128]{1,0:T(8,128)S(1)} %get-tuple-element.125.own), channel_id=1, source_target_pairs={{0,4},{4,0},{8,12},{12,8},{16,20},{20,16},{24,28},{28,24},{1,5},{5... | collective-permute-start | bytes 393224 | tf_op jit(solution)/shard_map/ppermute | solution.py:543
  46.3 3.2 %norm.1 = (bf16[256,2048]{1,0:T(8,128)(2,1)}, bf16[256,2048]{1,0:T(8,128)(2,1)}, f32[16,128]{1,0:T(8,128)S(1)}, f32[8,128]{1,0:T(8,128)S(1)}) custom-call(f32[512,128]{1,0:T(8,128)S(1)} %get-tuple-element.110.refs_0_, f32[4096,128]{1,0:T(8,128)S(1)} %get-tuple-element.107.refs_4_.refs_1_, f32[4096,128]{1,0:T(8,128)S(1)} %get-tuple-element.97.refs_3_.refs_5_.refs_2_, ...), custom_call_target="tpu_custom_call" | custom-call | flops 13107200 | bytes 2097152 | tf_op jit(solution)/shard_map/norm/pallas_call | solution.py:620
  51.2 6.0 %own_adjoint.1 = (f32[4096,128]{1,0:T(8,128)S(1)}, f32[256,128]{1,0:T(8,128)S(1)}, f32[256,128]{1,0:T(8,128)S(1)}, f32[16,128]{1,0:T(8,128)S(1)}, f32[8,128]{1,0:T(8,128)S(1)}) custom-call(f32[4096,128]{1,0:T(8,128)S(1)} %get-tuple-element.115.refs_0_, f32[4096,128]{1,0:T(8,128)S(1)} %get-tuple-element.92.refs_0_.refs_1_, ...), custom_call_target="tpu_custom_call" | custom-call | flops 39321600 | bytes 2097152 | tf_op jit(solution)/shard_map/own_adjoint/pallas_call | solution.py:620
  57.4 3.4 %collective-permute-start.9 = (f32[256,128]{1,0:T(8,128)S(1)}, f32[256,128]{1,0:T(8,128)S(1)}, u32[]{:S(2)}, u32[]{:S(2)}) collective-permute-start(f32[256,128]{1,0:T(8,128)S(1)} %get-tuple-element.131), channel_id=1, source_target_pairs={{0,16},{4,20},{8,24},{12,28},{16,0},{20,4},{24,8},{28,12},{1,17},{... | collective-permute-start | bytes 393224 | tf_op jit(solution)/shard_map/ppermute | solution.py:543
  60.8 2.4 %query_sums.1 = (f32[4096,128]{1,0:T(8,128)S(1)}, f32[400,128]{1,0:T(8,128)S(1)}, f32[8,128]{1,0:T(8,128)}) custom-call(f32[512,128]{1,0:T(8,128)S(1)} %get-tuple-element.110.refs_0_, f32[4096,128]{1,0:T(8,128)S(1)} %get-tuple-element.107.refs_4_.refs_1_, f32[4096,128]{1,0:T(8,128)S(1)} %get-tuple-element.97.refs_3_.refs_5_.refs_2_, ...), custom_call_target="tpu_custom_call" | custom-call | flops 15728640 | bytes 2097152 | tf_op jit(solution)/shard_map/query_sums/pallas_call | solution.py:620
  63.2 3.1 %collective-permute-done.9.other = f32[256,128]{1,0:T(8,128)S(1)} collective-permute-done((f32[256,128]{1,0:T(8,128)S(1)}, f32[256,128]{1,0:T(8,128)S(1)}, u32[]{:S(2)}, u32[]{:S(2)}) %collective-permute-start.9) | collective-permute-done | bytes 131104 | tf_op jit(solution)/shard_map/ppermute | solution.py:543
  66.9 3.8 %mixed.1 = (f32[4096,128]{1,0:T(8,128)S(1)}, f32[4096,128]{1,0:T(8,128)S(1)}, f32[3,2,64,128]{3,2,1,0:T(8,128)S(1)}, f32[8,128]{1,0:T(8,128)}) custom-call(f32[4096,128]{1,0:T(8,128)S(1)} %get-tuple-element.122.refs_0_, f32[4096,128]{1,0:T(8,128)S(1)} %get-tuple-element.123.refs_1_, f32[4096,128]{1,0:T(8,128)S(1)} %get-tuple-element.124.refs_2_, ...), custom_call_target="tpu_custom_call" | custom-call | flops 23592960 | bytes 2097152 | tf_op jit(solution)/shard_map/mixed/pallas_call | solution.py:620
  70.7 2.2 %filter_sums.1 = (f32[224,128]{1,0:T(8,128)S(1)}, f32[8,128]{1,0:T(8,128)S(1)}) custom-call(f32[4096,128]{1,0:T(8,128)S(1)} %get-tuple-element.138.refs_0_, f32[4096,128]{1,0:T(8,128)S(1)} %get-tuple-element.140.refs_0_.refs_1_, f32[4224,128]{1,0:T(8,128)S(1)} %get-tuple-element.144.refs_2_, f32[4224,128]{1,0:T(8,128)S(1)} %get-tuple-element.145.refs_3_), custom_call_target="tpu_custom_call" | custom-call | flops 15728640 | bytes 2097152 | tf_op jit(solution)/shard_map/filter_sums/pallas_call | solution.py:620
  73.1 3.5 %collective-permute-start.10 = (f32[3,2,64,128]{3,2,1,0:T(8,128)S(1)}, f32[3,2,64,128]{3,2,1,0:T(8,128)S(1)}, u32[]{:S(2)}, u32[]{:S(2)}) collective-permute-start(f32[3,2,64,128]{3,2,1,0:T(8,128)S(1)} %get-tuple-element.136), channel_id=1, source_target_pairs={{0,28},{4,0},{8,4},{12,8},{16,12},{20,16},{24,20},{28,24},{1,29},{... | collective-permute-start | bytes 589832 | tf_op jit(solution)/shard_map/ppermute | solution.py:539
  76.6 6.7 %collective-permute-done.10.refs_1_ = f32[3,2,64,128]{3,2,1,0:T(8,128)S(1)} collective-permute-done((f32[3,2,64,128]{3,2,1,0:T(8,128)S(1)}, f32[3,2,64,128]{3,2,1,0:T(8,128)S(1)}, u32[]{:S(2)}, u32[]{:S(2)}) %collective-permute-start.10) | collective-permute-done | bytes 196640 | tf_op jit(solution)/shard_map/ppermute | solution.py:539
  83.3 2.6 %back_query.1 = (bf16[256,2048]{1,0:T(8,128)(2,1)}, f32[8,128]{1,0:T(8,128)S(1)}) custom-call(f32[4096,128]{1,0:T(8,128)S(1)} %get-tuple-element.121.refs_3_.refs_0_, f32[3,2,64,128]{3,2,1,0:T(8,128)S(1)} %collective-permute-done.10.refs_1_, f32[336,128]{1,0:T(8,128)S(1)} %get-tuple-element.85.refs_3_.refs_2_), custom_call_target="tpu_custom_call" | custom-call | flops 10485760 | bytes 2097152 | tf_op jit(solution)/shard_map/back_query/pallas_call | solution.py:620
  86.0 2.6 %back_key.1 = (bf16[256,2048]{1,0:T(8,128)(2,1)}, f32[8,128]{1,0:T(8,128)S(1)}) custom-call(f32[4096,128]{1,0:T(8,128)S(1)} %get-tuple-element.138.refs_0_, f32[3,2,64,128]{3,2,1,0:T(8,128)S(1)} %collective-permute-done.10.refs_1_, f32[336,128]{1,0:T(8,128)S(1)} %get-tuple-element.85.refs_3_.refs_2_), custom_call_target="tpu_custom_call" | custom-call | flops 10485760 | bytes 2097152 | tf_op jit(solution)/shard_map/back_key/pallas_call | solution.py:620
  88.5 12.0 %collective-permute-done.13.other = f32[552,128]{1,0:T(8,128)S(1)} collective-permute-done((f32[552,128]{1,0:T(8,128)S(1)}, f32[552,128]{1,0:T(8,128)S(1)}, u32[]{:S(2)}, u32[]{:S(2)}) %collective-permute-start.13) | collective-permute-done | bytes 282656 | tf_op jit(solution)/shard_map/ppermute | solution.py:543
  100.6 3.2 %collective-permute-start.14 = (f32[552,128]{1,0:T(8,128)S(1)}, f32[552,128]{1,0:T(8,128)S(1)}, u32[]{:S(2)}, u32[]{:S(2)}) collective-permute-start(f32[552,128]{1,0:T(8,128)S(1)} %add.3.refs_0_), channel_id=1, source_target_pairs={{0,4},{4,0},{8,12},{12,8},{16,20},{20,16},{24,28},{28,24},{1,5},{5... | collective-permute-start | bytes 847880 | tf_op jit(solution)/shard_map/ppermute | solution.py:543
  103.7 2.6 %back_value.1 = (bf16[256,2048]{1,0:T(8,128)(2,1)}, f32[8,128]{1,0:T(8,128)S(1)}) custom-call(f32[4096,128]{1,0:T(8,128)S(1)} %get-tuple-element.140.refs_0_.refs_1_, f32[3,2,64,128]{3,2,1,0:T(8,128)S(1)} %collective-permute-done.10.refs_1_, f32[336,128]{1,0:T(8,128)S(1)} %get-tuple-element.85.refs_3_.refs_2_), custom_call_target="tpu_custom_call" | custom-call | flops 10485760 | bytes 2097152 | tf_op jit(solution)/shard_map/back_value/pallas_call | solution.py:620
  106.3 4.4 %collective-permute-done.14.refs_1_ = f32[552,128]{1,0:T(8,128)S(1)} collective-permute-done((f32[552,128]{1,0:T(8,128)S(1)}, f32[552,128]{1,0:T(8,128)S(1)}, u32[]{:S(2)}, u32[]{:S(2)}) %collective-permute-start.14) | collective-permute-done | bytes 282656 | tf_op jit(solution)/shard_map/ppermute | solution.py:543
  (28 shorter events, 4.7 us)
Async XLA Ops:
  1.6 10.1 %collective-permute-start = (bf16[3,8,2048]{2,1,0:T(8,128)(2,1)S(1)}, bf16[3,8,2048]{2,1,0:T(8,128)(2,1)S(1)}, u32[]{:S(2)}, u32[]{:S(2)}) collective-permute-start(bf16[3,8,2048]{2,1,0:T(8,128)(2,1)S(1)} %trailing.1), channel_id=1, source_target_pairs={{0,4},{4,8},{8,12},{12,16},{16,20},{20,24},{24,28},{28,0},{1,5},{5... | collective-permute-start | bytes 294920 | tf_op jit(solution)/shard_map/ppermute | solution.py:539
  12.4 12.9 %copy-start.1 = (f32[2048]{0:T(1024)S(1)}, f32[2048]{0:T(1024)}, u32[]{:S(2)}) copy-start(f32[2048]{0:T(1024)} %param.17) | copy-start | bytes 24580
  12.4 5.0 %collective-permute-start.1 = (f32[256,128]{1,0:T(8,128)S(1)}, f32[256,128]{1,0:T(8,128)S(1)}, u32[]{:S(2)}, u32[]{:S(2)}) collective-permute-start(f32[256,128]{1,0:T(8,128)S(1)} %get-tuple-element.99.own), channel_id=1, source_target_pairs={{0,4},{4,0},{8,12},{12,8},{16,20},{20,16},{24,28},{28,24},{1,5},{5... | collective-permute-start | bytes 393224 | tf_op jit(solution)/shard_map/ppermute | solution.py:543
  17.4 12.5 %copy-start = (f32[2048]{0:T(1024)S(1)}, f32[2048]{0:T(1024)}, u32[]{:S(2)}) copy-start(f32[2048]{0:T(1024)} %param.18) | copy-start | bytes 24580
  17.5 5.0 %collective-permute-start.2 = (f32[256,128]{1,0:T(8,128)S(1)}, f32[256,128]{1,0:T(8,128)S(1)}, u32[]{:S(2)}, u32[]{:S(2)}) collective-permute-start(f32[256,128]{1,0:T(8,128)S(1)} %get-tuple-element.101.own), channel_id=1, source_target_pairs={{0,8},{4,12},{8,0},{12,4},{16,24},{20,28},{24,16},{28,20},{1,9},{5... | collective-permute-start | bytes 393224 | tf_op jit(solution)/shard_map/ppermute | solution.py:543
  22.6 7.3 %collective-permute-start.3 = (f32[256,128]{1,0:T(8,128)S(1)}, f32[256,128]{1,0:T(8,128)S(1)}, u32[]{:S(2)}, u32[]{:S(2)}) collective-permute-start(f32[256,128]{1,0:T(8,128)S(1)} %get-tuple-element.105), channel_id=1, source_target_pairs={{0,16},{4,20},{8,24},{12,28},{16,0},{20,4},{24,8},{28,12},{1,17},{... | collective-permute-start | bytes 393224 | tf_op jit(solution)/shard_map/ppermute | solution.py:543
  34.7 5.9 %collective-permute-start.6 = (f32[2,256]{1,0:T(2,128)S(1)}, f32[2,256]{1,0:T(2,128)S(1)}, u32[]{:S(2)}, u32[]{:S(2)}) collective-permute-start(f32[2,256]{1,0:T(2,128)S(1)} %get-tuple-element.106.refs_0_), channel_id=1, source_target_pairs={{0,3},{1,2},{2,1},{3,0},{4,7},{5,6},{6,5},{7,4},{8,11},{9,10},{10,... | collective-permute-start | bytes 6152 | tf_op jit(solution)/shard_map/ppermute | solution.py:543
  34.7 5.9 %collective-permute-start.5 = (f32[2,256]{1,0:T(2,128)S(1)}, f32[2,256]{1,0:T(2,128)S(1)}, u32[]{:S(2)}, u32[]{:S(2)}) collective-permute-start(f32[2,256]{1,0:T(2,128)S(1)} %get-tuple-element.106.refs_0_), channel_id=1, source_target_pairs={{0,2},{1,3},{2,0},{3,1},{4,6},{5,7},{6,4},{7,5},{8,10},{9,11},{10,... | collective-permute-start | bytes 6152 | tf_op jit(solution)/shard_map/ppermute | solution.py:543
  36.2 4.3 %collective-permute-start.4 = (f32[2,256]{1,0:T(2,128)S(1)}, f32[2,256]{1,0:T(2,128)S(1)}, u32[]{:S(2)}, u32[]{:S(2)}) collective-permute-start(f32[2,256]{1,0:T(2,128)S(1)} %get-tuple-element.106.refs_0_), channel_id=1, source_target_pairs={{0,1},{1,0},{2,3},{3,2},{4,5},{5,4},{6,7},{7,6},{8,9},{9,8},{10,11... | collective-permute-start | bytes 6152 | tf_op jit(solution)/shard_map/ppermute | solution.py:543
  44.7 5.6 %collective-permute-start.7 = (f32[256,128]{1,0:T(8,128)S(1)}, f32[256,128]{1,0:T(8,128)S(1)}, u32[]{:S(2)}, u32[]{:S(2)}) collective-permute-start(f32[256,128]{1,0:T(8,128)S(1)} %get-tuple-element.125.own), channel_id=1, source_target_pairs={{0,4},{4,0},{8,12},{12,8},{16,20},{20,16},{24,28},{28,24},{1,5},{5... | collective-permute-start | bytes 393224 | tf_op jit(solution)/shard_map/ppermute | solution.py:543
  50.4 6.8 %collective-permute-start.8 = (f32[256,128]{1,0:T(8,128)S(1)}, f32[256,128]{1,0:T(8,128)S(1)}, u32[]{:S(2)}, u32[]{:S(2)}) collective-permute-start(f32[256,128]{1,0:T(8,128)S(1)} %get-tuple-element.127.own), channel_id=1, source_target_pairs={{0,8},{4,12},{8,0},{12,4},{16,24},{20,28},{24,16},{28,20},{1,9},{5... | collective-permute-start | bytes 393224 | tf_op jit(solution)/shard_map/ppermute | solution.py:543
  57.4 9.0 %collective-permute-start.9 = (f32[256,128]{1,0:T(8,128)S(1)}, f32[256,128]{1,0:T(8,128)S(1)}, u32[]{:S(2)}, u32[]{:S(2)}) collective-permute-start(f32[256,128]{1,0:T(8,128)S(1)} %get-tuple-element.131), channel_id=1, source_target_pairs={{0,16},{4,20},{8,24},{12,28},{16,0},{20,4},{24,8},{28,12},{1,17},{... | collective-permute-start | bytes 393224 | tf_op jit(solution)/shard_map/ppermute | solution.py:543
  66.5 6.5 %collective-permute-start.11 = (f32[328,128]{1,0:T(8,128)S(1)}, f32[328,128]{1,0:T(8,128)S(1)}, u32[]{:S(2)}, u32[]{:S(2)}) collective-permute-start(f32[328,128]{1,0:T(8,128)S(1)} %get-tuple-element.143), channel_id=1, source_target_pairs={{0,4},{4,0},{8,12},{12,8},{16,20},{20,16},{24,28},{28,24},{1,5},{5... | collective-permute-start | bytes 503816 | tf_op jit(solution)/shard_map/ppermute | solution.py:543
  73.0 12.8 %collective-permute-start.12 = (f32[552,128]{1,0:T(8,128)S(1)}, f32[552,128]{1,0:T(8,128)S(1)}, u32[]{:S(2)}, u32[]{:S(2)}) collective-permute-start(f32[552,128]{1,0:T(8,128)S(1)} %gather.1.one), channel_id=1, source_target_pairs={{0,8},{4,12},{8,0},{12,4},{16,24},{20,28},{24,16},{28,20},{1,9},{5... | collective-permute-start | bytes 847880 | tf_op jit(solution)/shard_map/ppermute | solution.py:543
  73.1 10.2 %collective-permute-start.10 = (f32[3,2,64,128]{3,2,1,0:T(8,128)S(1)}, f32[3,2,64,128]{3,2,1,0:T(8,128)S(1)}, u32[]{:S(2)}, u32[]{:S(2)}) collective-permute-start(f32[3,2,64,128]{3,2,1,0:T(8,128)S(1)} %get-tuple-element.136), channel_id=1, source_target_pairs={{0,28},{4,0},{8,4},{12,8},{16,12},{20,16},{24,20},{28,24},{1,29},{... | collective-permute-start | bytes 589832 | tf_op jit(solution)/shard_map/ppermute | solution.py:539
  85.9 14.6 %collective-permute-start.13 = (f32[552,128]{1,0:T(8,128)S(1)}, f32[552,128]{1,0:T(8,128)S(1)}, u32[]{:S(2)}, u32[]{:S(2)}) collective-permute-start(f32[552,128]{1,0:T(8,128)S(1)} %add.2.one), channel_id=1, source_target_pairs={{0,16},{4,20},{8,24},{12,28},{16,0},{20,4},{24,8},{28,12},{1,17},{... | collective-permute-start | bytes 847880 | tf_op jit(solution)/shard_map/ppermute | solution.py:543
  100.6 10.1 %collective-permute-start.14 = (f32[552,128]{1,0:T(8,128)S(1)}, f32[552,128]{1,0:T(8,128)S(1)}, u32[]{:S(2)}, u32[]{:S(2)}) collective-permute-start(f32[552,128]{1,0:T(8,128)S(1)} %add.3.refs_0_), channel_id=1, source_target_pairs={{0,4},{4,0},{8,12},{12,8},{16,20},{20,16},{24,28},{28,24},{1,5},{5... | collective-permute-start | bytes 847880 | tf_op jit(solution)/shard_map/ppermute | solution.py:543

commit v5 on v4

--- a/solution.py
+++ b/solution.py
@@ -210,14 +210,26 @@
     loop(0, steps // SUB, some, 0)
 
 
-def lags_kernel(modes, steps, u, x_at, lam, lag, lag_sum):
-    fade, skip = fades(lam, modes, 1), fades(lam, modes, SUB)
+def lags_kernel(modes, steps, u, lam, lag):
+    fade = fades(lam, modes, 1)
+
+    def some(c, carry):
+        now = [row(u, c * SUB + i) * float(SUB - i) for i in range(SUB)]
+        for m in range(modes):
+            put(lag, c * modes + m, horner(fade[m], now))
+        return carry
+
+    loop(0, steps // SUB, some, 0)
+
+
+def borders_kernel(modes, steps, own_lag, x_at, lam, lag, lag_sum):
+    skip = fades(lam, modes, SUB)
+    eight = [float(SUB) * v for v in skip]
 
     def some(c, sums):
-        now = [row(u, c * SUB + i) * float(SUB - i) for i in range(SUB)]
         new = []
         for m in range(modes):
-            border = horner(fade[m], now) + float(SUB) * skip[m] * row(x_at, c * modes + m)
+            border = row(own_lag, c * modes + m) + eight[m] * row(x_at, c * modes + m)
             put(lag, c * modes + m, border)
             new.append(skip[m] * sums[m] + border)
         return tuple(new)
@@ -227,7 +239,8 @@
         put(lag_sum, m, sums[m])
 
 
-def summed_kernel(modes, steps, blocks, group, y, f0, res_pos, cot_pos, g, before, other, lam, res, gain, modal, summed, x_at, sums, squares, inner):
+def summed_kernel(modes, steps, blocks, group, y, f0, res_pos, cot_pos, g, before, other, lam, res, gain, ready, modal, summed, x_at, sums, squares, inner):
+    del ready
     block = pl.program_id(0)
 
     @pl.when(block == 0)
@@ -314,22 +327,9 @@
         put(a_out, m, a[m])
 
 
-def own_adjoint_kernel(modes, steps, gm, u, adj, x_at, lag, lam, res, skip, gmy, res_sum, rate_sum, skip_sum):
-    near = near_taps(lam, res, skip, modes)
+def across_kernel(modes, steps, gm, adj, x_at, lag, lam, res_part, rate_part):
     fade, far = fades(lam, modes, 1), fades(lam, modes, SUB)
     last = steps // SUB - 1
-
-    def pairs(c, lags):
-        now = [row(gm, c * SUB + i) for i in range(SUB)]
-        for i in range(SUB):
-            put(gmy, c * SUB + i, total([near[k] * now[i + k] for k in range(SUB - i)]))
-        before = [row(u, c * SUB + i) for i in range(SUB)]
-        return tuple(
-            lags[k] + total([now[i] * before[i - k] for i in range(k, SUB)]) for k in range(SUB)
-        )
-
-    lags = loop(0, steps // SUB, pairs, zeros(SUB))
-    skip_sum[...] = lags[0]
     half = modes // 2
     for part in range(2):
         ms = range(part * half, (part + 1) * half)
@@ -349,23 +349,42 @@
         none = zeros(half)
         _, by_res, by_rate = loop(0, steps // SUB, across, (none, none, none))
         for i, m in enumerate(ms):
-            put(res_sum, m, by_res[i] + horner(fade[m], lags[::-1]))
-            weighted = [lags[k] * float(k) for k in range(1, SUB)]
-            put(rate_sum, m, by_rate[i] + fade[m] * horner(fade[m], weighted[::-1]))
-
-
-def norm_kernel(steps, scale, summed, cot_pos, gain, normed, grad_res, gain_out, work):
+            put(res_part, m, by_res[i])
+            put(rate_part, m, by_rate[i])
+
+
+def near_adjoint_kernel(modes, steps, gm, u, lam, res, skip, res_part, rate_part, gmy, res_sum, rate_sum, skip_sum):
+    near = near_taps(lam, res, skip, modes)
+
+    def pairs(c, lags):
+        now = [row(gm, c * SUB + i) for i in range(SUB)]
+        for i in range(SUB):
+            put(gmy, c * SUB + i, total([near[k] * now[i + k] for k in range(SUB - i)]))
+        before = [row(u, c * SUB + i) for i in range(SUB)]
+        return tuple(
+            lags[k] + total([now[i] * before[i - k] for i in range(k, SUB)]) for k in range(SUB)
+        )
+
+    lags = loop(0, steps // SUB, pairs, zeros(SUB))
+    skip_sum[...] = lags[0]
+    fade = fades(lam, modes, 1)
+    weighted = [lags[k] * float(k) for k in range(1, SUB)]
+    for m in range(modes):
+        put(res_sum, m, row(res_part, m) + horner(fade[m], lags[::-1]))
+        put(rate_sum, m, row(rate_part, m) + fade[m] * horner(fade[m], weighted[::-1]))
+
+
+def norm_kernel(steps, scale, summed, cot_pos, gain, ready, normed, grad_res, work):
+    del ready
     factor = gain[...]
 
-    def norm(c, acc):
+    def norm(c, carry):
         for i in range(SUB):
             t = c * SUB + i
-            here = row(summed, t) * scale[pl.ds(t, 1), :]
-            put(work, t, here * factor)
-            acc = acc + row(cot_pos, t) * here
-        return acc
-
-    gain_out[...] = loop(0, steps // SUB, norm, zeros(1)[0])
+            put(work, t, row(summed, t) * scale[pl.ds(t, 1), :] * factor)
+        return carry
+
+    loop(0, steps // SUB, norm, 0)
     gather_rows(work, normed, steps)
 
     def grads(c, carry):
@@ -380,25 +399,25 @@
     gather_rows(work, grad_res, steps)
 
 
-def query_sums_kernel(modes, taps, steps, scale, summed, cot_pos, modal, q_ext, gain, res_sum, skip_sum, gain_sum, gf0, early):
+def query_sums_kernel(modes, taps, steps, scale, summed, cot_pos, modal, q_ext, gain, res_sum, skip_sum, gf0, early):
     factor = gain[...]
 
-    def grads(c, carry):
+    def grads(c, by_gain):
         for i in range(SUB):
             t = c * SUB + i
-            inv = scale[pl.ds(t, 1), :]
-            coef = scale[pl.ds(steps + t, 1), :]
-            grad = inv * (factor * row(cot_pos, t)) - coef * row(summed, t)
+            now, here = row(cot_pos, t), row(summed, t)
+            scaled = scale[pl.ds(t, 1), :] * now
+            grad = factor * scaled - scale[pl.ds(steps + t, 1), :] * here
             put(gf0, t, grad * row(modal, t))
-        return carry
-
-    loop(0, steps // SUB, grads, 0)
+            by_gain = by_gain + scaled * here
+        return by_gain
+
+    put(early, taps + modes + 1, loop(0, steps // SUB, grads, zeros(1)[0]))
     sums = filter_pass(taps, steps, gf0, q_ext)
     for j in range(taps):
         put(early, j, sums[j])
     early[pl.ds(taps * SUB, modes * SUB), :] = res_sum[...]
     put(early, taps + modes, skip_sum[...])
-    put(early, taps + modes + 1, gain_sum[...])
 
 
 def filter_pass(taps, steps, grad, ext):
@@ -414,19 +433,6 @@
 
     zero = jnp.zeros((SUB, LANES), F32)
     return loop(0, steps // SUB, some, tuple(zero for _ in range(taps)))
-
-
-def back_pass(taps, steps, grad, weights, out):
-    margin = taps - 1
-
-    def some(c, carry):
-        t0 = c * SUB
-        window = [row(grad, t0 + i) for i in range(SUB + margin)]
-        for i in range(SUB):
-            put(out, t0 + i, total([weights[j] * window[i + j] for j in range(taps)]))
-        return carry
-
-    loop(0, steps // SUB, some, 0)
 
 
 def mixed_kernel(modes, taps, steps, gmy, f1, f2, gf0, adj, lam, res, alpha, gf1, gf2, heads):
@@ -445,7 +451,7 @@
 
     loop(0, steps // SUB, advance, tuple(row(alpha, m) for m in range(modes)))
     for which, grad in enumerate((gf0, gf1, gf2)):
-        heads[which, 0] = grad[: SUB * SUB, :]
+        heads[which, 0] = grad[: SUB * SUB, :].astype(BF16)
 
 
 def filter_sums_kernel(taps, steps, gf1, gf2, k_ext, v_ext, sums):
@@ -455,12 +461,25 @@
             put(sums, which * taps + j, parts[j])
 
 
-def back_kernel(which, taps, steps, last, grad, next_head, filt, out, work, ext):
+def back_kernel(which, taps, steps, last, grad, next_head, filt, out, work, head):
     there = jnp.where(lax.axis_index("ctx") < last, 1.0, 0.0)
-    ext[pl.ds(0, steps * SUB), :] = grad[...]
-    ext[pl.ds(steps * SUB, SUB * SUB), :] = next_head[which, 0] * there
-    back_pass(taps, steps, ext, taps_of(filt, which, taps), work)
+    head[...] = next_head[which, 0].astype(F32) * there
+    weights = taps_of(filt, which, taps)
+
+    def some(c, carry):
+        put_back(work, c * SUB, weights, [row(grad, c * SUB + i) for i in range(SUB + taps - 1)])
+        return carry
+
+    loop(0, steps // SUB - 1, some, 0)
+    start = steps - SUB
+    window = [row(grad, start + i) for i in range(SUB)] + [row(head, i) for i in range(taps - 1)]
+    put_back(work, start, weights, window)
     gather_rows(work, out, steps)
+
+
+def put_back(out, start, weights, window):
+    for i in range(SUB):
+        put(out, start + i, total([w * window[i + j] for j, w in enumerate(weights)]))
 
 
 def place(group, sign):
@@ -489,15 +508,8 @@
     ends[1][...] = inclusive(own[...], other[...], lam[...], span, group, sign)
 
 
-def add_kernel(one, other, after, out):
-    del after
-    out[...] = one[...] + other[...]
-
-
-def gather_kernel(early_rows, kept, other, late, after, out):
-    del after
-    out[:early_rows, :] = kept[...] + other[...]
-    out[early_rows:, :] = late[...]
+def add_kernel(one, other, *refs):
+    refs[-1][...] = one[...] + other[...]
 
 
 def pack_kernel(span, group, modes, first_rows, half, before, other, lam, early, res, rate_sum, lag_sum, alpha, kept, sent):
@@ -514,15 +526,12 @@
             out[pl.ds(b * rows + first_rows * SUB, modes * SUB), :] = -res[mine, :] * lagged
 
 
-def finish_kernel(modes, taps, half, early_rows, late_rows, mine, other, after, short, res, rate, skip, gain, late, early):
+def finish_kernel(modes, taps, half, early_rows, mine, other, late_mine, late_other, after, short, res, rate, skip, gain, late, early):
     del after
     block = pl.program_id(0)
-    at = pl.multiple_of((half * early_rows + block * late_rows) * SUB, SUB)
-    late[...] = mine[pl.ds(at, late_rows * SUB), :] + other[pl.ds(at, late_rows * SUB), :]
+    late[...] = late_mine[...] + late_other[...]
     own = jnp.where(lax.axis_index("ctx") % 2 == block // half, 1.0, 0.0)
-    at = pl.multiple_of((block % half) * (early_rows * SUB), SUB)
-    here = pl.ds(at, early_rows * SUB)
-    early[...] = own * mine[here, :] + (1.0 - own) * other[here, :]
+    early[...] = own * mine[...] + (1.0 - own) * other[...]
     for s in range(SUB):
         lanes = slice(s * LANES, (s + 1) * LANES)
         short[0, :, lanes] = early[pl.ds(s, taps, stride=SUB), :]
@@ -701,11 +710,20 @@
         10,
         "near",
     )
+    own_lag, own_lag_done = call(
+        functools.partial(lags_kernel, modes, steps),
+        (u, lam),
+        [seq_spec, mode_spec],
+        [eights],
+        [eights_spec],
+        32,
+        "lags",
+    )
     before, other, group = scan_but_last(x_own, lam, steps, 1, [query_done, inputs_done])
     modal, summed, x_at, sums, _ = call(
         functools.partial(summed_kernel, modes, steps, blocks, group),
-        (y, f0, res_pos, cot_pos, g, before, other, lam, res, gain),
-        [seq_spec] * 4 + [eights_spec] + [mode_spec] * 4 + [one_spec],
+        (y, f0, res_pos, cot_pos, g, before, other, lam, res, gain, own_lag_done),
+        [seq_spec] * 4 + [eights_spec] + [mode_spec] * 4 + [one_spec, any_spec],
         [seq, seq, eights, jax.ShapeDtypeStruct((2, steps), F32)],
         [seq_spec, seq_spec, eights_spec, pl.BlockSpec((2, steps), lambda h: (0, 0))],
         50,
@@ -714,13 +732,13 @@
     )
     all_sums = [sums, *(swap(sums, "tp", k) for k in range(1, lax.axis_size("tp")))]
     lag, lag_sum, lags_done = call(
-        functools.partial(lags_kernel, modes, steps),
-        (u, x_at, lam),
-        [seq_spec, eights_spec, mode_spec],
+        functools.partial(borders_kernel, modes, steps),
+        (own_lag, x_at, lam),
+        [eights_spec, eights_spec, mode_spec],
         [eights, mode],
         [eights_spec, mode_spec],
-        32,
-        "lags",
+        8,
+        "borders",
     )
     scale_spec = pl.BlockSpec((2 * steps, LANES), lambda h: (0, 0))
     scale, gm, adj, a_own, _ = call(
@@ -733,36 +751,35 @@
         45,
         "grad_modal",
     )
-    normed, grad_residual, gain_sum, norm_done = call(
-        functools.partial(norm_kernel, steps),
-        (scale, summed, cot_pos, gain),
-        [scale_spec, seq_spec, seq_spec, one_spec],
-        [wide, wide, one],
-        [wide_spec, wide_spec, one_spec],
-        25,
-        "norm",
-        scratch=[pltpu.VMEM((steps * SUB, LANES), F32)],
-    )
-    gmy, res_sum, rate_sum, skip_sum, adjoint_done = call(
-        functools.partial(own_adjoint_kernel, modes, steps),
-        (gm, u, adj, x_at, lag, lam, res, skip),
-        [seq_spec, seq_spec, eights_spec, eights_spec, eights_spec, mode_spec, mode_spec, one_spec],
+    res_part, rate_part, across_done = call(
+        functools.partial(across_kernel, modes, steps),
+        (gm, adj, x_at, lag, lam),
+        [seq_spec, eights_spec, eights_spec, eights_spec, mode_spec],
+        [mode, mode],
+        [mode_spec, mode_spec],
+        50,
+        "across",
+    )
+    gmy, res_sum, rate_sum, skip_sum, near_done = call(
+        functools.partial(near_adjoint_kernel, modes, steps),
+        (gm, u, lam, res, skip, res_part, rate_part),
+        [seq_spec, seq_spec, mode_spec, mode_spec, one_spec, mode_spec, mode_spec],
         [seq, mode, mode, one],
         [seq_spec, mode_spec, mode_spec, one_spec],
-        75,
-        "own_adjoint",
+        25,
+        "near_adjoint",
     )
     early_rows = taps + modes + 2
     gf0, early, _ = call(
         functools.partial(query_sums_kernel, modes, taps, steps),
-        (scale, summed, cot_pos, modal, q_ext, gain, res_sum, skip_sum, gain_sum),
-        [scale_spec, seq_spec, seq_spec, seq_spec, ext_spec, one_spec, mode_spec, one_spec, one_spec],
+        (scale, summed, cot_pos, modal, q_ext, gain, res_sum, skip_sum),
+        [scale_spec, seq_spec, seq_spec, seq_spec, ext_spec, one_spec, mode_spec, one_spec],
         [seq, pos(early_rows)],
         [seq_spec, pos_spec(early_rows)],
         30,
         "query_sums",
     )
-    before, other, group = scan_but_last(a_own, lam, steps, -1, [norm_done, adjoint_done])
+    before, other, group = scan_but_last(a_own, lam, steps, -1, [across_done, near_done])
 
     half = blocks // 2
     half_shape = (half * (early_rows + modes) * SUB, LANES)
@@ -777,11 +794,11 @@
     late_rows = 2 * taps
     next_spec = pl.BlockSpec((3, 1, SUB * SUB, LANES), lambda h: (0, h, 0, 0))
     other_half = swap(sent_half, "ctx", 1)
-    gf1, gf2, heads, _ = call(
+    gf1, gf2, heads, mixed_done = call(
         functools.partial(mixed_kernel, modes, taps, steps),
         (gmy, f1, f2, gf0, adj, lam, res, alpha),
         [seq_spec] * 4 + [eights_spec] + [mode_spec] * 3,
-        [seq, seq, jax.ShapeDtypeStruct((3, blocks, SUB * SUB, LANES), F32)],
+        [seq, seq, jax.ShapeDtypeStruct((3, blocks, SUB * SUB, LANES), BF16)],
         [seq_spec, seq_spec, next_spec],
         45,
         "mixed",
@@ -795,6 +812,17 @@
         [pos_spec(late_rows)],
         30,
         "filter_sums",
+    )
+
+    normed, grad_residual, norm_done = call(
+        functools.partial(norm_kernel, steps),
+        (scale, summed, cot_pos, gain, late_done),
+        [scale_spec, seq_spec, seq_spec, one_spec, any_spec],
+        [wide, wide],
+        [wide_spec, wide_spec],
+        25,
+        "norm",
+        scratch=[pltpu.VMEM((steps * SUB, LANES), F32)],
     )
 
     def back(which, grad, name):
@@ -808,32 +836,34 @@
             name,
             scratch=[
                 pltpu.VMEM((steps * SUB, LANES), F32),
-                pltpu.VMEM(((steps + SUB) * SUB, LANES), F32),
+                pltpu.VMEM((SUB * SUB, LANES), F32),
             ],
         )
 
     grad_query, query_done = back(0, gf0, "back_query")
     grad_key, key_done = back(1, gf1, "back_key")
     grad_value, value_done = back(2, gf2, "back_value")
-    both_shape = (half_shape[0] + late.shape[0], LANES)
-    mine = small(
-        functools.partial(gather_kernel, half_shape[0]),
-        [kept_half, other_half, late],
-        [late_done],
-        [both_shape],
-        "gather",
-    )[0]
-    step, under = 2, [query_done, key_done]
-    while step < lax.axis_size("ctx"):
-        after = under.pop(0) if under else late_done
-        mine = small(add_kernel, [mine, swap(mine, "ctx", step)], [after], [both_shape], "add")[0]
+    count, under = lax.axis_size("ctx"), [[late_done, next_head], [norm_done, query_done]]
+    mine = small(add_kernel, [kept_half, other_half], [mixed_done], [half_shape], "add")[0]
+    step = 2
+    while step < count:
+        after = under.pop(0) if under else [query_done]
+        mine = small(add_kernel, [mine, swap(mine, "ctx", step)], after, [half_shape], "add")[0]
         step *= 2
     other = swap(mine, "ctx", 1)
-    whole_spec = pl.BlockSpec(memory_space=pltpu.VMEM)
+    step, under = 1, [[norm_done, query_done], [key_done]]
+    late_other = swap(late, "ctx", step)
+    while 2 * step < count:
+        after = under.pop(0) if under else [key_done]
+        late = small(add_kernel, [late, late_other], after, [late.shape], "add")[0]
+        step *= 2
+        late_other = swap(late, "ctx", step)
+    half_spec = pl.BlockSpec((early_rows * SUB, LANES), lambda h: (h % half, 0))
+    late_spec = pos_spec(late_rows)
     grad_short, grad_residues, grad_rate, grad_skip, grad_gain, _ = call(
-        functools.partial(finish_kernel, modes, taps, half, early_rows, late_rows),
-        (mine, other, value_done),
-        [whole_spec, whole_spec, any_spec],
+        functools.partial(finish_kernel, modes, taps, half, early_rows),
+        (mine, other, late, late_other, value_done),
+        [half_spec, half_spec, late_spec, late_spec, any_spec],
         [
             jax.ShapeDtypeStruct(short_filter.shape, F32),
             jax.ShapeDtypeStruct(residues.shape, F32),

time: 112 us -> 97.6 us (0.87)
  waiting for transfers between devices: 32.5 us -> 18.7 us
  Pallas kernels: 54.3 us -> 52.4 us
  starting transfers between devices: 23.8 us -> 25.3 us
    ppermute x13 -> x16, waiting for transfers between devices: 25.8 us -> 18.7 us  [swap(): lax.ppermute(value, axis, [(i, i ^ step) for i in range(lax.axis_size(axi...]
    ppermute x2, waiting for transfers between devices: 6.68 us -> 0.01 us  [ring(): lax.ppermute(value, axis, [(i, (i + distance) % count) for i in range(cou...]
    pallas_call x17 -> x19, Pallas kernels: 52.9 us -> 51 us  [call(): pl.pallas_call(with_done, grid=(blocks,), in_specs=in_specs, out_specs=ou...]
    ppermute x13 -> x16, starting transfers between devices: 17.4 us -> 18.4 us  [swap(): lax.ppermute(value, axis, [(i, i ^ step) for i in range(lax.axis_size(axi...]
  transfers between devices with their start and end apart: 15 -> 18, of which waited for: 8 -> 10; matrix products, arithmetic and copies ran while one was open for 0% -> 0% of each run, Pallas kernels for 38% -> 42%
where the time goes in v5:
time: 97.6 us; the launch traced here: 97.3 us
  Pallas kernels  52.4 us (54%)
  starting transfers between devices  25.3 us (26%)
  waiting for transfers between devices  18.7 us (19%)
    pallas_call x19, Pallas kernels, call(): pl.pallas_call(with_done, grid=(blocks,), in_specs=in_specs, out_specs=ou...  51 us
    ppermute x16, waiting for transfers between devices, swap(): lax.ppermute(value, axis, [(i, i ^ step) for i in range(lax.axis_size(axi...  18.7 us
    ppermute x16, starting transfers between devices, swap(): lax.ppermute(value, axis, [(i, i ^ step) for i in range(lax.axis_size(axi...  18.4 us
    ppermute x2, starting transfers between devices, ring(): lax.ppermute(value, axis, [(i, (i + distance) % count) for i in range(cou...  6.93 us
  transfers between devices with their start and end apart: 18, of which 10 were waited for; matrix products, arithmetic and copies ran while one was open for 0% of the time, Pallas kernels for 42%

profile of v5, /device:TPU:0, one launch (start us, length us, event | category | flops | bytes accessed | tf_op | source)
XLA Modules:
  0.0 97.3 jit_solution(1129542740720557878)
XLA Ops:
  1.6 3.0 %collective-permute-start = (bf16[3,8,2048]{2,1,0:T(8,128)(2,1)S(1)}, bf16[3,8,2048]{2,1,0:T(8,128)(2,1)S(1)}, u32[]{:S(2)}, u32[]{:S(2)}) collective-permute-start(bf16[3,8,2048]{2,1,0:T(8,128)(2,1)S(1)} %trailing.1), channel_id=1, source_target_pairs={{0,4},{4,8},{8,12},{12,16},{16,20},{20,24},{24,28},{28,0},{1,5},{5... | collective-permute-start | bytes 294920 | tf_op jit(solution)/shard_map/ppermute | solution.py:548
  4.5 7.1 %features.1 = (f32[4224,128]{1,0:T(8,128)S(1)}, f32[4224,128]{1,0:T(8,128)S(1)}, f32[4096,128]{1,0:T(8,128)S(1)}, f32[4096,128]{1,0:T(8,128)S(1)}, f32[4096,128]...) custom-call(bf16[256,2048]{1,0:T(8,128)(2,1)} %refs_0_.3, ...), custom_call_target="tpu_custom_call" | custom-call | flops 33554432 | bytes 2097152 | tf_op jit(solution)/shard_map/features/pallas_call | solution.py:629
  12.4 1.5 %collective-permute-start.1 = (f32[256,128]{1,0:T(8,128)S(1)}, f32[256,128]{1,0:T(8,128)S(1)}, u32[]{:S(2)}, u32[]{:S(2)}) collective-permute-start(f32[256,128]{1,0:T(8,128)S(1)} %get-tuple-element.104.own), channel_id=1, source_target_pairs={{0,4},{4,0},{8,12},{12,8},{16,20},{20,16},{24,28},{28,24},{1,5},{5... | collective-permute-start | bytes 393224 | tf_op jit(solution)/shard_map/ppermute | solution.py:552
  14.0 2.5 %query.3 = (f32[4224,128]{1,0:T(8,128)S(1)}, f32[4096,128]{1,0:T(8,128)S(1)}, f32[8,128]{1,0:T(8,128)S(1)}) custom-call(bf16[256,2048]{1,0:T(8,128)(2,1)} %refs_0_.4, bf16[3,8,2048]{2,1,0:T(8,128)(2,1)S(1)} %collective-permute-done.refs_0_.refs_1_, f32[336,128]{1,0:T(8,128)S(1)} %get-tuple-element.90.refs_3_.refs_2_), custom_call_target="tpu_custom_call" | custom-call | flops 10485760 | bytes 2097152 | tf_op jit(solution)/shard_map/query/pallas_call | solution.py:629
  17.4 1.6 %collective-permute-start.2 = (f32[256,128]{1,0:T(8,128)S(1)}, f32[256,128]{1,0:T(8,128)S(1)}, u32[]{:S(2)}, u32[]{:S(2)}) collective-permute-start(f32[256,128]{1,0:T(8,128)S(1)} %get-tuple-element.106.own), channel_id=1, source_target_pairs={{0,8},{4,12},{8,0},{12,4},{16,24},{20,28},{24,16},{28,20},{1,9},{5... | collective-permute-start | bytes 393224 | tf_op jit(solution)/shard_map/ppermute | solution.py:552
  19.1 2.0 %inputs.1 = (f32[4096,128]{1,0:T(8,128)S(1)}, f32[4096,128]{1,0:T(8,128)S(1)}, f32[8,128]{1,0:T(8,128)S(1)}) custom-call(bf16[256,2048]{1,0:T(8,128)(2,1)} %refs_0_.5, bf16[256,2048]{1,0:T(8,128)(2,1)} %refs_1_.3), custom_call_target="tpu_custom_call" | custom-call | flops 5242880 | bytes 2097152 | tf_op jit(solution)/shard_map/inputs/pallas_call | solution.py:629
  21.1 1.4 %collective-permute-done.2.other = f32[256,128]{1,0:T(8,128)S(1)} collective-permute-done((f32[256,128]{1,0:T(8,128)S(1)}, f32[256,128]{1,0:T(8,128)S(1)}, u32[]{:S(2)}, u32[]{:S(2)}) %collective-permute-start.2) | collective-permute-done | bytes 131104 | tf_op jit(solution)/shard_map/ppermute | solution.py:552
  22.6 2.7 %collective-permute-start.3 = (f32[256,128]{1,0:T(8,128)S(1)}, f32[256,128]{1,0:T(8,128)S(1)}, u32[]{:S(2)}, u32[]{:S(2)}) collective-permute-start(f32[256,128]{1,0:T(8,128)S(1)} %get-tuple-element.110), channel_id=1, source_target_pairs={{0,16},{4,20},{8,24},{12,28},{16,0},{20,4},{24,8},{28,12},{1,17},{... | collective-permute-start | bytes 393224 | tf_op jit(solution)/shard_map/ppermute | solution.py:552
  25.3 1.4 %near.1 = (f32[4096,128]{1,0:T(8,128)S(1)}, f32[8,128]{1,0:T(8,128)}) custom-call(f32[4096,128]{1,0:T(8,128)S(1)} %get-tuple-element.97.refs_0_.refs_1_, f32[256,128]{1,0:T(8,128)S(1)} %get-tuple-element.91.refs_4_.refs_1_.lam.refs_7_.refs_2_.refs_5_, f32[256,128]{1,0:T(8,128)S(1)} %get-tuple-element.98.refs_2_.refs_8_.refs_3_.res.refs_6_, f32[16,128]{1,0:T(8,128)S(1)} %bitcast.8), custom_call_target="tpu_custom_call" | custom-call | flops 5242880 | bytes 2097152 | tf_op jit(solution)/shard_map/near/pallas_call | solution.py:629
  26.7 2.2 %lags.1 = (f32[8192,128]{1,0:T(8,128)S(1)}, f32[8,128]{1,0:T(8,128)S(1)}) custom-call(f32[4096,128]{1,0:T(8,128)S(1)} %get-tuple-element.97.refs_0_.refs_1_, f32[256,128]{1,0:T(8,128)S(1)} %get-tuple-element.91.refs_4_.refs_1_.lam.refs_7_.refs_2_.refs_5_), custom_call_target="tpu_custom_call" | custom-call | flops 16777216 | bytes 2097152 | tf_op jit(solution)/shard_map/lags/pallas_call | solution.py:629
  29.9 4.9 %summed.1 = (f32[4096,128]{1,0:T(8,128)S(1)}, f32[4096,128]{1,0:T(8,128)S(1)}, f32[8192,128]{1,0:T(8,128)S(1)}, f32[2,256]{1,0:T(2,128)S(1)}, f32[8,128]{1,0:T(8,128)}) custom-call(f32[4096,128]{1,0:T(8,128)S(1)} %get-tuple-element.99.refs_0_, f32[4096,128]{1,0:T(8,128)S(1)} %get-tuple-element.100.refs_1_.refs_6_, ...), custom_call_target="tpu_custom_call" | custom-call | flops 26214400 | bytes 2097152 | tf_op jit(solution)/shard_map/summed/pallas_call | solution.py:629
  34.8 1.6 %collective-permute-start.5 = (f32[2,256]{1,0:T(2,128)S(1)}, f32[2,256]{1,0:T(2,128)S(1)}, u32[]{:S(2)}, u32[]{:S(2)}) collective-permute-start(f32[2,256]{1,0:T(2,128)S(1)} %get-tuple-element.112.refs_0_), channel_id=1, source_target_pairs={{0,2},{1,3},{2,0},{3,1},{4,6},{5,7},{6,4},{7,5},{8,10},{9,11},{10,... | collective-permute-start | bytes 6152 | tf_op jit(solution)/shard_map/ppermute | solution.py:552
  38.5 4.1 %grad_modal.1 = (f32[512,128]{1,0:T(8,128)S(1)}, f32[4096,128]{1,0:T(8,128)S(1)}, f32[8192,128]{1,0:T(8,128)S(1)}, f32[256,128]{1,0:T(8,128)S(1)}, f32[8,128]{1,0:T(8,128)}) custom-call(f32[2,256]{1,0:T(2,128)S(1)} %get-tuple-element.112.refs_0_, f32[2,256]{1,0:T(2,128)S(1)} %collective-permute-done.4.refs_1_, f32[2,256]{1,0:T(2,128)S(1)} %collective-permute-done.5.refs_2_, ...), custom_call_target="tpu_custom_call" | custom-call | flops 23592960 | bytes 2097152 | tf_op jit(solution)/shard_map/grad_modal/pallas_call | solution.py:629
  42.5 1.5 %collective-permute-start.7 = (f32[256,128]{1,0:T(8,128)S(1)}, f32[256,128]{1,0:T(8,128)S(1)}, u32[]{:S(2)}, u32[]{:S(2)}) collective-permute-start(f32[256,128]{1,0:T(8,128)S(1)} %get-tuple-element.131.own), channel_id=1, source_target_pairs={{0,4},{4,0},{8,12},{12,8},{16,20},{20,16},{24,28},{28,24},{1,5},{5... | collective-permute-start | bytes 393224 | tf_op jit(solution)/shard_map/ppermute | solution.py:552
  44.1 4.7 %across.1 = (f32[256,128]{1,0:T(8,128)S(1)}, f32[256,128]{1,0:T(8,128)S(1)}, f32[8,128]{1,0:T(8,128)S(1)}) custom-call(f32[4096,128]{1,0:T(8,128)S(1)} %get-tuple-element.118.refs_0_, f32[8192,128]{1,0:T(8,128)S(1)} %get-tuple-element.119.refs_1_.refs_4_, f32[8192,128]{1,0:T(8,128)S(1)} %get-tuple-element.115.refs_1_.refs_2_, ...), custom_call_target="tpu_custom_call" | custom-call | flops 26214400 | bytes 2097152 | tf_op jit(solution)/shard_map/across/pallas_call | solution.py:629
  49.3 1.5 %near_adjoint.1 = (f32[4096,128]{1,0:T(8,128)S(1)}, f32[256,128]{1,0:T(8,128)S(1)}, f32[256,128]{1,0:T(8,128)S(1)}, f32[16,128]{1,0:T(8,128)S(1)}, f32[8,128]{1,0:T(8,128)S(1)}) custom-call(f32[4096,128]{1,0:T(8,128)S(1)} %get-tuple-element.118.refs_0_, f32[4096,128]{1,0:T(8,128)S(1)} %get-tuple-element.97.refs_0_.refs_1_, ...), custom_call_target="tpu_custom_call" | custom-call | flops 13107200 | bytes 2097152 | tf_op jit(solution)/shard_map/near_adjoint/pallas_call | solution.py:629
  50.8 3.7 %collective-permute-done.8.other = f32[256,128]{1,0:T(8,128)S(1)} collective-permute-done((f32[256,128]{1,0:T(8,128)S(1)}, f32[256,128]{1,0:T(8,128)S(1)}, u32[]{:S(2)}, u32[]{:S(2)}) %collective-permute-start.8) | collective-permute-done | bytes 131104 | tf_op jit(solution)/shard_map/ppermute | solution.py:552
  54.6 1.5 %collective-permute-start.9 = (f32[256,128]{1,0:T(8,128)S(1)}, f32[256,128]{1,0:T(8,128)S(1)}, u32[]{:S(2)}, u32[]{:S(2)}) collective-permute-start(f32[256,128]{1,0:T(8,128)S(1)} %get-tuple-element.137), channel_id=1, source_target_pairs={{0,16},{4,20},{8,24},{12,28},{16,0},{20,4},{24,8},{28,12},{1,17},{... | collective-permute-start | bytes 393224 | tf_op jit(solution)/shard_map/ppermute | solution.py:552
  56.1 2.5 %query_sums.1 = (f32[4096,128]{1,0:T(8,128)S(1)}, f32[400,128]{1,0:T(8,128)S(1)}, f32[8,128]{1,0:T(8,128)}) custom-call(f32[512,128]{1,0:T(8,128)S(1)} %get-tuple-element.117.refs_0_, f32[4096,128]{1,0:T(8,128)S(1)} %get-tuple-element.113.refs_4_.refs_1_, f32[4096,128]{1,0:T(8,128)S(1)} %get-tuple-element.102.refs_3_.refs_5_.refs_2_, ...), custom_call_target="tpu_custom_call" | custom-call | flops 15728640 | bytes 2097152 | tf_op jit(solution)/shard_map/query_sums/pallas_call | solution.py:629
  58.7 4.2 %collective-permute-done.9.other = f32[256,128]{1,0:T(8,128)S(1)} collective-permute-done((f32[256,128]{1,0:T(8,128)S(1)}, f32[256,128]{1,0:T(8,128)S(1)}, u32[]{:S(2)}, u32[]{:S(2)}) %collective-permute-start.9) | collective-permute-done | bytes 131104 | tf_op jit(solution)/shard_map/ppermute | solution.py:552
  63.9 3.4 %mixed.1 = (f32[4096,128]{1,0:T(8,128)S(1)}, f32[4096,128]{1,0:T(8,128)S(1)}, bf16[3,2,64,128]{3,2,1,0:T(8,128)(2,1)S(1)}, f32[8,128]{1,0:T(8,128)S(1)}) custom-call(f32[4096,128]{1,0:T(8,128)S(1)} %get-tuple-element.123.refs_0_, f32[4096,128]{1,0:T(8,128)S(1)} %get-tuple-element.124.refs_1_, f32[4096,128]{1,0:T(8,128)S(1)} %get-tuple-element.125.refs_2_, ...), custom_call_target="tpu_custom_call" | custom-call | flops 23592960 | bytes 2097152 | tf_op jit(solution)/shard_map/mixed/pallas_call | solution.py:629
  67.3 1.8 %collective-permute-done.11.other = f32[328,128]{1,0:T(8,128)S(1)} collective-permute-done((f32[328,128]{1,0:T(8,128)S(1)}, f32[328,128]{1,0:T(8,128)S(1)}, u32[]{:S(2)}, u32[]{:S(2)}) %collective-permute-start.11) | collective-permute-done | bytes 167968 | tf_op jit(solution)/shard_map/ppermute | solution.py:552
  69.1 4.0 %collective-permute-start.10 = (bf16[3,2,64,128]{3,2,1,0:T(8,128)(2,1)S(1)}, bf16[3,2,64,128]{3,2,1,0:T(8,128)(2,1)S(1)}, u32[]{:S(2)}, u32[]{:S(2)}) collective-permute-start(bf16[3,2,64,128]{3,2,1,0:T(8,128)(2,1)S(1)} %get-tuple-element.149), channel_id=1, source_target_pairs={{0,28},{4,0},{8,4},{12,8},{16,12},{20,16},{24,20},{28,24},{1,29},{... | collective-permute-start | bytes 294920 | tf_op jit(solution)/shard_map/ppermute | solution.py:548
  73.1 2.2 %filter_sums.1 = (f32[224,128]{1,0:T(8,128)S(1)}, f32[8,128]{1,0:T(8,128)S(1)}) custom-call(f32[4096,128]{1,0:T(8,128)S(1)} %get-tuple-element.142.refs_0_, f32[4096,128]{1,0:T(8,128)S(1)} %get-tuple-element.143.refs_1_.refs_0_, f32[4224,128]{1,0:T(8,128)S(1)} %get-tuple-element.144.refs_2_, f32[4224,128]{1,0:T(8,128)S(1)} %get-tuple-element.145.refs_3_), custom_call_target="tpu_custom_call" | custom-call | flops 15728640 | bytes 2097152 | tf_op jit(solution)/shard_map/filter_sums/pallas_call | solution.py:629
  75.5 2.3 %collective-permute-start.13 = (f32[328,128]{1,0:T(8,128)S(1)}, f32[328,128]{1,0:T(8,128)S(1)}, u32[]{:S(2)}, u32[]{:S(2)}) collective-permute-start(f32[328,128]{1,0:T(8,128)S(1)} %add.6.one), channel_id=1, source_target_pairs={{0,16},{4,20},{8,24},{12,28},{16,0},{20,4},{24,8},{28,12},{1,17},{... | collective-permute-start | bytes 503816 | tf_op jit(solution)/shard_map/ppermute | solution.py:552
  77.8 2.9 %norm.1 = (bf16[256,2048]{1,0:T(8,128)(2,1)}, bf16[256,2048]{1,0:T(8,128)(2,1)}, f32[8,128]{1,0:T(8,128)S(1)}) custom-call(f32[512,128]{1,0:T(8,128)S(1)} %get-tuple-element.117.refs_0_, f32[4096,128]{1,0:T(8,128)S(1)} %get-tuple-element.113.refs_4_.refs_1_, f32[4096,128]{1,0:T(8,128)S(1)} %get-tuple-element.102.refs_3_.refs_5_.refs_2_, ...), custom_call_target="tpu_custom_call" | custom-call | flops 13107200 | bytes 2097152 | tf_op jit(solution)/shard_map/norm/pallas_call | solution.py:629
  80.7 2.3 %back_query.1 = (bf16[256,2048]{1,0:T(8,128)(2,1)}, f32[8,128]{1,0:T(8,128)S(1)}) custom-call(f32[4096,128]{1,0:T(8,128)S(1)} %get-tuple-element.130.refs_3_.refs_0_, bf16[3,2,64,128]{3,2,1,0:T(8,128)(2,1)S(1)} %collective-permute-done.10.refs_1_, f32[336,128]{1,0:T(8,128)S(1)} %get-tuple-element.90.refs_3_.refs_2_), custom_call_target="tpu_custom_call" | custom-call | flops 10485760 | bytes 2097152 | tf_op jit(solution)/shard_map/back_query/pallas_call | solution.py:629
  83.0 1.4 %collective-permute-start.16 = (f32[224,128]{1,0:T(8,128)S(1)}, f32[224,128]{1,0:T(8,128)S(1)}, u32[]{:S(2)}, u32[]{:S(2)}) collective-permute-start(f32[224,128]{1,0:T(8,128)S(1)} %add.8.one), channel_id=1, source_target_pairs={{0,8},{4,12},{8,0},{12,4},{16,24},{20,28},{24,16},{28,20},{1,9},{5... | collective-permute-start | bytes 344072 | tf_op jit(solution)/shard_map/ppermute | solution.py:552
  84.9 2.2 %collective-permute-start.14 = (f32[328,128]{1,0:T(8,128)S(1)}, f32[328,128]{1,0:T(8,128)S(1)}, u32[]{:S(2)}, u32[]{:S(2)}) collective-permute-start(f32[328,128]{1,0:T(8,128)S(1)} %add.7.refs_0_), channel_id=1, source_target_pairs={{0,4},{4,0},{8,12},{12,8},{16,20},{20,16},{24,28},{28,24},{1,5},{5... | collective-permute-start | bytes 503816 | tf_op jit(solution)/shard_map/ppermute | solution.py:552
  87.1 2.3 %back_key.1 = (bf16[256,2048]{1,0:T(8,128)(2,1)}, f32[8,128]{1,0:T(8,128)S(1)}) custom-call(f32[4096,128]{1,0:T(8,128)S(1)} %get-tuple-element.142.refs_0_, bf16[3,2,64,128]{3,2,1,0:T(8,128)(2,1)S(1)} %collective-permute-done.10.refs_1_, f32[336,128]{1,0:T(8,128)S(1)} %get-tuple-element.90.refs_3_.refs_2_), custom_call_target="tpu_custom_call" | custom-call | flops 10485760 | bytes 2097152 | tf_op jit(solution)/shard_map/back_key/pallas_call | solution.py:629
  89.6 2.3 %back_value.1 = (bf16[256,2048]{1,0:T(8,128)(2,1)}, f32[8,128]{1,0:T(8,128)S(1)}) custom-call(f32[4096,128]{1,0:T(8,128)S(1)} %get-tuple-element.143.refs_1_.refs_0_, bf16[3,2,64,128]{3,2,1,0:T(8,128)(2,1)S(1)} %collective-permute-done.10.refs_1_, f32[336,128]{1,0:T(8,128)S(1)} %get-tuple-element.90.refs_3_.refs_2_), custom_call_target="tpu_custom_call" | custom-call | flops 10485760 | bytes 2097152 | tf_op jit(solution)/shard_map/back_value/pallas_call | solution.py:629
  92.0 4.5 %collective-permute-done.17.refs_3_ = f32[224,128]{1,0:T(8,128)S(1)} collective-permute-done((f32[224,128]{1,0:T(8,128)S(1)}, f32[224,128]{1,0:T(8,128)S(1)}, u32[]{:S(2)}, u32[]{:S(2)}) %collective-permute-start.17) | collective-permute-done | bytes 114720 | tf_op jit(solution)/shard_map/ppermute | solution.py:552
  (38 shorter events, 9.0 us)
Async XLA Ops:
  1.6 10.1 %collective-permute-start = (bf16[3,8,2048]{2,1,0:T(8,128)(2,1)S(1)}, bf16[3,8,2048]{2,1,0:T(8,128)(2,1)S(1)}, u32[]{:S(2)}, u32[]{:S(2)}) collective-permute-start(bf16[3,8,2048]{2,1,0:T(8,128)(2,1)S(1)} %trailing.1), channel_id=1, source_target_pairs={{0,4},{4,8},{8,12},{12,16},{16,20},{20,24},{24,28},{28,0},{1,5},{5... | collective-permute-start | bytes 294920 | tf_op jit(solution)/shard_map/ppermute | solution.py:548
  12.4 12.9 %copy-start.1 = (f32[2048]{0:T(1024)S(1)}, f32[2048]{0:T(1024)}, u32[]{:S(2)}) copy-start(f32[2048]{0:T(1024)} %param.17) | copy-start | bytes 24580
  12.4 5.0 %collective-permute-start.1 = (f32[256,128]{1,0:T(8,128)S(1)}, f32[256,128]{1,0:T(8,128)S(1)}, u32[]{:S(2)}, u32[]{:S(2)}) collective-permute-start(f32[256,128]{1,0:T(8,128)S(1)} %get-tuple-element.104.own), channel_id=1, source_target_pairs={{0,4},{4,0},{8,12},{12,8},{16,20},{20,16},{24,28},{28,24},{1,5},{5... | collective-permute-start | bytes 393224 | tf_op jit(solution)/shard_map/ppermute | solution.py:552
  17.4 5.0 %collective-permute-start.2 = (f32[256,128]{1,0:T(8,128)S(1)}, f32[256,128]{1,0:T(8,128)S(1)}, u32[]{:S(2)}, u32[]{:S(2)}) collective-permute-start(f32[256,128]{1,0:T(8,128)S(1)} %get-tuple-element.106.own), channel_id=1, source_target_pairs={{0,8},{4,12},{8,0},{12,4},{16,24},{20,28},{24,16},{28,20},{1,9},{5... | collective-permute-start | bytes 393224 | tf_op jit(solution)/shard_map/ppermute | solution.py:552
  22.6 7.3 %collective-permute-start.3 = (f32[256,128]{1,0:T(8,128)S(1)}, f32[256,128]{1,0:T(8,128)S(1)}, u32[]{:S(2)}, u32[]{:S(2)}) collective-permute-start(f32[256,128]{1,0:T(8,128)S(1)} %get-tuple-element.110), channel_id=1, source_target_pairs={{0,16},{4,20},{8,24},{12,28},{16,0},{20,4},{24,8},{28,12},{1,17},{... | collective-permute-start | bytes 393224 | tf_op jit(solution)/shard_map/ppermute | solution.py:552
  25.3 4.6 %copy-start = (f32[2048]{0:T(1024)S(1)}, f32[2048]{0:T(1024)}, u32[]{:S(2)}) copy-start(f32[2048]{0:T(1024)} %param.18) | copy-start | bytes 24580
  34.8 3.0 %collective-permute-start.6 = (f32[2,256]{1,0:T(2,128)S(1)}, f32[2,256]{1,0:T(2,128)S(1)}, u32[]{:S(2)}, u32[]{:S(2)}) collective-permute-start(f32[2,256]{1,0:T(2,128)S(1)} %get-tuple-element.112.refs_0_), channel_id=1, source_target_pairs={{0,3},{1,2},{2,1},{3,0},{4,7},{5,6},{6,5},{7,4},{8,11},{9,10},{10,... | collective-permute-start | bytes 6152 | tf_op jit(solution)/shard_map/ppermute | solution.py:552
  34.8 3.6 %collective-permute-start.5 = (f32[2,256]{1,0:T(2,128)S(1)}, f32[2,256]{1,0:T(2,128)S(1)}, u32[]{:S(2)}, u32[]{:S(2)}) collective-permute-start(f32[2,256]{1,0:T(2,128)S(1)} %get-tuple-element.112.refs_0_), channel_id=1, source_target_pairs={{0,2},{1,3},{2,0},{3,1},{4,6},{5,7},{6,4},{7,5},{8,10},{9,11},{10,... | collective-permute-start | bytes 6152 | tf_op jit(solution)/shard_map/ppermute | solution.py:552
  36.4 2.1 %collective-permute-start.4 = (f32[2,256]{1,0:T(2,128)S(1)}, f32[2,256]{1,0:T(2,128)S(1)}, u32[]{:S(2)}, u32[]{:S(2)}) collective-permute-start(f32[2,256]{1,0:T(2,128)S(1)} %get-tuple-element.112.refs_0_), channel_id=1, source_target_pairs={{0,1},{1,0},{2,3},{3,2},{4,5},{5,4},{6,7},{7,6},{8,9},{9,8},{10,11... | collective-permute-start | bytes 6152 | tf_op jit(solution)/shard_map/ppermute | solution.py:552
  42.5 6.3 %collective-permute-start.7 = (f32[256,128]{1,0:T(8,128)S(1)}, f32[256,128]{1,0:T(8,128)S(1)}, u32[]{:S(2)}, u32[]{:S(2)}) collective-permute-start(f32[256,128]{1,0:T(8,128)S(1)} %get-tuple-element.131.own), channel_id=1, source_target_pairs={{0,4},{4,0},{8,12},{12,8},{16,20},{20,16},{24,28},{28,24},{1,5},{5... | collective-permute-start | bytes 393224 | tf_op jit(solution)/shard_map/ppermute | solution.py:552
  48.9 5.6 %collective-permute-start.8 = (f32[256,128]{1,0:T(8,128)S(1)}, f32[256,128]{1,0:T(8,128)S(1)}, u32[]{:S(2)}, u32[]{:S(2)}) collective-permute-start(f32[256,128]{1,0:T(8,128)S(1)} %get-tuple-element.133.own), channel_id=1, source_target_pairs={{0,8},{4,12},{8,0},{12,4},{16,24},{20,28},{24,16},{28,20},{1,9},{5... | collective-permute-start | bytes 393224 | tf_op jit(solution)/shard_map/ppermute | solution.py:552
  54.6 8.2 %collective-permute-start.9 = (f32[256,128]{1,0:T(8,128)S(1)}, f32[256,128]{1,0:T(8,128)S(1)}, u32[]{:S(2)}, u32[]{:S(2)}) collective-permute-start(f32[256,128]{1,0:T(8,128)S(1)} %get-tuple-element.137), channel_id=1, source_target_pairs={{0,16},{4,20},{8,24},{12,28},{16,0},{20,4},{24,8},{28,12},{1,17},{... | collective-permute-start | bytes 393224 | tf_op jit(solution)/shard_map/ppermute | solution.py:552
  62.9 6.1 %collective-permute-start.11 = (f32[328,128]{1,0:T(8,128)S(1)}, f32[328,128]{1,0:T(8,128)S(1)}, u32[]{:S(2)}, u32[]{:S(2)}) collective-permute-start(f32[328,128]{1,0:T(8,128)S(1)} %get-tuple-element.154), channel_id=1, source_target_pairs={{0,4},{4,0},{8,12},{12,8},{16,20},{20,16},{24,28},{28,24},{1,5},{5... | collective-permute-start | bytes 503816 | tf_op jit(solution)/shard_map/ppermute | solution.py:552
  69.1 6.4 %collective-permute-start.12 = (f32[328,128]{1,0:T(8,128)S(1)}, f32[328,128]{1,0:T(8,128)S(1)}, u32[]{:S(2)}, u32[]{:S(2)}) collective-permute-start(f32[328,128]{1,0:T(8,128)S(1)} %add.5.one), channel_id=1, source_target_pairs={{0,8},{4,12},{8,0},{12,4},{16,24},{20,28},{24,16},{28,20},{1,9},{5... | collective-permute-start | bytes 503816 | tf_op jit(solution)/shard_map/ppermute | solution.py:552
  69.1 6.3 %collective-permute-start.10 = (bf16[3,2,64,128]{3,2,1,0:T(8,128)(2,1)S(1)}, bf16[3,2,64,128]{3,2,1,0:T(8,128)(2,1)S(1)}, u32[]{:S(2)}, u32[]{:S(2)}) collective-permute-start(bf16[3,2,64,128]{3,2,1,0:T(8,128)(2,1)S(1)} %get-tuple-element.149), channel_id=1, source_target_pairs={{0,28},{4,0},{8,4},{12,8},{16,12},{20,16},{24,20},{28,24},{1,29},{... | collective-permute-start | bytes 294920 | tf_op jit(solution)/shard_map/ppermute | solution.py:548
  75.4 7.7 %collective-permute-start.15 = (f32[224,128]{1,0:T(8,128)S(1)}, f32[224,128]{1,0:T(8,128)S(1)}, u32[]{:S(2)}, u32[]{:S(2)}) collective-permute-start(f32[224,128]{1,0:T(8,128)S(1)} %get-tuple-element.158.one), channel_id=1, source_target_pairs={{0,4},{4,0},{8,12},{12,8},{16,20},{20,16},{24,28},{28,24},{1,5},{5... | collective-permute-start | bytes 344072 | tf_op jit(solution)/shard_map/ppermute | solution.py:552
  75.5 9.4 %collective-permute-start.13 = (f32[328,128]{1,0:T(8,128)S(1)}, f32[328,128]{1,0:T(8,128)S(1)}, u32[]{:S(2)}, u32[]{:S(2)}) collective-permute-start(f32[328,128]{1,0:T(8,128)S(1)} %add.6.one), channel_id=1, source_target_pairs={{0,16},{4,20},{8,24},{12,28},{16,0},{20,4},{24,8},{28,12},{1,17},{... | collective-permute-start | bytes 503816 | tf_op jit(solution)/shard_map/ppermute | solution.py:552
  83.0 6.5 %collective-permute-start.16 = (f32[224,128]{1,0:T(8,128)S(1)}, f32[224,128]{1,0:T(8,128)S(1)}, u32[]{:S(2)}, u32[]{:S(2)}) collective-permute-start(f32[224,128]{1,0:T(8,128)S(1)} %add.8.one), channel_id=1, source_target_pairs={{0,8},{4,12},{8,0},{12,4},{16,24},{20,28},{24,16},{28,20},{1,9},{5... | collective-permute-start | bytes 344072 | tf_op jit(solution)/shard_map/ppermute | solution.py:552
  84.9 11.6 %collective-permute-start.14 = (f32[328,128]{1,0:T(8,128)S(1)}, f32[328,128]{1,0:T(8,128)S(1)}, u32[]{:S(2)}, u32[]{:S(2)}) collective-permute-start(f32[328,128]{1,0:T(8,128)S(1)} %add.7.refs_0_), channel_id=1, source_target_pairs={{0,4},{4,0},{8,12},{12,8},{16,20},{20,16},{24,28},{28,24},{1,5},{5... | collective-permute-start | bytes 503816 | tf_op jit(solution)/shard_map/ppermute | solution.py:552
  89.5 7.0 %collective-permute-start.17 = (f32[224,128]{1,0:T(8,128)S(1)}, f32[224,128]{1,0:T(8,128)S(1)}, u32[]{:S(2)}, u32[]{:S(2)}) collective-permute-start(f32[224,128]{1,0:T(8,128)S(1)} %add.9.refs_2_), channel_id=1, source_target_pairs={{0,16},{4,20},{8,24},{12,28},{16,0},{20,4},{24,8},{28,12},{1,17},{... | collective-permute-start | bytes 344072 | tf_op jit(solution)/shard_map/ppermute | solution.py:552

commit v6 on v5

--- a/solution.py
+++ b/solution.py
@@ -9,6 +9,7 @@
 
 LANES = 128
 SUB = 8
+CHUNK = 16
 WIDE = SUB * LANES
 F32 = jnp.float32
 BF16 = jnp.bfloat16
@@ -33,15 +34,19 @@
     return body(stop - 1, carry) if (stop - start) % 2 else carry
 
 
+def spread_chunk(src, dst, first, c):
+    start = pl.multiple_of(c * CHUNK, CHUNK)
+    for g in range(SUB):
+        piece = src[pl.ds(start, CHUNK), g * LANES : (g + 1) * LANES].astype(F32)
+        dst[pl.ds((start + first) * SUB + g, CHUNK, stride=SUB), :] = piece
+
+
 def spread(src, dst, first, count):
-    def some(i, carry):
-        start = pl.multiple_of(i * 16, 16)
-        for g in range(SUB):
-            piece = src[pl.ds(start, 16), g * LANES : (g + 1) * LANES].astype(F32)
-            dst[pl.ds((start + first) * SUB + g, 16, stride=SUB), :] = piece
+    def some(c, carry):
+        spread_chunk(src, dst, first, c)
         return carry
 
-    loop(0, count // 16, some, 0)
+    loop(0, count // CHUNK, some, 0)
 
 
 def gather_rows(src, dst, count):
@@ -80,7 +85,7 @@
 
 
 def features_kernel(
-    modes, taps, steps, key, value, filt3, decay, resid, k_ext, v_ext, f1, f2, u, g, lam, res, filt, x_out
+    modes, taps, steps, key, value, filt3, decay, resid, k_ext, v_ext, f1, f2, u, g, lam, res, faded, filt, x_out
 ):
     margin = taps - 1
     for s in range(SUB):
@@ -89,35 +94,52 @@
         res[pl.ds(s, modes, stride=SUB), :] = resid[:, lanes]
         for i in range(3):
             filt[pl.ds(i * taps * SUB + s, taps, stride=SUB), :] = filt3[i, :, lanes]
-    spread(key, k_ext, SUB, steps)
-    spread(value, v_ext, SUB, steps)
+    faded[...] = res[...] * jnp.exp(-lam[...])
     taps1, taps2 = taps_of(filt, 1, taps), taps_of(filt, 2, taps)
-
-    def conv(c, carry):
-        t0 = c * SUB
-        kw = [row(k_ext, t0 + SUB - margin + i) for i in range(SUB + margin)]
-        for i in range(SUB):
-            put(f1, t0 + i, conv_at(kw, taps1, i))
-        vw = [row(v_ext, t0 + SUB - margin + i) for i in range(SUB + margin)]
-        for i in range(SUB):
-            second = conv_at(vw, taps2, i)
-            put(f2, t0 + i, second)
-            put(u, t0 + i, second * row(f1, t0 + i))
-        return carry
-
-    loop(1, steps // SUB, conv, 0)
     fade, skip = fades(lam, modes, 1), fades(lam, modes, SUB)
-
-    def advance(c, x):
-        now = [row(u, c * SUB + i) for i in range(SUB)]
-        new = []
-        for m in range(modes):
-            own = horner(fade[m], now)
-            put(g, c * modes + m, own)
-            new.append(own + skip[m] * x[m])
-        return tuple(new)
-
-    x = loop(1, steps // SUB, advance, zeros(modes))
+    chunks = steps // CHUNK
+
+    def shape(c):
+        for src, dst in ((key, k_ext), (value, v_ext)):
+            spread_chunk(src, dst, SUB, c)
+
+    def conv(c, skipped=0):
+        t0 = c * CHUNK
+        kw = [row(k_ext, t0 + SUB - margin + i) for i in range(skipped, CHUNK + margin)]
+        vw = [row(v_ext, t0 + SUB - margin + i) for i in range(skipped, CHUNK + margin)]
+        for i in range(CHUNK - skipped):
+            first, second = conv_at(kw, taps1, i), conv_at(vw, taps2, i)
+            put(f1, t0 + skipped + i, first)
+            put(f2, t0 + skipped + i, second)
+            put(u, t0 + skipped + i, first * second)
+
+    def advance(c, x, skipped=0):
+        for b in range(skipped, CHUNK // SUB):
+            block = c * (CHUNK // SUB) + b
+            now = [row(u, block * SUB + i) for i in range(SUB)]
+            new = []
+            for m in range(modes):
+                own = horner(fade[m], now)
+                put(g, block * modes + m, own)
+                new.append(own + skip[m] * x[m])
+            x = tuple(new)
+        return x
+
+    shape(0)
+    shape(1)
+    conv(0, SUB)
+    shape(2)
+    conv(1)
+    x = advance(0, zeros(modes), 1)
+
+    def some(c, x):
+        shape(c + 1)
+        conv(c)
+        return advance(c - 1, x)
+
+    x = lax.fori_loop(2, chunks - 1, some, x)
+    conv(chunks - 1)
+    x = advance(chunks - 1, advance(chunks - 2, x))
     for m in range(modes):
         put(x_out, m, x[m])
 
@@ -239,7 +261,7 @@
         put(lag_sum, m, sums[m])
 
 
-def summed_kernel(modes, steps, blocks, group, y, f0, res_pos, cot_pos, g, before, other, lam, res, gain, ready, modal, summed, x_at, sums, squares, inner):
+def summed_kernel(modes, steps, blocks, group, y, f0, res_pos, cot_pos, g, before, other, lam, faded, gain, ready, modal, summed, x_at, sums, squares, inner):
     del ready
     block = pl.program_id(0)
 
@@ -254,12 +276,13 @@
     x_in = tuple(x_in[m * SUB : (m + 1) * SUB, :] for m in range(modes))
 
     def advance(c, x):
-        w = [row(res, m) * x[m] for m in range(modes)]
+        w = [row(faded, m) * x[m] for m in range(modes)]
         for m in range(modes):
             put(x_at, c * modes + m, x[m])
         for i in range(SUB):
             t = c * SUB + i
-            w = [f * v for f, v in zip(fade, w)]
+            if i:
+                w = [f * v for f, v in zip(fade, w)]
             long = row(y, t) + total(w)
             put(modal, t, long)
             now = row(res_pos, t) + row(f0, t) * long
@@ -317,7 +340,7 @@
             put(gm, t, now[i])
         new = []
         for m in range(modes):
-            own = fade[m] * horner(fade[m], now[::-1])
+            own = horner(fade[m], now[::-1])
             put(adj, block * modes + m, own)
             new.append(own + skip[m] * a[m])
         return tuple(new)
@@ -327,33 +350,32 @@
         put(a_out, m, a[m])
 
 
-def across_kernel(modes, steps, gm, adj, x_at, lag, lam, res_part, rate_part):
+def across_kernel(ms, modes, steps, gm, adj, x_at, lag, lam, res_part, rate_part):
     fade, far = fades(lam, modes, 1), fades(lam, modes, SUB)
     last = steps // SUB - 1
+
+    def across(c, state):
+        after, by_res, by_rate = (list(v) for v in state)
+        block = last - c
+        now = [row(gm, block * SUB + i) * float(i) for i in range(1, SUB)]
+        for i, m in enumerate(ms):
+            x, own = row(x_at, block * modes + m), row(adj, block * modes + m)
+            tail = fade[m] * horner(fade[m], now[::-1])
+            by_res[i] = by_res[i] + x * own
+            by_rate[i] = by_rate[i] + (x * tail + after[i] * row(lag, block * modes + m))
+            after[i] = own + far[m] * after[i]
+        return tuple(after), tuple(by_res), tuple(by_rate)
+
+    none = zeros(len(ms))
+    _, by_res, by_rate = loop(0, steps // SUB, across, (none, none, none))
+    for i, m in enumerate(ms):
+        put(res_part, i, fade[m] * by_res[i])
+        put(rate_part, i, fade[m] * by_rate[i])
+
+
+def near_adjoint_kernel(modes, steps, gm, u, lam, res, skip, *refs):
+    res_parts, rate_parts, (gmy, res_sum, rate_sum, skip_sum) = refs[:2], refs[2:4], refs[4:]
     half = modes // 2
-    for part in range(2):
-        ms = range(part * half, (part + 1) * half)
-
-        def across(c, state, ms=ms):
-            after, by_res, by_rate = (list(v) for v in state)
-            block = last - c
-            now = [row(gm, block * SUB + i) * float(i) for i in range(1, SUB)]
-            for i, m in enumerate(ms):
-                x, own = row(x_at, block * modes + m), row(adj, block * modes + m)
-                tail = fade[m] * fade[m] * horner(fade[m], now[::-1])
-                by_res[i] = by_res[i] + x * own
-                by_rate[i] = by_rate[i] + (x * tail + after[i] * row(lag, block * modes + m))
-                after[i] = own + far[m] * after[i]
-            return tuple(after), tuple(by_res), tuple(by_rate)
-
-        none = zeros(half)
-        _, by_res, by_rate = loop(0, steps // SUB, across, (none, none, none))
-        for i, m in enumerate(ms):
-            put(res_part, m, by_res[i])
-            put(rate_part, m, by_rate[i])
-
-
-def near_adjoint_kernel(modes, steps, gm, u, lam, res, skip, res_part, rate_part, gmy, res_sum, rate_sum, skip_sum):
     near = near_taps(lam, res, skip, modes)
 
     def pairs(c, lags):
@@ -370,8 +392,8 @@
     fade = fades(lam, modes, 1)
     weighted = [lags[k] * float(k) for k in range(1, SUB)]
     for m in range(modes):
-        put(res_sum, m, row(res_part, m) + horner(fade[m], lags[::-1]))
-        put(rate_sum, m, row(rate_part, m) + fade[m] * horner(fade[m], weighted[::-1]))
+        put(res_sum, m, row(res_parts[m // half], m % half) + horner(fade[m], lags[::-1]))
+        put(rate_sum, m, row(rate_parts[m // half], m % half) + fade[m] * horner(fade[m], weighted[::-1]))
 
 
 def norm_kernel(steps, scale, summed, cot_pos, gain, ready, normed, grad_res, work):
@@ -435,12 +457,12 @@
     return loop(0, steps // SUB, some, tuple(zero for _ in range(taps)))
 
 
-def mixed_kernel(modes, taps, steps, gmy, f1, f2, gf0, adj, lam, res, alpha, gf1, gf2, heads):
+def mixed_kernel(modes, taps, steps, gmy, f1, f2, gf0, adj, lam, faded, alpha, gf1, gf2, heads):
     fade, skip = fades(lam, modes, 1), fades(lam, modes, SUB)
 
     def advance(c, after):
         block = steps // SUB - 1 - c
-        w = [row(res, m) * after[m] for m in range(modes)]
+        w = [row(faded, m) * after[m] for m in range(modes)]
         for i in reversed(range(SUB)):
             t = block * SUB + i
             grad = row(gmy, t) + total(w)
@@ -522,7 +544,7 @@
             out[pl.ds(b * rows, first_rows * SUB), :] = early[pl.ds(source, first_rows * SUB), :]
             source = pl.multiple_of((start + b) * (modes * SUB), SUB)
             mine = pl.ds(source, modes * SUB)
-            lagged = rate_sum[mine, :] + alpha[mine, :] * lag_sum[mine, :]
+            lagged = rate_sum[mine, :] + jnp.exp(-lam[mine, :]) * alpha[mine, :] * lag_sum[mine, :]
             out[pl.ds(b * rows + first_rows * SUB, modes * SUB), :] = -res[mine, :] * lagged
 
 
@@ -660,12 +682,12 @@
     )(*far[1:4])
     halo = ring(trailing, "ctx", 1)
 
-    k_ext, v_ext, f1, f2, u, g, lam, res, filt, x_part, _ = call(
+    k_ext, v_ext, f1, f2, u, g, lam, res, faded, filt, x_part, _ = call(
         functools.partial(features_kernel, modes, taps, steps),
         (far[2], far[3], *far[5:]),
         [wide_spec, wide_spec, short_spec, param_spec, param_spec],
-        [ext, ext, seq, seq, seq, eights, mode, mode, pos(3 * taps), mode],
-        [ext_spec, ext_spec, seq_spec, seq_spec, seq_spec, eights_spec, mode_spec, mode_spec, filt_spec, mode_spec],
+        [ext, ext, seq, seq, seq, eights, mode, mode, mode, pos(3 * taps), mode],
+        [ext_spec, ext_spec, seq_spec, seq_spec, seq_spec, eights_spec, mode_spec, mode_spec, mode_spec, filt_spec, mode_spec],
         64,
         "features",
     )
@@ -722,7 +744,7 @@
     before, other, group = scan_but_last(x_own, lam, steps, 1, [query_done, inputs_done])
     modal, summed, x_at, sums, _ = call(
         functools.partial(summed_kernel, modes, steps, blocks, group),
-        (y, f0, res_pos, cot_pos, g, before, other, lam, res, gain, own_lag_done),
+        (y, f0, res_pos, cot_pos, g, before, other, lam, faded, gain, own_lag_done),
         [seq_spec] * 4 + [eights_spec] + [mode_spec] * 4 + [one_spec, any_spec],
         [seq, seq, eights, jax.ShapeDtypeStruct((2, steps), F32)],
         [seq_spec, seq_spec, eights_spec, pl.BlockSpec((2, steps), lambda h: (0, 0))],
@@ -751,19 +773,25 @@
         45,
         "grad_modal",
     )
-    res_part, rate_part, across_done = call(
-        functools.partial(across_kernel, modes, steps),
-        (gm, adj, x_at, lag, lam),
-        [seq_spec, eights_spec, eights_spec, eights_spec, mode_spec],
-        [mode, mode],
-        [mode_spec, mode_spec],
-        50,
-        "across",
-    )
-    gmy, res_sum, rate_sum, skip_sum, near_done = call(
+    few = modes // 2
+    res_parts, rate_parts, across_done = zip(
+        *(
+            call(
+                functools.partial(across_kernel, range(start, start + few), modes, steps),
+                (gm, adj, x_at, lag, lam),
+                [seq_spec, eights_spec, eights_spec, eights_spec, mode_spec],
+                [pos(few), pos(few)],
+                [pos_spec(few), pos_spec(few)],
+                25,
+                "across",
+            )
+            for start in (0, few)
+        )
+    )
+    gmy, res_sum, rate_sum, skip_sum, _ = call(
         functools.partial(near_adjoint_kernel, modes, steps),
-        (gm, u, lam, res, skip, res_part, rate_part),
-        [seq_spec, seq_spec, mode_spec, mode_spec, one_spec, mode_spec, mode_spec],
+        (gm, u, lam, res, skip, *res_parts, *rate_parts),
+        [seq_spec, seq_spec, mode_spec, mode_spec, one_spec] + [pos_spec(few)] * 4,
         [seq, mode, mode, one],
         [seq_spec, mode_spec, mode_spec, one_spec],
         25,
@@ -779,7 +807,7 @@
         30,
         "query_sums",
     )
-    before, other, group = scan_but_last(a_own, lam, steps, -1, [across_done, near_done])
+    before, other, group = scan_but_last(a_own, lam, steps, -1, across_done)
 
     half = blocks // 2
     half_shape = (half * (early_rows + modes) * SUB, LANES)
@@ -796,7 +824,7 @@
     other_half = swap(sent_half, "ctx", 1)
     gf1, gf2, heads, mixed_done = call(
         functools.partial(mixed_kernel, modes, taps, steps),
-        (gmy, f1, f2, gf0, adj, lam, res, alpha),
+        (gmy, f1, f2, gf0, adj, lam, faded, alpha),
         [seq_spec] * 4 + [eights_spec] + [mode_spec] * 3,
         [seq, seq, jax.ShapeDtypeStruct((3, blocks, SUB * SUB, LANES), BF16)],
         [seq_spec, seq_spec, next_spec],

time: 97.6 us -> 94.9 us (0.972)
  waiting for transfers between devices: 18.7 us -> 13 us
  starting transfers between devices: 25.3 us -> 27.8 us
    ppermute x16, waiting for transfers between devices: 18.7 us -> 13 us  [swap(): lax.ppermute(value, axis, [(i, i ^ step) for i in range(lax.axis_size(axi...]
    ppermute x16, starting transfers between devices: 18.4 us -> 22.3 us  [swap(): lax.ppermute(value, axis, [(i, i ^ step) for i in range(lax.axis_size(axi...]
    ppermute x2, starting transfers between devices: 6.93 us -> 5.57 us  [ring(): lax.ppermute(value, axis, [(i, (i + distance) % count) for i in range(cou...]
    pallas_call x19 -> x20, Pallas kernels: 51 us -> 50.9 us  [call(): pl.pallas_call(with_done, grid=(blocks,), in_specs=in_specs, out_specs=ou...]
  transfers between devices with their start and end apart: 18 -> 18, of which waited for: 10 -> 12; matrix products, arithmetic and copies ran while one was open for 0% -> 0% of each run, Pallas kernels for 42% -> 43%
where the time goes in v6:
time: 94.9 us; the launch traced here: 93.9 us
  Pallas kernels  52.3 us (55%)
  starting transfers between devices  27.8 us (29%)
  waiting for transfers between devices  13 us (14%)
    pallas_call x20, Pallas kernels, call(): pl.pallas_call(with_done, grid=(blocks,), in_specs=in_specs, out_specs=ou...  50.9 us
    ppermute x16, starting transfers between devices, swap(): lax.ppermute(value, axis, [(i, i ^ step) for i in range(lax.axis_size(axi...  22.3 us
    ppermute x16, waiting for transfers between devices, swap(): lax.ppermute(value, axis, [(i, i ^ step) for i in range(lax.axis_size(axi...  13 us
    ppermute x2, starting transfers between devices, ring(): lax.ppermute(value, axis, [(i, (i + distance) % count) for i in range(cou...  5.57 us
  transfers between devices with their start and end apart: 18, of which 12 were waited for; matrix products, arithmetic and copies ran while one was open for 0% of the time, Pallas kernels for 43%

profile of v6, /device:TPU:0, one launch (start us, length us, event | category | flops | bytes accessed | tf_op | source)
XLA Modules:
  0.0 93.9 jit_solution(5801643886773075752)
XLA Ops:
  1.6 3.0 %collective-permute-start = (bf16[3,8,2048]{2,1,0:T(8,128)(2,1)S(1)}, bf16[3,8,2048]{2,1,0:T(8,128)(2,1)S(1)}, u32[]{:S(2)}, u32[]{:S(2)}) collective-permute-start(bf16[3,8,2048]{2,1,0:T(8,128)(2,1)S(1)} %trailing.1), channel_id=1, source_target_pairs={{0,4},{4,8},{8,12},{12,16},{16,20},{20,24},{24,28},{28,0},{1,5},{5... | collective-permute-start | bytes 294920 | tf_op jit(solution)/shard_map/ppermute | solution.py:570
  4.5 6.7 %features.1 = (f32[4224,128]{1,0:T(8,128)S(1)}, f32[4224,128]{1,0:T(8,128)S(1)}, f32[4096,128]{1,0:T(8,128)S(1)}, f32[4096,128]{1,0:T(8,128)S(1)}, f32[4096,128]...) custom-call(bf16[256,2048]{1,0:T(8,128)(2,1)} %refs_0_.3, ...), custom_call_target="tpu_custom_call" | custom-call | flops 33554432 | bytes 2097152 | tf_op jit(solution)/shard_map/features/pallas_call | solution.py:651
  12.0 1.5 %collective-permute-start.1 = (f32[256,128]{1,0:T(8,128)S(1)}, f32[256,128]{1,0:T(8,128)S(1)}, u32[]{:S(2)}, u32[]{:S(2)}) collective-permute-start(f32[256,128]{1,0:T(8,128)S(1)} %get-tuple-element.107.own), channel_id=1, source_target_pairs={{0,4},{4,0},{8,12},{12,8},{16,20},{20,16},{24,28},{28,24},{1,5},{5... | collective-permute-start | bytes 393224 | tf_op jit(solution)/shard_map/ppermute | solution.py:574
  13.5 2.5 %query.3 = (f32[4224,128]{1,0:T(8,128)S(1)}, f32[4096,128]{1,0:T(8,128)S(1)}, f32[8,128]{1,0:T(8,128)S(1)}) custom-call(bf16[256,2048]{1,0:T(8,128)(2,1)} %refs_0_.4, bf16[3,8,2048]{2,1,0:T(8,128)(2,1)S(1)} %collective-permute-done.refs_0_.refs_1_, f32[336,128]{1,0:T(8,128)S(1)} %get-tuple-element.93.refs_3_.refs_2_), custom_call_target="tpu_custom_call" | custom-call | flops 10485760 | bytes 2097152 | tf_op jit(solution)/shard_map/query/pallas_call | solution.py:651
  17.0 1.6 %collective-permute-start.2 = (f32[256,128]{1,0:T(8,128)S(1)}, f32[256,128]{1,0:T(8,128)S(1)}, u32[]{:S(2)}, u32[]{:S(2)}) collective-permute-start(f32[256,128]{1,0:T(8,128)S(1)} %get-tuple-element.109.own), channel_id=1, source_target_pairs={{0,8},{4,12},{8,0},{12,4},{16,24},{20,28},{24,16},{28,20},{1,9},{5... | collective-permute-start | bytes 393224 | tf_op jit(solution)/shard_map/ppermute | solution.py:574
  18.7 2.0 %inputs.1 = (f32[4096,128]{1,0:T(8,128)S(1)}, f32[4096,128]{1,0:T(8,128)S(1)}, f32[8,128]{1,0:T(8,128)S(1)}) custom-call(bf16[256,2048]{1,0:T(8,128)(2,1)} %refs_0_.5, bf16[256,2048]{1,0:T(8,128)(2,1)} %refs_1_.3), custom_call_target="tpu_custom_call" | custom-call | flops 5242880 | bytes 2097152 | tf_op jit(solution)/shard_map/inputs/pallas_call | solution.py:651
  20.7 1.4 %collective-permute-done.2.other = f32[256,128]{1,0:T(8,128)S(1)} collective-permute-done((f32[256,128]{1,0:T(8,128)S(1)}, f32[256,128]{1,0:T(8,128)S(1)}, u32[]{:S(2)}, u32[]{:S(2)}) %collective-permute-start.2) | collective-permute-done | bytes 131104 | tf_op jit(solution)/shard_map/ppermute | solution.py:574
  22.2 2.7 %collective-permute-start.3 = (f32[256,128]{1,0:T(8,128)S(1)}, f32[256,128]{1,0:T(8,128)S(1)}, u32[]{:S(2)}, u32[]{:S(2)}) collective-permute-start(f32[256,128]{1,0:T(8,128)S(1)} %get-tuple-element.113), channel_id=1, source_target_pairs={{0,16},{4,20},{8,24},{12,28},{16,0},{20,4},{24,8},{28,12},{1,17},{... | collective-permute-start | bytes 393224 | tf_op jit(solution)/shard_map/ppermute | solution.py:574
  24.9 1.4 %near.1 = (f32[4096,128]{1,0:T(8,128)S(1)}, f32[8,128]{1,0:T(8,128)}) custom-call(f32[4096,128]{1,0:T(8,128)S(1)} %get-tuple-element.100.refs_0_.refs_1_, f32[256,128]{1,0:T(8,128)S(1)} %get-tuple-element.94.refs_4_.refs_1_.lam.refs_7_.refs_2_.refs_5_, f32[256,128]{1,0:T(8,128)S(1)} %get-tuple-element.101.refs_2_.refs_3_.res, f32[16,128]{1,0:T(8,128)S(1)} %bitcast.8), custom_call_target="tpu_custom_call" | custom-call | flops 5242880 | bytes 2097152 | tf_op jit(solution)/shard_map/near/pallas_call | solution.py:651
  26.3 2.2 %lags.1 = (f32[8192,128]{1,0:T(8,128)S(1)}, f32[8,128]{1,0:T(8,128)S(1)}) custom-call(f32[4096,128]{1,0:T(8,128)S(1)} %get-tuple-element.100.refs_0_.refs_1_, f32[256,128]{1,0:T(8,128)S(1)} %get-tuple-element.94.refs_4_.refs_1_.lam.refs_7_.refs_2_.refs_5_), custom_call_target="tpu_custom_call" | custom-call | flops 16777216 | bytes 2097152 | tf_op jit(solution)/shard_map/lags/pallas_call | solution.py:651
  29.5 4.9 %summed.1 = (f32[4096,128]{1,0:T(8,128)S(1)}, f32[4096,128]{1,0:T(8,128)S(1)}, f32[8192,128]{1,0:T(8,128)S(1)}, f32[2,256]{1,0:T(2,128)S(1)}, f32[8,128]{1,0:T(8,128)}) custom-call(f32[4096,128]{1,0:T(8,128)S(1)} %get-tuple-element.102.refs_0_, f32[4096,128]{1,0:T(8,128)S(1)} %get-tuple-element.103.refs_1_.refs_6_, ...), custom_call_target="tpu_custom_call" | custom-call | flops 26214400 | bytes 2097152 | tf_op jit(solution)/shard_map/summed/pallas_call | solution.py:651
  34.4 1.6 %collective-permute-start.5 = (f32[2,256]{1,0:T(2,128)S(1)}, f32[2,256]{1,0:T(2,128)S(1)}, u32[]{:S(2)}, u32[]{:S(2)}) collective-permute-start(f32[2,256]{1,0:T(2,128)S(1)} %get-tuple-element.116.refs_0_), channel_id=1, source_target_pairs={{0,2},{1,3},{2,0},{3,1},{4,6},{5,7},{6,4},{7,5},{8,10},{9,11},{10,... | collective-permute-start | bytes 6152 | tf_op jit(solution)/shard_map/ppermute | solution.py:574
  38.0 3.9 %grad_modal.1 = (f32[512,128]{1,0:T(8,128)S(1)}, f32[4096,128]{1,0:T(8,128)S(1)}, f32[8192,128]{1,0:T(8,128)S(1)}, f32[256,128]{1,0:T(8,128)S(1)}, f32[8,128]{1,0:T(8,128)}) custom-call(f32[2,256]{1,0:T(2,128)S(1)} %get-tuple-element.116.refs_0_, f32[2,256]{1,0:T(2,128)S(1)} %collective-permute-done.4.refs_1_, f32[2,256]{1,0:T(2,128)S(1)} %collective-permute-done.5.refs_2_, ...), custom_call_target="tpu_custom_call" | custom-call | flops 23592960 | bytes 2097152 | tf_op jit(solution)/shard_map/grad_modal/pallas_call | solution.py:651
  41.9 1.5 %collective-permute-start.7 = (f32[256,128]{1,0:T(8,128)S(1)}, f32[256,128]{1,0:T(8,128)S(1)}, u32[]{:S(2)}, u32[]{:S(2)}) collective-permute-start(f32[256,128]{1,0:T(8,128)S(1)} %get-tuple-element.137.own), channel_id=1, source_target_pairs={{0,4},{4,0},{8,12},{12,8},{16,20},{20,16},{24,28},{28,24},{1,5},{5... | collective-permute-start | bytes 393224 | tf_op jit(solution)/shard_map/ppermute | solution.py:574
  43.4 2.4 %across.2 = (f32[128,128]{1,0:T(8,128)S(1)}, f32[128,128]{1,0:T(8,128)S(1)}, f32[8,128]{1,0:T(8,128)S(1)}) custom-call(f32[4096,128]{1,0:T(8,128)S(1)} %get-tuple-element.122.refs_0_, f32[8192,128]{1,0:T(8,128)S(1)} %get-tuple-element.123.refs_1_.refs_4_, f32[8192,128]{1,0:T(8,128)S(1)} %get-tuple-element.119.refs_1_.refs_2_, ...), custom_call_target="tpu_custom_call" | custom-call | flops 13107200 | bytes 2097152 | tf_op jit(solution)/shard_map/across/pallas_call | solution.py:651
  45.8 1.9 %collective-permute-done.7.other = f32[256,128]{1,0:T(8,128)S(1)} collective-permute-done((f32[256,128]{1,0:T(8,128)S(1)}, f32[256,128]{1,0:T(8,128)S(1)}, u32[]{:S(2)}, u32[]{:S(2)}) %collective-permute-start.7) | collective-permute-done | bytes 131104 | tf_op jit(solution)/shard_map/ppermute | solution.py:574
  48.6 2.4 %across.3 = (f32[128,128]{1,0:T(8,128)S(1)}, f32[128,128]{1,0:T(8,128)S(1)}, f32[8,128]{1,0:T(8,128)S(1)}) custom-call(f32[4096,128]{1,0:T(8,128)S(1)} %get-tuple-element.122.refs_0_, f32[8192,128]{1,0:T(8,128)S(1)} %get-tuple-element.123.refs_1_.refs_4_, f32[8192,128]{1,0:T(8,128)S(1)} %get-tuple-element.119.refs_1_.refs_2_, ...), custom_call_target="tpu_custom_call" | custom-call | flops 13107200 | bytes 2097152 | tf_op jit(solution)/shard_map/across/pallas_call | solution.py:651
  51.0 2.0 %collective-permute-done.8.other = f32[256,128]{1,0:T(8,128)S(1)} collective-permute-done((f32[256,128]{1,0:T(8,128)S(1)}, f32[256,128]{1,0:T(8,128)S(1)}, u32[]{:S(2)}, u32[]{:S(2)}) %collective-permute-start.8) | collective-permute-done | bytes 131104 | tf_op jit(solution)/shard_map/ppermute | solution.py:574
  53.0 2.4 %collective-permute-start.9 = (f32[256,128]{1,0:T(8,128)S(1)}, f32[256,128]{1,0:T(8,128)S(1)}, u32[]{:S(2)}, u32[]{:S(2)}) collective-permute-start(f32[256,128]{1,0:T(8,128)S(1)} %get-tuple-element.143), channel_id=1, source_target_pairs={{0,16},{4,20},{8,24},{12,28},{16,0},{20,4},{24,8},{28,12},{1,17},{... | collective-permute-start | bytes 393224 | tf_op jit(solution)/shard_map/ppermute | solution.py:574
  55.5 2.1 %near_adjoint.1 = (f32[4096,128]{1,0:T(8,128)S(1)}, f32[256,128]{1,0:T(8,128)S(1)}, f32[256,128]{1,0:T(8,128)S(1)}, f32[16,128]{1,0:T(8,128)S(1)}, f32[8,128]{1,0:T(8,128)}) custom-call(f32[4096,128]{1,0:T(8,128)S(1)} %get-tuple-element.122.refs_0_, f32[4096,128]{1,0:T(8,128)S(1)} %get-tuple-element.100.refs_0_.refs_1_, ...), custom_call_target="tpu_custom_call" | custom-call | flops 13107200 | bytes 2097152 | tf_op jit(solution)/shard_map/near_adjoint/pallas_call | solution.py:651
  57.5 2.5 %query_sums.1 = (f32[4096,128]{1,0:T(8,128)S(1)}, f32[400,128]{1,0:T(8,128)S(1)}, f32[8,128]{1,0:T(8,128)}) custom-call(f32[512,128]{1,0:T(8,128)S(1)} %get-tuple-element.121.refs_0_, f32[4096,128]{1,0:T(8,128)S(1)} %get-tuple-element.117.refs_4_.refs_1_, f32[4096,128]{1,0:T(8,128)S(1)} %get-tuple-element.105.refs_3_.refs_5_.refs_2_, ...), custom_call_target="tpu_custom_call" | custom-call | flops 15728640 | bytes 2097152 | tf_op jit(solution)/shard_map/query_sums/pallas_call | solution.py:651
  61.1 1.3 %collective-permute-start.11 = (f32[328,128]{1,0:T(8,128)S(1)}, f32[328,128]{1,0:T(8,128)S(1)}, u32[]{:S(2)}, u32[]{:S(2)}) collective-permute-start(f32[328,128]{1,0:T(8,128)S(1)} %get-tuple-element.160), channel_id=1, source_target_pairs={{0,4},{4,0},{8,12},{12,8},{16,20},{20,16},{24,28},{28,24},{1,5},{5... | collective-permute-start | bytes 503816 | tf_op jit(solution)/shard_map/ppermute | solution.py:574
  62.4 3.4 %mixed.1 = (f32[4096,128]{1,0:T(8,128)S(1)}, f32[4096,128]{1,0:T(8,128)S(1)}, bf16[3,2,64,128]{3,2,1,0:T(8,128)(2,1)S(1)}, f32[8,128]{1,0:T(8,128)S(1)}) custom-call(f32[4096,128]{1,0:T(8,128)S(1)} %get-tuple-element.129.refs_0_, f32[4096,128]{1,0:T(8,128)S(1)} %get-tuple-element.130.refs_1_, f32[4096,128]{1,0:T(8,128)S(1)} %get-tuple-element.131.refs_2_, ...), custom_call_target="tpu_custom_call" | custom-call | flops 23592960 | bytes 2097152 | tf_op jit(solution)/shard_map/mixed/pallas_call | solution.py:651
  67.7 2.6 %collective-permute-start.10 = (bf16[3,2,64,128]{3,2,1,0:T(8,128)(2,1)S(1)}, bf16[3,2,64,128]{3,2,1,0:T(8,128)(2,1)S(1)}, u32[]{:S(2)}, u32[]{:S(2)}) collective-permute-start(bf16[3,2,64,128]{3,2,1,0:T(8,128)(2,1)S(1)} %get-tuple-element.155), channel_id=1, source_target_pairs={{0,28},{4,0},{8,4},{12,8},{16,12},{20,16},{24,20},{28,24},{1,29},{... | collective-permute-start | bytes 294920 | tf_op jit(solution)/shard_map/ppermute | solution.py:570
  70.3 2.2 %filter_sums.1 = (f32[224,128]{1,0:T(8,128)S(1)}, f32[8,128]{1,0:T(8,128)S(1)}) custom-call(f32[4096,128]{1,0:T(8,128)S(1)} %get-tuple-element.148.refs_0_, f32[4096,128]{1,0:T(8,128)S(1)} %get-tuple-element.149.refs_1_.refs_0_, f32[4224,128]{1,0:T(8,128)S(1)} %get-tuple-element.150.refs_2_, f32[4224,128]{1,0:T(8,128)S(1)} %get-tuple-element.151.refs_3_), custom_call_target="tpu_custom_call" | custom-call | flops 15728640 | bytes 2097152 | tf_op jit(solution)/shard_map/filter_sums/pallas_call | solution.py:651
  72.7 4.0 %collective-permute-start.13 = (f32[328,128]{1,0:T(8,128)S(1)}, f32[328,128]{1,0:T(8,128)S(1)}, u32[]{:S(2)}, u32[]{:S(2)}) collective-permute-start(f32[328,128]{1,0:T(8,128)S(1)} %add.6.one), channel_id=1, source_target_pairs={{0,16},{4,20},{8,24},{12,28},{16,0},{20,4},{24,8},{28,12},{1,17},{... | collective-permute-start | bytes 503816 | tf_op jit(solution)/shard_map/ppermute | solution.py:574
  76.7 2.9 %norm.1 = (bf16[256,2048]{1,0:T(8,128)(2,1)}, bf16[256,2048]{1,0:T(8,128)(2,1)}, f32[8,128]{1,0:T(8,128)S(1)}) custom-call(f32[512,128]{1,0:T(8,128)S(1)} %get-tuple-element.121.refs_0_, f32[4096,128]{1,0:T(8,128)S(1)} %get-tuple-element.117.refs_4_.refs_1_, f32[4096,128]{1,0:T(8,128)S(1)} %get-tuple-element.105.refs_3_.refs_5_.refs_2_, ...), custom_call_target="tpu_custom_call" | custom-call | flops 13107200 | bytes 2097152 | tf_op jit(solution)/shard_map/norm/pallas_call | solution.py:651
  79.5 2.3 %back_query.1 = (bf16[256,2048]{1,0:T(8,128)(2,1)}, f32[8,128]{1,0:T(8,128)S(1)}) custom-call(f32[4096,128]{1,0:T(8,128)S(1)} %get-tuple-element.136.refs_3_.refs_0_, bf16[3,2,64,128]{3,2,1,0:T(8,128)(2,1)S(1)} %collective-permute-done.10.refs_1_, f32[336,128]{1,0:T(8,128)S(1)} %get-tuple-element.93.refs_3_.refs_2_), custom_call_target="tpu_custom_call" | custom-call | flops 10485760 | bytes 2097152 | tf_op jit(solution)/shard_map/back_query/pallas_call | solution.py:651
  81.9 2.4 %collective-permute-start.16 = (f32[224,128]{1,0:T(8,128)S(1)}, f32[224,128]{1,0:T(8,128)S(1)}, u32[]{:S(2)}, u32[]{:S(2)}) collective-permute-start(f32[224,128]{1,0:T(8,128)S(1)} %add.8.one), channel_id=1, source_target_pairs={{0,8},{4,12},{8,0},{12,4},{16,24},{20,28},{24,16},{28,20},{1,9},{5... | collective-permute-start | bytes 344072 | tf_op jit(solution)/shard_map/ppermute | solution.py:574
  84.6 2.3 %back_key.1 = (bf16[256,2048]{1,0:T(8,128)(2,1)}, f32[8,128]{1,0:T(8,128)S(1)}) custom-call(f32[4096,128]{1,0:T(8,128)S(1)} %get-tuple-element.148.refs_0_, bf16[3,2,64,128]{3,2,1,0:T(8,128)(2,1)S(1)} %collective-permute-done.10.refs_1_, f32[336,128]{1,0:T(8,128)S(1)} %get-tuple-element.93.refs_3_.refs_2_), custom_call_target="tpu_custom_call" | custom-call | flops 10485760 | bytes 2097152 | tf_op jit(solution)/shard_map/back_key/pallas_call | solution.py:651
  87.9 2.3 %back_value.1 = (bf16[256,2048]{1,0:T(8,128)(2,1)}, f32[8,128]{1,0:T(8,128)S(1)}) custom-call(f32[4096,128]{1,0:T(8,128)S(1)} %get-tuple-element.149.refs_1_.refs_0_, bf16[3,2,64,128]{3,2,1,0:T(8,128)(2,1)S(1)} %collective-permute-done.10.refs_1_, f32[336,128]{1,0:T(8,128)S(1)} %get-tuple-element.93.refs_3_.refs_2_), custom_call_target="tpu_custom_call" | custom-call | flops 10485760 | bytes 2097152 | tf_op jit(solution)/shard_map/back_value/pallas_call | solution.py:651
  90.2 2.8 %collective-permute-done.17.refs_3_ = f32[224,128]{1,0:T(8,128)S(1)} collective-permute-done((f32[224,128]{1,0:T(8,128)S(1)}, f32[224,128]{1,0:T(8,128)S(1)}, u32[]{:S(2)}, u32[]{:S(2)}) %collective-permute-start.17) | collective-permute-done | bytes 114720 | tf_op jit(solution)/shard_map/ppermute | solution.py:574
  (39 shorter events, 12.0 us)
Async XLA Ops:
  1.6 9.7 %collective-permute-start = (bf16[3,8,2048]{2,1,0:T(8,128)(2,1)S(1)}, bf16[3,8,2048]{2,1,0:T(8,128)(2,1)S(1)}, u32[]{:S(2)}, u32[]{:S(2)}) collective-permute-start(bf16[3,8,2048]{2,1,0:T(8,128)(2,1)S(1)} %trailing.1), channel_id=1, source_target_pairs={{0,4},{4,8},{8,12},{12,16},{16,20},{20,24},{24,28},{28,0},{1,5},{5... | collective-permute-start | bytes 294920 | tf_op jit(solution)/shard_map/ppermute | solution.py:570
  12.0 12.9 %copy-start.1 = (f32[2048]{0:T(1024)S(1)}, f32[2048]{0:T(1024)}, u32[]{:S(2)}) copy-start(f32[2048]{0:T(1024)} %param.17) | copy-start | bytes 24580
  12.0 5.0 %collective-permute-start.1 = (f32[256,128]{1,0:T(8,128)S(1)}, f32[256,128]{1,0:T(8,128)S(1)}, u32[]{:S(2)}, u32[]{:S(2)}) collective-permute-start(f32[256,128]{1,0:T(8,128)S(1)} %get-tuple-element.107.own), channel_id=1, source_target_pairs={{0,4},{4,0},{8,12},{12,8},{16,20},{20,16},{24,28},{28,24},{1,5},{5... | collective-permute-start | bytes 393224 | tf_op jit(solution)/shard_map/ppermute | solution.py:574
  17.0 5.0 %collective-permute-start.2 = (f32[256,128]{1,0:T(8,128)S(1)}, f32[256,128]{1,0:T(8,128)S(1)}, u32[]{:S(2)}, u32[]{:S(2)}) collective-permute-start(f32[256,128]{1,0:T(8,128)S(1)} %get-tuple-element.109.own), channel_id=1, source_target_pairs={{0,8},{4,12},{8,0},{12,4},{16,24},{20,28},{24,16},{28,20},{1,9},{5... | collective-permute-start | bytes 393224 | tf_op jit(solution)/shard_map/ppermute | solution.py:574
  22.2 7.3 %collective-permute-start.3 = (f32[256,128]{1,0:T(8,128)S(1)}, f32[256,128]{1,0:T(8,128)S(1)}, u32[]{:S(2)}, u32[]{:S(2)}) collective-permute-start(f32[256,128]{1,0:T(8,128)S(1)} %get-tuple-element.113), channel_id=1, source_target_pairs={{0,16},{4,20},{8,24},{12,28},{16,0},{20,4},{24,8},{28,12},{1,17},{... | collective-permute-start | bytes 393224 | tf_op jit(solution)/shard_map/ppermute | solution.py:574
  24.9 4.6 %copy-start = (f32[2048]{0:T(1024)S(1)}, f32[2048]{0:T(1024)}, u32[]{:S(2)}) copy-start(f32[2048]{0:T(1024)} %param.18) | copy-start | bytes 24580
  34.4 3.0 %collective-permute-start.6 = (f32[2,256]{1,0:T(2,128)S(1)}, f32[2,256]{1,0:T(2,128)S(1)}, u32[]{:S(2)}, u32[]{:S(2)}) collective-permute-start(f32[2,256]{1,0:T(2,128)S(1)} %get-tuple-element.116.refs_0_), channel_id=1, source_target_pairs={{0,3},{1,2},{2,1},{3,0},{4,7},{5,6},{6,5},{7,4},{8,11},{9,10},{10,... | collective-permute-start | bytes 6152 | tf_op jit(solution)/shard_map/ppermute | solution.py:574
  34.4 3.6 %collective-permute-start.5 = (f32[2,256]{1,0:T(2,128)S(1)}, f32[2,256]{1,0:T(2,128)S(1)}, u32[]{:S(2)}, u32[]{:S(2)}) collective-permute-start(f32[2,256]{1,0:T(2,128)S(1)} %get-tuple-element.116.refs_0_), channel_id=1, source_target_pairs={{0,2},{1,3},{2,0},{3,1},{4,6},{5,7},{6,4},{7,5},{8,10},{9,11},{10,... | collective-permute-start | bytes 6152 | tf_op jit(solution)/shard_map/ppermute | solution.py:574
  35.9 2.1 %collective-permute-start.4 = (f32[2,256]{1,0:T(2,128)S(1)}, f32[2,256]{1,0:T(2,128)S(1)}, u32[]{:S(2)}, u32[]{:S(2)}) collective-permute-start(f32[2,256]{1,0:T(2,128)S(1)} %get-tuple-element.116.refs_0_), channel_id=1, source_target_pairs={{0,1},{1,0},{2,3},{3,2},{4,5},{5,4},{6,7},{7,6},{8,9},{9,8},{10,11... | collective-permute-start | bytes 6152 | tf_op jit(solution)/shard_map/ppermute | solution.py:574
  41.9 5.9 %collective-permute-start.7 = (f32[256,128]{1,0:T(8,128)S(1)}, f32[256,128]{1,0:T(8,128)S(1)}, u32[]{:S(2)}, u32[]{:S(2)}) collective-permute-start(f32[256,128]{1,0:T(8,128)S(1)} %get-tuple-element.137.own), channel_id=1, source_target_pairs={{0,4},{4,0},{8,12},{12,8},{16,20},{20,16},{24,28},{28,24},{1,5},{5... | collective-permute-start | bytes 393224 | tf_op jit(solution)/shard_map/ppermute | solution.py:574
  47.8 5.1 %collective-permute-start.8 = (f32[256,128]{1,0:T(8,128)S(1)}, f32[256,128]{1,0:T(8,128)S(1)}, u32[]{:S(2)}, u32[]{:S(2)}) collective-permute-start(f32[256,128]{1,0:T(8,128)S(1)} %get-tuple-element.139.own), channel_id=1, source_target_pairs={{0,8},{4,12},{8,0},{12,4},{16,24},{20,28},{24,16},{28,20},{1,9},{5... | collective-permute-start | bytes 393224 | tf_op jit(solution)/shard_map/ppermute | solution.py:574
  53.0 8.0 %collective-permute-start.9 = (f32[256,128]{1,0:T(8,128)S(1)}, f32[256,128]{1,0:T(8,128)S(1)}, u32[]{:S(2)}, u32[]{:S(2)}) collective-permute-start(f32[256,128]{1,0:T(8,128)S(1)} %get-tuple-element.143), channel_id=1, source_target_pairs={{0,16},{4,20},{8,24},{12,28},{16,0},{20,4},{24,8},{28,12},{1,17},{... | collective-permute-start | bytes 393224 | tf_op jit(solution)/shard_map/ppermute | solution.py:574
  61.1 5.4 %collective-permute-start.11 = (f32[328,128]{1,0:T(8,128)S(1)}, f32[328,128]{1,0:T(8,128)S(1)}, u32[]{:S(2)}, u32[]{:S(2)}) collective-permute-start(f32[328,128]{1,0:T(8,128)S(1)} %get-tuple-element.160), channel_id=1, source_target_pairs={{0,4},{4,0},{8,12},{12,8},{16,20},{20,16},{24,28},{28,24},{1,5},{5... | collective-permute-start | bytes 503816 | tf_op jit(solution)/shard_map/ppermute | solution.py:574
  66.6 6.1 %collective-permute-start.12 = (f32[328,128]{1,0:T(8,128)S(1)}, f32[328,128]{1,0:T(8,128)S(1)}, u32[]{:S(2)}, u32[]{:S(2)}) collective-permute-start(f32[328,128]{1,0:T(8,128)S(1)} %add.5.one), channel_id=1, source_target_pairs={{0,8},{4,12},{8,0},{12,4},{16,24},{20,28},{24,16},{28,20},{1,9},{5... | collective-permute-start | bytes 503816 | tf_op jit(solution)/shard_map/ppermute | solution.py:574
  67.7 5.0 %collective-permute-start.10 = (bf16[3,2,64,128]{3,2,1,0:T(8,128)(2,1)S(1)}, bf16[3,2,64,128]{3,2,1,0:T(8,128)(2,1)S(1)}, u32[]{:S(2)}, u32[]{:S(2)}) collective-permute-start(bf16[3,2,64,128]{3,2,1,0:T(8,128)(2,1)S(1)} %get-tuple-element.155), channel_id=1, source_target_pairs={{0,28},{4,0},{8,4},{12,8},{16,12},{20,16},{24,20},{28,24},{1,29},{... | collective-permute-start | bytes 294920 | tf_op jit(solution)/shard_map/ppermute | solution.py:570
  72.5 9.4 %collective-permute-start.15 = (f32[224,128]{1,0:T(8,128)S(1)}, f32[224,128]{1,0:T(8,128)S(1)}, u32[]{:S(2)}, u32[]{:S(2)}) collective-permute-start(f32[224,128]{1,0:T(8,128)S(1)} %get-tuple-element.164.one), channel_id=1, source_target_pairs={{0,4},{4,0},{8,12},{12,8},{16,20},{20,16},{24,28},{28,24},{1,5},{5... | collective-permute-start | bytes 344072 | tf_op jit(solution)/shard_map/ppermute | solution.py:574
  72.7 11.6 %collective-permute-start.13 = (f32[328,128]{1,0:T(8,128)S(1)}, f32[328,128]{1,0:T(8,128)S(1)}, u32[]{:S(2)}, u32[]{:S(2)}) collective-permute-start(f32[328,128]{1,0:T(8,128)S(1)} %add.6.one), channel_id=1, source_target_pairs={{0,16},{4,20},{8,24},{12,28},{16,0},{20,4},{24,8},{28,12},{1,17},{... | collective-permute-start | bytes 503816 | tf_op jit(solution)/shard_map/ppermute | solution.py:574
  81.9 5.4 %collective-permute-start.16 = (f32[224,128]{1,0:T(8,128)S(1)}, f32[224,128]{1,0:T(8,128)S(1)}, u32[]{:S(2)}, u32[]{:S(2)}) collective-permute-start(f32[224,128]{1,0:T(8,128)S(1)} %add.8.one), channel_id=1, source_target_pairs={{0,8},{4,12},{8,0},{12,4},{16,24},{20,28},{24,16},{28,20},{1,9},{5... | collective-permute-start | bytes 344072 | tf_op jit(solution)/shard_map/ppermute | solution.py:574
  84.3 8.8 %collective-permute-start.14 = (f32[328,128]{1,0:T(8,128)S(1)}, f32[328,128]{1,0:T(8,128)S(1)}, u32[]{:S(2)}, u32[]{:S(2)}) collective-permute-start(f32[328,128]{1,0:T(8,128)S(1)} %add.7.refs_0_), channel_id=1, source_target_pairs={{0,4},{4,0},{8,12},{12,8},{16,20},{20,16},{24,28},{28,24},{1,5},{5... | collective-permute-start | bytes 503816 | tf_op jit(solution)/shard_map/ppermute | solution.py:574
  87.3 5.8 %collective-permute-start.17 = (f32[224,128]{1,0:T(8,128)S(1)}, f32[224,128]{1,0:T(8,128)S(1)}, u32[]{:S(2)}, u32[]{:S(2)}) collective-permute-start(f32[224,128]{1,0:T(8,128)S(1)} %add.9.refs_2_), channel_id=1, source_target_pairs={{0,16},{4,20},{8,24},{12,28},{16,0},{20,4},{24,8},{28,12},{1,17},{... | collective-permute-start | bytes 344072 | tf_op jit(solution)/shard_map/ppermute | solution.py:574

commit v7 on v6

--- a/solution.py
+++ b/solution.py
@@ -187,13 +187,15 @@
         put(x_out, m, row(x_part, m) + rest[m] * own)
 
 
-def query_kernel(taps, steps, query, halo, filt, q_ext, f0):
+def query_kernel(taps, steps, query, residual, cot, halo, filt, q_ext, f0, res_pos, cot_pos):
     margin = taps - 1
     there = jnp.where(lax.axis_index("ctx") > 0, 1.0, 0.0)
     for s in range(SUB):
         lanes = slice(s * LANES, (s + 1) * LANES)
         q_ext[pl.ds(s, SUB, stride=SUB), :] = halo[0, :, lanes].astype(F32) * there
     spread(query, q_ext, SUB, steps)
+    spread(residual, res_pos, 0, steps)
+    spread(cot, cot_pos, 0, steps)
     taps0 = taps_of(filt, 0, taps)
 
     def conv(c, carry):
@@ -204,11 +206,6 @@
         return carry
 
     loop(0, steps // SUB, conv, 0)
-
-
-def inputs_kernel(steps, residual, cot, res_pos, cot_pos):
-    spread(residual, res_pos, 0, steps)
-    spread(cot, cot_pos, 0, steps)
 
 
 def near_taps(lam, res, skip, modes):
@@ -310,7 +307,7 @@
 
 def grad_modal_kernel(modes, steps, width, shares, *refs):
     own_sums, (summed, cot_pos, f0, lam, gain, ready) = refs[:shares], refs[shares : shares + 6]
-    scale, gm, adj, a_out = refs[shares + 6 :]
+    scale, gm, adj, a_out, a_next = refs[shares + 6 :]
     del ready
 
     @pl.when(pl.program_id(0) == 0)
@@ -340,6 +337,7 @@
             put(gm, t, now[i])
         new = []
         for m in range(modes):
+            put(a_next, m, a[m])
             own = horner(fade[m], now[::-1])
             put(adj, block * modes + m, own)
             new.append(own + skip[m] * a[m])
@@ -350,7 +348,12 @@
         put(a_out, m, a[m])
 
 
-def across_kernel(ms, modes, steps, gm, adj, x_at, lag, lam, res_part, rate_part):
+def across_kernel(modes, steps, *refs):
+    for start in (0, modes // 2):
+        across_part(range(start, start + modes // 2), modes, steps, *refs)
+
+
+def across_part(ms, modes, steps, gm, adj, x_at, lag, lam, res_part, rate_part):
     fade, far = fades(lam, modes, 1), fades(lam, modes, SUB)
     last = steps // SUB - 1
 
@@ -369,13 +372,11 @@
     none = zeros(len(ms))
     _, by_res, by_rate = loop(0, steps // SUB, across, (none, none, none))
     for i, m in enumerate(ms):
-        put(res_part, i, fade[m] * by_res[i])
-        put(rate_part, i, fade[m] * by_rate[i])
-
-
-def near_adjoint_kernel(modes, steps, gm, u, lam, res, skip, *refs):
-    res_parts, rate_parts, (gmy, res_sum, rate_sum, skip_sum) = refs[:2], refs[2:4], refs[4:]
-    half = modes // 2
+        put(res_part, m, fade[m] * by_res[i])
+        put(rate_part, m, fade[m] * by_rate[i])
+
+
+def near_adjoint_kernel(modes, taps, steps, gm, u, lam, res, skip, res_part, rate_part, scale, summed, cot_pos, modal, q_ext, gain, gmy, rate_sum, gf0, early):
     near = near_taps(lam, res, skip, modes)
 
     def pairs(c, lags):
@@ -388,16 +389,18 @@
         )
 
     lags = loop(0, steps // SUB, pairs, zeros(SUB))
-    skip_sum[...] = lags[0]
+    put(early, taps + modes, lags[0])
     fade = fades(lam, modes, 1)
     weighted = [lags[k] * float(k) for k in range(1, SUB)]
     for m in range(modes):
-        put(res_sum, m, row(res_parts[m // half], m % half) + horner(fade[m], lags[::-1]))
-        put(rate_sum, m, row(rate_parts[m // half], m % half) + fade[m] * horner(fade[m], weighted[::-1]))
-
-
-def norm_kernel(steps, scale, summed, cot_pos, gain, ready, normed, grad_res, work):
+        put(early, taps + m, row(res_part, m) + horner(fade[m], lags[::-1]))
+        put(rate_sum, m, row(rate_part, m) + fade[m] * horner(fade[m], weighted[::-1]))
+    query_sums(modes, taps, steps, scale, summed, cot_pos, modal, q_ext, gain, gf0, early)
+
+
+def norm_kernel(taps, steps, last, scale, summed, cot_pos, gain, gf0, next_head, filt, ready, normed, grad_res, grad_query, work, head):
     del ready
+    back(0, taps, steps, last, gf0, next_head, filt, grad_query, work, head)
     factor = gain[...]
 
     def norm(c, carry):
@@ -421,7 +424,7 @@
     gather_rows(work, grad_res, steps)
 
 
-def query_sums_kernel(modes, taps, steps, scale, summed, cot_pos, modal, q_ext, gain, res_sum, skip_sum, gf0, early):
+def query_sums(modes, taps, steps, scale, summed, cot_pos, modal, q_ext, gain, gf0, early):
     factor = gain[...]
 
     def grads(c, by_gain):
@@ -438,8 +441,6 @@
     sums = filter_pass(taps, steps, gf0, q_ext)
     for j in range(taps):
         put(early, j, sums[j])
-    early[pl.ds(taps * SUB, modes * SUB), :] = res_sum[...]
-    put(early, taps + modes, skip_sum[...])
 
 
 def filter_pass(taps, steps, grad, ext):
@@ -457,7 +458,7 @@
     return loop(0, steps // SUB, some, tuple(zero for _ in range(taps)))
 
 
-def mixed_kernel(modes, taps, steps, gmy, f1, f2, gf0, adj, lam, faded, alpha, gf1, gf2, heads):
+def mixed_kernel(modes, steps, gmy, f1, f2, adj, lam, faded, alpha, gf1, gf2):
     fade, skip = fades(lam, modes, 1), fades(lam, modes, SUB)
 
     def advance(c, after):
@@ -472,8 +473,6 @@
         return tuple(row(adj, block * modes + m) + skip[m] * after[m] for m in range(modes))
 
     loop(0, steps // SUB, advance, tuple(row(alpha, m) for m in range(modes)))
-    for which, grad in enumerate((gf0, gf1, gf2)):
-        heads[which, 0] = grad[: SUB * SUB, :].astype(BF16)
 
 
 def filter_sums_kernel(taps, steps, gf1, gf2, k_ext, v_ext, sums):
@@ -483,7 +482,12 @@
             put(sums, which * taps + j, parts[j])
 
 
-def back_kernel(which, taps, steps, last, grad, next_head, filt, out, work, head):
+def back_kernel(taps, steps, last, gf1, gf2, next_head, filt, grad_key, grad_value, work, head):
+    back(1, taps, steps, last, gf1, next_head, filt, grad_key, work, head)
+    back(2, taps, steps, last, gf2, next_head, filt, grad_value, work, head)
+
+
+def back(which, taps, steps, last, grad, next_head, filt, out, work, head):
     there = jnp.where(lax.axis_index("ctx") < last, 1.0, 0.0)
     head[...] = next_head[which, 0].astype(F32) * there
     weights = taps_of(filt, which, taps)
@@ -530,11 +534,34 @@
     ends[1][...] = inclusive(own[...], other[...], lam[...], span, group, sign)
 
 
+def join_four_kernel(span, sign, own, first, second, third, lam, *refs):
+    before, end = refs[-2:]
+    at, _ = place(4, sign)
+    here = lax.axis_index("ctx") if sign > 0 else lax.axis_size("ctx") - 1 - lax.axis_index("ctx")
+    here, rates = here % 4, lam[...]
+    total_end = jnp.exp(rates * ((3.0 - at) * -float(span))) * own[...]
+    total_before = None
+    for k, other in enumerate((first, second, third)):
+        there = (here ^ (k + 1)).astype(F32)
+        earlier = jnp.where(there < at, 1.0, 0.0)
+        gap = jnp.maximum(at - 1.0 - there, 0.0)
+        value = other[...]
+        share = earlier * jnp.exp(rates * (gap * -float(span))) * value
+        total_before = share if total_before is None else total_before + share
+        total_end = total_end + jnp.exp(rates * ((3.0 - there) * -float(span))) * value
+    before[...] = total_before
+    end[...] = total_end
+
+
+def add_four_kernel(own, first, second, third, *refs):
+    refs[-1][...] = (own[...] + first[...]) + (second[...] + third[...])
+
+
 def add_kernel(one, other, *refs):
     refs[-1][...] = one[...] + other[...]
 
 
-def pack_kernel(span, group, modes, first_rows, half, before, other, lam, early, res, rate_sum, lag_sum, alpha, kept, sent):
+def pack_kernel(span, group, modes, first_rows, half, before, other, lam, early, res, rate_sum, lag_sum, faded, a_next, gmy, f1, f2, gf0, alpha, kept, sent, heads):
     alpha[...] = exclusive(before[...], other[...], lam[...], span, group, -1)
     odd = lax.axis_index("ctx") % 2
     rows = (first_rows + modes) * SUB
@@ -546,10 +573,21 @@
             mine = pl.ds(source, modes * SUB)
             lagged = rate_sum[mine, :] + jnp.exp(-lam[mine, :]) * alpha[mine, :] * lag_sum[mine, :]
             out[pl.ds(b * rows + first_rows * SUB, modes * SUB), :] = -res[mine, :] * lagged
-
-
-def finish_kernel(modes, taps, half, early_rows, mine, other, late_mine, late_other, after, short, res, rate, skip, gain, late, early):
-    del after
+    for b in range(2 * half):
+        mine = slice(b * modes * SUB, (b + 1) * modes * SUB)
+        far = jnp.exp(lam[mine, :] * -float(span - SUB))
+        w, fade = faded[mine, :] * (a_next[mine, :] + far * alpha[mine, :]), jnp.exp(-lam[mine, :])
+        here, grads = slice(b * span * SUB, (b * span + SUB) * SUB), []
+        for t in range(SUB):
+            grads.append(total([w[m * SUB : (m + 1) * SUB, :] for m in range(modes)]))
+            w = fade * w
+        grad = gmy[here, :] + jnp.concatenate(grads[::-1], axis=0)
+        for which, value in enumerate((gf0[here, :], grad * f2[here, :], grad * f1[here, :])):
+            heads[which, b] = value.astype(BF16)
+
+
+def finish_kernel(modes, taps, half, early_rows, mine, other, late_mine, late_other, ready, short, res, rate, skip, gain, late, early):
+    del ready
     block = pl.program_id(0)
     late[...] = late_mine[...] + late_other[...]
     own = jnp.where(lax.axis_index("ctx") % 2 == block // half, 1.0, 0.0)
@@ -576,11 +614,12 @@
 
 def small(body, ins, after, outs, name):
     near = pl.BlockSpec(memory_space=pltpu.VMEM)
+    ins = [pltpu.with_memory_space_constraint(v, pltpu.VMEM) if v.size > 1 << 18 else v for v in ins]
     return pl.pallas_call(
         body,
         in_specs=[near] * len(ins) + [pl.BlockSpec(memory_space=pl.ANY)] * len(after),
         out_specs=[near] * len(outs),
-        out_shape=[jax.ShapeDtypeStruct(shape, F32) for shape in outs],
+        out_shape=[jax.ShapeDtypeStruct(shape, BF16 if len(shape) > 2 else F32) for shape in outs],
         compiler_params=pltpu.CompilerParams(vmem_limit_bytes=VMEM_LIMIT),
         cost_estimate=pl.CostEstimate(flops=ins[0].size, bytes_accessed=0, transcendentals=0),
         name=name,
@@ -590,6 +629,11 @@
 def scan_but_last(own, lam, span, sign, under):
     count, group, before = lax.axis_size("ctx"), 1, None
     under = list(under)
+    if count >= 8:
+        ins = [own, *(swap(own, "ctx", k) for k in (1, 2, 3)), lam]
+        body = functools.partial(join_four_kernel, span, sign)
+        before, own = small(body, ins, under, [own.shape] * 2, "join")
+        group, under = 4, []
     while True:
         other = swap(own, "ctx", group)
         if 2 * group >= count:
@@ -705,23 +749,14 @@
         "head",
         aliases={1: 0, 2: 1, 6: 2, 7: 3, 8: 4, 9: 5},
     )
-    q_ext, f0, query_done = call(
+    q_ext, f0, res_pos, cot_pos, query_done = call(
         functools.partial(query_kernel, taps, steps),
-        (far[1], halo, filt),
-        [wide_spec, halo_spec, filt_spec],
-        [ext, seq],
-        [ext_spec, seq_spec],
-        20,
+        (far[1], far[0], far[4], halo, filt),
+        [wide_spec, wide_spec, wide_spec, halo_spec, filt_spec],
+        [ext, seq, seq, seq],
+        [ext_spec, seq_spec, seq_spec, seq_spec],
+        30,
         "query",
-    )
-    res_pos, cot_pos, inputs_done = call(
-        functools.partial(inputs_kernel, steps),
-        (far[0], far[4]),
-        [wide_spec] * 2,
-        [seq, seq],
-        [seq_spec] * 2,
-        10,
-        "inputs",
     )
     y, _ = call(
         functools.partial(near_kernel, modes, steps),
@@ -741,7 +776,7 @@
         32,
         "lags",
     )
-    before, other, group = scan_but_last(x_own, lam, steps, 1, [query_done, inputs_done])
+    before, other, group = scan_but_last(x_own, lam, steps, 1, [query_done])
     modal, summed, x_at, sums, _ = call(
         functools.partial(summed_kernel, modes, steps, blocks, group),
         (y, f0, res_pos, cot_pos, g, before, other, lam, faded, gain, own_lag_done),
@@ -763,75 +798,60 @@
         "borders",
     )
     scale_spec = pl.BlockSpec((2 * steps, LANES), lambda h: (0, 0))
-    scale, gm, adj, a_own, _ = call(
+    scale, gm, adj, a_own, a_next, _ = call(
         functools.partial(grad_modal_kernel, modes, steps, width, len(all_sums)),
         (*all_sums, summed, cot_pos, f0, lam, gain, lags_done),
         [pl.BlockSpec((2, steps), lambda h: (0, 0))] * len(all_sums)
         + [seq_spec, seq_spec, seq_spec, mode_spec, one_spec, any_spec],
-        [pltpu.VMEM((2 * steps, LANES), F32), seq, eights, mode],
-        [scale_spec, seq_spec, eights_spec, mode_spec],
+        [pltpu.VMEM((2 * steps, LANES), F32), seq, eights, mode, mode],
+        [scale_spec, seq_spec, eights_spec, mode_spec, mode_spec],
         45,
         "grad_modal",
     )
-    few = modes // 2
-    res_parts, rate_parts, across_done = zip(
-        *(
-            call(
-                functools.partial(across_kernel, range(start, start + few), modes, steps),
-                (gm, adj, x_at, lag, lam),
-                [seq_spec, eights_spec, eights_spec, eights_spec, mode_spec],
-                [pos(few), pos(few)],
-                [pos_spec(few), pos_spec(few)],
-                25,
-                "across",
-            )
-            for start in (0, few)
-        )
-    )
-    gmy, res_sum, rate_sum, skip_sum, _ = call(
-        functools.partial(near_adjoint_kernel, modes, steps),
-        (gm, u, lam, res, skip, *res_parts, *rate_parts),
-        [seq_spec, seq_spec, mode_spec, mode_spec, one_spec] + [pos_spec(few)] * 4,
-        [seq, mode, mode, one],
-        [seq_spec, mode_spec, mode_spec, one_spec],
-        25,
+    res_part, rate_part, across_done = call(
+        functools.partial(across_kernel, modes, steps),
+        (gm, adj, x_at, lag, lam),
+        [seq_spec, eights_spec, eights_spec, eights_spec, mode_spec],
+        [mode, mode],
+        [mode_spec, mode_spec],
+        50,
+        "across",
+    )
+    early_rows = taps + modes + 2
+    gmy, rate_sum, gf0, early, _ = call(
+        functools.partial(near_adjoint_kernel, modes, taps, steps),
+        (gm, u, lam, res, skip, res_part, rate_part, scale, summed, cot_pos, modal, q_ext, gain),
+        [seq_spec, seq_spec, mode_spec, mode_spec, one_spec, mode_spec, mode_spec, scale_spec, seq_spec, seq_spec, seq_spec, ext_spec, one_spec],
+        [seq, mode, seq, pos(early_rows)],
+        [seq_spec, mode_spec, seq_spec, pos_spec(early_rows)],
+        55,
         "near_adjoint",
     )
-    early_rows = taps + modes + 2
-    gf0, early, _ = call(
-        functools.partial(query_sums_kernel, modes, taps, steps),
-        (scale, summed, cot_pos, modal, q_ext, gain, res_sum, skip_sum),
-        [scale_spec, seq_spec, seq_spec, seq_spec, ext_spec, one_spec, mode_spec, one_spec],
-        [seq, pos(early_rows)],
-        [seq_spec, pos_spec(early_rows)],
-        30,
-        "query_sums",
-    )
-    before, other, group = scan_but_last(a_own, lam, steps, -1, across_done)
+    before, other, group = scan_but_last(a_own, lam, steps, -1, [across_done])
 
     half = blocks // 2
     half_shape = (half * (early_rows + modes) * SUB, LANES)
-    alpha, kept_half, sent_half = small(
+    alpha, kept_half, sent_half, heads = small(
         functools.partial(pack_kernel, steps, group, modes, early_rows, half),
-        [before, other, lam, early, res, rate_sum, lag_sum],
+        [before, other, lam, early, res, rate_sum, lag_sum, faded, a_next, gmy, f1, f2, gf0],
         [],
-        [lam.shape, half_shape, half_shape],
+        [lam.shape, half_shape, half_shape, (3, blocks, SUB * SUB, LANES)],
         "pack",
     )
     early_rows += modes
     late_rows = 2 * taps
     next_spec = pl.BlockSpec((3, 1, SUB * SUB, LANES), lambda h: (0, h, 0, 0))
     other_half = swap(sent_half, "ctx", 1)
-    gf1, gf2, heads, mixed_done = call(
-        functools.partial(mixed_kernel, modes, taps, steps),
-        (gmy, f1, f2, gf0, adj, lam, faded, alpha),
-        [seq_spec] * 4 + [eights_spec] + [mode_spec] * 3,
-        [seq, seq, jax.ShapeDtypeStruct((3, blocks, SUB * SUB, LANES), BF16)],
-        [seq_spec, seq_spec, next_spec],
+    next_head = ring(heads, "ctx", -1)
+    gf1, gf2, mixed_done = call(
+        functools.partial(mixed_kernel, modes, steps),
+        (gmy, f1, f2, adj, lam, faded, alpha),
+        [seq_spec] * 3 + [eights_spec] + [mode_spec] * 3,
+        [seq, seq],
+        [seq_spec, seq_spec],
         45,
         "mixed",
     )
-    next_head = ring(heads, "ctx", -1)
     late, late_done = call(
         functools.partial(filter_sums_kernel, taps, steps),
         (gf1, gf2, k_ext, v_ext),
@@ -842,55 +862,51 @@
         "filter_sums",
     )
 
-    normed, grad_residual, norm_done = call(
-        functools.partial(norm_kernel, steps),
-        (scale, summed, cot_pos, gain, late_done),
-        [scale_spec, seq_spec, seq_spec, one_spec, any_spec],
+    last = lax.axis_size("ctx") - 1
+    back_scratch = [pltpu.VMEM((steps * SUB, LANES), F32), pltpu.VMEM((SUB * SUB, LANES), F32)]
+    normed, grad_residual, grad_query, norm_done = call(
+        functools.partial(norm_kernel, taps, steps, last),
+        (scale, summed, cot_pos, gain, gf0, next_head, filt, late_done),
+        [scale_spec, seq_spec, seq_spec, one_spec, seq_spec, next_spec, filt_spec, any_spec],
+        [wide, wide, wide],
+        [wide_spec, wide_spec, wide_spec],
+        45,
+        "norm",
+        scratch=back_scratch,
+    )
+    grad_key, grad_value, back_done = call(
+        functools.partial(back_kernel, taps, steps, last),
+        (gf1, gf2, next_head, filt),
+        [seq_spec, seq_spec, next_spec, filt_spec],
         [wide, wide],
         [wide_spec, wide_spec],
-        25,
-        "norm",
-        scratch=[pltpu.VMEM((steps * SUB, LANES), F32)],
-    )
-
-    def back(which, grad, name):
-        return call(
-            functools.partial(back_kernel, which, taps, steps, lax.axis_size("ctx") - 1),
-            (grad, next_head, filt),
-            [seq_spec, next_spec, filt_spec],
-            [wide],
-            [wide_spec],
-            20,
-            name,
-            scratch=[
-                pltpu.VMEM((steps * SUB, LANES), F32),
-                pltpu.VMEM((SUB * SUB, LANES), F32),
-            ],
-        )
-
-    grad_query, query_done = back(0, gf0, "back_query")
-    grad_key, key_done = back(1, gf1, "back_key")
-    grad_value, value_done = back(2, gf2, "back_value")
-    count, under = lax.axis_size("ctx"), [[late_done, next_head], [norm_done, query_done]]
-    mine = small(add_kernel, [kept_half, other_half], [mixed_done], [half_shape], "add")[0]
+        40,
+        "back",
+        scratch=back_scratch,
+    )
+    count, under = lax.axis_size("ctx"), [[late_done], [norm_done]]
+    mine = small(add_kernel, [kept_half, other_half], [mixed_done, next_head], [half_shape], "add")[0]
     step = 2
     while step < count:
-        after = under.pop(0) if under else [query_done]
+        after = under.pop(0) if under else [norm_done]
         mine = small(add_kernel, [mine, swap(mine, "ctx", step)], after, [half_shape], "add")[0]
         step *= 2
     other = swap(mine, "ctx", 1)
-    step, under = 1, [[norm_done, query_done], [key_done]]
+    step = 1
+    if count >= 8:
+        ins = [late, *(swap(late, "ctx", k) for k in (1, 2, 3))]
+        late = small(add_four_kernel, ins, [norm_done], [late.shape], "add")[0]
+        step = 4
     late_other = swap(late, "ctx", step)
     while 2 * step < count:
-        after = under.pop(0) if under else [key_done]
-        late = small(add_kernel, [late, late_other], after, [late.shape], "add")[0]
+        late = small(add_kernel, [late, late_other], [norm_done], [late.shape], "add")[0]
         step *= 2
         late_other = swap(late, "ctx", step)
     half_spec = pl.BlockSpec((early_rows * SUB, LANES), lambda h: (h % half, 0))
     late_spec = pos_spec(late_rows)
     grad_short, grad_residues, grad_rate, grad_skip, grad_gain, _ = call(
         functools.partial(finish_kernel, modes, taps, half, early_rows),
-        (mine, other, late, late_other, value_done),
+        (mine, other, late, late_other, back_done),
         [half_spec, half_spec, late_spec, late_spec, any_spec],
         [
             jax.ShapeDtypeStruct(short_filter.shape, F32),

time: 94.9 us -> 92.2 us (0.972)
  Pallas kernels: 52.3 us -> 50 us
    pallas_call x20 -> x15, Pallas kernels: 50.9 us -> 48.5 us  [call(): pl.pallas_call(with_done, grid=(blocks,), in_specs=in_specs, out_specs=ou...]
    ppermute x16 -> x19, starting transfers between devices: 22.3 us -> 21.9 us  [swap(): lax.ppermute(value, axis, [(i, i ^ step) for i in range(lax.axis_size(axi...]
    ppermute x16 -> x19, waiting for transfers between devices: 13 us -> 12.8 us  [swap(): lax.ppermute(value, axis, [(i, i ^ step) for i in range(lax.axis_size(axi...]
  transfers between devices with their start and end apart: 18 -> 21, of which waited for: 12 -> 9; matrix products, arithmetic and copies ran while one was open for 0% -> 0% of each run, Pallas kernels for 43% -> 41%
where the time goes in v7:
time: 92.2 us; the launch traced here: 92 us
  Pallas kernels  50 us (54%)
  starting transfers between devices  27.6 us (30%)
  waiting for transfers between devices  13.6 us (15%)
    pallas_call x15, Pallas kernels, call(): pl.pallas_call(with_done, grid=(blocks,), in_specs=in_specs, out_specs=ou...  48.5 us
    ppermute x19, starting transfers between devices, swap(): lax.ppermute(value, axis, [(i, i ^ step) for i in range(lax.axis_size(axi...  21.9 us
    ppermute x19, waiting for transfers between devices, swap(): lax.ppermute(value, axis, [(i, i ^ step) for i in range(lax.axis_size(axi...  12.8 us
    ppermute x2, starting transfers between devices, ring(): lax.ppermute(value, axis, [(i, (i + distance) % count) for i in range(cou...  5.66 us
  transfers between devices with their start and end apart: 21, of which 9 were waited for; matrix products, arithmetic and copies ran while one was open for 0% of the time, Pallas kernels for 41%

profile of v7, /device:TPU:0, one launch (start us, length us, event | category | flops | bytes accessed | tf_op | source)
XLA Modules:
  0.0 92.0 jit_solution(10006401421668216451)
XLA Ops:
  0.6 0.9 trailing.1
  1.6 3.0 %collective-permute-start = (bf16[3,8,2048]{2,1,0:T(8,128)(2,1)S(1)}, bf16[3,8,2048]{2,1,0:T(8,128)(2,1)S(1)}, u32[]{:S(2)}, u32[]{:S(2)}) collective-permute-start(bf16[3,8,2048]{2,1,0:T(8,128)(2,1)S(1)} %trailing.1), channel_id=1, source_target_pairs={{0,4},{4,8},{8,12},{12,16},{16,20},{20,24},{24,28},{28,0},{1,5},{5... | collective-permute-start | bytes 294920 | tf_op jit(solution)/shard_map/ppermute | solution.py:608
  4.5 6.7 %features.1 = (f32[4224,128]{1,0:T(8,128)S(1)}, f32[4224,128]{1,0:T(8,128)S(1)}, f32[4096,128]{1,0:T(8,128)S(1)}, f32[4096,128]{1,0:T(8,128)S(1)}, f32[4096,128]...) custom-call(bf16[256,2048]{1,0:T(8,128)(2,1)} %refs_0_.2, ...), custom_call_target="tpu_custom_call" | custom-call | flops 33554432 | bytes 2097152 | tf_op jit(solution)/shard_map/features/pallas_call | solution.py:695
  12.0 2.6 %collective-permute-start.3 = (f32[256,128]{1,0:T(8,128)S(1)}, f32[256,128]{1,0:T(8,128)S(1)}, u32[]{:S(2)}, u32[]{:S(2)}) collective-permute-start(f32[256,128]{1,0:T(8,128)S(1)} %get-tuple-element.96.own), channel_id=1, source_target_pairs={{0,12},{4,8},{8,4},{12,0},{16,28},{20,24},{24,20},{28,16},{1,13},{... | collective-permute-start | bytes 393224 | tf_op jit(solution)/shard_map/ppermute | solution.py:612
  15.5 3.6 %query.3 = (f32[4224,128]{1,0:T(8,128)S(1)}, f32[4096,128]{1,0:T(8,128)S(1)}, f32[4096,128]{1,0:T(8,128)S(1)}, f32[4096,128]{1,0:T(8,128)S(1)}, f32[8,128]{1,0:T(8,128)S(1)}) custom-call(bf16[256,2048]{1,0:T(8,128)(2,1)} %refs_0_.3, bf16[256,2048]{1,0:T(8,128)(2,1)} %refs_1_.3, bf16[256,2048]{1,0:T(8,128)(2,1)} %refs_2_.3, ...), custom_call_target="tpu_custom_call" | custom-call | flops 15728640 | bytes 2097152 | tf_op jit(solution)/shard_map/query/pallas_call | solution.py:695
  19.4 1.4 %collective-permute-done.2.second = f32[256,128]{1,0:T(8,128)S(1)} collective-permute-done((f32[256,128]{1,0:T(8,128)S(1)}, f32[256,128]{1,0:T(8,128)S(1)}, u32[]{:S(2)}, u32[]{:S(2)}) %collective-permute-start.2) | collective-permute-done | bytes 131104 | tf_op jit(solution)/shard_map/ppermute | solution.py:612
  20.9 2.7 %collective-permute-start.4 = (f32[256,128]{1,0:T(8,128)S(1)}, f32[256,128]{1,0:T(8,128)S(1)}, u32[]{:S(2)}, u32[]{:S(2)}) collective-permute-start(f32[256,128]{1,0:T(8,128)S(1)} %get-tuple-element.99), channel_id=1, source_target_pairs={{0,16},{4,20},{8,24},{12,28},{16,0},{20,4},{24,8},{28,12},{1,17},{... | collective-permute-start | bytes 393224 | tf_op jit(solution)/shard_map/ppermute | solution.py:612
  23.6 1.4 %near.1 = (f32[4096,128]{1,0:T(8,128)S(1)}, f32[8,128]{1,0:T(8,128)}) custom-call(f32[4096,128]{1,0:T(8,128)S(1)} %get-tuple-element.89.refs_0_.refs_1_, f32[256,128]{1,0:T(8,128)S(1)} %get-tuple-element.83.refs_4_.refs_1_.lam.refs_7_.refs_2_, f32[256,128]{1,0:T(8,128)S(1)} %get-tuple-element.90.refs_2_.refs_3_.res, f32[16,128]{1,0:T(8,128)S(1)} %bitcast.8), custom_call_target="tpu_custom_call" | custom-call | flops 5242880 | bytes 2097152 | tf_op jit(solution)/shard_map/near/pallas_call | solution.py:695
  25.0 2.2 %lags.1 = (f32[8192,128]{1,0:T(8,128)S(1)}, f32[8,128]{1,0:T(8,128)S(1)}) custom-call(f32[4096,128]{1,0:T(8,128)S(1)} %get-tuple-element.89.refs_0_.refs_1_, f32[256,128]{1,0:T(8,128)S(1)} %get-tuple-element.83.refs_4_.refs_1_.lam.refs_7_.refs_2_), custom_call_target="tpu_custom_call" | custom-call | flops 16777216 | bytes 2097152 | tf_op jit(solution)/shard_map/lags/pallas_call | solution.py:695
  27.2 2.2 %collective-permute-done.4.refs_6_ = f32[256,128]{1,0:T(8,128)S(1)} collective-permute-done((f32[256,128]{1,0:T(8,128)S(1)}, f32[256,128]{1,0:T(8,128)S(1)}, u32[]{:S(2)}, u32[]{:S(2)}) %collective-permute-start.4) | collective-permute-done | bytes 131104 | tf_op jit(solution)/shard_map/ppermute | solution.py:612
  29.3 4.9 %summed.1 = (f32[4096,128]{1,0:T(8,128)S(1)}, f32[4096,128]{1,0:T(8,128)S(1)}, f32[8192,128]{1,0:T(8,128)S(1)}, f32[2,256]{1,0:T(2,128)S(1)}, f32[8,128]{1,0:T(8,128)}) custom-call(f32[4096,128]{1,0:T(8,128)S(1)} %get-tuple-element.91.refs_0_, f32[4096,128]{1,0:T(8,128)S(1)} %get-tuple-element.92.refs_1_.refs_6_, f32[4096,128]{1,0:T(8,128)S(1)} %get-tuple-element.93.refs_2_, ...), custom_call_target="tpu_custom_call" | custom-call | flops 26214400 | bytes 2097152 | tf_op jit(solution)/shard_map/summed/pallas_call | solution.py:695
  34.2 1.4 %collective-permute-start.6 = (f32[2,256]{1,0:T(2,128)S(1)}, f32[2,256]{1,0:T(2,128)S(1)}, u32[]{:S(2)}, u32[]{:S(2)}) collective-permute-start(f32[2,256]{1,0:T(2,128)S(1)} %get-tuple-element.102.refs_0_), channel_id=1, source_target_pairs={{0,2},{1,3},{2,0},{3,1},{4,6},{5,7},{6,4},{7,5},{8,10},{9,11},{10,... | collective-permute-start | bytes 6152 | tf_op jit(solution)/shard_map/ppermute | solution.py:612
  36.1 1.0 %borders.1 = (f32[8192,128]{1,0:T(8,128)S(1)}, f32[256,128]{1,0:T(8,128)S(1)}, f32[8,128]{1,0:T(8,128)S(1)}) custom-call(f32[8192,128]{1,0:T(8,128)S(1)} %get-tuple-element.104.refs_0_, f32[8192,128]{1,0:T(8,128)S(1)} %get-tuple-element.105.refs_1_.refs_2_, f32[256,128]{1,0:T(8,128)S(1)} %get-tuple-element.83.refs_4_.refs_1_.lam.refs_7_.refs_2_), custom_call_target="tpu_custom_call" | custom-call | flops 4194304 | bytes 2097152 | tf_op jit(solution)/shard_map/borders/pallas_call | solution.py:695
  37.8 3.9 %grad_modal.1 = (f32[512,128]{1,0:T(8,128)S(1)}, f32[4096,128]{1,0:T(8,128)S(1)}, f32[8192,128]{1,0:T(8,128)S(1)}, f32[256,128]{1,0:T(8,128)S(1)}, f32[256,128]{1,0:T(8,128)S(1)}, /*index=5*/f32[8,128]{1,0:T(8,128)}) custom-call(f32[2,256]{1,0:T(2,128)S(1)} %get-tuple-element.102.refs_0_, f32[2,256]{1,0:T(2,128)S(1)} %collective-permute-done.5.refs_1_, ...), custom_call_target="tpu_custom_call" | custom-call | flops 23592960 | bytes 2097152 | tf_op jit(solution)/shard_map/grad_modal/pallas_call | solution.py:695
  42.1 2.8 %collective-permute-start.9 = (f32[256,128]{1,0:T(8,128)S(1)}, f32[256,128]{1,0:T(8,128)S(1)}, u32[]{:S(2)}, u32[]{:S(2)}) collective-permute-start(f32[256,128]{1,0:T(8,128)S(1)} %get-tuple-element.116.own), channel_id=1, source_target_pairs={{0,8},{4,12},{8,0},{12,4},{16,24},{20,28},{24,16},{28,20},{1,9},{5... | collective-permute-start | bytes 393224 | tf_op jit(solution)/shard_map/ppermute | solution.py:612
  45.2 4.7 %across.1 = (f32[256,128]{1,0:T(8,128)S(1)}, f32[256,128]{1,0:T(8,128)S(1)}, f32[8,128]{1,0:T(8,128)S(1)}) custom-call(f32[4096,128]{1,0:T(8,128)S(1)} %get-tuple-element.108.refs_0_, f32[8192,128]{1,0:T(8,128)S(1)} %get-tuple-element.109.refs_1_.refs_3_, f32[8192,128]{1,0:T(8,128)S(1)} %get-tuple-element.105.refs_1_.refs_2_, ...), custom_call_target="tpu_custom_call" | custom-call | flops 26214400 | bytes 2097152 | tf_op jit(solution)/shard_map/across/pallas_call | solution.py:695
  50.0 1.6 %collective-permute-done.9.second = f32[256,128]{1,0:T(8,128)S(1)} collective-permute-done((f32[256,128]{1,0:T(8,128)S(1)}, f32[256,128]{1,0:T(8,128)S(1)}, u32[]{:S(2)}, u32[]{:S(2)}) %collective-permute-start.9) | collective-permute-done | bytes 131104 | tf_op jit(solution)/shard_map/ppermute | solution.py:612
  51.8 1.0 %collective-permute-start.11 = (f32[256,128]{1,0:T(8,128)S(1)}, f32[256,128]{1,0:T(8,128)S(1)}, u32[]{:S(2)}, u32[]{:S(2)}) collective-permute-start(f32[256,128]{1,0:T(8,128)S(1)} %get-tuple-element.119), channel_id=1, source_target_pairs={{0,16},{4,20},{8,24},{12,28},{16,0},{20,4},{24,8},{28,12},{1,17},{... | collective-permute-start | bytes 393224 | tf_op jit(solution)/shard_map/ppermute | solution.py:612
  52.8 4.3 %near_adjoint.1 = (f32[4096,128]{1,0:T(8,128)S(1)}, f32[256,128]{1,0:T(8,128)S(1)}, f32[4096,128]{1,0:T(8,128)S(1)}, f32[400,128]{1,0:T(8,128)S(1)}, f32[8,128]{1,0:T(8,128)}) custom-call(f32[4096,128]{1,0:T(8,128)S(1)} %get-tuple-element.108.refs_0_, f32[4096,128]{1,0:T(8,128)S(1)} %get-tuple-element.89.refs_0_.refs_1_, ...), custom_call_target="tpu_custom_call" | custom-call | flops 28835840 | bytes 2097152 | tf_op jit(solution)/shard_map/near_adjoint/pallas_call | solution.py:695
  57.1 3.5 %collective-permute-done.11.other = f32[256,128]{1,0:T(8,128)S(1)} collective-permute-done((f32[256,128]{1,0:T(8,128)S(1)}, f32[256,128]{1,0:T(8,128)S(1)}, u32[]{:S(2)}, u32[]{:S(2)}) %collective-permute-start.11) | collective-permute-done | bytes 131104 | tf_op jit(solution)/shard_map/ppermute | solution.py:612
  61.6 2.7 %collective-permute-start.12 = (bf16[3,2,64,128]{3,2,1,0:T(8,128)(2,1)S(1)}, bf16[3,2,64,128]{3,2,1,0:T(8,128)(2,1)S(1)}, u32[]{:S(2)}, u32[]{:S(2)}) collective-permute-start(bf16[3,2,64,128]{3,2,1,0:T(8,128)(2,1)S(1)} %get-tuple-element.127), channel_id=1, source_target_pairs={{0,28},{4,0},{8,4},{12,8},{16,12},{20,16},{24,20},{28,24},{1,29},{... | collective-permute-start | bytes 294920 | tf_op jit(solution)/shard_map/ppermute | solution.py:608
  64.3 3.3 %mixed.1 = (f32[4096,128]{1,0:T(8,128)S(1)}, f32[4096,128]{1,0:T(8,128)S(1)}, f32[8,128]{1,0:T(8,128)S(1)}) custom-call(f32[4096,128]{1,0:T(8,128)S(1)} %get-tuple-element.124.gmy.refs_0_, f32[4096,128]{1,0:T(8,128)S(1)} %get-tuple-element.125.f1.refs_1_, f32[4096,128]{1,0:T(8,128)S(1)} %get-tuple-element.126.f2.refs_2_, ...), custom_call_target="tpu_custom_call" | custom-call | flops 23592960 | bytes 2097152 | tf_op jit(solution)/shard_map/mixed/pallas_call | solution.py:695
  68.5 2.3 %filter_sums.1 = (f32[224,128]{1,0:T(8,128)S(1)}, f32[8,128]{1,0:T(8,128)S(1)}) custom-call(f32[4096,128]{1,0:T(8,128)S(1)} %get-tuple-element.129.refs_0_, f32[4096,128]{1,0:T(8,128)S(1)} %get-tuple-element.130.refs_1_, f32[4224,128]{1,0:T(8,128)S(1)} %get-tuple-element.131.refs_2_, f32[4224,128]{1,0:T(8,128)S(1)} %get-tuple-element.132.refs_3_), custom_call_target="tpu_custom_call" | custom-call | flops 15728640 | bytes 2097152 | tf_op jit(solution)/shard_map/filter_sums/pallas_call | solution.py:695
  70.8 3.1 %collective-permute-done.14.other = f32[328,128]{1,0:T(8,128)S(1)} collective-permute-done((f32[328,128]{1,0:T(8,128)S(1)}, f32[328,128]{1,0:T(8,128)S(1)}, u32[]{:S(2)}, u32[]{:S(2)}) %collective-permute-start.14) | collective-permute-done | bytes 167968 | tf_op jit(solution)/shard_map/ppermute | solution.py:612
  73.9 1.7 %collective-permute-start.15 = (f32[328,128]{1,0:T(8,128)S(1)}, f32[328,128]{1,0:T(8,128)S(1)}, u32[]{:S(2)}, u32[]{:S(2)}) collective-permute-start(f32[328,128]{1,0:T(8,128)S(1)} %add.5.one), channel_id=1, source_target_pairs={{0,16},{4,20},{8,24},{12,28},{16,0},{20,4},{24,8},{28,12},{1,17},{... | collective-permute-start | bytes 503816 | tf_op jit(solution)/shard_map/ppermute | solution.py:612
  75.6 2.4 %collective-permute-start.19 = (f32[224,128]{1,0:T(8,128)S(1)}, f32[224,128]{1,0:T(8,128)S(1)}, u32[]{:S(2)}, u32[]{:S(2)}) collective-permute-start(f32[224,128]{1,0:T(8,128)S(1)} %get-tuple-element.143.own), channel_id=1, source_target_pairs={{0,12},{4,8},{8,4},{12,0},{16,28},{20,24},{24,20},{28,16},{1,13},{... | collective-permute-start | bytes 344072 | tf_op jit(solution)/shard_map/ppermute | solution.py:612
  77.9 1.1 %collective-permute-start.17 = (f32[224,128]{1,0:T(8,128)S(1)}, f32[224,128]{1,0:T(8,128)S(1)}, u32[]{:S(2)}, u32[]{:S(2)}) collective-permute-start(f32[224,128]{1,0:T(8,128)S(1)} %get-tuple-element.143.own), channel_id=1, source_target_pairs={{0,4},{4,0},{8,12},{12,8},{16,20},{20,16},{24,28},{28,24},{1,5},{5... | collective-permute-start | bytes 344072 | tf_op jit(solution)/shard_map/ppermute | solution.py:612
  79.0 4.5 %norm.1 = (bf16[256,2048]{1,0:T(8,128)(2,1)}, bf16[256,2048]{1,0:T(8,128)(2,1)}, bf16[256,2048]{1,0:T(8,128)(2,1)}, f32[8,128]{1,0:T(8,128)S(1)}) custom-call(f32[512,128]{1,0:T(8,128)S(1)} %get-tuple-element.107.refs_7_.refs_0_, f32[4096,128]{1,0:T(8,128)S(1)} %get-tuple-element.103.refs_4_.refs_8_.refs_1_, ...), custom_call_target="tpu_custom_call" | custom-call | flops 23592960 | bytes 2097152 | tf_op jit(solution)/shard_map/norm/pallas_call | solution.py:695
  83.6 1.0 %collective-permute-start.16 = (f32[328,128]{1,0:T(8,128)S(1)}, f32[328,128]{1,0:T(8,128)S(1)}, u32[]{:S(2)}, u32[]{:S(2)}) collective-permute-start(f32[328,128]{1,0:T(8,128)S(1)} %add.6.refs_0_), channel_id=1, source_target_pairs={{0,4},{4,0},{8,12},{12,8},{16,20},{20,16},{24,28},{28,24},{1,5},{5... | collective-permute-start | bytes 503816 | tf_op jit(solution)/shard_map/ppermute | solution.py:612
  84.7 2.4 %collective-permute-start.20 = (f32[224,128]{1,0:T(8,128)S(1)}, f32[224,128]{1,0:T(8,128)S(1)}, u32[]{:S(2)}, u32[]{:S(2)}) collective-permute-start(f32[224,128]{1,0:T(8,128)S(1)} %add.7.refs_2_), channel_id=1, source_target_pairs={{0,16},{4,20},{8,24},{12,28},{16,0},{20,4},{24,8},{28,12},{1,17},{... | collective-permute-start | bytes 344072 | tf_op jit(solution)/shard_map/ppermute | solution.py:612
  87.0 4.0 %back.1 = (bf16[256,2048]{1,0:T(8,128)(2,1)}, bf16[256,2048]{1,0:T(8,128)(2,1)}, f32[8,128]{1,0:T(8,128)S(1)}) custom-call(f32[4096,128]{1,0:T(8,128)S(1)} %get-tuple-element.129.refs_0_, f32[4096,128]{1,0:T(8,128)S(1)} %get-tuple-element.130.refs_1_, bf16[3,2,64,128]{3,2,1,0:T(8,128)(2,1)S(1)} %collective-permute-done.12.refs_5_.refs_2_.refs_1_, ...), custom_call_target="tpu_custom_call" | custom-call | flops 20971520 | bytes 2097152 | tf_op jit(solution)/shard_map/back/pallas_call | solution.py:695
  91.1 0.9 finish.1
  (37 shorter events, 6.2 us)
Async XLA Ops:
  1.6 9.7 %collective-permute-start = (bf16[3,8,2048]{2,1,0:T(8,128)(2,1)S(1)}, bf16[3,8,2048]{2,1,0:T(8,128)(2,1)S(1)}, u32[]{:S(2)}, u32[]{:S(2)}) collective-permute-start(bf16[3,8,2048]{2,1,0:T(8,128)(2,1)S(1)} %trailing.1), channel_id=1, source_target_pairs={{0,4},{4,8},{8,12},{12,16},{16,20},{20,24},{24,28},{28,0},{1,5},{5... | collective-permute-start | bytes 294920 | tf_op jit(solution)/shard_map/ppermute | solution.py:608
  12.0 11.6 %copy-start.1 = (f32[2048]{0:T(1024)S(1)}, f32[2048]{0:T(1024)}, u32[]{:S(2)}) copy-start(f32[2048]{0:T(1024)} %param.17) | copy-start | bytes 24580
  12.0 7.4 %collective-permute-start.3 = (f32[256,128]{1,0:T(8,128)S(1)}, f32[256,128]{1,0:T(8,128)S(1)}, u32[]{:S(2)}, u32[]{:S(2)}) collective-permute-start(f32[256,128]{1,0:T(8,128)S(1)} %get-tuple-element.96.own), channel_id=1, source_target_pairs={{0,12},{4,8},{8,4},{12,0},{16,28},{20,24},{24,20},{28,16},{1,13},{... | collective-permute-start | bytes 393224 | tf_op jit(solution)/shard_map/ppermute | solution.py:612
  14.6 6.2 %collective-permute-start.2 = (f32[256,128]{1,0:T(8,128)S(1)}, f32[256,128]{1,0:T(8,128)S(1)}, u32[]{:S(2)}, u32[]{:S(2)}) collective-permute-start(f32[256,128]{1,0:T(8,128)S(1)} %get-tuple-element.96.own), channel_id=1, source_target_pairs={{0,8},{4,12},{8,0},{12,4},{16,24},{20,28},{24,16},{28,20},{1,9},{5... | collective-permute-start | bytes 393224 | tf_op jit(solution)/shard_map/ppermute | solution.py:612
  15.0 5.8 %collective-permute-start.1 = (f32[256,128]{1,0:T(8,128)S(1)}, f32[256,128]{1,0:T(8,128)S(1)}, u32[]{:S(2)}, u32[]{:S(2)}) collective-permute-start(f32[256,128]{1,0:T(8,128)S(1)} %get-tuple-element.96.own), channel_id=1, source_target_pairs={{0,4},{4,0},{8,12},{12,8},{16,20},{20,16},{24,28},{28,24},{1,5},{5... | collective-permute-start | bytes 393224 | tf_op jit(solution)/shard_map/ppermute | solution.py:612
  20.9 8.4 %collective-permute-start.4 = (f32[256,128]{1,0:T(8,128)S(1)}, f32[256,128]{1,0:T(8,128)S(1)}, u32[]{:S(2)}, u32[]{:S(2)}) collective-permute-start(f32[256,128]{1,0:T(8,128)S(1)} %get-tuple-element.99), channel_id=1, source_target_pairs={{0,16},{4,20},{8,24},{12,28},{16,0},{20,4},{24,8},{28,12},{1,17},{... | collective-permute-start | bytes 393224 | tf_op jit(solution)/shard_map/ppermute | solution.py:612
  23.6 5.8 %copy-start = (f32[2048]{0:T(1024)S(1)}, f32[2048]{0:T(1024)}, u32[]{:S(2)}) copy-start(f32[2048]{0:T(1024)} %param.18) | copy-start | bytes 24580
  34.2 3.0 %collective-permute-start.7 = (f32[2,256]{1,0:T(2,128)S(1)}, f32[2,256]{1,0:T(2,128)S(1)}, u32[]{:S(2)}, u32[]{:S(2)}) collective-permute-start(f32[2,256]{1,0:T(2,128)S(1)} %get-tuple-element.102.refs_0_), channel_id=1, source_target_pairs={{0,3},{1,2},{2,1},{3,0},{4,7},{5,6},{6,5},{7,4},{8,11},{9,10},{10,... | collective-permute-start | bytes 6152 | tf_op jit(solution)/shard_map/ppermute | solution.py:612
  34.2 3.6 %collective-permute-start.6 = (f32[2,256]{1,0:T(2,128)S(1)}, f32[2,256]{1,0:T(2,128)S(1)}, u32[]{:S(2)}, u32[]{:S(2)}) collective-permute-start(f32[2,256]{1,0:T(2,128)S(1)} %get-tuple-element.102.refs_0_), channel_id=1, source_target_pairs={{0,2},{1,3},{2,0},{3,1},{4,6},{5,7},{6,4},{7,5},{8,10},{9,11},{10,... | collective-permute-start | bytes 6152 | tf_op jit(solution)/shard_map/ppermute | solution.py:612
  35.6 2.2 %collective-permute-start.5 = (f32[2,256]{1,0:T(2,128)S(1)}, f32[2,256]{1,0:T(2,128)S(1)}, u32[]{:S(2)}, u32[]{:S(2)}) collective-permute-start(f32[2,256]{1,0:T(2,128)S(1)} %get-tuple-element.102.refs_0_), channel_id=1, source_target_pairs={{0,1},{1,0},{2,3},{3,2},{4,5},{5,4},{6,7},{7,6},{8,9},{9,8},{10,11... | collective-permute-start | bytes 6152 | tf_op jit(solution)/shard_map/ppermute | solution.py:612
  41.7 8.2 %collective-permute-start.10 = (f32[256,128]{1,0:T(8,128)S(1)}, f32[256,128]{1,0:T(8,128)S(1)}, u32[]{:S(2)}, u32[]{:S(2)}) collective-permute-start(f32[256,128]{1,0:T(8,128)S(1)} %get-tuple-element.116.own), channel_id=1, source_target_pairs={{0,12},{4,8},{8,4},{12,0},{16,28},{20,24},{24,20},{28,16},{1,13},{... | collective-permute-start | bytes 393224 | tf_op jit(solution)/shard_map/ppermute | solution.py:612
  42.1 9.5 %collective-permute-start.9 = (f32[256,128]{1,0:T(8,128)S(1)}, f32[256,128]{1,0:T(8,128)S(1)}, u32[]{:S(2)}, u32[]{:S(2)}) collective-permute-start(f32[256,128]{1,0:T(8,128)S(1)} %get-tuple-element.116.own), channel_id=1, source_target_pairs={{0,8},{4,12},{8,0},{12,4},{16,24},{20,28},{24,16},{28,20},{1,9},{5... | collective-permute-start | bytes 393224 | tf_op jit(solution)/shard_map/ppermute | solution.py:612
  44.9 6.7 %collective-permute-start.8 = (f32[256,128]{1,0:T(8,128)S(1)}, f32[256,128]{1,0:T(8,128)S(1)}, u32[]{:S(2)}, u32[]{:S(2)}) collective-permute-start(f32[256,128]{1,0:T(8,128)S(1)} %get-tuple-element.116.own), channel_id=1, source_target_pairs={{0,4},{4,0},{8,12},{12,8},{16,20},{20,16},{24,28},{28,24},{1,5},{5... | collective-permute-start | bytes 393224 | tf_op jit(solution)/shard_map/ppermute | solution.py:612
  51.8 8.8 %collective-permute-start.11 = (f32[256,128]{1,0:T(8,128)S(1)}, f32[256,128]{1,0:T(8,128)S(1)}, u32[]{:S(2)}, u32[]{:S(2)}) collective-permute-start(f32[256,128]{1,0:T(8,128)S(1)} %get-tuple-element.119), channel_id=1, source_target_pairs={{0,16},{4,20},{8,24},{12,28},{16,0},{20,4},{24,8},{28,12},{1,17},{... | collective-permute-start | bytes 393224 | tf_op jit(solution)/shard_map/ppermute | solution.py:612
  60.8 7.6 %collective-permute-start.13 = (f32[328,128]{1,0:T(8,128)S(1)}, f32[328,128]{1,0:T(8,128)S(1)}, u32[]{:S(2)}, u32[]{:S(2)}) collective-permute-start(f32[328,128]{1,0:T(8,128)S(1)} %get-tuple-element.140), channel_id=1, source_target_pairs={{0,4},{4,0},{8,12},{12,8},{16,20},{20,16},{24,28},{28,24},{1,5},{5... | collective-permute-start | bytes 503816 | tf_op jit(solution)/shard_map/ppermute | solution.py:612
  61.6 6.8 %collective-permute-start.12 = (bf16[3,2,64,128]{3,2,1,0:T(8,128)(2,1)S(1)}, bf16[3,2,64,128]{3,2,1,0:T(8,128)(2,1)S(1)}, u32[]{:S(2)}, u32[]{:S(2)}) collective-permute-start(bf16[3,2,64,128]{3,2,1,0:T(8,128)(2,1)S(1)} %get-tuple-element.127), channel_id=1, source_target_pairs={{0,28},{4,0},{8,4},{12,8},{16,12},{20,16},{24,20},{28,24},{1,29},{... | collective-permute-start | bytes 294920 | tf_op jit(solution)/shard_map/ppermute | solution.py:608
  68.4 5.4 %collective-permute-start.14 = (f32[328,128]{1,0:T(8,128)S(1)}, f32[328,128]{1,0:T(8,128)S(1)}, u32[]{:S(2)}, u32[]{:S(2)}) collective-permute-start(f32[328,128]{1,0:T(8,128)S(1)} %add.4.one), channel_id=1, source_target_pairs={{0,8},{4,12},{8,0},{12,4},{16,24},{20,28},{24,16},{28,20},{1,9},{5... | collective-permute-start | bytes 503816 | tf_op jit(solution)/shard_map/ppermute | solution.py:612
  73.9 9.7 %collective-permute-start.15 = (f32[328,128]{1,0:T(8,128)S(1)}, f32[328,128]{1,0:T(8,128)S(1)}, u32[]{:S(2)}, u32[]{:S(2)}) collective-permute-start(f32[328,128]{1,0:T(8,128)S(1)} %add.5.one), channel_id=1, source_target_pairs={{0,16},{4,20},{8,24},{12,28},{16,0},{20,4},{24,8},{28,12},{1,17},{... | collective-permute-start | bytes 503816 | tf_op jit(solution)/shard_map/ppermute | solution.py:612
  75.6 9.1 %collective-permute-start.19 = (f32[224,128]{1,0:T(8,128)S(1)}, f32[224,128]{1,0:T(8,128)S(1)}, u32[]{:S(2)}, u32[]{:S(2)}) collective-permute-start(f32[224,128]{1,0:T(8,128)S(1)} %get-tuple-element.143.own), channel_id=1, source_target_pairs={{0,12},{4,8},{8,4},{12,0},{16,28},{20,24},{24,20},{28,16},{1,13},{... | collective-permute-start | bytes 344072 | tf_op jit(solution)/shard_map/ppermute | solution.py:612
  77.9 6.7 %collective-permute-start.18 = (f32[224,128]{1,0:T(8,128)S(1)}, f32[224,128]{1,0:T(8,128)S(1)}, u32[]{:S(2)}, u32[]{:S(2)}) collective-permute-start(f32[224,128]{1,0:T(8,128)S(1)} %get-tuple-element.143.own), channel_id=1, source_target_pairs={{0,8},{4,12},{8,0},{12,4},{16,24},{20,28},{24,16},{28,20},{1,9},{5... | collective-permute-start | bytes 344072 | tf_op jit(solution)/shard_map/ppermute | solution.py:612
  77.9 6.7 %collective-permute-start.17 = (f32[224,128]{1,0:T(8,128)S(1)}, f32[224,128]{1,0:T(8,128)S(1)}, u32[]{:S(2)}, u32[]{:S(2)}) collective-permute-start(f32[224,128]{1,0:T(8,128)S(1)} %get-tuple-element.143.own), channel_id=1, source_target_pairs={{0,4},{4,0},{8,12},{12,8},{16,20},{20,16},{24,28},{28,24},{1,5},{5... | collective-permute-start | bytes 344072 | tf_op jit(solution)/shard_map/ppermute | solution.py:612
  83.6 7.5 %collective-permute-start.16 = (f32[328,128]{1,0:T(8,128)S(1)}, f32[328,128]{1,0:T(8,128)S(1)}, u32[]{:S(2)}, u32[]{:S(2)}) collective-permute-start(f32[328,128]{1,0:T(8,128)S(1)} %add.6.refs_0_), channel_id=1, source_target_pairs={{0,4},{4,0},{8,12},{12,8},{16,20},{20,16},{24,28},{28,24},{1,5},{5... | collective-permute-start | bytes 503816 | tf_op jit(solution)/shard_map/ppermute | solution.py:612
  84.7 6.4 %collective-permute-start.20 = (f32[224,128]{1,0:T(8,128)S(1)}, f32[224,128]{1,0:T(8,128)S(1)}, u32[]{:S(2)}, u32[]{:S(2)}) collective-permute-start(f32[224,128]{1,0:T(8,128)S(1)} %add.7.refs_2_), channel_id=1, source_target_pairs={{0,16},{4,20},{8,24},{12,28},{16,0},{20,4},{24,8},{28,12},{1,17},{... | collective-permute-start | bytes 344072 | tf_op jit(solution)/shard_map/ppermute | solution.py:612

commit v8 on v7

--- a/solution.py
+++ b/solution.py
@@ -25,13 +25,17 @@
 
 
 def loop(start, stop, body, carry):
-    pairs = (stop - start) // 2
-
-    def two(i, carry):
-        return body(start + 2 * i + 1, body(start + 2 * i, carry))
-
-    carry = lax.fori_loop(0, pairs, two, carry)
-    return body(stop - 1, carry) if (stop - start) % 2 else carry
+    fours = (stop - start) // 4
+
+    def four(i, carry):
+        for k in range(4):
+            carry = body(start + 4 * i + k, carry)
+        return carry
+
+    carry = lax.fori_loop(0, fours, four, carry)
+    for i in range(start + 4 * fours, stop):
+        carry = body(i, carry)
+    return carry
 
 
 def spread_chunk(src, dst, first, c):
@@ -41,23 +45,25 @@
         dst[pl.ds((start + first) * SUB + g, CHUNK, stride=SUB), :] = piece
 
 
-def spread(src, dst, first, count):
+def gather_chunk(src, dst, c):
+    start = pl.multiple_of(c * CHUNK, CHUNK)
+    for g in range(SUB):
+        piece = src[pl.ds(start * SUB + g, CHUNK, stride=SUB), :]
+        dst[pl.ds(start, CHUNK), g * LANES : (g + 1) * LANES] = piece.astype(dst.dtype)
+
+
+def skewed(chunks, make, lay, make_last=None):
+    make(0)
+
     def some(c, carry):
-        spread_chunk(src, dst, first, c)
+        lay(c - 1)
+        make(c)
         return carry
 
-    loop(0, count // CHUNK, some, 0)
-
-
-def gather_rows(src, dst, count):
-    def some(i, carry):
-        start = pl.multiple_of(i * 16, 16)
-        for g in range(SUB):
-            piece = src[pl.ds(start * SUB + g, 16, stride=SUB), :]
-            dst[pl.ds(start, 16), g * LANES : (g + 1) * LANES] = piece.astype(dst.dtype)
-        return carry
-
-    loop(0, count // 16, some, 0)
+    lax.fori_loop(1, chunks - 1, some, 0)
+    lay(chunks - 2)
+    (make_last or make)(chunks - 1)
+    lay(chunks - 1)
 
 
 def total(values):
@@ -193,19 +199,28 @@
     for s in range(SUB):
         lanes = slice(s * LANES, (s + 1) * LANES)
         q_ext[pl.ds(s, SUB, stride=SUB), :] = halo[0, :, lanes].astype(F32) * there
-    spread(query, q_ext, SUB, steps)
-    spread(residual, res_pos, 0, steps)
-    spread(cot, cot_pos, 0, steps)
-    taps0 = taps_of(filt, 0, taps)
-
-    def conv(c, carry):
-        t0 = c * SUB
-        qw = [row(q_ext, t0 + SUB - margin + i) for i in range(SUB + margin)]
-        for i in range(SUB):
+    taps0, chunks = taps_of(filt, 0, taps), steps // CHUNK
+
+    def conv(c):
+        t0 = c * CHUNK
+        qw = [row(q_ext, t0 + SUB - margin + i) for i in range(CHUNK + margin)]
+        for i in range(CHUNK):
             put(f0, t0 + i, conv_at(qw, taps0, i))
+
+    def shape(c):
+        spread_chunk(query, q_ext, SUB, c)
+        spread_chunk(residual, res_pos, 0, c)
+        spread_chunk(cot, cot_pos, 0, c)
+
+    shape(0)
+
+    def some(c, carry):
+        conv(c - 1)
+        shape(c)
         return carry
 
-    loop(0, steps // SUB, conv, 0)
+    lax.fori_loop(1, chunks, some, 0)
+    conv(chunks - 1)
 
 
 def near_taps(lam, res, skip, modes):
@@ -398,49 +413,48 @@
     query_sums(modes, taps, steps, scale, summed, cot_pos, modal, q_ext, gain, gf0, early)
 
 
-def norm_kernel(taps, steps, last, scale, summed, cot_pos, gain, gf0, next_head, filt, ready, normed, grad_res, grad_query, work, head):
+def norm_kernel(taps, steps, last, scale, summed, cot_pos, gain, gf0, next_head, filt, ready, normed, grad_res, grad_query, work, head, work2):
     del ready
     back(0, taps, steps, last, gf0, next_head, filt, grad_query, work, head)
     factor = gain[...]
 
-    def norm(c, carry):
-        for i in range(SUB):
-            t = c * SUB + i
-            put(work, t, row(summed, t) * scale[pl.ds(t, 1), :] * factor)
-        return carry
-
-    loop(0, steps // SUB, norm, 0)
-    gather_rows(work, normed, steps)
-
-    def grads(c, carry):
-        for i in range(SUB):
-            t = c * SUB + i
-            inv = scale[pl.ds(t, 1), :]
-            coef = scale[pl.ds(steps + t, 1), :]
-            put(work, t, inv * (factor * row(cot_pos, t)) - coef * row(summed, t))
-        return carry
-
-    loop(0, steps // SUB, grads, 0)
-    gather_rows(work, grad_res, steps)
+    def make(c):
+        for i in range(CHUNK):
+            t = c * CHUNK + i
+            inv, now = scale[pl.ds(t, 1), :], row(summed, t)
+            put(work, t, now * inv * factor)
+            put(work2, t, inv * (factor * row(cot_pos, t)) - scale[pl.ds(steps + t, 1), :] * now)
+
+    def lay(c):
+        gather_chunk(work, normed, c)
+        gather_chunk(work2, grad_res, c)
+
+    skewed(steps // CHUNK, make, lay)
 
 
 def query_sums(modes, taps, steps, scale, summed, cot_pos, modal, q_ext, gain, gf0, early):
     factor = gain[...]
 
-    def grads(c, by_gain):
+    margin = taps - 1
+
+    def grads(c, sums):
+        by_gain, acc = sums
+        window = [row(q_ext, c * SUB + SUB - margin + i) for i in range(SUB + margin)]
         for i in range(SUB):
             t = c * SUB + i
             now, here = row(cot_pos, t), row(summed, t)
             scaled = scale[pl.ds(t, 1), :] * now
             grad = factor * scaled - scale[pl.ds(steps + t, 1), :] * here
-            put(gf0, t, grad * row(modal, t))
+            front = grad * row(modal, t)
+            put(gf0, t, front)
             by_gain = by_gain + scaled * here
-        return by_gain
-
-    put(early, taps + modes + 1, loop(0, steps // SUB, grads, zeros(1)[0]))
-    sums = filter_pass(taps, steps, gf0, q_ext)
+            acc = tuple(acc[j] + front * window[margin + i - j] for j in range(taps))
+        return by_gain, acc
+
+    by_gain, acc = loop(0, steps // SUB, grads, (zeros(1)[0], zeros(taps)))
+    put(early, taps + modes + 1, by_gain)
     for j in range(taps):
-        put(early, j, sums[j])
+        put(early, j, acc[j])
 
 
 def filter_pass(taps, steps, grad, ext):
@@ -492,19 +506,19 @@
     head[...] = next_head[which, 0].astype(F32) * there
     weights = taps_of(filt, which, taps)
 
-    def some(c, carry):
-        put_back(work, c * SUB, weights, [row(grad, c * SUB + i) for i in range(SUB + taps - 1)])
-        return carry
-
-    loop(0, steps // SUB - 1, some, 0)
-    start = steps - SUB
-    window = [row(grad, start + i) for i in range(SUB)] + [row(head, i) for i in range(taps - 1)]
-    put_back(work, start, weights, window)
-    gather_rows(work, out, steps)
+    def make(c):
+        window = [row(grad, c * CHUNK + i) for i in range(CHUNK + taps - 1)]
+        put_back(work, c * CHUNK, weights, window)
+
+    def make_last(c):
+        window = [row(grad, c * CHUNK + i) for i in range(CHUNK)]
+        put_back(work, c * CHUNK, weights, window + [row(head, i) for i in range(taps - 1)])
+
+    skewed(steps // CHUNK, make, lambda c: gather_chunk(work, out, c), make_last)
 
 
 def put_back(out, start, weights, window):
-    for i in range(SUB):
+    for i in range(CHUNK):
         put(out, start + i, total([w * window[i + j] for j, w in enumerate(weights)]))
 
 
@@ -872,7 +886,7 @@
         [wide_spec, wide_spec, wide_spec],
         45,
         "norm",
-        scratch=back_scratch,
+        scratch=[*back_scratch, pltpu.VMEM((steps * SUB, LANES), F32)],
     )
     grad_key, grad_value, back_done = call(
         functools.partial(back_kernel, taps, steps, last),

time: 92.2 us -> 91.3 us (level)
  Pallas kernels: 50 us -> 46.4 us
  waiting for transfers between devices: 13.6 us -> 15.6 us
    pallas_call x15, Pallas kernels: 48.5 us -> 44.9 us  [call(): pl.pallas_call(with_done, grid=(blocks,), in_specs=in_specs, out_specs=ou...]
    ppermute x19, waiting for transfers between devices: 12.8 us -> 14.8 us  [swap(): lax.ppermute(value, axis, [(i, i ^ step) for i in range(lax.axis_size(axi...]
  transfers between devices with their start and end apart: 21 -> 21, of which waited for: 9 -> 9; matrix products, arithmetic and copies ran while one was open for 0% -> 0% of each run, Pallas kernels for 41% -> 38%
where the time goes in v8:
time: 91.3 us; the launch traced here: 91.1 us
  Pallas kernels  46.4 us (51%)
  starting transfers between devices  28.4 us (31%)
  waiting for transfers between devices  15.6 us (17%)
    pallas_call x15, Pallas kernels, call(): pl.pallas_call(with_done, grid=(blocks,), in_specs=in_specs, out_specs=ou...  44.9 us
    ppermute x19, starting transfers between devices, swap(): lax.ppermute(value, axis, [(i, i ^ step) for i in range(lax.axis_size(axi...  22.7 us
    ppermute x19, waiting for transfers between devices, swap(): lax.ppermute(value, axis, [(i, i ^ step) for i in range(lax.axis_size(axi...  14.8 us
    ppermute x2, starting transfers between devices, ring(): lax.ppermute(value, axis, [(i, (i + distance) % count) for i in range(cou...  5.66 us
  transfers between devices with their start and end apart: 21, of which 9 were waited for; matrix products, arithmetic and copies ran while one was open for 0% of the time, Pallas kernels for 38%

profile of v8, /device:TPU:0, one launch (start us, length us, event | category | flops | bytes accessed | tf_op | source)
XLA Modules:
  0.0 91.1 jit_solution(14021840192391337320)
XLA Ops:
  0.6 0.9 %trailing.1 = bf16[3,8,2048]{2,1,0:T(8,128)(2,1)S(1)} custom-call(bf16[256,2048]{1,0:T(8,128)(2,1)} %refs_0_.3, bf16[256,2048]{1,0:T(8,128)(2,1)} %refs_0_.2, bf16[256,2048]{1,0:T(8,128)(2,1)} %refs_1_.2), custom_call_target="tpu_custom_call" | custom-call | flops 2048 | bytes 2048 | tf_op jit(solution)/shard_map/trailing/pallas_call | solution.py:731
  1.6 3.0 %collective-permute-start = (bf16[3,8,2048]{2,1,0:T(8,128)(2,1)S(1)}, bf16[3,8,2048]{2,1,0:T(8,128)(2,1)S(1)}, u32[]{:S(2)}, u32[]{:S(2)}) collective-permute-start(bf16[3,8,2048]{2,1,0:T(8,128)(2,1)S(1)} %trailing.1), channel_id=1, source_target_pairs={{0,4},{4,8},{8,12},{12,16},{16,20},{20,24},{24,28},{28,0},{1,5},{5... | collective-permute-start | bytes 294920 | tf_op jit(solution)/shard_map/ppermute | solution.py:622
  4.5 6.7 %features.1 = (f32[4224,128]{1,0:T(8,128)S(1)}, f32[4224,128]{1,0:T(8,128)S(1)}, f32[4096,128]{1,0:T(8,128)S(1)}, f32[4096,128]{1,0:T(8,128)S(1)}, f32[4096,128]...) custom-call(bf16[256,2048]{1,0:T(8,128)(2,1)} %refs_0_.2, ...), custom_call_target="tpu_custom_call" | custom-call | flops 33554432 | bytes 2097152 | tf_op jit(solution)/shard_map/features/pallas_call | solution.py:709
  12.0 2.6 %collective-permute-start.3 = (f32[256,128]{1,0:T(8,128)S(1)}, f32[256,128]{1,0:T(8,128)S(1)}, u32[]{:S(2)}, u32[]{:S(2)}) collective-permute-start(f32[256,128]{1,0:T(8,128)S(1)} %get-tuple-element.96.own), channel_id=1, source_target_pairs={{0,12},{4,8},{8,4},{12,0},{16,28},{20,24},{24,20},{28,16},{1,13},{... | collective-permute-start | bytes 393224 | tf_op jit(solution)/shard_map/ppermute | solution.py:626
  15.5 3.2 %query.3 = (f32[4224,128]{1,0:T(8,128)S(1)}, f32[4096,128]{1,0:T(8,128)S(1)}, f32[4096,128]{1,0:T(8,128)S(1)}, f32[4096,128]{1,0:T(8,128)S(1)}, f32[8,128]{1,0:T(8,128)S(1)}) custom-call(bf16[256,2048]{1,0:T(8,128)(2,1)} %refs_0_.3, bf16[256,2048]{1,0:T(8,128)(2,1)} %refs_1_.3, bf16[256,2048]{1,0:T(8,128)(2,1)} %refs_2_.3, ...), custom_call_target="tpu_custom_call" | custom-call | flops 15728640 | bytes 2097152 | tf_op jit(solution)/shard_map/query/pallas_call | solution.py:709
  19.4 1.4 %collective-permute-done.2.second = f32[256,128]{1,0:T(8,128)S(1)} collective-permute-done((f32[256,128]{1,0:T(8,128)S(1)}, f32[256,128]{1,0:T(8,128)S(1)}, u32[]{:S(2)}, u32[]{:S(2)}) %collective-permute-start.2) | collective-permute-done | bytes 131104 | tf_op jit(solution)/shard_map/ppermute | solution.py:626
  20.9 2.7 %collective-permute-start.4 = (f32[256,128]{1,0:T(8,128)S(1)}, f32[256,128]{1,0:T(8,128)S(1)}, u32[]{:S(2)}, u32[]{:S(2)}) collective-permute-start(f32[256,128]{1,0:T(8,128)S(1)} %get-tuple-element.99), channel_id=1, source_target_pairs={{0,16},{4,20},{8,24},{12,28},{16,0},{20,4},{24,8},{28,12},{1,17},{... | collective-permute-start | bytes 393224 | tf_op jit(solution)/shard_map/ppermute | solution.py:626
  23.6 1.3 %near.1 = (f32[4096,128]{1,0:T(8,128)S(1)}, f32[8,128]{1,0:T(8,128)}) custom-call(f32[4096,128]{1,0:T(8,128)S(1)} %get-tuple-element.89.refs_0_.refs_1_, f32[256,128]{1,0:T(8,128)S(1)} %get-tuple-element.83.refs_4_.refs_1_.lam.refs_7_.refs_2_, f32[256,128]{1,0:T(8,128)S(1)} %get-tuple-element.90.refs_2_.refs_3_.res, f32[16,128]{1,0:T(8,128)S(1)} %bitcast.8), custom_call_target="tpu_custom_call" | custom-call | flops 5242880 | bytes 2097152 | tf_op jit(solution)/shard_map/near/pallas_call | solution.py:709
  24.9 2.1 %lags.1 = (f32[8192,128]{1,0:T(8,128)S(1)}, f32[8,128]{1,0:T(8,128)S(1)}) custom-call(f32[4096,128]{1,0:T(8,128)S(1)} %get-tuple-element.89.refs_0_.refs_1_, f32[256,128]{1,0:T(8,128)S(1)} %get-tuple-element.83.refs_4_.refs_1_.lam.refs_7_.refs_2_), custom_call_target="tpu_custom_call" | custom-call | flops 16777216 | bytes 2097152 | tf_op jit(solution)/shard_map/lags/pallas_call | solution.py:709
  27.0 2.3 %collective-permute-done.4.refs_6_ = f32[256,128]{1,0:T(8,128)S(1)} collective-permute-done((f32[256,128]{1,0:T(8,128)S(1)}, f32[256,128]{1,0:T(8,128)S(1)}, u32[]{:S(2)}, u32[]{:S(2)}) %collective-permute-start.4) | collective-permute-done | bytes 131104 | tf_op jit(solution)/shard_map/ppermute | solution.py:626
  29.3 4.6 %summed.1 = (f32[4096,128]{1,0:T(8,128)S(1)}, f32[4096,128]{1,0:T(8,128)S(1)}, f32[8192,128]{1,0:T(8,128)S(1)}, f32[2,256]{1,0:T(2,128)S(1)}, f32[8,128]{1,0:T(8,128)}) custom-call(f32[4096,128]{1,0:T(8,128)S(1)} %get-tuple-element.91.refs_0_, f32[4096,128]{1,0:T(8,128)S(1)} %get-tuple-element.92.refs_1_.refs_6_, f32[4096,128]{1,0:T(8,128)S(1)} %get-tuple-element.93.refs_2_, ...), custom_call_target="tpu_custom_call" | custom-call | flops 26214400 | bytes 2097152 | tf_op jit(solution)/shard_map/summed/pallas_call | solution.py:709
  34.0 1.4 %collective-permute-start.6 = (f32[2,256]{1,0:T(2,128)S(1)}, f32[2,256]{1,0:T(2,128)S(1)}, u32[]{:S(2)}, u32[]{:S(2)}) collective-permute-start(f32[2,256]{1,0:T(2,128)S(1)} %get-tuple-element.102.refs_0_), channel_id=1, source_target_pairs={{0,2},{1,3},{2,0},{3,1},{4,6},{5,7},{6,4},{7,5},{8,10},{9,11},{10,... | collective-permute-start | bytes 6152 | tf_op jit(solution)/shard_map/ppermute | solution.py:626
  35.8 0.8 borders.1
  37.6 3.9 %grad_modal.1 = (f32[512,128]{1,0:T(8,128)S(1)}, f32[4096,128]{1,0:T(8,128)S(1)}, f32[8192,128]{1,0:T(8,128)S(1)}, f32[256,128]{1,0:T(8,128)S(1)}, f32[256,128]{1,0:T(8,128)S(1)}, /*index=5*/f32[8,128]{1,0:T(8,128)}) custom-call(f32[2,256]{1,0:T(2,128)S(1)} %get-tuple-element.102.refs_0_, f32[2,256]{1,0:T(2,128)S(1)} %collective-permute-done.5.refs_1_, ...), custom_call_target="tpu_custom_call" | custom-call | flops 23592960 | bytes 2097152 | tf_op jit(solution)/shard_map/grad_modal/pallas_call | solution.py:709
  41.8 2.8 %collective-permute-start.9 = (f32[256,128]{1,0:T(8,128)S(1)}, f32[256,128]{1,0:T(8,128)S(1)}, u32[]{:S(2)}, u32[]{:S(2)}) collective-permute-start(f32[256,128]{1,0:T(8,128)S(1)} %get-tuple-element.116.own), channel_id=1, source_target_pairs={{0,8},{4,12},{8,0},{12,4},{16,24},{20,28},{24,16},{28,20},{1,9},{5... | collective-permute-start | bytes 393224 | tf_op jit(solution)/shard_map/ppermute | solution.py:626
  44.9 4.1 %across.1 = (f32[256,128]{1,0:T(8,128)S(1)}, f32[256,128]{1,0:T(8,128)S(1)}, f32[8,128]{1,0:T(8,128)S(1)}) custom-call(f32[4096,128]{1,0:T(8,128)S(1)} %get-tuple-element.108.refs_0_, f32[8192,128]{1,0:T(8,128)S(1)} %get-tuple-element.109.refs_1_.refs_3_, f32[8192,128]{1,0:T(8,128)S(1)} %get-tuple-element.105.refs_1_.refs_2_, ...), custom_call_target="tpu_custom_call" | custom-call | flops 26214400 | bytes 2097152 | tf_op jit(solution)/shard_map/across/pallas_call | solution.py:709
  49.1 2.2 %collective-permute-done.9.second = f32[256,128]{1,0:T(8,128)S(1)} collective-permute-done((f32[256,128]{1,0:T(8,128)S(1)}, f32[256,128]{1,0:T(8,128)S(1)}, u32[]{:S(2)}, u32[]{:S(2)}) %collective-permute-start.9) | collective-permute-done | bytes 131104 | tf_op jit(solution)/shard_map/ppermute | solution.py:626
  51.5 1.0 %collective-permute-start.11 = (f32[256,128]{1,0:T(8,128)S(1)}, f32[256,128]{1,0:T(8,128)S(1)}, u32[]{:S(2)}, u32[]{:S(2)}) collective-permute-start(f32[256,128]{1,0:T(8,128)S(1)} %get-tuple-element.119), channel_id=1, source_target_pairs={{0,16},{4,20},{8,24},{12,28},{16,0},{20,4},{24,8},{28,12},{1,17},{... | collective-permute-start | bytes 393224 | tf_op jit(solution)/shard_map/ppermute | solution.py:626
  52.5 3.8 %near_adjoint.1 = (f32[4096,128]{1,0:T(8,128)S(1)}, f32[256,128]{1,0:T(8,128)S(1)}, f32[4096,128]{1,0:T(8,128)S(1)}, f32[400,128]{1,0:T(8,128)S(1)}, f32[8,128]{1,0:T(8,128)}) custom-call(f32[4096,128]{1,0:T(8,128)S(1)} %get-tuple-element.108.refs_0_, f32[4096,128]{1,0:T(8,128)S(1)} %get-tuple-element.89.refs_0_.refs_1_, ...), custom_call_target="tpu_custom_call" | custom-call | flops 28835840 | bytes 2097152 | tf_op jit(solution)/shard_map/near_adjoint/pallas_call | solution.py:709
  56.3 4.0 %collective-permute-done.11.other = f32[256,128]{1,0:T(8,128)S(1)} collective-permute-done((f32[256,128]{1,0:T(8,128)S(1)}, f32[256,128]{1,0:T(8,128)S(1)}, u32[]{:S(2)}, u32[]{:S(2)}) %collective-permute-start.11) | collective-permute-done | bytes 131104 | tf_op jit(solution)/shard_map/ppermute | solution.py:626
  61.3 2.7 %collective-permute-start.12 = (bf16[3,2,64,128]{3,2,1,0:T(8,128)(2,1)S(1)}, bf16[3,2,64,128]{3,2,1,0:T(8,128)(2,1)S(1)}, u32[]{:S(2)}, u32[]{:S(2)}) collective-permute-start(bf16[3,2,64,128]{3,2,1,0:T(8,128)(2,1)S(1)} %get-tuple-element.127), channel_id=1, source_target_pairs={{0,28},{4,0},{8,4},{12,8},{16,12},{20,16},{24,20},{28,24},{1,29},{... | collective-permute-start | bytes 294920 | tf_op jit(solution)/shard_map/ppermute | solution.py:622
  64.0 3.3 %mixed.1 = (f32[4096,128]{1,0:T(8,128)S(1)}, f32[4096,128]{1,0:T(8,128)S(1)}, f32[8,128]{1,0:T(8,128)S(1)}) custom-call(f32[4096,128]{1,0:T(8,128)S(1)} %get-tuple-element.124.gmy.refs_0_, f32[4096,128]{1,0:T(8,128)S(1)} %get-tuple-element.125.f1.refs_1_, f32[4096,128]{1,0:T(8,128)S(1)} %get-tuple-element.126.f2.refs_2_, ...), custom_call_target="tpu_custom_call" | custom-call | flops 23592960 | bytes 2097152 | tf_op jit(solution)/shard_map/mixed/pallas_call | solution.py:709
  68.2 2.1 %filter_sums.1 = (f32[224,128]{1,0:T(8,128)S(1)}, f32[8,128]{1,0:T(8,128)S(1)}) custom-call(f32[4096,128]{1,0:T(8,128)S(1)} %get-tuple-element.129.refs_0_, f32[4096,128]{1,0:T(8,128)S(1)} %get-tuple-element.130.refs_1_, f32[4224,128]{1,0:T(8,128)S(1)} %get-tuple-element.131.refs_2_, f32[4224,128]{1,0:T(8,128)S(1)} %get-tuple-element.132.refs_3_), custom_call_target="tpu_custom_call" | custom-call | flops 15728640 | bytes 2097152 | tf_op jit(solution)/shard_map/filter_sums/pallas_call | solution.py:709
  70.3 3.2 %collective-permute-done.14.other = f32[328,128]{1,0:T(8,128)S(1)} collective-permute-done((f32[328,128]{1,0:T(8,128)S(1)}, f32[328,128]{1,0:T(8,128)S(1)}, u32[]{:S(2)}, u32[]{:S(2)}) %collective-permute-start.14) | collective-permute-done | bytes 167968 | tf_op jit(solution)/shard_map/ppermute | solution.py:626
  73.6 1.7 %collective-permute-start.15 = (f32[328,128]{1,0:T(8,128)S(1)}, f32[328,128]{1,0:T(8,128)S(1)}, u32[]{:S(2)}, u32[]{:S(2)}) collective-permute-start(f32[328,128]{1,0:T(8,128)S(1)} %add.5.one), channel_id=1, source_target_pairs={{0,16},{4,20},{8,24},{12,28},{16,0},{20,4},{24,8},{28,12},{1,17},{... | collective-permute-start | bytes 503816 | tf_op jit(solution)/shard_map/ppermute | solution.py:626
  75.3 2.4 %collective-permute-start.19 = (f32[224,128]{1,0:T(8,128)S(1)}, f32[224,128]{1,0:T(8,128)S(1)}, u32[]{:S(2)}, u32[]{:S(2)}) collective-permute-start(f32[224,128]{1,0:T(8,128)S(1)} %get-tuple-element.143.own), channel_id=1, source_target_pairs={{0,12},{4,8},{8,4},{12,0},{16,28},{20,24},{24,20},{28,16},{1,13},{... | collective-permute-start | bytes 344072 | tf_op jit(solution)/shard_map/ppermute | solution.py:626
  77.7 1.1 %collective-permute-start.17 = (f32[224,128]{1,0:T(8,128)S(1)}, f32[224,128]{1,0:T(8,128)S(1)}, u32[]{:S(2)}, u32[]{:S(2)}) collective-permute-start(f32[224,128]{1,0:T(8,128)S(1)} %get-tuple-element.143.own), channel_id=1, source_target_pairs={{0,4},{4,0},{8,12},{12,8},{16,20},{20,16},{24,28},{28,24},{1,5},{5... | collective-permute-start | bytes 344072 | tf_op jit(solution)/shard_map/ppermute | solution.py:626
  78.8 3.8 %norm.1 = (bf16[256,2048]{1,0:T(8,128)(2,1)}, bf16[256,2048]{1,0:T(8,128)(2,1)}, bf16[256,2048]{1,0:T(8,128)(2,1)}, f32[8,128]{1,0:T(8,128)S(1)}) custom-call(f32[512,128]{1,0:T(8,128)S(1)} %get-tuple-element.107.refs_7_.refs_0_, f32[4096,128]{1,0:T(8,128)S(1)} %get-tuple-element.103.refs_4_.refs_8_.refs_1_, ...), custom_call_target="tpu_custom_call" | custom-call | flops 23592960 | bytes 2097152 | tf_op jit(solution)/shard_map/norm/pallas_call | solution.py:709
  82.6 1.4 %collective-permute-start.16 = (f32[328,128]{1,0:T(8,128)S(1)}, f32[328,128]{1,0:T(8,128)S(1)}, u32[]{:S(2)}, u32[]{:S(2)}) collective-permute-start(f32[328,128]{1,0:T(8,128)S(1)} %add.6.refs_0_), channel_id=1, source_target_pairs={{0,4},{4,0},{8,12},{12,8},{16,20},{20,16},{24,28},{28,24},{1,5},{5... | collective-permute-start | bytes 503816 | tf_op jit(solution)/shard_map/ppermute | solution.py:626
  84.1 2.8 %collective-permute-start.20 = (f32[224,128]{1,0:T(8,128)S(1)}, f32[224,128]{1,0:T(8,128)S(1)}, u32[]{:S(2)}, u32[]{:S(2)}) collective-permute-start(f32[224,128]{1,0:T(8,128)S(1)} %add.7.refs_2_), channel_id=1, source_target_pairs={{0,16},{4,20},{8,24},{12,28},{16,0},{20,4},{24,8},{28,12},{1,17},{... | collective-permute-start | bytes 344072 | tf_op jit(solution)/shard_map/ppermute | solution.py:626
  86.8 3.4 %back.1 = (bf16[256,2048]{1,0:T(8,128)(2,1)}, bf16[256,2048]{1,0:T(8,128)(2,1)}, f32[8,128]{1,0:T(8,128)S(1)}) custom-call(f32[4096,128]{1,0:T(8,128)S(1)} %get-tuple-element.129.refs_0_, f32[4096,128]{1,0:T(8,128)S(1)} %get-tuple-element.130.refs_1_, bf16[3,2,64,128]{3,2,1,0:T(8,128)(2,1)S(1)} %collective-permute-done.12.refs_5_.refs_2_.refs_1_, ...), custom_call_target="tpu_custom_call" | custom-call | flops 20971520 | bytes 2097152 | tf_op jit(solution)/shard_map/back/pallas_call | solution.py:709
  90.2 0.9 finish.1
  (37 shorter events, 6.8 us)
Async XLA Ops:
  1.6 9.7 %collective-permute-start = (bf16[3,8,2048]{2,1,0:T(8,128)(2,1)S(1)}, bf16[3,8,2048]{2,1,0:T(8,128)(2,1)S(1)}, u32[]{:S(2)}, u32[]{:S(2)}) collective-permute-start(bf16[3,8,2048]{2,1,0:T(8,128)(2,1)S(1)} %trailing.1), channel_id=1, source_target_pairs={{0,4},{4,8},{8,12},{12,16},{16,20},{20,24},{24,28},{28,0},{1,5},{5... | collective-permute-start | bytes 294920 | tf_op jit(solution)/shard_map/ppermute | solution.py:622
  12.0 11.6 %copy-start.1 = (f32[2048]{0:T(1024)S(1)}, f32[2048]{0:T(1024)}, u32[]{:S(2)}) copy-start(f32[2048]{0:T(1024)} %param.17) | copy-start | bytes 24580
  12.0 7.4 %collective-permute-start.3 = (f32[256,128]{1,0:T(8,128)S(1)}, f32[256,128]{1,0:T(8,128)S(1)}, u32[]{:S(2)}, u32[]{:S(2)}) collective-permute-start(f32[256,128]{1,0:T(8,128)S(1)} %get-tuple-element.96.own), channel_id=1, source_target_pairs={{0,12},{4,8},{8,4},{12,0},{16,28},{20,24},{24,20},{28,16},{1,13},{... | collective-permute-start | bytes 393224 | tf_op jit(solution)/shard_map/ppermute | solution.py:626
  14.6 6.2 %collective-permute-start.2 = (f32[256,128]{1,0:T(8,128)S(1)}, f32[256,128]{1,0:T(8,128)S(1)}, u32[]{:S(2)}, u32[]{:S(2)}) collective-permute-start(f32[256,128]{1,0:T(8,128)S(1)} %get-tuple-element.96.own), channel_id=1, source_target_pairs={{0,8},{4,12},{8,0},{12,4},{16,24},{20,28},{24,16},{28,20},{1,9},{5... | collective-permute-start | bytes 393224 | tf_op jit(solution)/shard_map/ppermute | solution.py:626
  15.0 5.8 %collective-permute-start.1 = (f32[256,128]{1,0:T(8,128)S(1)}, f32[256,128]{1,0:T(8,128)S(1)}, u32[]{:S(2)}, u32[]{:S(2)}) collective-permute-start(f32[256,128]{1,0:T(8,128)S(1)} %get-tuple-element.96.own), channel_id=1, source_target_pairs={{0,4},{4,0},{8,12},{12,8},{16,20},{20,16},{24,28},{28,24},{1,5},{5... | collective-permute-start | bytes 393224 | tf_op jit(solution)/shard_map/ppermute | solution.py:626
  20.9 8.4 %collective-permute-start.4 = (f32[256,128]{1,0:T(8,128)S(1)}, f32[256,128]{1,0:T(8,128)S(1)}, u32[]{:S(2)}, u32[]{:S(2)}) collective-permute-start(f32[256,128]{1,0:T(8,128)S(1)} %get-tuple-element.99), channel_id=1, source_target_pairs={{0,16},{4,20},{8,24},{12,28},{16,0},{20,4},{24,8},{28,12},{1,17},{... | collective-permute-start | bytes 393224 | tf_op jit(solution)/shard_map/ppermute | solution.py:626
  23.6 5.8 %copy-start = (f32[2048]{0:T(1024)S(1)}, f32[2048]{0:T(1024)}, u32[]{:S(2)}) copy-start(f32[2048]{0:T(1024)} %param.18) | copy-start | bytes 24580
  34.0 3.0 %collective-permute-start.7 = (f32[2,256]{1,0:T(2,128)S(1)}, f32[2,256]{1,0:T(2,128)S(1)}, u32[]{:S(2)}, u32[]{:S(2)}) collective-permute-start(f32[2,256]{1,0:T(2,128)S(1)} %get-tuple-element.102.refs_0_), channel_id=1, source_target_pairs={{0,3},{1,2},{2,1},{3,0},{4,7},{5,6},{6,5},{7,4},{8,11},{9,10},{10,... | collective-permute-start | bytes 6152 | tf_op jit(solution)/shard_map/ppermute | solution.py:626
  34.0 3.6 %collective-permute-start.6 = (f32[2,256]{1,0:T(2,128)S(1)}, f32[2,256]{1,0:T(2,128)S(1)}, u32[]{:S(2)}, u32[]{:S(2)}) collective-permute-start(f32[2,256]{1,0:T(2,128)S(1)} %get-tuple-element.102.refs_0_), channel_id=1, source_target_pairs={{0,2},{1,3},{2,0},{3,1},{4,6},{5,7},{6,4},{7,5},{8,10},{9,11},{10,... | collective-permute-start | bytes 6152 | tf_op jit(solution)/shard_map/ppermute | solution.py:626
  35.4 2.2 %collective-permute-start.5 = (f32[2,256]{1,0:T(2,128)S(1)}, f32[2,256]{1,0:T(2,128)S(1)}, u32[]{:S(2)}, u32[]{:S(2)}) collective-permute-start(f32[2,256]{1,0:T(2,128)S(1)} %get-tuple-element.102.refs_0_), channel_id=1, source_target_pairs={{0,1},{1,0},{2,3},{3,2},{4,5},{5,4},{6,7},{7,6},{8,9},{9,8},{10,11... | collective-permute-start | bytes 6152 | tf_op jit(solution)/shard_map/ppermute | solution.py:626
  41.4 7.6 %collective-permute-start.10 = (f32[256,128]{1,0:T(8,128)S(1)}, f32[256,128]{1,0:T(8,128)S(1)}, u32[]{:S(2)}, u32[]{:S(2)}) collective-permute-start(f32[256,128]{1,0:T(8,128)S(1)} %get-tuple-element.116.own), channel_id=1, source_target_pairs={{0,12},{4,8},{8,4},{12,0},{16,28},{20,24},{24,20},{28,16},{1,13},{... | collective-permute-start | bytes 393224 | tf_op jit(solution)/shard_map/ppermute | solution.py:626
  41.8 9.5 %collective-permute-start.9 = (f32[256,128]{1,0:T(8,128)S(1)}, f32[256,128]{1,0:T(8,128)S(1)}, u32[]{:S(2)}, u32[]{:S(2)}) collective-permute-start(f32[256,128]{1,0:T(8,128)S(1)} %get-tuple-element.116.own), channel_id=1, source_target_pairs={{0,8},{4,12},{8,0},{12,4},{16,24},{20,28},{24,16},{28,20},{1,9},{5... | collective-permute-start | bytes 393224 | tf_op jit(solution)/shard_map/ppermute | solution.py:626
  44.6 6.7 %collective-permute-start.8 = (f32[256,128]{1,0:T(8,128)S(1)}, f32[256,128]{1,0:T(8,128)S(1)}, u32[]{:S(2)}, u32[]{:S(2)}) collective-permute-start(f32[256,128]{1,0:T(8,128)S(1)} %get-tuple-element.116.own), channel_id=1, source_target_pairs={{0,4},{4,0},{8,12},{12,8},{16,20},{20,16},{24,28},{28,24},{1,5},{5... | collective-permute-start | bytes 393224 | tf_op jit(solution)/shard_map/ppermute | solution.py:626
  51.5 8.8 %collective-permute-start.11 = (f32[256,128]{1,0:T(8,128)S(1)}, f32[256,128]{1,0:T(8,128)S(1)}, u32[]{:S(2)}, u32[]{:S(2)}) collective-permute-start(f32[256,128]{1,0:T(8,128)S(1)} %get-tuple-element.119), channel_id=1, source_target_pairs={{0,16},{4,20},{8,24},{12,28},{16,0},{20,4},{24,8},{28,12},{1,17},{... | collective-permute-start | bytes 393224 | tf_op jit(solution)/shard_map/ppermute | solution.py:626
  60.5 7.6 %collective-permute-start.13 = (f32[328,128]{1,0:T(8,128)S(1)}, f32[328,128]{1,0:T(8,128)S(1)}, u32[]{:S(2)}, u32[]{:S(2)}) collective-permute-start(f32[328,128]{1,0:T(8,128)S(1)} %get-tuple-element.140), channel_id=1, source_target_pairs={{0,4},{4,0},{8,12},{12,8},{16,20},{20,16},{24,28},{28,24},{1,5},{5... | collective-permute-start | bytes 503816 | tf_op jit(solution)/shard_map/ppermute | solution.py:626
  61.3 6.8 %collective-permute-start.12 = (bf16[3,2,64,128]{3,2,1,0:T(8,128)(2,1)S(1)}, bf16[3,2,64,128]{3,2,1,0:T(8,128)(2,1)S(1)}, u32[]{:S(2)}, u32[]{:S(2)}) collective-permute-start(bf16[3,2,64,128]{3,2,1,0:T(8,128)(2,1)S(1)} %get-tuple-element.127), channel_id=1, source_target_pairs={{0,28},{4,0},{8,4},{12,8},{16,12},{20,16},{24,20},{28,24},{1,29},{... | collective-permute-start | bytes 294920 | tf_op jit(solution)/shard_map/ppermute | solution.py:622
  68.1 5.4 %collective-permute-start.14 = (f32[328,128]{1,0:T(8,128)S(1)}, f32[328,128]{1,0:T(8,128)S(1)}, u32[]{:S(2)}, u32[]{:S(2)}) collective-permute-start(f32[328,128]{1,0:T(8,128)S(1)} %add.4.one), channel_id=1, source_target_pairs={{0,8},{4,12},{8,0},{12,4},{16,24},{20,28},{24,16},{28,20},{1,9},{5... | collective-permute-start | bytes 503816 | tf_op jit(solution)/shard_map/ppermute | solution.py:626
  73.6 9.0 %collective-permute-start.15 = (f32[328,128]{1,0:T(8,128)S(1)}, f32[328,128]{1,0:T(8,128)S(1)}, u32[]{:S(2)}, u32[]{:S(2)}) collective-permute-start(f32[328,128]{1,0:T(8,128)S(1)} %add.5.one), channel_id=1, source_target_pairs={{0,16},{4,20},{8,24},{12,28},{16,0},{20,4},{24,8},{28,12},{1,17},{... | collective-permute-start | bytes 503816 | tf_op jit(solution)/shard_map/ppermute | solution.py:626
  75.3 8.8 %collective-permute-start.19 = (f32[224,128]{1,0:T(8,128)S(1)}, f32[224,128]{1,0:T(8,128)S(1)}, u32[]{:S(2)}, u32[]{:S(2)}) collective-permute-start(f32[224,128]{1,0:T(8,128)S(1)} %get-tuple-element.143.own), channel_id=1, source_target_pairs={{0,12},{4,8},{8,4},{12,0},{16,28},{20,24},{24,20},{28,16},{1,13},{... | collective-permute-start | bytes 344072 | tf_op jit(solution)/shard_map/ppermute | solution.py:626
  77.7 6.4 %collective-permute-start.18 = (f32[224,128]{1,0:T(8,128)S(1)}, f32[224,128]{1,0:T(8,128)S(1)}, u32[]{:S(2)}, u32[]{:S(2)}) collective-permute-start(f32[224,128]{1,0:T(8,128)S(1)} %get-tuple-element.143.own), channel_id=1, source_target_pairs={{0,8},{4,12},{8,0},{12,4},{16,24},{20,28},{24,16},{28,20},{1,9},{5... | collective-permute-start | bytes 344072 | tf_op jit(solution)/shard_map/ppermute | solution.py:626
  77.7 6.4 %collective-permute-start.17 = (f32[224,128]{1,0:T(8,128)S(1)}, f32[224,128]{1,0:T(8,128)S(1)}, u32[]{:S(2)}, u32[]{:S(2)}) collective-permute-start(f32[224,128]{1,0:T(8,128)S(1)} %get-tuple-element.143.own), channel_id=1, source_target_pairs={{0,4},{4,0},{8,12},{12,8},{16,20},{20,16},{24,28},{28,24},{1,5},{5... | collective-permute-start | bytes 344072 | tf_op jit(solution)/shard_map/ppermute | solution.py:626
  82.6 7.6 %collective-permute-start.16 = (f32[328,128]{1,0:T(8,128)S(1)}, f32[328,128]{1,0:T(8,128)S(1)}, u32[]{:S(2)}, u32[]{:S(2)}) collective-permute-start(f32[328,128]{1,0:T(8,128)S(1)} %add.6.refs_0_), channel_id=1, source_target_pairs={{0,4},{4,0},{8,12},{12,8},{16,20},{20,16},{24,28},{28,24},{1,5},{5... | collective-permute-start | bytes 503816 | tf_op jit(solution)/shard_map/ppermute | solution.py:626
  84.1 6.2 %collective-permute-start.20 = (f32[224,128]{1,0:T(8,128)S(1)}, f32[224,128]{1,0:T(8,128)S(1)}, u32[]{:S(2)}, u32[]{:S(2)}) collective-permute-start(f32[224,128]{1,0:T(8,128)S(1)} %add.7.refs_2_), channel_id=1, source_target_pairs={{0,16},{4,20},{8,24},{12,28},{16,0},{20,4},{24,8},{28,12},{1,17},{... | collective-permute-start | bytes 344072 | tf_op jit(solution)/shard_map/ppermute | solution.py:626

commit v9 on v8

--- a/solution.py
+++ b/solution.py
@@ -413,7 +413,19 @@
     query_sums(modes, taps, steps, scale, summed, cot_pos, modal, q_ext, gain, gf0, early)
 
 
-def norm_kernel(taps, steps, last, scale, summed, cot_pos, gain, gf0, next_head, filt, ready, normed, grad_res, grad_query, work, head, work2):
+def normed_kernel(steps, scale, summed, gain, ready, normed, work):
+    del ready
+    factor = gain[...]
+
+    def make(c):
+        for i in range(CHUNK):
+            t = c * CHUNK + i
+            put(work, t, row(summed, t) * scale[pl.ds(t, 1), :] * factor)
+
+    skewed(steps // CHUNK, make, lambda c: gather_chunk(work, normed, c))
+
+
+def residual_kernel(taps, steps, last, scale, summed, cot_pos, gain, gf0, next_head, filt, ready, grad_res, grad_query, work, head):
     del ready
     back(0, taps, steps, last, gf0, next_head, filt, grad_query, work, head)
     factor = gain[...]
@@ -421,15 +433,10 @@
     def make(c):
         for i in range(CHUNK):
             t = c * CHUNK + i
-            inv, now = scale[pl.ds(t, 1), :], row(summed, t)
-            put(work, t, now * inv * factor)
-            put(work2, t, inv * (factor * row(cot_pos, t)) - scale[pl.ds(steps + t, 1), :] * now)
-
-    def lay(c):
-        gather_chunk(work, normed, c)
-        gather_chunk(work2, grad_res, c)
-
-    skewed(steps // CHUNK, make, lay)
+            scaled = scale[pl.ds(t, 1), :] * (factor * row(cot_pos, t))
+            put(work, t, scaled - scale[pl.ds(steps + t, 1), :] * row(summed, t))
+
+    skewed(steps // CHUNK, make, lambda c: gather_chunk(work, grad_res, c))
 
 
 def query_sums(modes, taps, steps, scale, summed, cot_pos, modal, q_ext, gain, gf0, early):
@@ -532,24 +539,25 @@
 
 def exclusive(before, other, lam, span, group, sign):
     at, later = place(group, sign)
-    here = later * jnp.exp(lam * (at * -float(span))) * other
+    here = later * jnp.exp(lam * (at * -float(span))) * other.astype(F32)
     return here if before is None else before + here
 
 
 def inclusive(own, other, lam, span, group, sign):
     _, later = place(group, sign)
     fall = -float(span * group)
-    return jnp.exp(lam * ((1.0 - later) * fall)) * own + jnp.exp(lam * (later * fall)) * other
+    return jnp.exp(lam * ((1.0 - later) * fall)) * own + jnp.exp(lam * (later * fall)) * other.astype(F32)
 
 
 def join_kernel(span, group, sign, first, own, other, lam, *refs):
-    before, ends = (None, refs[-2:]) if first else (refs[0][...], refs[-2:])
+    before, ends = (None, refs[-3:]) if first else (refs[0][...], refs[-3:])
     ends[0][...] = exclusive(before, other[...], lam[...], span, group, sign)
     ends[1][...] = inclusive(own[...], other[...], lam[...], span, group, sign)
+    ends[2][...] = ends[1][...].astype(BF16)
 
 
 def join_four_kernel(span, sign, own, first, second, third, lam, *refs):
-    before, end = refs[-2:]
+    before, end, sent = refs[-3:]
     at, _ = place(4, sign)
     here = lax.axis_index("ctx") if sign > 0 else lax.axis_size("ctx") - 1 - lax.axis_index("ctx")
     here, rates = here % 4, lam[...]
@@ -565,6 +573,7 @@
         total_end = total_end + jnp.exp(rates * ((3.0 - there) * -float(span))) * value
     before[...] = total_before
     end[...] = total_end
+    sent[...] = total_end.astype(BF16)
 
 
 def add_four_kernel(own, first, second, third, *refs):
@@ -633,7 +642,7 @@
         body,
         in_specs=[near] * len(ins) + [pl.BlockSpec(memory_space=pl.ANY)] * len(after),
         out_specs=[near] * len(outs),
-        out_shape=[jax.ShapeDtypeStruct(shape, BF16 if len(shape) > 2 else F32) for shape in outs],
+        out_shape=[jax.ShapeDtypeStruct(v, F32) if isinstance(v, tuple) else v for v in outs],
         compiler_params=pltpu.CompilerParams(vmem_limit_bytes=VMEM_LIMIT),
         cost_estimate=pl.CostEstimate(flops=ins[0].size, bytes_accessed=0, transcendentals=0),
         name=name,
@@ -642,20 +651,21 @@
 
 def scan_but_last(own, lam, span, sign, under):
     count, group, before = lax.axis_size("ctx"), 1, None
-    under = list(under)
+    under, sent = list(under), own
+    outs = [own.shape, own.shape, jax.ShapeDtypeStruct(own.shape, BF16)]
     if count >= 8:
         ins = [own, *(swap(own, "ctx", k) for k in (1, 2, 3)), lam]
         body = functools.partial(join_four_kernel, span, sign)
-        before, own = small(body, ins, under, [own.shape] * 2, "join")
+        before, own, sent = small(body, ins, under, outs, "join")
         group, under = 4, []
     while True:
-        other = swap(own, "ctx", group)
+        other = swap(sent, "ctx", group)
         if 2 * group >= count:
             return before, other, group
         body = functools.partial(join_kernel, span, group, sign, before is None)
         ins = [own, other, lam] + ([] if before is None else [before])
         after = [under.pop(0)] if under else []
-        before, own = small(body, ins, after, [own.shape] * 2, "join")
+        before, own, sent = small(body, ins, after, outs, "join")
         group *= 2
 
 
@@ -772,7 +782,7 @@
         30,
         "query",
     )
-    y, _ = call(
+    y, near_done = call(
         functools.partial(near_kernel, modes, steps),
         (u, lam, res, skip),
         [seq_spec, mode_spec, mode_spec, one_spec],
@@ -790,7 +800,7 @@
         32,
         "lags",
     )
-    before, other, group = scan_but_last(x_own, lam, steps, 1, [query_done])
+    before, other, group = scan_but_last(x_own, lam, steps, 1, [query_done, near_done])
     modal, summed, x_at, sums, _ = call(
         functools.partial(summed_kernel, modes, steps, blocks, group),
         (y, f0, res_pos, cot_pos, g, before, other, lam, faded, gain, own_lag_done),
@@ -849,7 +859,7 @@
         functools.partial(pack_kernel, steps, group, modes, early_rows, half),
         [before, other, lam, early, res, rate_sum, lag_sum, faded, a_next, gmy, f1, f2, gf0],
         [],
-        [lam.shape, half_shape, half_shape, (3, blocks, SUB * SUB, LANES)],
+        [lam.shape, half_shape, half_shape, jax.ShapeDtypeStruct((3, blocks, SUB * SUB, LANES), BF16)],
         "pack",
     )
     early_rows += modes
@@ -878,15 +888,25 @@
 
     last = lax.axis_size("ctx") - 1
     back_scratch = [pltpu.VMEM((steps * SUB, LANES), F32), pltpu.VMEM((SUB * SUB, LANES), F32)]
-    normed, grad_residual, grad_query, norm_done = call(
-        functools.partial(norm_kernel, taps, steps, last),
+    normed, normed_done = call(
+        functools.partial(normed_kernel, steps),
+        (scale, summed, gain, mixed_done),
+        [scale_spec, seq_spec, one_spec, any_spec],
+        [wide],
+        [wide_spec],
+        10,
+        "normed",
+        scratch=back_scratch[:1],
+    )
+    grad_residual, grad_query, norm_done = call(
+        functools.partial(residual_kernel, taps, steps, last),
         (scale, summed, cot_pos, gain, gf0, next_head, filt, late_done),
         [scale_spec, seq_spec, seq_spec, one_spec, seq_spec, next_spec, filt_spec, any_spec],
-        [wide, wide, wide],
-        [wide_spec, wide_spec, wide_spec],
-        45,
-        "norm",
-        scratch=[*back_scratch, pltpu.VMEM((steps * SUB, LANES), F32)],
+        [wide, wide],
+        [wide_spec, wide_spec],
+        35,
+        "residual",
+        scratch=back_scratch,
     )
     grad_key, grad_value, back_done = call(
         functools.partial(back_kernel, taps, steps, last),
@@ -898,7 +918,7 @@
         "back",
         scratch=back_scratch,
     )
-    count, under = lax.axis_size("ctx"), [[late_done], [norm_done]]
+    count, under = lax.axis_size("ctx"), [[late_done, normed_done], [norm_done]]
     mine = small(add_kernel, [kept_half, other_half], [mixed_done, next_head], [half_shape], "add")[0]
     step = 2
     while step < count:

time: 91.3 us -> 88.1 us (0.965)
  waiting for transfers between devices: 15.6 us -> 8.48 us
  starting transfers between devices: 28.4 us -> 30.6 us
  Pallas kernels: 46.4 us -> 48 us
    ppermute x19, waiting for transfers between devices: 14.8 us -> 8.47 us  [swap(): lax.ppermute(value, axis, [(i, i ^ step) for i in range(lax.axis_size(axi...]
    ppermute x19, starting transfers between devices: 22.7 us -> 24.4 us  [swap(): lax.ppermute(value, axis, [(i, i ^ step) for i in range(lax.axis_size(axi...]
    pallas_call x7, Pallas kernels: 0.65 us -> 1.82 us  [small(): pl.pallas_call(body, in_specs=[near] * len(ins) + [pl.BlockSpec(memory_sp...]
    pallas_call x15 -> x16, Pallas kernels: 44.9 us -> 45.2 us  [call(): pl.pallas_call(with_done, grid=(blocks,), in_specs=in_specs, out_specs=ou...]
  transfers between devices with their start and end apart: 21 -> 21, of which waited for: 9 -> 10; matrix products, arithmetic and copies ran while one was open for 0% -> 0% of each run, Pallas kernels for 38% -> 40%
where the time goes in v9:
time: 88.1 us; the launch traced here: 87.9 us
  Pallas kernels  48 us (54%)
  starting transfers between devices  30.6 us (35%)
  waiting for transfers between devices  8.48 us (10%)
    pallas_call x16, Pallas kernels, call(): pl.pallas_call(with_done, grid=(blocks,), in_specs=in_specs, out_specs=ou...  45.2 us
    ppermute x19, starting transfers between devices, swap(): lax.ppermute(value, axis, [(i, i ^ step) for i in range(lax.axis_size(axi...  24.4 us
    ppermute x19, waiting for transfers between devices, swap(): lax.ppermute(value, axis, [(i, i ^ step) for i in range(lax.axis_size(axi...  8.47 us
    ppermute x2, starting transfers between devices, ring(): lax.ppermute(value, axis, [(i, (i + distance) % count) for i in range(cou...  6.23 us
    pallas_call x7, Pallas kernels, small(): pl.pallas_call(body, in_specs=[near] * len(ins) + [pl.BlockSpec(memory_sp...  1.82 us
  transfers between devices with their start and end apart: 21, of which 10 were waited for; matrix products, arithmetic and copies ran while one was open for 0% of the time, Pallas kernels for 40%

profile of v9, /device:TPU:0, one launch (start us, length us, event | category | flops | bytes accessed | tf_op | source)
XLA Modules:
  0.0 87.9 jit_solution(5290217235493679075)
XLA Ops:
  0.6 0.9 %trailing.1 = bf16[3,8,2048]{2,1,0:T(8,128)(2,1)S(1)} custom-call(bf16[256,2048]{1,0:T(8,128)(2,1)} %refs_0_.3, bf16[256,2048]{1,0:T(8,128)(2,1)} %refs_0_.2, bf16[256,2048]{1,0:T(8,128)(2,1)} %refs_1_.2), custom_call_target="tpu_custom_call" | custom-call | flops 2048 | bytes 2048 | tf_op jit(solution)/shard_map/trailing/pallas_call | solution.py:741
  1.6 3.0 %collective-permute-start = (bf16[3,8,2048]{2,1,0:T(8,128)(2,1)S(1)}, bf16[3,8,2048]{2,1,0:T(8,128)(2,1)S(1)}, u32[]{:S(2)}, u32[]{:S(2)}) collective-permute-start(bf16[3,8,2048]{2,1,0:T(8,128)(2,1)S(1)} %trailing.1), channel_id=1, source_target_pairs={{0,4},{4,8},{8,12},{12,16},{16,20},{20,24},{24,28},{28,0},{1,5},{5... | collective-permute-start | bytes 294920 | tf_op jit(solution)/shard_map/ppermute | solution.py:631
  4.5 6.7 %features.1 = (f32[4224,128]{1,0:T(8,128)S(1)}, f32[4224,128]{1,0:T(8,128)S(1)}, f32[4096,128]{1,0:T(8,128)S(1)}, f32[4096,128]{1,0:T(8,128)S(1)}, f32[4096,128]...) custom-call(bf16[256,2048]{1,0:T(8,128)(2,1)} %refs_0_.2, ...), custom_call_target="tpu_custom_call" | custom-call | flops 33554432 | bytes 2097152 | tf_op jit(solution)/shard_map/features/pallas_call | solution.py:719
  12.0 2.6 %collective-permute-start.3 = (f32[256,128]{1,0:T(8,128)S(1)}, f32[256,128]{1,0:T(8,128)S(1)}, u32[]{:S(2)}, u32[]{:S(2)}) collective-permute-start(f32[256,128]{1,0:T(8,128)S(1)} %get-tuple-element.98.own), channel_id=1, source_target_pairs={{0,12},{4,8},{8,4},{12,0},{16,28},{20,24},{24,20},{28,16},{1,13},{... | collective-permute-start | bytes 393224 | tf_op jit(solution)/shard_map/ppermute | solution.py:635
  16.2 3.2 %query.3 = (f32[4224,128]{1,0:T(8,128)S(1)}, f32[4096,128]{1,0:T(8,128)S(1)}, f32[4096,128]{1,0:T(8,128)S(1)}, f32[4096,128]{1,0:T(8,128)S(1)}, f32[8,128]{1,0:T(8,128)S(1)}) custom-call(bf16[256,2048]{1,0:T(8,128)(2,1)} %refs_0_.3, bf16[256,2048]{1,0:T(8,128)(2,1)} %refs_1_.3, bf16[256,2048]{1,0:T(8,128)(2,1)} %refs_2_.3, ...), custom_call_target="tpu_custom_call" | custom-call | flops 15728640 | bytes 2097152 | tf_op jit(solution)/shard_map/query/pallas_call | solution.py:719
  19.5 1.3 %collective-permute-done.2.second = f32[256,128]{1,0:T(8,128)S(1)} collective-permute-done((f32[256,128]{1,0:T(8,128)S(1)}, f32[256,128]{1,0:T(8,128)S(1)}, u32[]{:S(2)}, u32[]{:S(2)}) %collective-permute-start.2) | collective-permute-done | bytes 131104 | tf_op jit(solution)/shard_map/ppermute | solution.py:635
  21.5 2.6 %collective-permute-start.4 = (bf16[256,128]{1,0:T(8,128)(2,1)S(1)}, bf16[256,128]{1,0:T(8,128)(2,1)S(1)}, u32[]{:S(2)}, u32[]{:S(2)}) collective-permute-start(bf16[256,128]{1,0:T(8,128)(2,1)S(1)} %get-tuple-element.102), channel_id=1, source_target_pairs={{0,16},{4,20},{8,24},{12,28},{16,0},{20,4},{24,8},{28,12},{1,17},{... | collective-permute-start | bytes 196616 | tf_op jit(solution)/shard_map/ppermute | solution.py:635
  24.1 2.1 %lags.1 = (f32[8192,128]{1,0:T(8,128)S(1)}, f32[8,128]{1,0:T(8,128)S(1)}) custom-call(f32[4096,128]{1,0:T(8,128)S(1)} %get-tuple-element.91.refs_0_.refs_1_, f32[256,128]{1,0:T(8,128)S(1)} %get-tuple-element.85.refs_4_.refs_1_.lam.refs_7_.refs_2_), custom_call_target="tpu_custom_call" | custom-call | flops 16777216 | bytes 2097152 | tf_op jit(solution)/shard_map/lags/pallas_call | solution.py:719
  27.1 4.6 %summed.1 = (f32[4096,128]{1,0:T(8,128)S(1)}, f32[4096,128]{1,0:T(8,128)S(1)}, f32[8192,128]{1,0:T(8,128)S(1)}, f32[2,256]{1,0:T(2,128)S(1)}, f32[8,128]{1,0:T(8,128)}) custom-call(f32[4096,128]{1,0:T(8,128)S(1)} %get-tuple-element.93.refs_0_, f32[4096,128]{1,0:T(8,128)S(1)} %get-tuple-element.94.refs_1_.refs_6_, f32[4096,128]{1,0:T(8,128)S(1)} %get-tuple-element.95.refs_2_, ...), custom_call_target="tpu_custom_call" | custom-call | flops 26214400 | bytes 2097152 | tf_op jit(solution)/shard_map/summed/pallas_call | solution.py:719
  31.7 1.4 %collective-permute-start.6 = (f32[2,256]{1,0:T(2,128)S(1)}, f32[2,256]{1,0:T(2,128)S(1)}, u32[]{:S(2)}, u32[]{:S(2)}) collective-permute-start(f32[2,256]{1,0:T(2,128)S(1)} %get-tuple-element.105.refs_0_), channel_id=1, source_target_pairs={{0,2},{1,3},{2,0},{3,1},{4,6},{5,7},{6,4},{7,5},{8,10},{9,11},{10,... | collective-permute-start | bytes 6152 | tf_op jit(solution)/shard_map/ppermute | solution.py:635
  33.6 0.8 borders.1
  35.3 3.9 %grad_modal.1 = (f32[512,128]{1,0:T(8,128)S(1)}, f32[4096,128]{1,0:T(8,128)S(1)}, f32[8192,128]{1,0:T(8,128)S(1)}, f32[256,128]{1,0:T(8,128)S(1)}, f32[256,128]{1,0:T(8,128)S(1)}, /*index=5*/f32[8,128]{1,0:T(8,128)}) custom-call(f32[2,256]{1,0:T(2,128)S(1)} %get-tuple-element.105.refs_0_, f32[2,256]{1,0:T(2,128)S(1)} %collective-permute-done.5.refs_1_, ...), custom_call_target="tpu_custom_call" | custom-call | flops 23592960 | bytes 2097152 | tf_op jit(solution)/shard_map/grad_modal/pallas_call | solution.py:719
  39.2 2.1 %collective-permute-start.10 = (f32[256,128]{1,0:T(8,128)S(1)}, f32[256,128]{1,0:T(8,128)S(1)}, u32[]{:S(2)}, u32[]{:S(2)}) collective-permute-start(f32[256,128]{1,0:T(8,128)S(1)} %get-tuple-element.121.own), channel_id=1, source_target_pairs={{0,12},{4,8},{8,4},{12,0},{16,28},{20,24},{24,20},{28,16},{1,13},{... | collective-permute-start | bytes 393224 | tf_op jit(solution)/shard_map/ppermute | solution.py:635
  42.7 4.1 %across.1 = (f32[256,128]{1,0:T(8,128)S(1)}, f32[256,128]{1,0:T(8,128)S(1)}, f32[8,128]{1,0:T(8,128)S(1)}) custom-call(f32[4096,128]{1,0:T(8,128)S(1)} %get-tuple-element.111.refs_0_, f32[8192,128]{1,0:T(8,128)S(1)} %get-tuple-element.112.refs_1_.refs_3_, f32[8192,128]{1,0:T(8,128)S(1)} %get-tuple-element.108.refs_1_.refs_2_, ...), custom_call_target="tpu_custom_call" | custom-call | flops 26214400 | bytes 2097152 | tf_op jit(solution)/shard_map/across/pallas_call | solution.py:719
  46.8 1.8 %collective-permute-done.9.second = f32[256,128]{1,0:T(8,128)S(1)} collective-permute-done((f32[256,128]{1,0:T(8,128)S(1)}, f32[256,128]{1,0:T(8,128)S(1)}, u32[]{:S(2)}, u32[]{:S(2)}) %collective-permute-start.9) | collective-permute-done | bytes 131104 | tf_op jit(solution)/shard_map/ppermute | solution.py:635
  49.4 2.4 %collective-permute-start.11 = (bf16[256,128]{1,0:T(8,128)(2,1)S(1)}, bf16[256,128]{1,0:T(8,128)(2,1)S(1)}, u32[]{:S(2)}, u32[]{:S(2)}) collective-permute-start(bf16[256,128]{1,0:T(8,128)(2,1)S(1)} %get-tuple-element.124), channel_id=1, source_target_pairs={{0,16},{4,20},{8,24},{12,28},{16,0},{20,4},{24,8},{28,12},{1,17},{... | collective-permute-start | bytes 196616 | tf_op jit(solution)/shard_map/ppermute | solution.py:635
  51.8 3.8 %near_adjoint.1 = (f32[4096,128]{1,0:T(8,128)S(1)}, f32[256,128]{1,0:T(8,128)S(1)}, f32[4096,128]{1,0:T(8,128)S(1)}, f32[400,128]{1,0:T(8,128)S(1)}, f32[8,128]{1,0:T(8,128)}) custom-call(f32[4096,128]{1,0:T(8,128)S(1)} %get-tuple-element.111.refs_0_, f32[4096,128]{1,0:T(8,128)S(1)} %get-tuple-element.91.refs_0_.refs_1_, ...), custom_call_target="tpu_custom_call" | custom-call | flops 28835840 | bytes 2097152 | tf_op jit(solution)/shard_map/near_adjoint/pallas_call | solution.py:719
  56.2 1.3 %collective-permute-start.13 = (f32[328,128]{1,0:T(8,128)S(1)}, f32[328,128]{1,0:T(8,128)S(1)}, u32[]{:S(2)}, u32[]{:S(2)}) collective-permute-start(f32[328,128]{1,0:T(8,128)S(1)} %get-tuple-element.144), channel_id=1, source_target_pairs={{0,4},{4,0},{8,12},{12,8},{16,20},{20,16},{24,28},{28,24},{1,5},{5... | collective-permute-start | bytes 503816 | tf_op jit(solution)/shard_map/ppermute | solution.py:635
  57.5 3.3 %collective-permute-start.12 = (bf16[3,2,64,128]{3,2,1,0:T(8,128)(2,1)S(1)}, bf16[3,2,64,128]{3,2,1,0:T(8,128)(2,1)S(1)}, u32[]{:S(2)}, u32[]{:S(2)}) collective-permute-start(bf16[3,2,64,128]{3,2,1,0:T(8,128)(2,1)S(1)} %get-tuple-element.133), channel_id=1, source_target_pairs={{0,28},{4,0},{8,4},{12,8},{16,12},{20,16},{24,20},{28,24},{1,29},{... | collective-permute-start | bytes 294920 | tf_op jit(solution)/shard_map/ppermute | solution.py:631
  60.8 3.3 %mixed.1 = (f32[4096,128]{1,0:T(8,128)S(1)}, f32[4096,128]{1,0:T(8,128)S(1)}, f32[8,128]{1,0:T(8,128)S(1)}) custom-call(f32[4096,128]{1,0:T(8,128)S(1)} %get-tuple-element.118.gmy.refs_0_, f32[4096,128]{1,0:T(8,128)S(1)} %get-tuple-element.119.f1.refs_1_, f32[4096,128]{1,0:T(8,128)S(1)} %get-tuple-element.120.f2.refs_2_, ...), custom_call_target="tpu_custom_call" | custom-call | flops 23592960 | bytes 2097152 | tf_op jit(solution)/shard_map/mixed/pallas_call | solution.py:719
  64.1 2.1 %collective-permute-start.14 = (f32[328,128]{1,0:T(8,128)S(1)}, f32[328,128]{1,0:T(8,128)S(1)}, u32[]{:S(2)}, u32[]{:S(2)}) collective-permute-start(f32[328,128]{1,0:T(8,128)S(1)} %add.4.one), channel_id=1, source_target_pairs={{0,8},{4,12},{8,0},{12,4},{16,24},{20,28},{24,16},{28,20},{1,9},{5... | collective-permute-start | bytes 503816 | tf_op jit(solution)/shard_map/ppermute | solution.py:635
  66.2 1.6 %normed.1 = (bf16[256,2048]{1,0:T(8,128)(2,1)}, f32[8,128]{1,0:T(8,128)S(1)}) custom-call(f32[512,128]{1,0:T(8,128)S(1)} %get-tuple-element.110.refs_7_.refs_0_, f32[4096,128]{1,0:T(8,128)S(1)} %get-tuple-element.106.refs_4_.refs_8_.refs_1_, f32[16,128]{1,0:T(8,128)S(1)} %bitcast.7, f32[8,128]{1,0:T(8,128)S(1)} %get-tuple-element.131.refs_3_.refs_0_), custom_call_target="tpu_custom_call" | custom-call | flops 5242880 | bytes 2097152 | tf_op jit(solution)/shard_map/normed/pallas_call | solution.py:719
  67.8 2.1 %filter_sums.1 = (f32[224,128]{1,0:T(8,128)S(1)}, f32[8,128]{1,0:T(8,128)S(1)}) custom-call(f32[4096,128]{1,0:T(8,128)S(1)} %get-tuple-element.134.refs_0_, f32[4096,128]{1,0:T(8,128)S(1)} %get-tuple-element.135.refs_1_, f32[4224,128]{1,0:T(8,128)S(1)} %get-tuple-element.136.refs_2_, f32[4224,128]{1,0:T(8,128)S(1)} %get-tuple-element.137.refs_3_), custom_call_target="tpu_custom_call" | custom-call | flops 15728640 | bytes 2097152 | tf_op jit(solution)/shard_map/filter_sums/pallas_call | solution.py:719
  69.9 2.0 %collective-permute-start.15 = (f32[328,128]{1,0:T(8,128)S(1)}, f32[328,128]{1,0:T(8,128)S(1)}, u32[]{:S(2)}, u32[]{:S(2)}) collective-permute-start(f32[328,128]{1,0:T(8,128)S(1)} %add.5.one), channel_id=1, source_target_pairs={{0,16},{4,20},{8,24},{12,28},{16,0},{20,4},{24,8},{28,12},{1,17},{... | collective-permute-start | bytes 503816 | tf_op jit(solution)/shard_map/ppermute | solution.py:635
  71.9 2.3 %collective-permute-start.19 = (f32[224,128]{1,0:T(8,128)S(1)}, f32[224,128]{1,0:T(8,128)S(1)}, u32[]{:S(2)}, u32[]{:S(2)}) collective-permute-start(f32[224,128]{1,0:T(8,128)S(1)} %get-tuple-element.147.own), channel_id=1, source_target_pairs={{0,12},{4,8},{8,4},{12,0},{16,28},{20,24},{24,20},{28,16},{1,13},{... | collective-permute-start | bytes 344072 | tf_op jit(solution)/shard_map/ppermute | solution.py:635
  74.6 0.8 collective-permute-start.17
  75.4 3.2 %residual.1 = (bf16[256,2048]{1,0:T(8,128)(2,1)}, bf16[256,2048]{1,0:T(8,128)(2,1)}, f32[8,128]{1,0:T(8,128)S(1)}) custom-call(f32[512,128]{1,0:T(8,128)S(1)} %get-tuple-element.110.refs_7_.refs_0_, f32[4096,128]{1,0:T(8,128)S(1)} %get-tuple-element.106.refs_4_.refs_8_.refs_1_, f32[4096,128]{1,0:T(8,128)S(1)} %get-tuple-element.96.refs_3_.refs_5_.refs_9_.refs_2_, ...), custom_call_target="tpu_custom_call" | custom-call | flops 18350080 | bytes 2097152 | tf_op jit(solution)/shard_map/residual/pallas_call | solution.py:719
  80.1 1.1 %collective-permute-done.18.second = f32[224,128]{1,0:T(8,128)S(1)} collective-permute-done((f32[224,128]{1,0:T(8,128)S(1)}, f32[224,128]{1,0:T(8,128)S(1)}, u32[]{:S(2)}, u32[]{:S(2)}) %collective-permute-start.18) | collective-permute-done | bytes 114720 | tf_op jit(solution)/shard_map/ppermute | solution.py:635
  81.3 1.1 %collective-permute-start.20 = (f32[224,128]{1,0:T(8,128)S(1)}, f32[224,128]{1,0:T(8,128)S(1)}, u32[]{:S(2)}, u32[]{:S(2)}) collective-permute-start(f32[224,128]{1,0:T(8,128)S(1)} %add.7.refs_2_), channel_id=1, source_target_pairs={{0,16},{4,20},{8,24},{12,28},{16,0},{20,4},{24,8},{28,12},{1,17},{... | collective-permute-start | bytes 344072 | tf_op jit(solution)/shard_map/ppermute | solution.py:635
  82.4 3.4 %back.1 = (bf16[256,2048]{1,0:T(8,128)(2,1)}, bf16[256,2048]{1,0:T(8,128)(2,1)}, f32[8,128]{1,0:T(8,128)S(1)}) custom-call(f32[4096,128]{1,0:T(8,128)S(1)} %get-tuple-element.134.refs_0_, f32[4096,128]{1,0:T(8,128)S(1)} %get-tuple-element.135.refs_1_, bf16[3,2,64,128]{3,2,1,0:T(8,128)(2,1)S(1)} %collective-permute-done.12.refs_5_.refs_2_.refs_1_, ...), custom_call_target="tpu_custom_call" | custom-call | flops 20971520 | bytes 2097152 | tf_op jit(solution)/shard_map/back/pallas_call | solution.py:719
  85.8 1.2 %collective-permute-done.20.refs_3_ = f32[224,128]{1,0:T(8,128)S(1)} collective-permute-done((f32[224,128]{1,0:T(8,128)S(1)}, f32[224,128]{1,0:T(8,128)S(1)}, u32[]{:S(2)}, u32[]{:S(2)}) %collective-permute-start.20) | collective-permute-done | bytes 114720 | tf_op jit(solution)/shard_map/ppermute | solution.py:635
  87.0 0.8 finish.1
  (38 shorter events, 10.0 us)
Async XLA Ops:
  1.6 9.7 %collective-permute-start = (bf16[3,8,2048]{2,1,0:T(8,128)(2,1)S(1)}, bf16[3,8,2048]{2,1,0:T(8,128)(2,1)S(1)}, u32[]{:S(2)}, u32[]{:S(2)}) collective-permute-start(bf16[3,8,2048]{2,1,0:T(8,128)(2,1)S(1)} %trailing.1), channel_id=1, source_target_pairs={{0,4},{4,8},{8,12},{12,16},{16,20},{20,24},{24,28},{28,0},{1,5},{5... | collective-permute-start | bytes 294920 | tf_op jit(solution)/shard_map/ppermute | solution.py:631
  11.2 4.3 %copy-start.1 = (f32[2048]{0:T(1024)S(1)}, f32[2048]{0:T(1024)}, u32[]{:S(2)}) copy-start(f32[2048]{0:T(1024)} %param.17) | copy-start | bytes 24580
  12.0 7.5 %collective-permute-start.3 = (f32[256,128]{1,0:T(8,128)S(1)}, f32[256,128]{1,0:T(8,128)S(1)}, u32[]{:S(2)}, u32[]{:S(2)}) collective-permute-start(f32[256,128]{1,0:T(8,128)S(1)} %get-tuple-element.98.own), channel_id=1, source_target_pairs={{0,12},{4,8},{8,4},{12,0},{16,28},{20,24},{24,20},{28,16},{1,13},{... | collective-permute-start | bytes 393224 | tf_op jit(solution)/shard_map/ppermute | solution.py:635
  14.6 6.2 %collective-permute-start.2 = (f32[256,128]{1,0:T(8,128)S(1)}, f32[256,128]{1,0:T(8,128)S(1)}, u32[]{:S(2)}, u32[]{:S(2)}) collective-permute-start(f32[256,128]{1,0:T(8,128)S(1)} %get-tuple-element.98.own), channel_id=1, source_target_pairs={{0,8},{4,12},{8,0},{12,4},{16,24},{20,28},{24,16},{28,20},{1,9},{5... | collective-permute-start | bytes 393224 | tf_op jit(solution)/shard_map/ppermute | solution.py:635
  15.0 5.8 %collective-permute-start.1 = (f32[256,128]{1,0:T(8,128)S(1)}, f32[256,128]{1,0:T(8,128)S(1)}, u32[]{:S(2)}, u32[]{:S(2)}) collective-permute-start(f32[256,128]{1,0:T(8,128)S(1)} %get-tuple-element.98.own), channel_id=1, source_target_pairs={{0,4},{4,0},{8,12},{12,8},{16,20},{20,16},{24,28},{28,24},{1,5},{5... | collective-permute-start | bytes 393224 | tf_op jit(solution)/shard_map/ppermute | solution.py:635
  19.5 7.6 %copy-start = (f32[2048]{0:T(1024)S(1)}, f32[2048]{0:T(1024)}, u32[]{:S(2)}) copy-start(f32[2048]{0:T(1024)} %param.18) | copy-start | bytes 24580
  21.5 5.5 %collective-permute-start.4 = (bf16[256,128]{1,0:T(8,128)(2,1)S(1)}, bf16[256,128]{1,0:T(8,128)(2,1)S(1)}, u32[]{:S(2)}, u32[]{:S(2)}) collective-permute-start(bf16[256,128]{1,0:T(8,128)(2,1)S(1)} %get-tuple-element.102), channel_id=1, source_target_pairs={{0,16},{4,20},{8,24},{12,28},{16,0},{20,4},{24,8},{28,12},{1,17},{... | collective-permute-start | bytes 196616 | tf_op jit(solution)/shard_map/ppermute | solution.py:635
  31.7 3.0 %collective-permute-start.7 = (f32[2,256]{1,0:T(2,128)S(1)}, f32[2,256]{1,0:T(2,128)S(1)}, u32[]{:S(2)}, u32[]{:S(2)}) collective-permute-start(f32[2,256]{1,0:T(2,128)S(1)} %get-tuple-element.105.refs_0_), channel_id=1, source_target_pairs={{0,3},{1,2},{2,1},{3,0},{4,7},{5,6},{6,5},{7,4},{8,11},{9,10},{10,... | collective-permute-start | bytes 6152 | tf_op jit(solution)/shard_map/ppermute | solution.py:635
  31.7 3.6 %collective-permute-start.6 = (f32[2,256]{1,0:T(2,128)S(1)}, f32[2,256]{1,0:T(2,128)S(1)}, u32[]{:S(2)}, u32[]{:S(2)}) collective-permute-start(f32[2,256]{1,0:T(2,128)S(1)} %get-tuple-element.105.refs_0_), channel_id=1, source_target_pairs={{0,2},{1,3},{2,0},{3,1},{4,6},{5,7},{6,4},{7,5},{8,10},{9,11},{10,... | collective-permute-start | bytes 6152 | tf_op jit(solution)/shard_map/ppermute | solution.py:635
  33.1 2.2 %collective-permute-start.5 = (f32[2,256]{1,0:T(2,128)S(1)}, f32[2,256]{1,0:T(2,128)S(1)}, u32[]{:S(2)}, u32[]{:S(2)}) collective-permute-start(f32[2,256]{1,0:T(2,128)S(1)} %get-tuple-element.105.refs_0_), channel_id=1, source_target_pairs={{0,1},{1,0},{2,3},{3,2},{4,5},{5,4},{6,7},{7,6},{8,9},{9,8},{10,11... | collective-permute-start | bytes 6152 | tf_op jit(solution)/shard_map/ppermute | solution.py:635
  39.2 7.6 %collective-permute-start.10 = (f32[256,128]{1,0:T(8,128)S(1)}, f32[256,128]{1,0:T(8,128)S(1)}, u32[]{:S(2)}, u32[]{:S(2)}) collective-permute-start(f32[256,128]{1,0:T(8,128)S(1)} %get-tuple-element.121.own), channel_id=1, source_target_pairs={{0,12},{4,8},{8,4},{12,0},{16,28},{20,24},{24,20},{28,16},{1,13},{... | collective-permute-start | bytes 393224 | tf_op jit(solution)/shard_map/ppermute | solution.py:635
  41.3 7.4 %collective-permute-start.9 = (f32[256,128]{1,0:T(8,128)S(1)}, f32[256,128]{1,0:T(8,128)S(1)}, u32[]{:S(2)}, u32[]{:S(2)}) collective-permute-start(f32[256,128]{1,0:T(8,128)S(1)} %get-tuple-element.121.own), channel_id=1, source_target_pairs={{0,8},{4,12},{8,0},{12,4},{16,24},{20,28},{24,16},{28,20},{1,9},{5... | collective-permute-start | bytes 393224 | tf_op jit(solution)/shard_map/ppermute | solution.py:635
  42.0 6.7 %collective-permute-start.8 = (f32[256,128]{1,0:T(8,128)S(1)}, f32[256,128]{1,0:T(8,128)S(1)}, u32[]{:S(2)}, u32[]{:S(2)}) collective-permute-start(f32[256,128]{1,0:T(8,128)S(1)} %get-tuple-element.121.own), channel_id=1, source_target_pairs={{0,4},{4,0},{8,12},{12,8},{16,20},{20,16},{24,28},{28,24},{1,5},{5... | collective-permute-start | bytes 393224 | tf_op jit(solution)/shard_map/ppermute | solution.py:635
  49.4 6.6 %collective-permute-start.11 = (bf16[256,128]{1,0:T(8,128)(2,1)S(1)}, bf16[256,128]{1,0:T(8,128)(2,1)S(1)}, u32[]{:S(2)}, u32[]{:S(2)}) collective-permute-start(bf16[256,128]{1,0:T(8,128)(2,1)S(1)} %get-tuple-element.124), channel_id=1, source_target_pairs={{0,16},{4,20},{8,24},{12,28},{16,0},{20,4},{24,8},{28,12},{1,17},{... | collective-permute-start | bytes 196616 | tf_op jit(solution)/shard_map/ppermute | solution.py:635
  56.2 7.9 %collective-permute-start.13 = (f32[328,128]{1,0:T(8,128)S(1)}, f32[328,128]{1,0:T(8,128)S(1)}, u32[]{:S(2)}, u32[]{:S(2)}) collective-permute-start(f32[328,128]{1,0:T(8,128)S(1)} %get-tuple-element.144), channel_id=1, source_target_pairs={{0,4},{4,0},{8,12},{12,8},{16,20},{20,16},{24,28},{28,24},{1,5},{5... | collective-permute-start | bytes 503816 | tf_op jit(solution)/shard_map/ppermute | solution.py:635
  57.5 6.6 %collective-permute-start.12 = (bf16[3,2,64,128]{3,2,1,0:T(8,128)(2,1)S(1)}, bf16[3,2,64,128]{3,2,1,0:T(8,128)(2,1)S(1)}, u32[]{:S(2)}, u32[]{:S(2)}) collective-permute-start(bf16[3,2,64,128]{3,2,1,0:T(8,128)(2,1)S(1)} %get-tuple-element.133), channel_id=1, source_target_pairs={{0,28},{4,0},{8,4},{12,8},{16,12},{20,16},{24,20},{28,24},{1,29},{... | collective-permute-start | bytes 294920 | tf_op jit(solution)/shard_map/ppermute | solution.py:631
  64.1 5.8 %collective-permute-start.14 = (f32[328,128]{1,0:T(8,128)S(1)}, f32[328,128]{1,0:T(8,128)S(1)}, u32[]{:S(2)}, u32[]{:S(2)}) collective-permute-start(f32[328,128]{1,0:T(8,128)S(1)} %add.4.one), channel_id=1, source_target_pairs={{0,8},{4,12},{8,0},{12,4},{16,24},{20,28},{24,16},{28,20},{1,9},{5... | collective-permute-start | bytes 503816 | tf_op jit(solution)/shard_map/ppermute | solution.py:635
  69.9 9.5 %collective-permute-start.15 = (f32[328,128]{1,0:T(8,128)S(1)}, f32[328,128]{1,0:T(8,128)S(1)}, u32[]{:S(2)}, u32[]{:S(2)}) collective-permute-start(f32[328,128]{1,0:T(8,128)S(1)} %add.5.one), channel_id=1, source_target_pairs={{0,16},{4,20},{8,24},{12,28},{16,0},{20,4},{24,8},{28,12},{1,17},{... | collective-permute-start | bytes 503816 | tf_op jit(solution)/shard_map/ppermute | solution.py:635
  71.9 8.2 %collective-permute-start.19 = (f32[224,128]{1,0:T(8,128)S(1)}, f32[224,128]{1,0:T(8,128)S(1)}, u32[]{:S(2)}, u32[]{:S(2)}) collective-permute-start(f32[224,128]{1,0:T(8,128)S(1)} %get-tuple-element.147.own), channel_id=1, source_target_pairs={{0,12},{4,8},{8,4},{12,0},{16,28},{20,24},{24,20},{28,16},{1,13},{... | collective-permute-start | bytes 344072 | tf_op jit(solution)/shard_map/ppermute | solution.py:635
  74.2 7.0 %collective-permute-start.18 = (f32[224,128]{1,0:T(8,128)S(1)}, f32[224,128]{1,0:T(8,128)S(1)}, u32[]{:S(2)}, u32[]{:S(2)}) collective-permute-start(f32[224,128]{1,0:T(8,128)S(1)} %get-tuple-element.147.own), channel_id=1, source_target_pairs={{0,8},{4,12},{8,0},{12,4},{16,24},{20,28},{24,16},{28,20},{1,9},{5... | collective-permute-start | bytes 344072 | tf_op jit(solution)/shard_map/ppermute | solution.py:635
  74.6 6.7 %collective-permute-start.17 = (f32[224,128]{1,0:T(8,128)S(1)}, f32[224,128]{1,0:T(8,128)S(1)}, u32[]{:S(2)}, u32[]{:S(2)}) collective-permute-start(f32[224,128]{1,0:T(8,128)S(1)} %get-tuple-element.147.own), channel_id=1, source_target_pairs={{0,4},{4,0},{8,12},{12,8},{16,20},{20,16},{24,28},{28,24},{1,5},{5... | collective-permute-start | bytes 344072 | tf_op jit(solution)/shard_map/ppermute | solution.py:635
  79.4 7.6 %collective-permute-start.16 = (f32[328,128]{1,0:T(8,128)S(1)}, f32[328,128]{1,0:T(8,128)S(1)}, u32[]{:S(2)}, u32[]{:S(2)}) collective-permute-start(f32[328,128]{1,0:T(8,128)S(1)} %add.6.refs_0_), channel_id=1, source_target_pairs={{0,4},{4,0},{8,12},{12,8},{16,20},{20,16},{24,28},{28,24},{1,5},{5... | collective-permute-start | bytes 503816 | tf_op jit(solution)/shard_map/ppermute | solution.py:635
  81.3 5.8 %collective-permute-start.20 = (f32[224,128]{1,0:T(8,128)S(1)}, f32[224,128]{1,0:T(8,128)S(1)}, u32[]{:S(2)}, u32[]{:S(2)}) collective-permute-start(f32[224,128]{1,0:T(8,128)S(1)} %add.7.refs_2_), channel_id=1, source_target_pairs={{0,16},{4,20},{8,24},{12,28},{16,0},{20,4},{24,8},{28,12},{1,17},{... | collective-permute-start | bytes 344072 | tf_op jit(solution)/shard_map/ppermute | solution.py:635

commit v10 on v9

--- a/solution.py
+++ b/solution.py
@@ -25,15 +25,15 @@
 
 
 def loop(start, stop, body, carry):
-    fours = (stop - start) // 4
-
-    def four(i, carry):
-        for k in range(4):
-            carry = body(start + 4 * i + k, carry)
+    eights = (stop - start) // 8
+
+    def eight(i, carry):
+        for k in range(8):
+            carry = body(start + 8 * i + k, carry)
         return carry
 
-    carry = lax.fori_loop(0, fours, four, carry)
-    for i in range(start + 4 * fours, stop):
+    carry = lax.fori_loop(0, eights, eight, carry)
+    for i in range(start + 8 * eights, stop):
         carry = body(i, carry)
     return carry
 

time: 88.1 us -> 87.8 us (level)
  no operation moved by 1% of the time
where the time goes in v10:
time: 87.8 us; the launch traced here: 87.6 us
  Pallas kernels  47.5 us (54%)
  starting transfers between devices  30.8 us (35%)
  waiting for transfers between devices  8.47 us (10%)
    pallas_call x16, Pallas kernels, call(): pl.pallas_call(with_done, grid=(blocks,), in_specs=in_specs, out_specs=ou...  44.7 us
    ppermute x19, starting transfers between devices, swap(): lax.ppermute(value, axis, [(i, i ^ step) for i in range(lax.axis_size(axi...  24.6 us
    ppermute x19, waiting for transfers between devices, swap(): lax.ppermute(value, axis, [(i, i ^ step) for i in range(lax.axis_size(axi...  8.46 us
    ppermute x2, starting transfers between devices, ring(): lax.ppermute(value, axis, [(i, (i + distance) % count) for i in range(cou...  6.23 us
    pallas_call x7, Pallas kernels, small(): pl.pallas_call(body, in_specs=[near] * len(ins) + [pl.BlockSpec(memory_sp...  1.82 us
  transfers between devices with their start and end apart: 21, of which 10 were waited for; matrix products, arithmetic and copies ran while one was open for 0% of the time, Pallas kernels for 40%

profile of v10, /device:TPU:0, one launch (start us, length us, event | category | flops | bytes accessed | tf_op | source)
XLA Modules:
  0.0 87.6 jit_solution(12493182575438288759)
XLA Ops:
  0.6 0.9 %trailing.1 = bf16[3,8,2048]{2,1,0:T(8,128)(2,1)S(1)} custom-call(bf16[256,2048]{1,0:T(8,128)(2,1)} %refs_0_.3, bf16[256,2048]{1,0:T(8,128)(2,1)} %refs_0_.2, bf16[256,2048]{1,0:T(8,128)(2,1)} %refs_1_.2), custom_call_target="tpu_custom_call" | custom-call | flops 2048 | bytes 2048 | tf_op jit(solution)/shard_map/trailing/pallas_call | solution.py:741
  1.6 3.0 %collective-permute-start = (bf16[3,8,2048]{2,1,0:T(8,128)(2,1)S(1)}, bf16[3,8,2048]{2,1,0:T(8,128)(2,1)S(1)}, u32[]{:S(2)}, u32[]{:S(2)}) collective-permute-start(bf16[3,8,2048]{2,1,0:T(8,128)(2,1)S(1)} %trailing.1), channel_id=1, source_target_pairs={{0,4},{4,8},{8,12},{12,16},{16,20},{20,24},{24,28},{28,0},{1,5},{5... | collective-permute-start | bytes 294920 | tf_op jit(solution)/shard_map/ppermute | solution.py:631
  4.5 6.7 %features.1 = (f32[4224,128]{1,0:T(8,128)S(1)}, f32[4224,128]{1,0:T(8,128)S(1)}, f32[4096,128]{1,0:T(8,128)S(1)}, f32[4096,128]{1,0:T(8,128)S(1)}, f32[4096,128]...) custom-call(bf16[256,2048]{1,0:T(8,128)(2,1)} %refs_0_.2, ...), custom_call_target="tpu_custom_call" | custom-call | flops 33554432 | bytes 2097152 | tf_op jit(solution)/shard_map/features/pallas_call | solution.py:719
  12.0 2.6 %collective-permute-start.3 = (f32[256,128]{1,0:T(8,128)S(1)}, f32[256,128]{1,0:T(8,128)S(1)}, u32[]{:S(2)}, u32[]{:S(2)}) collective-permute-start(f32[256,128]{1,0:T(8,128)S(1)} %get-tuple-element.98.own), channel_id=1, source_target_pairs={{0,12},{4,8},{8,4},{12,0},{16,28},{20,24},{24,20},{28,16},{1,13},{... | collective-permute-start | bytes 393224 | tf_op jit(solution)/shard_map/ppermute | solution.py:635
  16.2 3.2 %query.3 = (f32[4224,128]{1,0:T(8,128)S(1)}, f32[4096,128]{1,0:T(8,128)S(1)}, f32[4096,128]{1,0:T(8,128)S(1)}, f32[4096,128]{1,0:T(8,128)S(1)}, f32[8,128]{1,0:T(8,128)S(1)}) custom-call(bf16[256,2048]{1,0:T(8,128)(2,1)} %refs_0_.3, bf16[256,2048]{1,0:T(8,128)(2,1)} %refs_1_.3, bf16[256,2048]{1,0:T(8,128)(2,1)} %refs_2_.3, ...), custom_call_target="tpu_custom_call" | custom-call | flops 15728640 | bytes 2097152 | tf_op jit(solution)/shard_map/query/pallas_call | solution.py:719
  19.5 1.3 %collective-permute-done.2.second = f32[256,128]{1,0:T(8,128)S(1)} collective-permute-done((f32[256,128]{1,0:T(8,128)S(1)}, f32[256,128]{1,0:T(8,128)S(1)}, u32[]{:S(2)}, u32[]{:S(2)}) %collective-permute-start.2) | collective-permute-done | bytes 131104 | tf_op jit(solution)/shard_map/ppermute | solution.py:635
  21.5 2.6 %collective-permute-start.4 = (bf16[256,128]{1,0:T(8,128)(2,1)S(1)}, bf16[256,128]{1,0:T(8,128)(2,1)S(1)}, u32[]{:S(2)}, u32[]{:S(2)}) collective-permute-start(bf16[256,128]{1,0:T(8,128)(2,1)S(1)} %get-tuple-element.102), channel_id=1, source_target_pairs={{0,16},{4,20},{8,24},{12,28},{16,0},{20,4},{24,8},{28,12},{1,17},{... | collective-permute-start | bytes 196616 | tf_op jit(solution)/shard_map/ppermute | solution.py:635
  24.1 2.1 %lags.1 = (f32[8192,128]{1,0:T(8,128)S(1)}, f32[8,128]{1,0:T(8,128)S(1)}) custom-call(f32[4096,128]{1,0:T(8,128)S(1)} %get-tuple-element.91.refs_0_.refs_1_, f32[256,128]{1,0:T(8,128)S(1)} %get-tuple-element.85.refs_4_.refs_1_.lam.refs_7_.refs_2_), custom_call_target="tpu_custom_call" | custom-call | flops 16777216 | bytes 2097152 | tf_op jit(solution)/shard_map/lags/pallas_call | solution.py:719
  26.2 0.9 collective-permute-done.4.refs_6_
  27.1 4.5 %summed.1 = (f32[4096,128]{1,0:T(8,128)S(1)}, f32[4096,128]{1,0:T(8,128)S(1)}, f32[8192,128]{1,0:T(8,128)S(1)}, f32[2,256]{1,0:T(2,128)S(1)}, f32[8,128]{1,0:T(8,128)}) custom-call(f32[4096,128]{1,0:T(8,128)S(1)} %get-tuple-element.93.refs_0_, f32[4096,128]{1,0:T(8,128)S(1)} %get-tuple-element.94.refs_1_.refs_6_, f32[4096,128]{1,0:T(8,128)S(1)} %get-tuple-element.95.refs_2_, ...), custom_call_target="tpu_custom_call" | custom-call | flops 26214400 | bytes 2097152 | tf_op jit(solution)/shard_map/summed/pallas_call | solution.py:719
  31.6 1.4 %collective-permute-start.6 = (f32[2,256]{1,0:T(2,128)S(1)}, f32[2,256]{1,0:T(2,128)S(1)}, u32[]{:S(2)}, u32[]{:S(2)}) collective-permute-start(f32[2,256]{1,0:T(2,128)S(1)} %get-tuple-element.105.refs_0_), channel_id=1, source_target_pairs={{0,2},{1,3},{2,0},{3,1},{4,6},{5,7},{6,4},{7,5},{8,10},{9,11},{10,... | collective-permute-start | bytes 6152 | tf_op jit(solution)/shard_map/ppermute | solution.py:635
  35.2 3.8 %grad_modal.1 = (f32[512,128]{1,0:T(8,128)S(1)}, f32[4096,128]{1,0:T(8,128)S(1)}, f32[8192,128]{1,0:T(8,128)S(1)}, f32[256,128]{1,0:T(8,128)S(1)}, f32[256,128]{1,0:T(8,128)S(1)}, /*index=5*/f32[8,128]{1,0:T(8,128)}) custom-call(f32[2,256]{1,0:T(2,128)S(1)} %get-tuple-element.105.refs_0_, f32[2,256]{1,0:T(2,128)S(1)} %collective-permute-done.5.refs_1_, ...), custom_call_target="tpu_custom_call" | custom-call | flops 23592960 | bytes 2097152 | tf_op jit(solution)/shard_map/grad_modal/pallas_call | solution.py:719
  39.1 2.1 %collective-permute-start.10 = (f32[256,128]{1,0:T(8,128)S(1)}, f32[256,128]{1,0:T(8,128)S(1)}, u32[]{:S(2)}, u32[]{:S(2)}) collective-permute-start(f32[256,128]{1,0:T(8,128)S(1)} %get-tuple-element.121.own), channel_id=1, source_target_pairs={{0,12},{4,8},{8,4},{12,0},{16,28},{20,24},{24,20},{28,16},{1,13},{... | collective-permute-start | bytes 393224 | tf_op jit(solution)/shard_map/ppermute | solution.py:635
  42.6 4.0 %across.1 = (f32[256,128]{1,0:T(8,128)S(1)}, f32[256,128]{1,0:T(8,128)S(1)}, f32[8,128]{1,0:T(8,128)S(1)}) custom-call(f32[4096,128]{1,0:T(8,128)S(1)} %get-tuple-element.111.refs_0_, f32[8192,128]{1,0:T(8,128)S(1)} %get-tuple-element.112.refs_1_.refs_3_, f32[8192,128]{1,0:T(8,128)S(1)} %get-tuple-element.108.refs_1_.refs_2_, ...), custom_call_target="tpu_custom_call" | custom-call | flops 26214400 | bytes 2097152 | tf_op jit(solution)/shard_map/across/pallas_call | solution.py:719
  46.6 1.9 %collective-permute-done.9.second = f32[256,128]{1,0:T(8,128)S(1)} collective-permute-done((f32[256,128]{1,0:T(8,128)S(1)}, f32[256,128]{1,0:T(8,128)S(1)}, u32[]{:S(2)}, u32[]{:S(2)}) %collective-permute-start.9) | collective-permute-done | bytes 131104 | tf_op jit(solution)/shard_map/ppermute | solution.py:635
  49.3 2.4 %collective-permute-start.11 = (bf16[256,128]{1,0:T(8,128)(2,1)S(1)}, bf16[256,128]{1,0:T(8,128)(2,1)S(1)}, u32[]{:S(2)}, u32[]{:S(2)}) collective-permute-start(bf16[256,128]{1,0:T(8,128)(2,1)S(1)} %get-tuple-element.124), channel_id=1, source_target_pairs={{0,16},{4,20},{8,24},{12,28},{16,0},{20,4},{24,8},{28,12},{1,17},{... | collective-permute-start | bytes 196616 | tf_op jit(solution)/shard_map/ppermute | solution.py:635
  51.7 3.7 %near_adjoint.1 = (f32[4096,128]{1,0:T(8,128)S(1)}, f32[256,128]{1,0:T(8,128)S(1)}, f32[4096,128]{1,0:T(8,128)S(1)}, f32[400,128]{1,0:T(8,128)S(1)}, f32[8,128]{1,0:T(8,128)}) custom-call(f32[4096,128]{1,0:T(8,128)S(1)} %get-tuple-element.111.refs_0_, f32[4096,128]{1,0:T(8,128)S(1)} %get-tuple-element.91.refs_0_.refs_1_, ...), custom_call_target="tpu_custom_call" | custom-call | flops 28835840 | bytes 2097152 | tf_op jit(solution)/shard_map/near_adjoint/pallas_call | solution.py:719
  56.1 1.3 %collective-permute-start.13 = (f32[328,128]{1,0:T(8,128)S(1)}, f32[328,128]{1,0:T(8,128)S(1)}, u32[]{:S(2)}, u32[]{:S(2)}) collective-permute-start(f32[328,128]{1,0:T(8,128)S(1)} %get-tuple-element.144), channel_id=1, source_target_pairs={{0,4},{4,0},{8,12},{12,8},{16,20},{20,16},{24,28},{28,24},{1,5},{5... | collective-permute-start | bytes 503816 | tf_op jit(solution)/shard_map/ppermute | solution.py:635
  57.4 3.3 %collective-permute-start.12 = (bf16[3,2,64,128]{3,2,1,0:T(8,128)(2,1)S(1)}, bf16[3,2,64,128]{3,2,1,0:T(8,128)(2,1)S(1)}, u32[]{:S(2)}, u32[]{:S(2)}) collective-permute-start(bf16[3,2,64,128]{3,2,1,0:T(8,128)(2,1)S(1)} %get-tuple-element.133), channel_id=1, source_target_pairs={{0,28},{4,0},{8,4},{12,8},{16,12},{20,16},{24,20},{28,24},{1,29},{... | collective-permute-start | bytes 294920 | tf_op jit(solution)/shard_map/ppermute | solution.py:631
  60.6 3.3 %mixed.1 = (f32[4096,128]{1,0:T(8,128)S(1)}, f32[4096,128]{1,0:T(8,128)S(1)}, f32[8,128]{1,0:T(8,128)S(1)}) custom-call(f32[4096,128]{1,0:T(8,128)S(1)} %get-tuple-element.118.gmy.refs_0_, f32[4096,128]{1,0:T(8,128)S(1)} %get-tuple-element.119.f1.refs_1_, f32[4096,128]{1,0:T(8,128)S(1)} %get-tuple-element.120.f2.refs_2_, ...), custom_call_target="tpu_custom_call" | custom-call | flops 23592960 | bytes 2097152 | tf_op jit(solution)/shard_map/mixed/pallas_call | solution.py:719
  64.0 2.0 %collective-permute-start.14 = (f32[328,128]{1,0:T(8,128)S(1)}, f32[328,128]{1,0:T(8,128)S(1)}, u32[]{:S(2)}, u32[]{:S(2)}) collective-permute-start(f32[328,128]{1,0:T(8,128)S(1)} %add.4.one), channel_id=1, source_target_pairs={{0,8},{4,12},{8,0},{12,4},{16,24},{20,28},{24,16},{28,20},{1,9},{5... | collective-permute-start | bytes 503816 | tf_op jit(solution)/shard_map/ppermute | solution.py:635
  65.9 1.6 %normed.1 = (bf16[256,2048]{1,0:T(8,128)(2,1)}, f32[8,128]{1,0:T(8,128)S(1)}) custom-call(f32[512,128]{1,0:T(8,128)S(1)} %get-tuple-element.110.refs_7_.refs_0_, f32[4096,128]{1,0:T(8,128)S(1)} %get-tuple-element.106.refs_4_.refs_8_.refs_1_, f32[16,128]{1,0:T(8,128)S(1)} %bitcast.7, f32[8,128]{1,0:T(8,128)S(1)} %get-tuple-element.131.refs_3_.refs_0_), custom_call_target="tpu_custom_call" | custom-call | flops 5242880 | bytes 2097152 | tf_op jit(solution)/shard_map/normed/pallas_call | solution.py:719
  67.6 2.0 %filter_sums.1 = (f32[224,128]{1,0:T(8,128)S(1)}, f32[8,128]{1,0:T(8,128)S(1)}) custom-call(f32[4096,128]{1,0:T(8,128)S(1)} %get-tuple-element.134.refs_0_, f32[4096,128]{1,0:T(8,128)S(1)} %get-tuple-element.135.refs_1_, f32[4224,128]{1,0:T(8,128)S(1)} %get-tuple-element.136.refs_2_, f32[4224,128]{1,0:T(8,128)S(1)} %get-tuple-element.137.refs_3_), custom_call_target="tpu_custom_call" | custom-call | flops 15728640 | bytes 2097152 | tf_op jit(solution)/shard_map/filter_sums/pallas_call | solution.py:719
  69.6 2.1 %collective-permute-start.15 = (f32[328,128]{1,0:T(8,128)S(1)}, f32[328,128]{1,0:T(8,128)S(1)}, u32[]{:S(2)}, u32[]{:S(2)}) collective-permute-start(f32[328,128]{1,0:T(8,128)S(1)} %add.5.one), channel_id=1, source_target_pairs={{0,16},{4,20},{8,24},{12,28},{16,0},{20,4},{24,8},{28,12},{1,17},{... | collective-permute-start | bytes 503816 | tf_op jit(solution)/shard_map/ppermute | solution.py:635
  71.7 2.3 %collective-permute-start.19 = (f32[224,128]{1,0:T(8,128)S(1)}, f32[224,128]{1,0:T(8,128)S(1)}, u32[]{:S(2)}, u32[]{:S(2)}) collective-permute-start(f32[224,128]{1,0:T(8,128)S(1)} %get-tuple-element.147.own), channel_id=1, source_target_pairs={{0,12},{4,8},{8,4},{12,0},{16,28},{20,24},{24,20},{28,16},{1,13},{... | collective-permute-start | bytes 344072 | tf_op jit(solution)/shard_map/ppermute | solution.py:635
  74.4 0.8 collective-permute-start.17
  75.2 3.2 %residual.1 = (bf16[256,2048]{1,0:T(8,128)(2,1)}, bf16[256,2048]{1,0:T(8,128)(2,1)}, f32[8,128]{1,0:T(8,128)S(1)}) custom-call(f32[512,128]{1,0:T(8,128)S(1)} %get-tuple-element.110.refs_7_.refs_0_, f32[4096,128]{1,0:T(8,128)S(1)} %get-tuple-element.106.refs_4_.refs_8_.refs_1_, f32[4096,128]{1,0:T(8,128)S(1)} %get-tuple-element.96.refs_3_.refs_5_.refs_9_.refs_2_, ...), custom_call_target="tpu_custom_call" | custom-call | flops 18350080 | bytes 2097152 | tf_op jit(solution)/shard_map/residual/pallas_call | solution.py:719
  79.8 1.1 %collective-permute-done.18.second = f32[224,128]{1,0:T(8,128)S(1)} collective-permute-done((f32[224,128]{1,0:T(8,128)S(1)}, f32[224,128]{1,0:T(8,128)S(1)}, u32[]{:S(2)}, u32[]{:S(2)}) %collective-permute-start.18) | collective-permute-done | bytes 114720 | tf_op jit(solution)/shard_map/ppermute | solution.py:635
  81.0 1.3 %collective-permute-start.20 = (f32[224,128]{1,0:T(8,128)S(1)}, f32[224,128]{1,0:T(8,128)S(1)}, u32[]{:S(2)}, u32[]{:S(2)}) collective-permute-start(f32[224,128]{1,0:T(8,128)S(1)} %add.7.refs_2_), channel_id=1, source_target_pairs={{0,16},{4,20},{8,24},{12,28},{16,0},{20,4},{24,8},{28,12},{1,17},{... | collective-permute-start | bytes 344072 | tf_op jit(solution)/shard_map/ppermute | solution.py:635
  82.2 3.4 %back.1 = (bf16[256,2048]{1,0:T(8,128)(2,1)}, bf16[256,2048]{1,0:T(8,128)(2,1)}, f32[8,128]{1,0:T(8,128)S(1)}) custom-call(f32[4096,128]{1,0:T(8,128)S(1)} %get-tuple-element.134.refs_0_, f32[4096,128]{1,0:T(8,128)S(1)} %get-tuple-element.135.refs_1_, bf16[3,2,64,128]{3,2,1,0:T(8,128)(2,1)S(1)} %collective-permute-done.12.refs_5_.refs_2_.refs_1_, ...), custom_call_target="tpu_custom_call" | custom-call | flops 20971520 | bytes 2097152 | tf_op jit(solution)/shard_map/back/pallas_call | solution.py:719
  85.7 1.1 %collective-permute-done.20.refs_3_ = f32[224,128]{1,0:T(8,128)S(1)} collective-permute-done((f32[224,128]{1,0:T(8,128)S(1)}, f32[224,128]{1,0:T(8,128)S(1)}, u32[]{:S(2)}, u32[]{:S(2)}) %collective-permute-start.20) | collective-permute-done | bytes 114720 | tf_op jit(solution)/shard_map/ppermute | solution.py:635
  86.7 0.8 finish.1
  (38 shorter events, 10.0 us)
Async XLA Ops:
  1.6 9.7 %collective-permute-start = (bf16[3,8,2048]{2,1,0:T(8,128)(2,1)S(1)}, bf16[3,8,2048]{2,1,0:T(8,128)(2,1)S(1)}, u32[]{:S(2)}, u32[]{:S(2)}) collective-permute-start(bf16[3,8,2048]{2,1,0:T(8,128)(2,1)S(1)} %trailing.1), channel_id=1, source_target_pairs={{0,4},{4,8},{8,12},{12,16},{16,20},{20,24},{24,28},{28,0},{1,5},{5... | collective-permute-start | bytes 294920 | tf_op jit(solution)/shard_map/ppermute | solution.py:631
  11.2 4.3 %copy-start.1 = (f32[2048]{0:T(1024)S(1)}, f32[2048]{0:T(1024)}, u32[]{:S(2)}) copy-start(f32[2048]{0:T(1024)} %param.17) | copy-start | bytes 24580
  12.0 7.4 %collective-permute-start.3 = (f32[256,128]{1,0:T(8,128)S(1)}, f32[256,128]{1,0:T(8,128)S(1)}, u32[]{:S(2)}, u32[]{:S(2)}) collective-permute-start(f32[256,128]{1,0:T(8,128)S(1)} %get-tuple-element.98.own), channel_id=1, source_target_pairs={{0,12},{4,8},{8,4},{12,0},{16,28},{20,24},{24,20},{28,16},{1,13},{... | collective-permute-start | bytes 393224 | tf_op jit(solution)/shard_map/ppermute | solution.py:635
  14.6 6.2 %collective-permute-start.2 = (f32[256,128]{1,0:T(8,128)S(1)}, f32[256,128]{1,0:T(8,128)S(1)}, u32[]{:S(2)}, u32[]{:S(2)}) collective-permute-start(f32[256,128]{1,0:T(8,128)S(1)} %get-tuple-element.98.own), channel_id=1, source_target_pairs={{0,8},{4,12},{8,0},{12,4},{16,24},{20,28},{24,16},{28,20},{1,9},{5... | collective-permute-start | bytes 393224 | tf_op jit(solution)/shard_map/ppermute | solution.py:635
  15.0 5.8 %collective-permute-start.1 = (f32[256,128]{1,0:T(8,128)S(1)}, f32[256,128]{1,0:T(8,128)S(1)}, u32[]{:S(2)}, u32[]{:S(2)}) collective-permute-start(f32[256,128]{1,0:T(8,128)S(1)} %get-tuple-element.98.own), channel_id=1, source_target_pairs={{0,4},{4,0},{8,12},{12,8},{16,20},{20,16},{24,28},{28,24},{1,5},{5... | collective-permute-start | bytes 393224 | tf_op jit(solution)/shard_map/ppermute | solution.py:635
  19.4 7.6 %copy-start = (f32[2048]{0:T(1024)S(1)}, f32[2048]{0:T(1024)}, u32[]{:S(2)}) copy-start(f32[2048]{0:T(1024)} %param.18) | copy-start | bytes 24580
  21.5 5.5 %collective-permute-start.4 = (bf16[256,128]{1,0:T(8,128)(2,1)S(1)}, bf16[256,128]{1,0:T(8,128)(2,1)S(1)}, u32[]{:S(2)}, u32[]{:S(2)}) collective-permute-start(bf16[256,128]{1,0:T(8,128)(2,1)S(1)} %get-tuple-element.102), channel_id=1, source_target_pairs={{0,16},{4,20},{8,24},{12,28},{16,0},{20,4},{24,8},{28,12},{1,17},{... | collective-permute-start | bytes 196616 | tf_op jit(solution)/shard_map/ppermute | solution.py:635
  31.6 3.0 %collective-permute-start.7 = (f32[2,256]{1,0:T(2,128)S(1)}, f32[2,256]{1,0:T(2,128)S(1)}, u32[]{:S(2)}, u32[]{:S(2)}) collective-permute-start(f32[2,256]{1,0:T(2,128)S(1)} %get-tuple-element.105.refs_0_), channel_id=1, source_target_pairs={{0,3},{1,2},{2,1},{3,0},{4,7},{5,6},{6,5},{7,4},{8,11},{9,10},{10,... | collective-permute-start | bytes 6152 | tf_op jit(solution)/shard_map/ppermute | solution.py:635
  31.6 3.6 %collective-permute-start.6 = (f32[2,256]{1,0:T(2,128)S(1)}, f32[2,256]{1,0:T(2,128)S(1)}, u32[]{:S(2)}, u32[]{:S(2)}) collective-permute-start(f32[2,256]{1,0:T(2,128)S(1)} %get-tuple-element.105.refs_0_), channel_id=1, source_target_pairs={{0,2},{1,3},{2,0},{3,1},{4,6},{5,7},{6,4},{7,5},{8,10},{9,11},{10,... | collective-permute-start | bytes 6152 | tf_op jit(solution)/shard_map/ppermute | solution.py:635
  33.0 2.2 %collective-permute-start.5 = (f32[2,256]{1,0:T(2,128)S(1)}, f32[2,256]{1,0:T(2,128)S(1)}, u32[]{:S(2)}, u32[]{:S(2)}) collective-permute-start(f32[2,256]{1,0:T(2,128)S(1)} %get-tuple-element.105.refs_0_), channel_id=1, source_target_pairs={{0,1},{1,0},{2,3},{3,2},{4,5},{5,4},{6,7},{7,6},{8,9},{9,8},{10,11... | collective-permute-start | bytes 6152 | tf_op jit(solution)/shard_map/ppermute | solution.py:635
  39.1 7.5 %collective-permute-start.10 = (f32[256,128]{1,0:T(8,128)S(1)}, f32[256,128]{1,0:T(8,128)S(1)}, u32[]{:S(2)}, u32[]{:S(2)}) collective-permute-start(f32[256,128]{1,0:T(8,128)S(1)} %get-tuple-element.121.own), channel_id=1, source_target_pairs={{0,12},{4,8},{8,4},{12,0},{16,28},{20,24},{24,20},{28,16},{1,13},{... | collective-permute-start | bytes 393224 | tf_op jit(solution)/shard_map/ppermute | solution.py:635
  41.2 7.4 %collective-permute-start.9 = (f32[256,128]{1,0:T(8,128)S(1)}, f32[256,128]{1,0:T(8,128)S(1)}, u32[]{:S(2)}, u32[]{:S(2)}) collective-permute-start(f32[256,128]{1,0:T(8,128)S(1)} %get-tuple-element.121.own), channel_id=1, source_target_pairs={{0,8},{4,12},{8,0},{12,4},{16,24},{20,28},{24,16},{28,20},{1,9},{5... | collective-permute-start | bytes 393224 | tf_op jit(solution)/shard_map/ppermute | solution.py:635
  41.8 6.7 %collective-permute-start.8 = (f32[256,128]{1,0:T(8,128)S(1)}, f32[256,128]{1,0:T(8,128)S(1)}, u32[]{:S(2)}, u32[]{:S(2)}) collective-permute-start(f32[256,128]{1,0:T(8,128)S(1)} %get-tuple-element.121.own), channel_id=1, source_target_pairs={{0,4},{4,0},{8,12},{12,8},{16,20},{20,16},{24,28},{28,24},{1,5},{5... | collective-permute-start | bytes 393224 | tf_op jit(solution)/shard_map/ppermute | solution.py:635
  49.3 6.6 %collective-permute-start.11 = (bf16[256,128]{1,0:T(8,128)(2,1)S(1)}, bf16[256,128]{1,0:T(8,128)(2,1)S(1)}, u32[]{:S(2)}, u32[]{:S(2)}) collective-permute-start(bf16[256,128]{1,0:T(8,128)(2,1)S(1)} %get-tuple-element.124), channel_id=1, source_target_pairs={{0,16},{4,20},{8,24},{12,28},{16,0},{20,4},{24,8},{28,12},{1,17},{... | collective-permute-start | bytes 196616 | tf_op jit(solution)/shard_map/ppermute | solution.py:635
  56.1 7.9 %collective-permute-start.13 = (f32[328,128]{1,0:T(8,128)S(1)}, f32[328,128]{1,0:T(8,128)S(1)}, u32[]{:S(2)}, u32[]{:S(2)}) collective-permute-start(f32[328,128]{1,0:T(8,128)S(1)} %get-tuple-element.144), channel_id=1, source_target_pairs={{0,4},{4,0},{8,12},{12,8},{16,20},{20,16},{24,28},{28,24},{1,5},{5... | collective-permute-start | bytes 503816 | tf_op jit(solution)/shard_map/ppermute | solution.py:635
  57.4 6.5 %collective-permute-start.12 = (bf16[3,2,64,128]{3,2,1,0:T(8,128)(2,1)S(1)}, bf16[3,2,64,128]{3,2,1,0:T(8,128)(2,1)S(1)}, u32[]{:S(2)}, u32[]{:S(2)}) collective-permute-start(bf16[3,2,64,128]{3,2,1,0:T(8,128)(2,1)S(1)} %get-tuple-element.133), channel_id=1, source_target_pairs={{0,28},{4,0},{8,4},{12,8},{16,12},{20,16},{24,20},{28,24},{1,29},{... | collective-permute-start | bytes 294920 | tf_op jit(solution)/shard_map/ppermute | solution.py:631
  64.0 5.6 %collective-permute-start.14 = (f32[328,128]{1,0:T(8,128)S(1)}, f32[328,128]{1,0:T(8,128)S(1)}, u32[]{:S(2)}, u32[]{:S(2)}) collective-permute-start(f32[328,128]{1,0:T(8,128)S(1)} %add.4.one), channel_id=1, source_target_pairs={{0,8},{4,12},{8,0},{12,4},{16,24},{20,28},{24,16},{28,20},{1,9},{5... | collective-permute-start | bytes 503816 | tf_op jit(solution)/shard_map/ppermute | solution.py:635
  69.6 9.5 %collective-permute-start.15 = (f32[328,128]{1,0:T(8,128)S(1)}, f32[328,128]{1,0:T(8,128)S(1)}, u32[]{:S(2)}, u32[]{:S(2)}) collective-permute-start(f32[328,128]{1,0:T(8,128)S(1)} %add.5.one), channel_id=1, source_target_pairs={{0,16},{4,20},{8,24},{12,28},{16,0},{20,4},{24,8},{28,12},{1,17},{... | collective-permute-start | bytes 503816 | tf_op jit(solution)/shard_map/ppermute | solution.py:635
  71.7 8.1 %collective-permute-start.19 = (f32[224,128]{1,0:T(8,128)S(1)}, f32[224,128]{1,0:T(8,128)S(1)}, u32[]{:S(2)}, u32[]{:S(2)}) collective-permute-start(f32[224,128]{1,0:T(8,128)S(1)} %get-tuple-element.147.own), channel_id=1, source_target_pairs={{0,12},{4,8},{8,4},{12,0},{16,28},{20,24},{24,20},{28,16},{1,13},{... | collective-permute-start | bytes 344072 | tf_op jit(solution)/shard_map/ppermute | solution.py:635
  74.1 6.9 %collective-permute-start.18 = (f32[224,128]{1,0:T(8,128)S(1)}, f32[224,128]{1,0:T(8,128)S(1)}, u32[]{:S(2)}, u32[]{:S(2)}) collective-permute-start(f32[224,128]{1,0:T(8,128)S(1)} %get-tuple-element.147.own), channel_id=1, source_target_pairs={{0,8},{4,12},{8,0},{12,4},{16,24},{20,28},{24,16},{28,20},{1,9},{5... | collective-permute-start | bytes 344072 | tf_op jit(solution)/shard_map/ppermute | solution.py:635
  74.4 6.6 %collective-permute-start.17 = (f32[224,128]{1,0:T(8,128)S(1)}, f32[224,128]{1,0:T(8,128)S(1)}, u32[]{:S(2)}, u32[]{:S(2)}) collective-permute-start(f32[224,128]{1,0:T(8,128)S(1)} %get-tuple-element.147.own), channel_id=1, source_target_pairs={{0,4},{4,0},{8,12},{12,8},{16,20},{20,16},{24,28},{28,24},{1,5},{5... | collective-permute-start | bytes 344072 | tf_op jit(solution)/shard_map/ppermute | solution.py:635
  79.1 7.6 %collective-permute-start.16 = (f32[328,128]{1,0:T(8,128)S(1)}, f32[328,128]{1,0:T(8,128)S(1)}, u32[]{:S(2)}, u32[]{:S(2)}) collective-permute-start(f32[328,128]{1,0:T(8,128)S(1)} %add.6.refs_0_), channel_id=1, source_target_pairs={{0,4},{4,0},{8,12},{12,8},{16,20},{20,16},{24,28},{28,24},{1,5},{5... | collective-permute-start | bytes 503816 | tf_op jit(solution)/shard_map/ppermute | solution.py:635
  81.0 5.8 %collective-permute-start.20 = (f32[224,128]{1,0:T(8,128)S(1)}, f32[224,128]{1,0:T(8,128)S(1)}, u32[]{:S(2)}, u32[]{:S(2)}) collective-permute-start(f32[224,128]{1,0:T(8,128)S(1)} %add.7.refs_2_), channel_id=1, source_target_pairs={{0,16},{4,20},{8,24},{12,28},{16,0},{20,4},{24,8},{28,12},{1,17},{... | collective-permute-start | bytes 344072 | tf_op jit(solution)/shard_map/ppermute | solution.py:635
